TPU v7x, 32 devices: a whole 2x2x4 slice. The times are simulated.
32 devices in a mesh: dp: 16 (over z, y, core), tensor: 2 (over x).
Axes of the slice: x: 2, y: 2, z: 4, core: 2. Of those that a mesh axis runs over, the one named last changes fastest.
Arguments:
- residual: bfloat16 [16384, 1024], P(('dp', 'tensor')), may hold values from -6 to 6
- cotangent: bfloat16 [16384, 1024], P(('dp', 'tensor')), may hold values from -6 to 6
- sequence_ids: int32 [16384], P('dp'), may hold values from 0 to 4, as said below
- inner_proj: float32 [2, 1024, 2048], P(None, 'dp', 'tensor'), may hold values from -0.1875 to 0.1875
- inner_mean: float32 [2, 1024, 2048], P(None, 'dp', 'tensor'), may hold values from -40 to 40
- inner_square: float32 [2, 1024, 2048], P(None, 'dp', 'tensor'), may hold values from 204.8 to 819.2
- shared_proj: float32 [1024, 288], P(('dp', 'tensor')), may hold values from -0.1875 to 0.1875
- shared_mean: float32 [1024, 288], P(('dp', 'tensor')), may hold values from -40 to 40
- shared_square: float32 [1024, 288], P(('dp', 'tensor')), may hold values from 204.8 to 819.2
- outer_proj: float32 [2048, 1024], P('tensor', 'dp'), may hold values from -0.125 to 0.125
- outer_mean: float32 [2048, 1024], P('tensor', 'dp'), may hold values from -64 to 64
- outer_square: float32 [2048, 1024], P('tensor', 'dp'), may hold values from 655.36 to 2621.44
- conv_params: float32 [5, 2304], P(None, ('dp', 'tensor')), may hold values from -3 to 3
- conv_mean: float32 [5, 2304], P(None, ('dp', 'tensor')), may hold values from -40 to 40
- conv_square: float32 [5, 2304], P(None, ('dp', 'tensor')), may hold values from 204.8 to 819.2
- norm_gains: float32 [3072], P(('dp', 'tensor')), may hold values from 0.5 to 1.5
- gains_mean: float32 [3072], P(('dp', 'tensor')), may hold values from -40 to 40
- gains_square: float32 [3072], P(('dp', 'tensor')), may hold values from 204.8 to 819.2
- head_params: float32 [3, 32], P(None, 'tensor'), may hold values from -10 to 1, as said below
- heads_mean: float32 [3, 32], P(None, 'tensor'), may hold values from -40 to 40
- heads_square: float32 [3, 32], P(None, 'tensor'), may hold values from 204.8 to 819.2
Outputs:
- block_out: bfloat16 [16384, 1024], P(('dp', 'tensor'))
- residual_grad: bfloat16 [16384, 1024], P(('dp', 'tensor'))
- inner_next: float32 [2, 1024, 2048], P(None, 'dp', 'tensor')
- inner_mean_next: float32 [2, 1024, 2048], P(None, 'dp', 'tensor')
- inner_square_next: float32 [2, 1024, 2048], P(None, 'dp', 'tensor')
- shared_next: float32 [1024, 288], P(('dp', 'tensor'))
- shared_mean_next: float32 [1024, 288], P(('dp', 'tensor'))
- shared_square_next: float32 [1024, 288], P(('dp', 'tensor'))
- outer_next: float32 [2048, 1024], P('tensor', 'dp')
- outer_mean_next: float32 [2048, 1024], P('tensor', 'dp')
- outer_square_next: float32 [2048, 1024], P('tensor', 'dp')
- conv_next: float32 [5, 2304], P(None, ('dp', 'tensor'))
- conv_mean_next: float32 [5, 2304], P(None, ('dp', 'tensor'))
- conv_square_next: float32 [5, 2304], P(None, ('dp', 'tensor'))
- gains_next: float32 [3072], P(('dp', 'tensor'))
- gains_mean_next: float32 [3072], P(('dp', 'tensor'))
- gains_square_next: float32 [3072], P(('dp', 'tensor'))
- heads_next: float32 [3, 32], P(None, 'tensor')
- heads_mean_next: float32 [3, 32], P(None, 'tensor')
- heads_square_next: float32 [3, 32], P(None, 'tensor')
Inputs may be any that keep to these rules, and one draw needn't show every extreme that they name: `sequence_ids`: within each data group (aligned block of 1024 positions) the values never fall; positions with one value below 4 form one sequence; the value 4 marks empty positions at the group's end. Every group has at least half of its positions in sequences, and in one group a single sequence fills all 1024 positions. `head_params`: row 0 is the step bias, row 1 the logarithm of the decay rate, row 2 the skip factor, which is positive.
All inputs are finite; a program needn't handle non-finite values.
Results may differ from a plain program's by a relative error of at most 0.008.
The roundings to bfloat16 on the way count: a program that leaves them out, or rounds other values in their place, can miss the bound.
Values may be sent and summed in bfloat16 or wider, within the bound.
No kernel may reach another device: no remote copies, remote signals or barrier semaphores. Data moves between devices by JAX's collectives and lax.ppermute only.
A program may use at most 192 MiB of HBM per device.

v0:
```python
import jax
import jax.numpy as jnp
from jax import lax
from jax.sharding import PartitionSpec as P

D = 1024
H = 32
N = 128
DI = 2048
Q = 256
SEQ_SLOTS = 4
STEP = 10


highest = lax.Precision.HIGHEST
norm_epsilon = 1e-05
beta_first = 0.9
beta_second = 0.95
adam_epsilon = 1e-08
weight_decay = 0.1
rate_matrix = 0.02
rate_vector = 0.3
rate_heads = 1.0


def rounded(value):
    return lax.optimization_barrier(value.astype(jnp.bfloat16)).astype(jnp.float32)


def convolve(channels, weights, segment):
    length = channels.shape[0]
    kernel_size = weights.shape[0] - 1
    summed = weights[kernel_size][None, :] + weights[kernel_size - 1][None, :] * channels
    for offset in range(1, kernel_size):
        shifted = jnp.concatenate(
            [jnp.zeros((offset, channels.shape[1]), jnp.float32), channels[: length - offset]],
            axis=0,
        )
        earlier = jnp.concatenate([jnp.full((offset,), -1, jnp.int32), segment[: length - offset]])
        matches = (earlier == segment).astype(jnp.float32)
        summed = summed + weights[kernel_size - 1 - offset][None, :] * shifted * matches[:, None]
    return jax.nn.silu(summed)


def scan_state(mixed, step_input, head_values, segment, block, head_size, state_size):
    length = mixed.shape[0]
    heads_here = step_input.shape[1]
    inner_width = heads_here * head_size
    blocks = length // block
    values = mixed[:, :inner_width].reshape(blocks, block, heads_here, head_size)
    in_state = mixed[:, inner_width : inner_width + state_size].reshape(blocks, block, state_size)
    out_state = mixed[:, inner_width + state_size :].reshape(blocks, block, state_size)
    step_size = jax.nn.softplus(step_input + head_values[0][None, :])
    step_blocks = step_size.reshape(blocks, block, heads_here).transpose(0, 2, 1)
    log_decay = -step_blocks * jnp.exp(head_values[1])[None, :, None]
    running = jnp.cumsum(log_decay, axis=2)
    segments = segment.reshape(blocks, block)
    places = jnp.arange(block)
    causal = places[:, None] >= places[None, :]
    allowed = (segments[:, :, None] == segments[:, None, :]) & causal[None]
    spread = running[:, :, :, None] - running[:, :, None, :]
    kernel = jnp.exp(jnp.where(allowed[:, None], spread, -1e30))
    scores = jnp.einsum("bin,bjn->bij", out_state, in_state, precision=highest)
    mixing = kernel * scores[:, None] * step_blocks[:, :, None, :]
    local_part = jnp.einsum("bhij,bjhp->bihp", mixing, values, precision=highest)
    ending = running[:, :, -1:]
    tail_match = (segments == segments[:, -1:]).astype(jnp.float32)
    tail_weight = jnp.exp(ending - running) * step_blocks * tail_match[:, None, :]
    weighted = values * tail_weight.transpose(0, 2, 1)[..., None]
    fresh_state = jnp.einsum("bjhp,bjn->bhpn", weighted, in_state, precision=highest)
    linked = jnp.concatenate(
        [jnp.zeros((1,), jnp.float32), (segments[1:, -1] == segments[:-1, -1]).astype(jnp.float32)]
    )
    factors = jnp.exp(ending[:, :, 0]) * linked[:, None]

    def carry_state(previous, pieces):
        current = pieces[0] + pieces[1][:, None, None] * previous
        return (current, previous)

    initial = jnp.zeros((heads_here, head_size, state_size), jnp.float32)
    entering = lax.scan(carry_state, initial, (fresh_state, factors))[1]
    before_end = jnp.concatenate([jnp.full((1,), -1, jnp.int32), segments[:-1, -1]])
    inherit = (segments == before_end[:, None]).astype(jnp.float32)
    entry_scale = jnp.exp(running) * inherit[:, None, :]
    carried = (
        jnp.einsum("bhpn,bin->bihp", entering, out_state, precision=highest)
        * entry_scale.transpose(0, 2, 1)[..., None]
    )
    result = local_part + carried + head_values[2][None, None, :, None] * values
    return result.reshape(length, inner_width)


def adam_step(weight, moment, square, gradient, rate, decay):
    moment_next = beta_first * moment + (1.0 - beta_first) * gradient
    square_next = beta_second * square + (1.0 - beta_second) * gradient * gradient
    moment_hat = moment_next / (1.0 - beta_first**STEP)
    square_hat = square_next / (1.0 - beta_second**STEP)
    weight_next = weight - rate * (
        moment_hat / (jnp.sqrt(square_hat) + adam_epsilon) + decay * weight
    )
    return (weight_next, moment_next, square_next)


def shards(
    residual,
    cotangent,
    sequence_ids,
    inner_proj,
    inner_mean,
    inner_square,
    shared_proj,
    shared_mean,
    shared_square,
    outer_proj,
    outer_mean,
    outer_square,
    conv_params,
    conv_mean,
    conv_square,
    norm_gains,
    gains_mean,
    gains_square,
    head_params,
    heads_mean,
    heads_square,
):
    tensor_rank = lax.axis_index("tensor")
    inner_full, outer_full = (
        lax.all_gather(inner_proj.astype(jnp.bfloat16), "dp", axis=1, tiled=True),
        lax.all_gather(outer_proj.astype(jnp.bfloat16), "dp", axis=1, tiled=True),
    )
    shared_full, conv_full, gains_full = (
        lax.all_gather(shared_proj, ("dp", "tensor"), axis=0, tiled=True),
        lax.all_gather(conv_params, ("dp", "tensor"), axis=1, tiled=True),
        lax.all_gather(norm_gains, ("dp", "tensor"), axis=0, tiled=True),
    )
    inner_width = inner_full.shape[2]
    heads_here = head_params.shape[1]
    head_size = inner_width // heads_here
    rows_here = residual.shape[0]
    head_columns = 2 * inner_width
    shared_low = shared_full.astype(jnp.bfloat16)
    shared_back = shared_low.astype(jnp.float32)
    projection = jnp.concatenate([inner_full[0], inner_full[1], shared_low], axis=1)
    pre_gain = gains_full[:D]
    norm_gain = lax.dynamic_slice_in_dim(gains_full, D + tensor_rank * inner_width, inner_width)
    live_mask = sequence_ids < SEQ_SLOTS
    live_rows = live_mask.astype(jnp.float32)
    tokens = residual.astype(jnp.float32)
    inverse = lax.rsqrt(jnp.mean(tokens * tokens, axis=1, keepdims=True) + norm_epsilon)
    normal_tokens = tokens * inverse
    normed = (normal_tokens * pre_gain[None, :]).astype(jnp.bfloat16)
    gathered = lax.all_gather(normed, "tensor", axis=0, tiled=True)
    projected = jnp.dot(gathered, projection, preferred_element_type=jnp.float32)
    gate_input = projected[:, :inner_width]
    common = projected[:, head_columns:]
    channels = jnp.concatenate([projected[:, inner_width:head_columns], common[:, : 2 * N]], axis=1)
    conv_here = jnp.concatenate(
        [
            lax.dynamic_slice_in_dim(conv_full, tensor_rank * inner_width, inner_width, 1),
            conv_full[:, DI:],
        ],
        axis=1,
    )
    step_input = lax.dynamic_slice_in_dim(common, 2 * N + tensor_rank * heads_here, heads_here, 1)
    conv_out, conv_pull = jax.vjp(
        lambda source, kernel_weights: convolve(source, kernel_weights, sequence_ids),
        channels,
        conv_here,
    )
    mixed_channels = rounded(conv_out)
    ssd_out, ssd_pull = jax.vjp(
        lambda source, step_values, head_values: scan_state(
            source, step_values, head_values, sequence_ids, Q, head_size, N
        ),
        mixed_channels,
        step_input,
        head_params,
    )
    gate_sigmoid = jax.nn.sigmoid(gate_input)
    gate_silu = gate_input * gate_sigmoid
    gated_out = ssd_out * gate_silu
    squares = lax.psum(jnp.sum(gated_out * gated_out, axis=1), "tensor")
    norm_scale = lax.rsqrt(squares / DI + norm_epsilon)[:, None]
    scaled = (gated_out * norm_scale * norm_gain[None, :]).astype(jnp.bfloat16)
    branch = lax.psum_scatter(
        jnp.dot(scaled, outer_full, preferred_element_type=jnp.float32).astype(jnp.bfloat16),
        "tensor",
        scatter_dimension=0,
        tiled=True,
    ).astype(jnp.float32)
    live_here = lax.dynamic_slice_in_dim(live_rows, tensor_rank * rows_here, rows_here)
    block_out = (tokens + branch * live_here[:, None]).astype(jnp.bfloat16)
    cotangent_all = lax.all_gather(cotangent, "tensor", axis=0, tiled=True)
    returned = jnp.where(live_mask[:, None], cotangent_all, jnp.zeros_like(cotangent_all))
    outer_grad = jnp.einsum("tc,td->cd", scaled, returned, preferred_element_type=jnp.float32)
    scaled_grad = jnp.einsum("td,cd->tc", returned, outer_full, preferred_element_type=jnp.float32)
    weighted = scaled_grad * norm_gain[None, :]
    gain_grad = jnp.sum(scaled_grad * gated_out * norm_scale, axis=0)
    crossed = lax.psum(jnp.sum(weighted * gated_out, axis=1), "tensor")
    gated_grad = norm_scale * weighted - gated_out * norm_scale**3 * (crossed[:, None] / DI)
    ssd_grad = rounded(gated_grad * gate_silu)
    gate_grad = gated_grad * ssd_out * gate_sigmoid * (1.0 + gate_input * (1.0 - gate_sigmoid))
    mixed_grad, step_grad, head_grad = ssd_pull(ssd_grad)
    channels_grad, conv_grad_here = conv_pull(mixed_grad)
    product_grad = jnp.concatenate([gate_grad, channels_grad[:, :inner_width]], axis=1).astype(
        jnp.bfloat16
    )
    step_full = lax.dynamic_update_slice_in_dim(
        jnp.zeros((step_grad.shape[0], H), jnp.float32), step_grad, tensor_rank * heads_here, 1
    )
    common_grad = jnp.concatenate([channels_grad[:, inner_width:], step_full], axis=1)
    inner_grad = jnp.einsum("td,tc->dc", gathered, product_grad, preferred_element_type=jnp.float32)
    shared_grad = jnp.einsum(
        "td,tc->dc", gathered.astype(jnp.float32), common_grad, precision=highest
    )
    from_heads = jnp.einsum(
        "tc,dc->td", product_grad, projection[:, :head_columns], preferred_element_type=jnp.float32
    )
    from_common = jnp.einsum("tc,dc->td", common_grad, shared_back, precision=highest)
    normed_grad = lax.psum_scatter(
        from_heads + from_common, "tensor", scatter_dimension=0, tiled=True
    )
    pre_grad = jnp.sum(normed_grad * normal_tokens, axis=0)
    normal_grad = normed_grad * pre_gain[None, :]
    centered = normal_grad - normal_tokens * jnp.mean(
        normal_grad * normal_tokens, axis=1, keepdims=True
    )
    residual_grad = (cotangent.astype(jnp.float32) + inverse * centered).astype(jnp.bfloat16)
    inner_stack = jnp.stack([inner_grad[:, :inner_width], inner_grad[:, inner_width:]])
    conv_inner = lax.dynamic_update_slice_in_dim(
        jnp.zeros((conv_full.shape[0], DI), jnp.float32),
        conv_grad_here[:, :inner_width],
        tensor_rank * inner_width,
        1,
    )
    conv_grad = jnp.concatenate([conv_inner, conv_grad_here[:, inner_width:]], axis=1)
    gain_inner = lax.dynamic_update_slice_in_dim(
        jnp.zeros((DI,), jnp.float32), gain_grad, tensor_rank * inner_width, 0
    )
    gains_grad = jnp.concatenate([pre_grad, gain_inner])
    inner_part, outer_part = (
        lax.psum_scatter(inner_stack, "dp", scatter_dimension=1, tiled=True),
        lax.psum_scatter(outer_grad, "dp", scatter_dimension=1, tiled=True),
    )
    shared_part, conv_part, gains_part = (
        lax.psum_scatter(shared_grad, ("dp", "tensor"), scatter_dimension=0, tiled=True),
        lax.psum_scatter(conv_grad, ("dp", "tensor"), scatter_dimension=1, tiled=True),
        lax.psum_scatter(gains_grad, ("dp", "tensor"), scatter_dimension=0, tiled=True),
    )
    heads_part = lax.psum(head_grad, "dp")
    inner_new = adam_step(
        inner_proj, inner_mean, inner_square, inner_part, rate_matrix, weight_decay
    )
    shared_new = adam_step(
        shared_proj, shared_mean, shared_square, shared_part, rate_matrix, weight_decay
    )
    outer_new = adam_step(
        outer_proj, outer_mean, outer_square, outer_part, rate_matrix, weight_decay
    )
    conv_new = adam_step(conv_params, conv_mean, conv_square, conv_part, rate_vector, 0.0)
    gains_new = adam_step(norm_gains, gains_mean, gains_square, gains_part, rate_vector, 0.0)
    heads_new = adam_step(head_params, heads_mean, heads_square, heads_part, rate_heads, 0.0)
    return (
        block_out,
        residual_grad,
        inner_new[0],
        inner_new[1],
        inner_new[2],
        shared_new[0],
        shared_new[1],
        shared_new[2],
        outer_new[0],
        outer_new[1],
        outer_new[2],
        conv_new[0],
        conv_new[1],
        conv_new[2],
        gains_new[0],
        gains_new[1],
        gains_new[2],
        heads_new[0],
        heads_new[1],
        heads_new[2],
    )


def solution(mesh):
    return jax.shard_map(
        shards,
        mesh=mesh,
        in_specs=(
            P(("dp", "tensor"), None),
            P(("dp", "tensor"), None),
            P("dp"),
            P(None, "dp", "tensor"),
            P(None, "dp", "tensor"),
            P(None, "dp", "tensor"),
            P(("dp", "tensor"), None),
            P(("dp", "tensor"), None),
            P(("dp", "tensor"), None),
            P("tensor", "dp"),
            P("tensor", "dp"),
            P("tensor", "dp"),
            P(None, ("dp", "tensor")),
            P(None, ("dp", "tensor")),
            P(None, ("dp", "tensor")),
            P(("dp", "tensor")),
            P(("dp", "tensor")),
            P(("dp", "tensor")),
            P(None, "tensor"),
            P(None, "tensor"),
            P(None, "tensor"),
        ),
        out_specs=(
            P(("dp", "tensor"), None),
            P(("dp", "tensor"), None),
            P(None, "dp", "tensor"),
            P(None, "dp", "tensor"),
            P(None, "dp", "tensor"),
            P(("dp", "tensor"), None),
            P(("dp", "tensor"), None),
            P(("dp", "tensor"), None),
            P("tensor", "dp"),
            P("tensor", "dp"),
            P("tensor", "dp"),
            P(None, ("dp", "tensor")),
            P(None, ("dp", "tensor")),
            P(None, ("dp", "tensor")),
            P(("dp", "tensor")),
            P(("dp", "tensor")),
            P(("dp", "tensor")),
            P(None, "tensor"),
            P(None, "tensor"),
            P(None, "tensor"),
        ),
        check_vma=False,
    )
```

profile of v0, /device:TPU:0, one launch (start us, length us, event | category | flops | bytes accessed | tf_op | source)
XLA Modules:
  0.0 904.1 jit_solution(3842752920551107949)
XLA Ops:
  10.0 42.9 %all-reduce.20 = f32[3072]{0:T(1024)S(1)} all-reduce(f32[3072]{0:T(1024)S(1)} %dynamic-update-slice), channel_id=1, replica_groups=mesh['dp'=16,'tensor'=2] {'dp','tensor'}, use_global_device_ids=true, to_apply=%add.20 | all-reduce | flops 3072 | bytes 24576
  59.5 67.3 %all-gather = f32[32,72,5]{1,2,0:T(8,128)S(1)} all-gather(f32[1,72,5]{1,2,0:T(8,128)S(1)} %bitcast.282), channel_id=1, replica_groups=mesh['dp'=16,'tensor'=2] {'dp','tensor'}, dimensions={0}, use_global_device_ids=true | all-gather | bytes 47520 | tf_op jit(solution)/shard_map/all_gather | solution.py:134
  127.9 68.3 %all_gather.25 = bf16[1024,288]{1,0:T(8,128)(2,1)S(1)} all-gather(bf16[32,288]{1,0:T(8,128)(2,1)S(1)} %convert.25), channel_id=1, replica_groups=mesh['dp'=16,'tensor'=2] {'dp','tensor'}, dimensions={0}, use_global_device_ids=true | all-gather | bytes 608256 | tf_op jit(solution)/shard_map/all_gather | solution.py:133
  202.3 8.4 fusion.25
  219.0 7.6 multiply_convert_fusion
  254.5 12.5 %while.34 = (s32[]{:T(128)}, f32[16,64,128]{2,1,0:T(8,128)S(1)}, f32[4,16,64,128]{3,2,1,0:T(8,128)S(1)}, f32[4,16,1,1]{1,3,2,0:T(1,128)}, f32[4,16,64,128]{3,2,1...) while((s32[]{:T(128)}, f32[16,64,128]{2,1,0:T(8,128)S(1)}, ...), condition=%wide.region_4.5_spmd.clone, body=%wide.region_3.4_spmd.clone.sunk | while | flops 524291 | bytes 2622776 | solution.py:81
  272.4 13.2 %fusion.35 = f32[4,256,16,64]{1,3,2,0:T(8,128)S(1)} fusion(f32[4,256,16,64]{1,3,2,0:T(8,128)S(1)} %fusion.142, f32[4,256,16,64]{1,0,3,2:T(4,128)S(1)} %copy-done.1, f32[4,16,256]{2,1,0:T(8,128)S(1)} %bitcast.279, f32[4,256,256]{2,1,0:T(8,128)S(1)} %fusion.141, f32[4,16,256]{2,1,0:T(8,128)S(1)} %copy-done.41, pred[4,256,256]{2,1,0:T(8,128)(4,1)S(1)} %copy-done.36, ...), kind=kOutput, calls=%fused_computation.64 | convolution fusion | flops 3242196992 | bytes 16187456 | tf_op jit(solution)/shard_map/jvp(bhij,bjhp->bihp)/dot_general | solution.py:65
  289.5 7.0 multiply_reduce_fusion.11
  302.9 7.3 fusion.85
  310.4 70.4 %reduce-scatter.15.cloned.1.call-done = f32[1024,64]{0,1:T(8,128)} async-done(((f32[1024,1024]{0,1:T(8,128)}), f32[1024,64]{0,1:T(8,128)}) %reduce-scatter.15.cloned.1.call-update) | async-done | bytes 262160 | tf_op jit(solution)/shard_map/reduce_scatter | solution.py:244
  383.0 41.1 %all-gather.10.cloned.1.call-done = bf16[1024,1024]{0,1:T(8,128)(2,1)} async-done(((bf16[1024,64]{0,1:T(8,128)(2,1)}), bf16[1024,1024]{0,1:T(8,128)(2,1)}) %all-gather.10.cloned.1.call-update) | async-done | bytes 2097168 | tf_op jit(solution)/shard_map/all_gather | solution.py:130
  424.0 9.0 multiply_reduce_fusion.7
  439.4 8.7 multiply_convert_fusion.2
  463.3 7.6 fusion.81
  476.3 11.4 %while.35 = (s32[]{:T(128)}, f32[16,64,128]{2,1,0:T(8,128)S(1)}, f32[4,16,64,128]{3,2,1,0:T(8,128)}, f32[4,16]{1,0:T(4,128)S(1)}, f32[4,16,64,128]{3,2,1,0:T(8,1...) while((s32[]{:T(128)}, f32[16,64,128]{2,1,0:T(8,128)S(1)}, ...), condition=%wide.region_13.14_spmd.clone, body=%wide.region_11.13_spmd.clone.sunk | while | flops 786420 | bytes 3146260 | solution.py:81
  488.3 10.8 %fusion.78 = f32[4,256,128]{2,1,0:T(8,128)} fusion(f32[4,16,64,128]{3,2,1,0:T(8,128)} %get-tuple-element.197, f32[4,256,16,64]{1,0,3,2:T(4,128)} %reshape.282, f32[4,256,16]{1,2,0:T(8,128)S(1)} %copy-done.30), kind=kOutput, calls=%fused_computation.127 | convolution fusion | flops 1611661312 | bytes 6881280 | tf_op jit(solution)/shard_map/transpose(jvp(bjhp,bjn->bhpn))/dot_general | solution.py:70
  503.5 12.9 %fusion.10 = (f32[4,16,256]{2,1,0:T(8,128)}, f32[4,16,256]{2,1,0:T(8,128)}, f32[4,16,256]{2,1,0:T(8,128)S(1)}, f32[4,256,256]{2,1,0:T(8,128)S(1)}) fusion(f32[4,16,256]{2,1,0:T(8,128)S(1)} %bitcast.280, f32[4,256,256]{2,1,0:T(8,128)S(1)} %copy-done.28, f32[4,16,256]{2,1,0:T(8,128)S(1)} %copy-done.42, pred[4,256,256]{2,1,0:T(8,128)(4,1)S(1)} %copy-done.37, ...), kind=kOutput, calls=%fused_computation.20 | convolution fusion | flops 591085568 | bytes 6881280 | tf_op jit(solution)/shard_map/transpose(jvp(bhij,bjhp->bihp))/dot_general | solution.py:65
  519.4 14.6 %bitcast_add_fusion.2 = f32[4,256,16,64]{1,3,2,0:T(8,128)S(1)} fusion(f32[4,256,16,64]{1,3,2,0:T(8,128)} %get-tuple-element.358, f32[4,256,16,64]{1,0,3,2:T(4,128)} %reshape.284, f32[4,16,256]{2,1,0:T(8,128)} %bitcast.278, f32[4,256,256]{2,1,0:T(8,128)} %copy-done.27, f32[4,16,256]{2,1,0:T(8,128)S(1)} %copy-done.42, ...), kind=kOutput, calls=%fused_computation.62 | convolution fusion | flops 3242196992 | bytes 16187456 | tf_op jit(solution)/shard_map/transpose(jvp(bhij,bjhp->bihp))/dot_general | solution.py:65
  540.0 8.6 multiply_reduce_fusion.5
  548.7 7.9 multiply_reduce_fusion.4
  567.4 6.8 multiply_reduce_fusion.2
  580.1 10.1 %reduce-window.16 = f32[4,16,2,128]{3,1,2,0:T(8,128)S(1)} reduce-window(f32[4,16,2,128]{3,1,2,0:T(8,128)S(1)} %copy_bitcast_fusion.1, f32[]{:T(128)} %constant.81.clone.1), window={size=1x1x1x128 pad=0_0x0_0x0_0x0_127}, to_apply=%region_20.21 | reduce-window | flops 2080768 | bytes 131076 | tf_op jit(solution)/shard_map/reduce-window.2
  591.7 6.8 fusion.84
  598.7 8.1 fusion.31
  606.7 6.7 convolution_add_fusion
  614.1 6.9 convolution_convert_fusion
  621.1 6.8 fusion.53
  638.2 30.3 %psum.23 = f32[3,16]{1,0:T(4,128)S(1)} all-reduce(f32[3,16]{1,0:T(4,128)S(1)} %pad_add_fusion.2), channel_id=1, replica_groups=mesh['dp'=16,'tensor'=2] {'dp'}, use_global_device_ids=true, to_apply=%region_40.41 | all-reduce | flops 48 | bytes 384 | tf_op jit(solution)/shard_map/psum | solution.py:251
  669.2 25.4 %reduce-scatter.13.cloned.1.call-done = f32[32,288]{1,0:T(8,128)} async-done(((f32[1024,288]{1,0:T(8,128)}), f32[32,288]{1,0:T(8,128)}) %reduce-scatter.13.cloned.1.call-update) | async-done | bytes 36880 | tf_op jit(solution)/shard_map/reduce_scatter | solution.py:247
  696.1 54.3 %reduce-scatter.9.cloned.1.call-done = f32[512,1024]{1,0:T(8,128)} async-done(((f32[1024,1024]{1,0:T(8,128)}), f32[512,1024]{1,0:T(8,128)}) %reduce-scatter.9.cloned.1.call-update) | async-done | bytes 2097168 | tf_op jit(solution)/shard_map/reduce_scatter | solution.py:221
  752.8 40.9 %all-reduce.23 = (f32[5,2304]{1,0:T(8,128)S(1)}, f32[3072]{0:T(1024)S(1)}) all-reduce(f32[5,2304]{1,0:T(8,128)S(1)} %pad_maximum_fusion.7, f32[3072]{0:T(1024)S(1)} %pad_maximum_fusion.8), channel_id=7, replica_groups=mesh['dp'=16,'tensor'=2] {'dp','tensor'}, use_global_device_ids=true, to_apply=%region_32.33.clone | all-reduce | flops 14592 | bytes 116736
  798.8 95.3 %reduce-scatter.11.cloned.1.call-done = f32[2,64,1024]{2,1,0:T(8,128)} async-done(((f32[2,1024,1024]{2,1,0:T(8,128)}), f32[2,64,1024]{2,1,0:T(8,128)}) %reduce-scatter.11.cloned.1.call-update) | async-done | bytes 524304 | tf_op jit(solution)/shard_map/reduce_scatter | solution.py:243
  (382 shorter events, 175.9 us)
Async XLA Ops:
  7.2 51.2 %copy-start.43 = (s32[1024]{0:T(1024)S(1)}, s32[1024]{0:T(1024)}, u32[]{:S(2)}) copy-start(s32[1024]{0:T(1024)} %param.27) | copy-start | bytes 12292
  7.2 51.6 %copy-start.77 = (f32[3,16]{1,0:T(4,128)S(1)}, f32[3,16]{1,0:T(4,128)}, u32[]{:S(2)}) copy-start(f32[3,16]{1,0:T(4,128)} %param.43) | copy-start | bytes 580
  7.2 52.2 %copy-start.38 = (f32[32,288]{1,0:T(8,128)S(1)}, f32[32,288]{1,0:T(8,128)}, u32[]{:S(2)}) copy-start(f32[32,288]{1,0:T(8,128)} %param.31) | copy-start | bytes 110596
  7.2 52.3 %copy-start.72 = (f32[5,72]{1,0:T(8,128)S(1)}, f32[5,72]{1,0:T(8,128)}, u32[]{:S(2)}) copy-start(f32[5,72]{1,0:T(8,128)} %param.37) | copy-start | bytes 4324
  7.2 191.0 %all-gather.8.cloned.1.call-start = ((), (), s32[]{:S(2)}) async-start(), calls=%async_computation.6 | async-start | bytes 4456448 | tf_op jit(solution)/shard_map/all_gather | solution.py:129
  9.1 193.2 %all-gather.6.cloned.1.call-start = ((), (), s32[]{:S(2)}) async-start(), calls=%async_computation.5 | async-start | bytes 3145728 | tf_op jit(solution)/shard_map/all_gather | solution.py:153
  57.6 244.8 %all-gather.12.cloned.1.call-start = ((), (), s32[]{:S(2)}) async-start(), calls=%async_computation.9 | async-start | bytes 3145728 | tf_op jit(solution)/shard_map/all_gather | solution.py:194
  58.3 322.5 %reduce-scatter.15.cloned.1.call-start = ((), (), s32[]{:S(2)}) async-start(), calls=%async_computation.13 | async-start | bytes 4456448 | tf_op jit(solution)/shard_map/reduce_scatter | solution.py:244
  59.4 170.6 %copy-start.79 = (f32[16]{0:T(128)}, f32[16]{0:T(128)S(1)}, u32[]{:S(2)}) copy-start(f32[16]{0:T(128)S(1)} %get-tuple-element.355) | copy-start | bytes 196
  59.4 171.3 %copy-start.81 = (f32[16]{0:T(128)}, f32[16]{0:T(128)S(1)}, u32[]{:S(2)}) copy-start(f32[16]{0:T(128)S(1)} %get-tuple-element.354) | copy-start | bytes 196
  310.3 70.5 %copy-start.34 = (f32[1024,64]{0,1:T(8,128)S(1)}, f32[1024,64]{0,1:T(8,128)}, u32[]{:S(2)}) copy-start(f32[1024,64]{0,1:T(8,128)} %param.34) | copy-start | bytes 786436
  310.3 70.5 %copy-start.35 = (f32[1024,64]{0,1:T(8,128)S(1)}, f32[1024,64]{0,1:T(8,128)}, u32[]{:S(2)}) copy-start(f32[1024,64]{0,1:T(8,128)} %param.35) | copy-start | bytes 786436
  310.3 113.7 %all-gather.10.cloned.1.call-start = ((), (), s32[]{:S(2)}) async-start(), calls=%async_computation.7 | async-start | bytes 2228224 | tf_op jit(solution)/shard_map/all_gather | solution.py:130
  382.9 311.7 %reduce-scatter.13.cloned.1.call-start = ((), (), s32[]{:S(2)}) async-start(), calls=%async_computation.12 | async-start | bytes 1622016 | tf_op jit(solution)/shard_map/reduce_scatter | solution.py:247
  598.6 151.8 %reduce-scatter.9.cloned.1.call-start = ((), (), s32[]{:S(2)}) async-start(), calls=%async_computation.10 | async-start | bytes 6291456 | tf_op jit(solution)/shard_map/reduce_scatter | solution.py:221
  613.5 181.6 %reduce-scatter.7.cloned.1.call-start = ((), (), s32[]{:S(2)}) async-start(), calls=%async_computation.8 | async-start | bytes 3145728 | tf_op jit(solution)/shard_map/reduce_scatter | solution.py:186
  621.1 273.1 %reduce-scatter.11.cloned.1.call-start = ((), (), s32[]{:S(2)}) async-start(), calls=%async_computation.11 | async-start | bytes 8912896 | tf_op jit(solution)/shard_map/reduce_scatter | solution.py:243
  633.8 34.7 %copy-start.86 = (f32[3,16]{1,0:T(4,128)S(1)}, f32[3,16]{1,0:T(4,128)}, u32[]{:S(2)}) copy-start(f32[3,16]{1,0:T(4,128)} %param.44) | copy-start | bytes 580
  633.8 34.7 %copy-start.87 = (f32[3,16]{1,0:T(4,128)S(1)}, f32[3,16]{1,0:T(4,128)}, u32[]{:S(2)}) copy-start(f32[3,16]{1,0:T(4,128)} %param.45) | copy-start | bytes 580
  633.8 60.8 %copy-start.39 = (f32[32,288]{1,0:T(8,128)S(1)}, f32[32,288]{1,0:T(8,128)}, u32[]{:S(2)}) copy-start(f32[32,288]{1,0:T(8,128)} %param.31) | copy-start | bytes 110596
  633.8 60.8 %copy-start.58 = (f32[32,288]{1,0:T(8,128)S(1)}, f32[32,288]{1,0:T(8,128)}, u32[]{:S(2)}) copy-start(f32[32,288]{1,0:T(8,128)} %param.32) | copy-start | bytes 110596
  633.8 60.8 %copy-start.59 = (f32[32,288]{1,0:T(8,128)S(1)}, f32[32,288]{1,0:T(8,128)}, u32[]{:S(2)}) copy-start(f32[32,288]{1,0:T(8,128)} %param.33) | copy-start | bytes 110596
  633.9 116.5 %copy-start.13 = (bf16[512,1024]{1,0:T(8,128)(2,1)S(1)}, bf16[512,1024]{1,0:T(8,128)(2,1)}, u32[]{:S(2)}) copy-start(bf16[512,1024]{1,0:T(8,128)(2,1)} %param.25) | copy-start | bytes 3145732
  633.9 116.5 %copy-start.53 = (f32[1024]{0:T(1024)S(1)}, f32[1024]{0:T(1024)}, u32[]{:S(2)}) copy-start(f32[1024]{0:T(1024)} %copy-done.52) | copy-start | bytes 12292
  633.9 116.5 %copy-start.67 = (f32[512]{0:T(512)S(1)}, f32[512]{0:T(512)}, u32[]{:S(2)}) copy-start(f32[512]{0:T(512)} %copy-done.66) | copy-start | bytes 6148
  633.9 159.8 %copy-start.92 = (f32[96]{0:T(128)S(1)}, f32[96]{0:T(128)}, u32[]{:S(2)}) copy-start(f32[96]{0:T(128)} %param.40) | copy-start | bytes 1156
  633.9 159.8 %copy-start.93 = (f32[96]{0:T(128)S(1)}, f32[96]{0:T(128)}, u32[]{:S(2)}) copy-start(f32[96]{0:T(128)} %param.41) | copy-start | bytes 1156
  633.9 159.8 %copy-start.94 = (f32[96]{0:T(128)S(1)}, f32[96]{0:T(128)}, u32[]{:S(2)}) copy-start(f32[96]{0:T(128)} %param.42) | copy-start | bytes 1156
  633.9 160.5 %copy-start.73 = (f32[5,72]{1,0:T(8,128)S(1)}, f32[5,72]{1,0:T(8,128)}, u32[]{:S(2)}) copy-start(f32[5,72]{1,0:T(8,128)} %param.37) | copy-start | bytes 4324
  633.9 160.4 %copy-start.83 = (f32[5,72]{1,0:T(8,128)S(1)}, f32[5,72]{1,0:T(8,128)}, u32[]{:S(2)}) copy-start(f32[5,72]{1,0:T(8,128)} %param.38) | copy-start | bytes 4324
  633.9 160.4 %copy-start.84 = (f32[5,72]{1,0:T(8,128)S(1)}, f32[5,72]{1,0:T(8,128)}, u32[]{:S(2)}) copy-start(f32[5,72]{1,0:T(8,128)} %param.39) | copy-start | bytes 4324
  750.4 44.7 %copy-start.15 = (f32[512,1024]{1,0:T(8,128)S(1)}, f32[512,1024]{1,0:T(8,128)}, u32[]{:S(2)}) copy-start(f32[512,1024]{1,0:T(8,128)} %reduce-scatter.9.cloned.1.call-done) | copy-start | bytes 6291460
  (77 other events, 541.2 us)
Sparse Core Ops, SparseCore 0:
  10.8 54.5 all-gather.7
  67.5 32.4 all-gather.5
  101.6 35.7 all-gather.11
  310.4 70.3 reduce-scatter.14
  383.6 40.3 all-gather.9
  598.7 95.8 reduce-scatter.12
  697.0 53.3 reduce-scatter.8
  752.6 32.4 reduce-scatter.6
  789.7 104.4 reduce-scatter.10
where the time goes:
time: 913 us; the launch traced here: 904 us
  waiting for transfers between devices  287 us (31%)
  blocking collectives  261 us (29%)
  matrix products  139 us (15%)
  other arithmetic  125 us (14%)
  local copies, waits for them, and re-layouts  75.4 us (8%)
  between operations  15.7 us (2%)
    reduce_scatter x1, waiting for transfers between devices, shards(): lax.psum_scatter(inner_stack, 'dp', scatter_dimension=1, tiled=True)  95.3 us
    unnamed x2, blocking collectives  83.8 us
    reduce_scatter x1, waiting for transfers between devices, shards(): lax.psum_scatter(outer_grad, 'dp', scatter_dimension=1, tiled=True)  70.4 us
    all_gather x1, blocking collectives, shards(): lax.all_gather(shared_proj, ('dp', 'tensor'), axis=0, tiled=True)  68.3 us
    all_gather x1, blocking collectives, shards(): lax.all_gather(conv_params, ('dp', 'tensor'), axis=1, tiled=True)  67.3 us
    reduce_scatter x1, waiting for transfers between devices, shards(): lax.psum_scatter(from_heads + from_common, 'tensor', scatter_dimension=0,...  54.3 us
    all_gather x1, waiting for transfers between devices, shards(): lax.all_gather(outer_proj.astype(jnp.bfloat16), 'dp', axis=1, tiled=True)  41.1 us
    dot_general x3, matrix products, scan_state(): jnp.einsum('bhij,bjhp->bihp', mixing, values, precision=highest)  40.7 us
  transfers between devices with their start and end apart: 9, of which 5 were waited for; matrix products, arithmetic and copies ran while one was open for 16% of the time, Pallas kernels for 0%

commit v1 on v0

v1 whole, which is shorter than its diff:
```python
import functools

import jax
import jax.numpy as jnp
from jax import lax
from jax.experimental import pallas as pl
from jax.experimental.pallas import tpu as pltpu
from jax.sharding import PartitionSpec as P

D = 1024
H = 32
N = 128
DI = 2048
SEQ_SLOTS = 4
STEP = 10
CHUNK = 128
LANES = 128
CORES = 2
HIGH_AXIS = 4

highest = lax.Precision.HIGHEST
f32 = jnp.float32
bf16 = jnp.bfloat16
norm_epsilon = 1e-05
beta_first = 0.9
beta_second = 0.95
adam_epsilon = 1e-08
weight_decay = 0.1
rate_matrix = 0.02
rate_vector = 0.3
rate_heads = 1.0

SEG, BACK, AHEAD, INHERIT, TAIL, LINKED, NEXT, LIVE = 0, 0, 3, 7, 8, 9, 10, 11


def adam_step(weight, moment, square, gradient, rate, decay):
    moment_next = beta_first * moment + (1.0 - beta_first) * gradient
    square_next = beta_second * square + (1.0 - beta_second) * gradient * gradient
    moment_hat = moment_next / (1.0 - beta_first**STEP)
    square_hat = square_next / (1.0 - beta_second**STEP)
    weight_next = weight - rate * (
        moment_hat / (jnp.sqrt(square_hat) + adam_epsilon) + decay * weight
    )
    return (weight_next, moment_next, square_next)


def swap(value, axis, size, distance):
    return lax.ppermute(value, axis, [(i, i ^ distance) for i in range(size)])


def after(value, *others):
    return lax.optimization_barrier((value,) + others)[0]


def axis_parts(dp):
    high = HIGH_AXIS
    middle = dp // (CORES * high)
    return high, middle


def gather_halves(shard, dp):
    high, middle = axis_parts(dp)
    pieces = [shard[None]]
    for step in range(1, high):
        pieces.append(swap(shard, "dp", dp, step * middle * CORES)[None])
    line = jnp.concatenate(pieces, axis=0)
    lines = [line]
    for step in range(1, middle):
        lines.append(swap(line, "dp", dp, step * CORES))
    plane = jnp.concatenate(lines, axis=0)
    return plane, swap(plane, "dp", dp, 1)


def scatter_sum(keep, send, dp):
    high, middle = axis_parts(dp)
    total = keep.astype(f32) + swap(send, "dp", dp, 1).astype(f32)
    total = total.reshape((middle, high) + total.shape[1:])
    line = total[0]
    for step in range(1, middle):
        line = line + swap(total[step].astype(bf16), "dp", dp, step * CORES).astype(f32)
    block = line[0]
    for step in range(1, high):
        block = block + swap(line[step].astype(bf16), "dp", dp, step * middle * CORES).astype(f32)
    return block


def sum_everywhere(value, dp, nt):
    distance = 1
    while distance < nt:
        value = value + swap(value, "tensor", nt, distance)
        distance *= 2
    distance = 1
    while distance < dp:
        value = value + swap(value, "dp", dp, distance)
        distance *= 2
    return value


def relative_places(dp):
    high, middle = axis_parts(dp)
    return [
        (h * middle + m) * CORES + c for c in range(CORES) for m in range(middle) for h in range(high)
    ]


def call(kernel, grid, in_specs, out_specs, out_shape, scratch, flops, scalars=0):
    params = pltpu.CompilerParams(vmem_limit_bytes=50 * 1024 * 1024)
    moved = sum(2 * s.dtype.itemsize * s.size for s in jax.tree.leaves(out_shape))
    return pl.pallas_call(
        kernel,
        grid_spec=pltpu.PrefetchScalarGridSpec(
            num_scalar_prefetch=scalars,
            grid=grid,
            in_specs=in_specs,
            out_specs=out_specs,
            scratch_shapes=scratch,
        ),
        out_shape=out_shape,
        compiler_params=params,
        cost_estimate=pl.CostEstimate(flops=int(flops), bytes_accessed=int(moved), transcendentals=0),
    )


def whole(shape):
    return pl.BlockSpec(shape, lambda *i: (0,) * len(shape))


def rows(count, width, index=lambda i: i):
    return pl.BlockSpec((count, width), lambda i, *s: (index(i), 0))


def shape(*dims, dtype=f32):
    return jax.ShapeDtypeStruct(dims, dtype)


def split(value):
    high = value.astype(bf16)
    return high, (value - high.astype(f32)).astype(bf16)


def mm(a, b, ca=1, cb=0):
    return lax.dot_general(a, b, (((ca,), (cb,)), ((), ())), preferred_element_type=f32)


def mm_left(value, exact, ca=1, cb=0):
    high, low = split(value)
    return mm(high, exact, ca, cb) + mm(low, exact, ca, cb)


def mm_right(exact, value, ca=1, cb=0):
    high, low = split(value)
    return mm(exact, high, ca, cb) + mm(exact, low, ca, cb)


def mm_both(a, b, ca=1, cb=0):
    a_high, a_low = split(a)
    b_high, b_low = split(b)
    return mm(a_high, b_high, ca, cb) + mm(a_low, b_high, ca, cb) + mm(a_high, b_low, ca, cb)


def softplus(value):
    return jnp.maximum(value, 0.0) + jnp.log1p(jnp.exp(-jnp.abs(value)))


def iota(axis):
    return lax.broadcasted_iota(jnp.int32, (CHUNK, LANES), axis)


def pair_spread(tile, pair, left):
    rows_here = tile.shape[0]
    return jnp.where(
        left[:rows_here],
        jnp.broadcast_to(tile[:, 2 * pair : 2 * pair + 1], (rows_here, LANES)),
        jnp.broadcast_to(tile[:, 2 * pair + 1 : 2 * pair + 2], (rows_here, LANES)),
    )


def assemble_kernel(dp, me, near, far, out, sems):
    half = dp // CORES
    places = relative_places(dp)
    copies = []
    for place, distance in enumerate(places):
        source = near.at[place] if place < half else far.at[place - half]
        copies.append(pltpu.make_async_copy(source, out.at[me[0] ^ distance], sems.at[place]))
    for copy in copies:
        copy.start()
    for copy in copies:
        copy.wait()


def assemble(near, far, dp, dp_rank):
    any_spec = pl.BlockSpec(memory_space=pl.ANY)
    return pl.pallas_call(
        functools.partial(assemble_kernel, dp),
        in_specs=[pl.BlockSpec(memory_space=pltpu.SMEM), any_spec, any_spec],
        out_specs=any_spec,
        out_shape=shape(dp, *near.shape[1:], dtype=near.dtype),
        scratch_shapes=[pltpu.SemaphoreType.DMA((dp,))],
        cost_estimate=pl.CostEstimate(flops=0, bytes_accessed=4 * near.size * 2, transcendentals=0),
    )(dp_rank, near, far).reshape(dp * near.shape[1], near.shape[2])


def scan_kernel(
    tok, gain, wv, shw, conv, skip, hp, aux, segr,
    normed_o, ch_o, pre_o, mix_o, ssd_o, hin_o, step_o,
    win, state,
):
    count = tok.shape[0]
    width = wv.shape[1]
    channels = width + 2 * N

    @pl.when(pl.program_id(0) == 0)
    def _():
        win[0:8, :] = jnp.zeros((8, channels), f32)
        state[...] = jnp.zeros(state.shape, f32)

    x = tok[...].astype(f32)
    inverse = lax.rsqrt(jnp.mean(x * x, axis=1, keepdims=True) + norm_epsilon)
    normed = (x * inverse * gain[...]).astype(bf16)
    normed_o[...] = normed
    win[8 : 8 + count, :width] = mm(normed, wv[...])
    common = mm(normed, shw[...])
    win[8 : 8 + count, width:] = common[:, : 2 * N]
    step_o[...] = common[:, 2 * N :] + hp[0:1, :]
    table = aux[...]
    for start in range(0, channels, 256):
        cols = slice(start, start + 256)
        here = win[8 : 8 + count, cols]
        pre = conv[4:5, cols] + conv[3:4, cols] * here
        for back in range(1, 4):
            pre = pre + conv[3 - back : 4 - back, cols] * (
                win[8 - back : 8 - back + count, cols] * table[:, BACK + back : BACK + back + 1]
            )
        ch_o[:, cols] = here
        pre_o[:, cols] = pre
        mix_o[:, cols] = (pre * jax.nn.sigmoid(pre)).astype(bf16)
    win[0:8, :] = win[count : count + 8, :]

    row, col = iota(0), iota(1)
    left = col < 64
    tri = (row >= col).astype(f32)
    for sub in range(count // CHUNK):
        at = slice(sub * CHUNK, (sub + 1) * CHUNK)
        dt = softplus(step_o[at, :])
        run = jnp.dot(tri, -(dt * hp[1:2, :]), precision=highest, preferred_element_type=f32)
        run_t, dt_t = run.T, dt.T
        allowed = (table[at, SEG : SEG + 1] == segr[:, at]) & (row >= col)
        b_in = mix_o[at, width : width + N]
        c_out = mix_o[at, width + N :]
        scores = mm(c_out, b_in, 1, 1)
        ending = run[CHUNK - 1 : CHUNK, :]
        entry = jnp.exp(run) * table[at, INHERIT : INHERIT + 1]
        tail = jnp.exp(ending - run) * dt * table[at, TAIL : TAIL + 1]
        factor = jnp.exp(ending) * table[at, LINKED : LINKED + 1][CHUNK - 1 :, :]
        entering = state[...]
        hin_o[sub] = entering
        for pair in range(width // LANES):
            lanes = slice(pair * LANES, (pair + 1) * LANES)
            x_pair = mix_o[at, lanes].astype(f32)
            mixing = []
            for head in (2 * pair, 2 * pair + 1):
                spread = run[:, head : head + 1] - run_t[head : head + 1, :]
                decays = jnp.exp(jnp.where(allowed, spread, -1e30))
                mixing.append(decays * scores * dt_t[head : head + 1, :])
            x_cross = jnp.concatenate(
                [jnp.where(left, x_pair, 0.0), jnp.where(left, 0.0, x_pair)], axis=0
            ).astype(bf16)
            local = mm_left(jnp.concatenate(mixing, axis=1), x_cross)
            before = entering[:, lanes]
            carried = mm_right(c_out, before) * pair_spread(entry, pair, left)
            ssd_o[at, lanes] = local + carried + skip[:, lanes] * x_pair
            fresh = mm_right(b_in, x_pair * pair_spread(tail, pair, left), 0, 0)
            state[:, lanes] = pair_spread(factor, pair, left) * before + fresh


def gate_kernel(normed, cot, aux, ssd, wg, out_t, gain, gate_o, sg_o, ret_o, sums_o):
    returned = (cot[...].astype(f32) * aux[:, LIVE : LIVE + 1]).astype(bf16)
    ret_o[...] = returned
    gate = mm(normed[...], wg[...])
    gate_o[...] = gate
    scaled_grad = mm(returned, out_t[...])
    sg_o[...] = scaled_grad
    gated = ssd[...] * (gate * jax.nn.sigmoid(gate))
    squares = jnp.sum(gated * gated, axis=1, keepdims=True)
    crossed = jnp.sum(scaled_grad * gain[...] * gated, axis=1, keepdims=True)
    lane = lax.broadcasted_iota(jnp.int32, sums_o.shape, 1)
    sums_o[...] = jnp.where(lane == 0, squares, jnp.where(lane == 1, crossed, 0.0))


def norm_kernel(
    rank, gate_r, sg_r, ssd_r, sums, out_t, gain, branch_o, scaled_o, dssd_o, dgate_o, gain_o
):
    @pl.when(pl.program_id(0) == 0)
    def _():
        gain_o[...] = jnp.zeros(gain_o.shape, f32)

    gate, ssd, scaled_grad = gate_r[...], ssd_r[...], sg_r[...]
    scale = lax.rsqrt(sums[:, 0:1] / DI + norm_epsilon)
    sig = jax.nn.sigmoid(gate)
    silu = gate * sig
    gated = ssd * silu
    scaled = (gated * scale * gain[...]).astype(bf16)
    scaled_o[...] = scaled
    branch_o[...] = mm(scaled, out_t[...], 1, 1).astype(bf16)
    gain_o[...] += jnp.sum(scaled_grad * gated * scale, axis=0, keepdims=True)
    grad = scale * (scaled_grad * gain[...]) - gated * (scale * scale * scale * (sums[:, 1:2] / DI))
    dssd_o[...] = (grad * silu).astype(bf16)
    dgate_o[...] = (grad * ssd * sig * (1.0 + gate * (1.0 - sig))).astype(bf16)


def scan_back_kernel(
    dssd, mix, pre, ch, ssd, hin, step, conv, skip, hp, aux, segr, heads_of,
    dval_o, dcommon_o, dconv_o, dheads_o, dskip_o,
    dmix, dwin, both, dstate, carry,
):
    width = dssd.shape[1]
    channels = width + 2 * N

    @pl.when(pl.program_id(0) == 0)
    def _():
        dwin[CHUNK:, :] = jnp.zeros((8, channels), f32)
        dstate[...] = jnp.zeros(dstate.shape, f32)
        carry[...] = jnp.zeros(carry.shape, f32)
        dconv_o[...] = jnp.zeros(dconv_o.shape, f32)
        dheads_o[...] = jnp.zeros(dheads_o.shape, f32)
        dskip_o[...] = jnp.zeros(dskip_o.shape, f32)

    row, col = iota(0), iota(1)
    left = col < 64
    table = aux[...]
    step_in = step[...]
    dt = softplus(step_in)
    rate = hp[1:2, :]
    tri = (row >= col).astype(f32)
    run = jnp.dot(tri, -(dt * rate), precision=highest, preferred_element_type=f32)
    run_t = run.T
    allowed = (table[:, SEG : SEG + 1] == segr[...]) & (col >= row)
    b_in = mix[:, width : width + N]
    c_out = mix[:, width + N :]
    scores = mm(b_in, c_out, 1, 1)
    ending = run[CHUNK - 1 : CHUNK, :]
    entry = jnp.exp(run) * table[:, INHERIT : INHERIT + 1]
    tail = jnp.exp(ending - run) * table[:, TAIL : TAIL + 1]
    factor = jnp.exp(ending) * table[:, LINKED : LINKED + 1][CHUNK - 1 :, :]
    pairs = jnp.zeros((CHUNK, CHUNK), f32)
    dc = jnp.zeros((CHUNK, N), f32)
    db = jnp.zeros((CHUNK, N), f32)
    for pair in range(width // LANES):
        lanes = slice(pair * LANES, (pair + 1) * LANES)
        x_pair = mix[:, lanes].astype(f32)
        dy_low = dssd[:, lanes]
        dy = dy_low.astype(f32)
        dt_pair = pair_spread(dt, pair, left)
        x_cross = jnp.concatenate(
            [jnp.where(left, x_pair, 0.0), jnp.where(left, 0.0, x_pair)], axis=0
        ).astype(bf16)
        dy_cross = jnp.concatenate(
            [jnp.where(left, dy, 0.0), jnp.where(left, 0.0, dy)], axis=0
        ).astype(bf16)
        inner = mm(x_cross, dy_low, 1, 1)
        mixing = []
        for place, head in enumerate((2 * pair, 2 * pair + 1)):
            spread = run_t[head : head + 1, :] - run[:, head : head + 1]
            decays = jnp.exp(jnp.where(allowed, spread, -1e30))
            mixing.append(decays * scores)
            pairs = pairs + inner[place * CHUNK : (place + 1) * CHUNK] * decays * dt[:, head : head + 1]
        d_state = dstate[:, lanes]
        tail_pair = pair_spread(tail, pair, left)
        flow = mm_left(jnp.concatenate(mixing, axis=1), dy_cross)
        flow = flow + tail_pair * mm_right(b_in, d_state)
        dmix[:, lanes] = dt_pair * flow + skip[:, lanes] * dy
        both[0:CHUNK, lanes] = flow * x_pair
        both[CHUNK:, lanes] = dy * (ssd[:, lanes] - skip[:, lanes] * x_pair)
        dskip_o[:, lanes] += jnp.sum(dy * x_pair, axis=0, keepdims=True)
        entry_dy = pair_spread(entry, pair, left) * dy
        db = db + mm_both(tail_pair * dt_pair * x_pair, d_state, 1, 1)
        dc = dc + mm_both(entry_dy, hin[0, :, lanes], 1, 1)
        dstate[:, lanes] = pair_spread(factor, pair, left) * d_state + mm_right(c_out, entry_dy, 0, 0)
    dmix[:, width : width + N] = db + mm_left(pairs, c_out)
    dmix[:, width + N :] = dc + mm_left(pairs, b_in, 0, 0)

    by_head = mm_left(both[...], heads_of[...])
    direct = by_head[0:CHUNK]
    balance = by_head[CHUNK:] - dt * direct
    later = allowed.astype(f32)
    log_grad = jnp.dot(later, balance, precision=highest, preferred_element_type=f32)
    log_grad = log_grad + table[:, NEXT : NEXT + 1] * carry[0:1, :]
    carry[0:1, :] = log_grad[0:1, :]
    step_grad = (direct - rate * log_grad) * jax.nn.sigmoid(step_in)
    dcommon_o[:, 2 * N :] = step_grad
    dheads_o[0:1, :] += jnp.sum(step_grad, axis=0, keepdims=True)
    dheads_o[1:2, :] += jnp.sum(-(log_grad * dt * rate), axis=0, keepdims=True)

    for start in range(0, channels, 256):
        cols = slice(start, start + 256)
        value = pre[:, cols]
        sig = jax.nn.sigmoid(value)
        dwin[0:CHUNK, cols] = dmix[:, cols] * (sig * (1.0 + value * (1.0 - sig)))
        here = ch[:, cols]
        own = dwin[0:CHUNK, cols]
        total = conv[3:4, cols] * own
        dconv_o[4:5, cols] += jnp.sum(own, axis=0, keepdims=True)
        dconv_o[3:4, cols] += jnp.sum(own * here, axis=0, keepdims=True)
        for ahead in range(1, 4):
            moved = dwin[ahead : ahead + CHUNK, cols] * table[:, AHEAD + ahead : AHEAD + ahead + 1]
            total = total + conv[3 - ahead : 4 - ahead, cols] * moved
            dconv_o[3 - ahead : 4 - ahead, cols] += jnp.sum(moved * here, axis=0, keepdims=True)
        if start < width:
            dval_o[:, cols] = total.astype(bf16)
        else:
            dcommon_o[:, : 2 * N] = total
    dwin[CHUNK:, :] = dwin[0:8, :]


def weight_grad_kernel(dp, me, lhs, rhs, keep_o, send_o, full):
    full[...] = mm(lhs[...], rhs[...], 0, 0)
    half = dp // CORES
    block = lhs.shape[1] // dp
    for place, distance in enumerate(relative_places(dp)):
        start = pl.multiple_of((me[0] ^ distance) * block, block)
        part = full[pl.ds(start, block), :]
        if place < half:
            keep_o[place] = part
        else:
            send_o[place - half] = part.astype(bf16)


def weight_grad(lhs, rhs, dp, dp_rank):
    length, width = rhs.shape
    depth = lhs.shape[1]
    block, half = depth // dp, dp // CORES
    piece = pl.BlockSpec((half, block, 256), lambda i, *s: (0, 0, i))
    return call(
        functools.partial(weight_grad_kernel, dp),
        (width // 256,),
        [whole((length, depth)), pl.BlockSpec((length, 256), lambda i, *s: (0, i))],
        [piece, piece],
        [shape(half, block, width), shape(half, block, width, dtype=bf16)],
        [pltpu.VMEM((depth, 256), f32)],
        2 * length * width * depth,
        scalars=1,
    )(dp_rank, lhs, rhs)


def shared_grad_kernel(lhs, rhs, out):
    out[...] = mm_right(lhs[...], rhs[...], 0, 0)


def input_grad_kernel(rank, dgate, dval, dcommon, tok, wg, wv, shw, ng_o, gain_o):
    @pl.when(pl.program_id(0) == 0)
    def _():
        gain_o[...] = jnp.zeros(gain_o.shape, f32)

    grad = mm(dgate[...], wg[...], 1, 1) + mm(dval[...], wv[...], 1, 1)
    grad = grad + mm_left(dcommon[...], shw[...], 1, 1)
    x = tok[...].astype(f32)
    inverse = lax.rsqrt(jnp.mean(x * x, axis=1, keepdims=True) + norm_epsilon)
    gain_o[...] += jnp.sum(grad * (x * inverse), axis=0, keepdims=True)
    ng_o[...] = grad.astype(ng_o.dtype)


def shards(
    dp, nt,
    residual, cotangent, sequence_ids,
    inner_proj, inner_mean, inner_square,
    shared_proj, shared_mean, shared_square,
    outer_proj, outer_mean, outer_square,
    conv_params, conv_mean, conv_square,
    norm_gains, gains_mean, gains_square,
    head_params, heads_mean, heads_square,
):
    t_rank = lax.axis_index("tensor").astype(jnp.int32)
    d_rank = lax.axis_index("dp").astype(jnp.int32)
    dp_me = d_rank[None]
    t_me = t_rank[None]
    rows_here = residual.shape[0]
    length = rows_here * nt
    width = inner_proj.shape[2]
    heads_here = head_params.shape[1]
    head_size = width // heads_here
    channels = width + 2 * N
    chunks = length // CHUNK
    wide = 2 * CHUNK
    band = min(2 * CHUNK, rows_here)
    per_piece = rows_here // band
    places = jnp.array(relative_places(dp), jnp.int32)

    def over_tensor(value):
        pieces = [value] + [swap(value, "tensor", nt, d) for d in range(1, nt)]
        if nt == 2:
            first = jnp.concatenate(pieces, axis=0)
            second = jnp.concatenate(pieces[::-1], axis=0)
            return jnp.where(t_rank == 0, first, second)
        stacked = jnp.take(jnp.stack(pieces), jnp.arange(nt) ^ t_rank, axis=0)
        return stacked.reshape((nt * value.shape[0],) + value.shape[1:])

    tokens_all = over_tensor(residual)

    def everywhere(value):
        pieces = jnp.stack([value] + [swap(value, "tensor", nt, d) for d in range(1, nt)])
        pieces = jnp.take(pieces, jnp.arange(nt) ^ t_rank, axis=0)
        both = jnp.concatenate(gather_halves(pieces, dp), axis=0)
        spots = jnp.argsort(places ^ d_rank)
        return jnp.take(both, spots, axis=0)

    small = jnp.concatenate([conv_params.reshape(1, -1), norm_gains.reshape(1, -1)], axis=1)
    small_all = everywhere(small).reshape(dp * nt, -1)
    kernel_rows, columns = conv_params.shape
    conv_full = (
        small_all[:, : kernel_rows * columns]
        .reshape(dp * nt, kernel_rows, columns)
        .transpose(1, 0, 2)
        .reshape(kernel_rows, -1)
    )
    gains_full = small_all[:, kernel_rows * columns :].reshape(-1)
    shared_full = everywhere(shared_proj.astype(bf16)).reshape(D, -1)

    value_shard = inner_proj[1].astype(bf16)
    gate_shard = inner_proj[0].astype(bf16)
    outer_shard = outer_proj.T.astype(bf16)
    value_w = assemble(*gather_halves(value_shard, dp), dp, dp_me)
    gate_w = assemble(*gather_halves(gate_shard, dp), dp, dp_me)
    outer_t = assemble(*gather_halves(outer_shard, dp), dp, dp_me)
    cot_all = over_tensor(after(cotangent, tokens_all))

    pre_gain = gains_full[:D].reshape(1, D)
    post_gain = lax.dynamic_slice_in_dim(gains_full, D + t_rank * width, width).reshape(1, width)
    conv_here = jnp.concatenate(
        [lax.dynamic_slice_in_dim(conv_full, t_rank * width, width, 1), conv_full[:, DI:]], axis=1
    )
    conv_here = jnp.pad(conv_here, ((0, 8 - kernel_rows), (0, 0)))
    shared_here = jnp.concatenate(
        [
            shared_full[:, : 2 * N],
            lax.dynamic_slice_in_dim(shared_full, 2 * N + t_rank * heads_here, heads_here, 1),
            jnp.zeros((D, LANES - heads_here), bf16),
        ],
        axis=1,
    )
    common_width = 2 * N + LANES
    head_rows = jnp.stack([head_params[0], jnp.exp(head_params[1])])
    head_rows = jnp.pad(head_rows, ((0, 6), (0, LANES - heads_here)))
    skip = jnp.repeat(head_params[2], head_size).reshape(1, width)
    heads_of = (
        jnp.arange(width)[:, None] // head_size == jnp.arange(LANES)[None, :]
    ).astype(bf16)

    ids = sequence_ids
    blocked = ids.reshape(chunks, CHUNK)
    ends, firsts = blocked[:, -1], blocked[:, 0]
    none = jnp.full((1,), -1, jnp.int32)
    before = jnp.concatenate([none, ends[:-1]])
    following = jnp.concatenate([firsts[1:], none])
    fills = [jnp.full((o,), -1, jnp.int32) for o in range(1, 4)]
    marks = [ids]
    marks += [jnp.concatenate([fills[o - 1], ids[:-o]]) == ids for o in range(1, 4)]
    marks += [jnp.concatenate([ids[o:], fills[o - 1]]) == ids for o in range(1, 4)]
    marks += [
        (blocked == before[:, None]).reshape(-1),
        (blocked == ends[:, None]).reshape(-1),
        jnp.broadcast_to((ends == before)[:, None], blocked.shape).reshape(-1),
        (blocked == following[:, None]).reshape(-1),
        ids < SEQ_SLOTS,
    ]
    aux = jnp.stack([m.astype(f32) for m in marks] + [jnp.zeros((length,), f32)] * 4, axis=1)
    segr = ids.astype(f32).reshape(1, length)
    aux_cols = aux.shape[1]

    steps = length // wide
    normed, chans, pre, mixed, ssd, entering, step_in = call(
        scan_kernel,
        (steps,),
        [
            rows(wide, D), whole((1, D)), whole((D, width)), whole((D, common_width)),
            whole((8, channels)), whole((1, width)), whole((8, LANES)), rows(wide, aux_cols),
            pl.BlockSpec((1, wide), lambda i: (0, i)),
        ],
        [
            rows(wide, D), rows(wide, channels), rows(wide, channels), rows(wide, channels),
            rows(wide, width), pl.BlockSpec((wide // CHUNK, N, width), lambda i: (i, 0, 0)),
            rows(wide, LANES),
        ],
        [
            shape(length, D, dtype=bf16), shape(length, channels), shape(length, channels),
            shape(length, channels, dtype=bf16), shape(length, width),
            shape(chunks, N, width), shape(length, LANES),
        ],
        [pltpu.VMEM((wide + 8, channels), f32), pltpu.VMEM((N, width), f32)],
        length * (2 * D * (width + common_width) + 12 * width * CHUNK),
    )(tokens_all, pre_gain, value_w, shared_here, conv_here, skip, head_rows, aux, segr)

    gate, scaled_grad, returned, sums = call(
        gate_kernel,
        (steps,),
        [
            rows(wide, D), rows(wide, D), rows(wide, aux_cols), rows(wide, width),
            whole((D, width)), whole((D, width)), whole((1, width)),
        ],
        [rows(wide, width), rows(wide, width), rows(wide, D), rows(wide, LANES)],
        [
            shape(length, width), shape(length, width), shape(length, D, dtype=bf16),
            shape(length, LANES),
        ],
        [],
        4 * length * D * width,
    )(normed, cot_all, aux, ssd, gate_w, outer_t, post_gain)
    sums = sums[:, :2].T
    distance = 1
    while distance < nt:
        sums = sums + swap(sums, "tensor", nt, distance)
        distance *= 2
    sums = sums.T

    def relative(block, rank):
        return (rank ^ (block // per_piece)) * per_piece + block % per_piece

    def rel_rows(width_here, offset=0):
        return pl.BlockSpec((band, width_here), lambda i, r: (relative(i + offset, r[0]), 0))

    plain = lambda width_here: pl.BlockSpec((band, width_here), lambda i, r: (i, 0))
    branch, scaled, dssd, dgate, post_grad = call(
        norm_kernel,
        (length // band,),
        [
            rel_rows(width), rel_rows(width), rel_rows(width), rel_rows(2),
            whole((D, width)), whole((1, width)),
        ],
        [plain(D), rel_rows(width), rel_rows(width), rel_rows(width), whole((1, width))],
        [
            shape(length, D, dtype=bf16), shape(length, width, dtype=bf16),
            shape(length, width, dtype=bf16), shape(length, width, dtype=bf16), shape(1, width),
        ],
        [],
        2 * length * D * width,
        scalars=1,
    )(t_me, gate, scaled_grad, ssd, sums, outer_t, post_gain)
    outer_part = scatter_sum(*weight_grad(returned, scaled, dp, dp_me), dp)
    gate_part = scatter_sum(*weight_grad(normed, dgate, dp, dp_me), dp)

    branch = branch.reshape(nt, rows_here, D)
    branch_sum = branch[0].astype(f32)
    for d in range(1, nt):
        branch_sum = branch_sum + swap(branch[d], "tensor", nt, d).astype(f32)
    live_here = lax.dynamic_slice_in_dim(aux[:, LIVE], t_rank * rows_here, rows_here)
    tokens = residual.astype(f32)
    block_out = (tokens + branch_sum * live_here[:, None]).astype(bf16)

    back = lambda i: chunks - 1 - i
    dval, dcommon, dconv, dheads, dskip = call(
        scan_back_kernel,
        (chunks,),
        [
            rows(CHUNK, width, back), rows(CHUNK, channels, back), rows(CHUNK, channels, back),
            rows(CHUNK, channels, back), rows(CHUNK, width, back),
            pl.BlockSpec((1, N, width), lambda i: (chunks - 1 - i, 0, 0)),
            rows(CHUNK, LANES, back), whole((8, channels)), whole((1, width)),
            whole((8, LANES)), rows(CHUNK, aux_cols, back),
            pl.BlockSpec((1, CHUNK), lambda i: (0, chunks - 1 - i)), whole((width, LANES)),
        ],
        [
            rows(CHUNK, width, back), rows(CHUNK, common_width, back), whole((8, channels)),
            whole((8, LANES)), whole((1, width)),
        ],
        [
            shape(length, width, dtype=bf16), shape(length, common_width), shape(8, channels),
            shape(8, LANES), shape(1, width),
        ],
        [
            pltpu.VMEM((CHUNK, channels), f32), pltpu.VMEM((CHUNK + 8, channels), f32),
            pltpu.VMEM((2 * CHUNK, width), f32), pltpu.VMEM((N, width), f32),
            pltpu.VMEM((8, LANES), f32),
        ],
        length * 30 * width * CHUNK,
    )(dssd, mixed, pre, chans, ssd, entering, step_in, conv_here, skip, head_rows, aux, segr, heads_of)

    def input_grad(count, offset, dtype):
        return call(
            input_grad_kernel,
            (count * per_piece,),
            [
                rel_rows(width, offset), rel_rows(width, offset), rel_rows(common_width, offset),
                rel_rows(D, offset), whole((D, width)), whole((D, width)), whole((D, common_width)),
            ],
            [plain(D), whole((1, D))],
            [shape(count * rows_here, D, dtype=dtype), shape(1, D)],
            [],
            4 * count * rows_here * D * (width + common_width),
            scalars=1,
        )(t_me, dgate, dval, dcommon, tokens_all, gate_w, value_w, shared_here)

    sent, pre_grad_sent = input_grad(nt - 1, per_piece, bf16)
    sent = sent.reshape(nt - 1, rows_here, D)
    value_part = scatter_sum(*weight_grad(normed, dval, dp, dp_me), dp)
    own, pre_grad_own = input_grad(1, 0, f32)
    normed_grad = own
    for d in range(1, nt):
        normed_grad = normed_grad + swap(sent[d - 1], "tensor", nt, d).astype(f32)

    shared_grad = pl.pallas_call(
        shared_grad_kernel,
        out_shape=shape(D, common_width),
        compiler_params=pltpu.CompilerParams(vmem_limit_bytes=50 * 1024 * 1024),
        cost_estimate=pl.CostEstimate(
            flops=4 * length * D * common_width, bytes_accessed=6 * D * common_width, transcendentals=0
        ),
    )(normed, dcommon)
    shared_rows = shared_proj.shape[0]
    shared_grad = lax.dynamic_update_slice(
        jnp.pad(shared_grad[:, : 2 * N], ((0, 0), (0, H))),
        shared_grad[:, 2 * N : 2 * N + heads_here],
        (0, 2 * N + t_rank * heads_here),
    )
    shared_grad = shared_grad.reshape(dp, nt, shared_rows, 2 * N + H)
    shared_mine = lax.dynamic_index_in_dim(shared_grad, t_rank, 1, False)
    for d in range(1, nt):
        part = lax.dynamic_index_in_dim(shared_grad, t_rank ^ d, 1, False).astype(bf16)
        shared_mine = shared_mine + swap(part, "tensor", nt, d).astype(f32)
    shared_mine = jnp.take(shared_mine, places ^ d_rank, axis=0)
    half = dp // CORES
    shared_part = scatter_sum(shared_mine[:half], shared_mine[half:].astype(bf16), dp)

    conv_grad = lax.dynamic_update_slice(
        jnp.pad(dconv[:kernel_rows, width:], ((0, 0), (DI, 0))),
        dconv[:kernel_rows, :width],
        (0, t_rank * width),
    )
    post_all = lax.dynamic_update_slice(
        jnp.zeros((1, DI), f32), post_grad, (0, t_rank * width)
    )
    head_grad = jnp.stack(
        [
            dheads[0, :heads_here],
            dheads[1, :heads_here],
            jnp.sum(dskip.reshape(heads_here, head_size), axis=1),
        ]
    )
    head_all = lax.dynamic_update_slice(
        jnp.zeros((3, H), f32), head_grad, (0, t_rank * heads_here)
    )
    vector = jnp.concatenate(
        [
            conv_grad.reshape(1, -1), pre_grad_sent + pre_grad_own, post_all, head_all.reshape(1, -1),
        ],
        axis=1,
    )
    vector = sum_everywhere(vector, dp, nt)
    conv_size = kernel_rows * (DI + 2 * N)
    place = d_rank * nt + t_rank
    conv_part = lax.dynamic_slice_in_dim(
        vector[0, :conv_size].reshape(kernel_rows, -1), place * columns, columns, 1
    )
    gain_count = norm_gains.shape[0]
    gains_part = lax.dynamic_slice_in_dim(vector[0], conv_size + place * gain_count, gain_count)
    heads_part = lax.dynamic_slice_in_dim(
        vector[0, conv_size + D + DI :].reshape(3, H), t_rank * heads_here, heads_here, 1
    )

    inverse = lax.rsqrt(jnp.mean(tokens * tokens, axis=1, keepdims=True) + norm_epsilon)
    normal_tokens = tokens * inverse
    normal_grad = normed_grad * pre_gain
    centered = normal_grad - normal_tokens * jnp.mean(
        normal_grad * normal_tokens, axis=1, keepdims=True
    )
    residual_grad = (cotangent.astype(f32) + inverse * centered).astype(bf16)

    inner_new = adam_step(
        inner_proj, inner_mean, inner_square, jnp.stack([gate_part, value_part]),
        rate_matrix, weight_decay,
    )
    shared_new = adam_step(
        shared_proj, shared_mean, shared_square, shared_part.reshape(shared_proj.shape),
        rate_matrix, weight_decay,
    )
    outer_new = adam_step(
        outer_proj, outer_mean, outer_square, outer_part.T, rate_matrix, weight_decay
    )
    conv_new = adam_step(conv_params, conv_mean, conv_square, conv_part, rate_vector, 0.0)
    gains_new = adam_step(norm_gains, gains_mean, gains_square, gains_part, rate_vector, 0.0)
    heads_new = adam_step(head_params, heads_mean, heads_square, heads_part, rate_heads, 0.0)
    return (
        (block_out, residual_grad)
        + inner_new + shared_new + outer_new + conv_new + gains_new + heads_new
    )


def solution(mesh):
    return jax.shard_map(
        functools.partial(shards, mesh.shape["dp"], mesh.shape["tensor"]),
        mesh=mesh,
        in_specs=(
            P(("dp", "tensor"), None),
            P(("dp", "tensor"), None),
            P("dp"),
            P(None, "dp", "tensor"),
            P(None, "dp", "tensor"),
            P(None, "dp", "tensor"),
            P(("dp", "tensor"), None),
            P(("dp", "tensor"), None),
            P(("dp", "tensor"), None),
            P("tensor", "dp"),
            P("tensor", "dp"),
            P("tensor", "dp"),
            P(None, ("dp", "tensor")),
            P(None, ("dp", "tensor")),
            P(None, ("dp", "tensor")),
            P(("dp", "tensor")),
            P(("dp", "tensor")),
            P(("dp", "tensor")),
            P(None, "tensor"),
            P(None, "tensor"),
            P(None, "tensor"),
        ),
        out_specs=(
            P(("dp", "tensor"), None),
            P(("dp", "tensor"), None),
            P(None, "dp", "tensor"),
            P(None, "dp", "tensor"),
            P(None, "dp", "tensor"),
            P(("dp", "tensor"), None),
            P(("dp", "tensor"), None),
            P(("dp", "tensor"), None),
            P("tensor", "dp"),
            P("tensor", "dp"),
            P("tensor", "dp"),
            P(None, ("dp", "tensor")),
            P(None, ("dp", "tensor")),
            P(None, ("dp", "tensor")),
            P(("dp", "tensor")),
            P(("dp", "tensor")),
            P(("dp", "tensor")),
            P(None, "tensor"),
            P(None, "tensor"),
            P(None, "tensor"),
        ),
        check_vma=False,
    )
```

time: 913 us -> 597 us (0.65)
  Pallas kernels: 0 us -> 312 us
  blocking collectives: 261 us -> 0 us
  waiting for transfers between devices: 287 us -> 110 us
  matrix products: 139 us -> 0 us
  other arithmetic: 125 us -> 47 us
  starting transfers between devices: 0.62 us -> 76.3 us
  local copies, waits for them, and re-layouts: 75.4 us -> 42.9 us
  between operations: 15.7 us -> 1.99 us
    pallas_call x0 -> x13, Pallas kernels: none -> 312 us  [the longest x3 194 us: assemble(): pl.pallas_call(functools.partial(assemble_kernel, dp), in_specs=[pl.Block...]
    reduce_scatter x5 -> x0, waiting for transfers between devices: 245 us -> none  [the longest x1 95.3 us: shards(): lax.psum_scatter(inner_stack, 'dp', scatter_dimension=1, tiled=True)]
    dot_general x20 -> x0, matrix products: 139 us -> none  [the longest x3 40.7 us: scan_state(): jnp.einsum('bhij,bjhp->bihp', mixing, values, precision=highest)]
    all_gather x2 -> x0, blocking collectives: 136 us -> none  [the longest x1 68.3 us: shards(): lax.all_gather(shared_proj, ('dp', 'tensor'), axis=0, tiled=True)]
    ppermute x0 -> x58, waiting for transfers between devices: none -> 110 us  [swap(): return lax.ppermute(value, axis, [(i, i ^ distance) for i in range(size)])]
    unnamed x2 -> x0, blocking collectives: 83.8 us -> none
    ppermute x0 -> x58, starting transfers between devices: none -> 76.3 us  [swap(): return lax.ppermute(value, axis, [(i, i ^ distance) for i in range(size)])]
    reduce_sum x15 -> x2, other arithmetic: 47 us -> 0.72 us  [the longest x1 0.6 us: shards(): jnp.mean(normal_grad * normal_tokens, axis=1, keepdims=True)]
  transfers between devices with their start and end apart: 9 -> 58, of which waited for: 5 -> 21; matrix products, arithmetic and copies ran while one was open for 16% -> 12% of each run, Pallas kernels for 0% -> 40%
where the time goes in v1:
time: 597 us; the launch traced here: 590 us
  Pallas kernels  312 us (52%)
  waiting for transfers between devices  110 us (18%)
  starting transfers between devices  76.3 us (13%)
  other arithmetic  47 us (8%)
  local copies, waits for them, and re-layouts  42.9 us (7%)
    pallas_call x3, Pallas kernels, assemble(): pl.pallas_call(functools.partial(assemble_kernel, dp), in_specs=[pl.Block...  194 us
    ppermute x58, waiting for transfers between devices, swap(): return lax.ppermute(value, axis, [(i, i ^ distance) for i in range(size)])  110 us
    ppermute x58, starting transfers between devices, swap(): return lax.ppermute(value, axis, [(i, i ^ distance) for i in range(size)])  76.3 us
    pallas_call x1, Pallas kernels, shards(): call(scan_back_kernel, (chunks,), [rows(CHUNK, width, back), rows(CHUNK,...  34.7 us
    pallas_call x1, Pallas kernels, shards(): call(scan_kernel, (steps,), [rows(wide, D), whole((1, D)), whole((D, widt...  24.6 us
    unnamed x85, local copies, waits for them, and re-layouts  19.8 us
    pallas_call x3, Pallas kernels, weight_grad(): call(functools.partial(weight_grad_kernel, dp), (width // 256,), [whole((...  19.4 us
    pallas_call x2, Pallas kernels, input_grad(): call(input_grad_kernel, (count * per_piece,), [rel_rows(width, offset), r...  14.7 us
  transfers between devices with their start and end apart: 58, of which 21 were waited for; matrix products, arithmetic and copies ran while one was open for 12% of the time, Pallas kernels for 40%

profile of v1, /device:TPU:0, one launch (start us, length us, event | category | flops | bytes accessed | tf_op | source)
XLA Modules:
  0.0 590.4 jit_solution(11950636336509678391)
XLA Ops:
  37.1 3.8 collective-permute-start.4
  53.6 4.2 collective-permute-start.14
  63.2 3.5 collective-permute-done.15
  75.7 6.1 %collective-permute-done.20 = bf16[64,1024]{1,0:T(8,128)(2,1)S(1)} collective-permute-done((bf16[64,1024]{1,0:T(8,128)(2,1)}, bf16[64,1024]{1,0:T(8,128)(2,1)S(1)}, u32[]{:S(2)}, u32[]{:S(2)}) %collective-permute-start.20) | collective-permute-done | bytes 131104 | tf_op jit(solution)/shard_map/ppermute | solution.py:48
  96.6 4.1 collective-permute-done.10
  101.5 9.9 %collective-permute-done.22 = bf16[4,64,1024]{2,1,0:T(8,128)(2,1)S(1)} collective-permute-done((bf16[4,64,1024]{2,1,0:T(8,128)(2,1)S(1)}, bf16[4,64,1024]{2,1,0:T(8,128)(2,1)S(1)}, u32[]{:S(2)}, u32[]{:S(2)}) %collective-permute-start.22) | collective-permute-done | bytes 524320 | tf_op jit(solution)/shard_map/ppermute | solution.py:48
  112.2 4.8 collective-permute-done.27
  118.7 3.7 maximum_select_fusion.tok
  124.0 64.8 %shard_map.365 = bf16[16,64,1024]{2,1,0:T(8,128)(2,1)} custom-call(s32[1]{0:T(128)} %bitcast.13.me, bf16[8,64,1024]{2,1,0:T(8,128)(2,1)} %constant_dynamic-update-slice_fusion.11.near, bf16[8,64,1024]{2,1,0:T(8,128)(2,1)} %collective-permute-done.11.far), custom_call_target="tpu_custom_call" | custom-call | bytes 4194304 | tf_op jit(solution)/shard_map/pallas_call | solution.py:193
  188.8 64.8 %shard_map.367 = bf16[16,64,1024]{2,1,0:T(8,128)(2,1)} custom-call(s32[1]{0:T(128)} %bitcast.13.me, bf16[8,64,1024]{2,1,0:T(8,128)(2,1)} %constant_dynamic-update-slice_fusion.27.near, bf16[8,64,1024]{2,1,0:T(8,128)(2,1)} %collective-permute-done.23.far), custom_call_target="tpu_custom_call" | custom-call | bytes 4194304 | tf_op jit(solution)/shard_map/pallas_call | solution.py:193
  253.6 64.8 %shard_map.368 = bf16[16,64,1024]{2,1,0:T(8,128)(2,1)} custom-call(s32[1]{0:T(128)} %bitcast.13.me, bf16[8,64,1024]{2,1,0:T(8,128)(2,1)} %constant_dynamic-update-slice_fusion.32.near, bf16[8,64,1024]{2,1,0:T(8,128)(2,1)} %collective-permute-done.28.far), custom_call_target="tpu_custom_call" | custom-call | bytes 4194304 | tf_op jit(solution)/shard_map/pallas_call | solution.py:193
  318.4 24.6 %shard_map.366 = (bf16[1024,1024]{1,0:T(8,128)(2,1)S(1)}, f32[1024,1280]{1,0:T(8,128)}, f32[1024,1280]{1,0:T(8,128)}, bf16[1024,1280]{1,0:T(8,128)(2,1)}, f32[10...) custom-call(bf16[1024,1024]{1,0:T(8,128)(2,1)} %maximum_select_fusion.tok, ...), custom_call_target="tpu_custom_call" | custom-call | flops 4563402752 | bytes 48234496 | tf_op jit(solution)/shard_map/pallas_call | solution.py:570
  343.0 4.5 maximum_select_fusion.1.cot
  347.5 10.4 %shard_map.369 = (f32[1024,1024]{1,0:T(8,128)}, f32[1024,1024]{1,0:T(8,128)}, bf16[1024,1024]{1,0:T(8,128)(2,1)S(1)}, f32[1024,128]{1,0:T(8,128)S(1)}) custom-call(bf16[1024,1024]{1,0:T(8,128)(2,1)} %copy-done.8, bf16[1024,1024]{1,0:T(8,128)(2,1)} %maximum_select_fusion.1.cot, f32[1024,16]{1,0:T(8,128)S(1)} %copy.75.aux, ...), custom_call_target="tpu_custom_call" | custom-call | flops 4294967296 | bytes 22020096 | tf_op jit(solution)/shard_map/pallas_call | solution.py:592
  361.2 13.1 %collective-permute-done.29 = f32[2,1024]{0,1:T(8,128)S(1)} collective-permute-done((f32[2,1024]{0,1:T(8,128)}, f32[2,1024]{0,1:T(8,128)S(1)}, u32[]{:S(2)}, u32[]{:S(2)}) %collective-permute-start.29) | collective-permute-done | bytes 8224 | tf_op jit(solution)/shard_map/ppermute | solution.py:48
  374.4 10.2 %shard_map.370 = (bf16[1024,1024]{1,0:T(8,128)(2,1)S(1)}, bf16[1024,1024]{1,0:T(8,128)(2,1)}, bf16[1024,1024]{1,0:T(8,128)(2,1)}, bf16[1024,1024]{1,0:T(8,128)(2,1)}, f32[1,1024]{1,0:T(1,128)S(1)}) custom-call(s32[1]{0:T(128)} %bitcast.rank, f32[1024,1024]{1,0:T(8,128)} %get-tuple-element.57.gate_r, f32[1024,1024]{1,0:T(8,128)} %get-tuple-element.58.sg_r, ...), custom_call_target="tpu_custom_call" | custom-call | flops 2147483648 | bytes 16785408 | tf_op jit(solution)/shard_map/pallas_call | solution.py:621
  385.9 34.7 %shard_map.371 = (bf16[1024,1024]{1,0:T(8,128)(2,1)}, f32[1024,384]{1,0:T(8,128)S(1)}, f32[8,1280]{1,0:T(8,128)S(1)}, f32[8,128]{1,0:T(8,128)S(1)}, f32[1,1024]{1,0:T(1,128)S(1)}) custom-call(bf16[1024,1024]{1,0:T(8,128)(2,1)} %get-tuple-element.62.dssd, bf16[1024,1280]{1,0:T(8,128)(2,1)} %get-tuple-element.63.mix, f32[1024,1280]{1,0:T(8,128)} %get-tuple-element.64.pre, ...), custom_call_target="tpu_custom_call" | custom-call | flops 4026531840 | bytes 7438336 | tf_op jit(solution)/shard_map/pallas_call | solution.py:649
  420.5 6.7 %shard_map.373 = (bf16[512,1024]{1,0:T(8,128)(2,1)S(1)}, f32[1,1024]{1,0:T(1,128)S(1)}) custom-call(s32[1]{0:T(128)} %bitcast.rank, bf16[1024,1024]{1,0:T(8,128)(2,1)} %get-tuple-element.61.dgate.rhs, bf16[1024,1024]{1,0:T(8,128)(2,1)} %get-tuple-element.68.dval.rhs, f32[1024,384]{1,0:T(8,128)S(1)} %get-tuple-element.69.dcommon.rhs, ...), custom_call_target="tpu_custom_call" | custom-call | flops 2952790016 | bytes 2105344 | tf_op jit(solution)/shard_map/pallas_call | solution.py:677
  427.3 8.0 %shard_map.372 = (f32[512,1024]{1,0:T(8,128)}, f32[1,1024]{1,0:T(1,128)S(1)}) custom-call(s32[1]{0:T(128)} %bitcast.rank, bf16[1024,1024]{1,0:T(8,128)(2,1)} %get-tuple-element.61.dgate.rhs, bf16[1024,1024]{1,0:T(8,128)(2,1)} %get-tuple-element.68.dval.rhs, f32[1024,384]{1,0:T(8,128)S(1)} %get-tuple-element.69.dcommon.rhs, ...), custom_call_target="tpu_custom_call" | custom-call | flops 2952790016 | bytes 4202496 | tf_op jit(solution)/shard_map/pallas_call | solution.py:677
  435.3 4.0 shard_map.376
  445.5 6.4 %shard_map.374 = (f32[8,64,1024]{2,1,0:T(8,128)S(1)}, bf16[8,64,1024]{2,1,0:T(8,128)(2,1)}) custom-call(s32[1]{0:T(128)} %bitcast.13.me, bf16[1024,1024]{1,0:T(8,128)(2,1)} %copy-done.8, bf16[1024,1024]{1,0:T(8,128)(2,1)} %get-tuple-element.61.dgate.rhs), custom_call_target="tpu_custom_call" | custom-call | flops 2147483648 | bytes 6291456 | tf_op jit(solution)/shard_map/pallas_call | solution.py:433
  454.5 6.4 %shard_map.375 = (f32[8,64,1024]{2,1,0:T(8,128)S(1)}, bf16[8,64,1024]{2,1,0:T(8,128)(2,1)}) custom-call(s32[1]{0:T(128)} %bitcast.13.me, bf16[1024,1024]{1,0:T(8,128)(2,1)} %copy-done.8, bf16[1024,1024]{1,0:T(8,128)(2,1)} %get-tuple-element.68.dval.rhs), custom_call_target="tpu_custom_call" | custom-call | flops 2147483648 | bytes 6291456 | tf_op jit(solution)/shard_map/pallas_call | solution.py:433
  465.4 8.2 %collective-permute-start.56 = (f32[1,14688]{1,0:T(1,128)S(1)}, f32[1,14688]{1,0:T(1,128)S(1)}, u32[]{:S(2)}, u32[]{:S(2)}) collective-permute-start(f32[1,14688]{1,0:T(1,128)S(1)} %add.354), channel_id=1, source_target_pairs={{0,8},{2,10},{4,12},{6,14},{8,0},{10,2},{12,4},{14,6},{16,24},{18,... | collective-permute-start | bytes 176264 | tf_op jit(solution)/shard_map/ppermute | solution.py:48
  476.9 6.6 %shard_map.377 = (f32[8,64,1024]{2,1,0:T(8,128)S(1)}, bf16[8,64,1024]{2,1,0:T(8,128)(2,1)}) custom-call(s32[1]{0:T(128)} %bitcast.13.me, bf16[1024,1024]{1,0:T(8,128)(2,1)} %copy-done.9, bf16[1024,1024]{1,0:T(8,128)(2,1)} %get-tuple-element.77.rhs), custom_call_target="tpu_custom_call" | custom-call | flops 2147483648 | bytes 6291456 | tf_op jit(solution)/shard_map/pallas_call | solution.py:433
  493.5 4.2 collective-permute-done.44
  519.6 12.4 %collective-permute-done.31 = bf16[512,1024]{1,0:T(8,128)(2,1)S(1)} collective-permute-done((bf16[512,1024]{1,0:T(8,128)(2,1)}, bf16[512,1024]{1,0:T(8,128)(2,1)S(1)}, u32[]{:S(2)}, u32[]{:S(2)}) %collective-permute-start.31) | collective-permute-done | bytes 1048608 | tf_op jit(solution)/shard_map/ppermute | solution.py:48
  532.6 18.9 %collective-permute-done.30 = bf16[512,1024]{1,0:T(8,128)(2,1)S(1)} collective-permute-done((bf16[512,1024]{1,0:T(8,128)(2,1)}, bf16[512,1024]{1,0:T(8,128)(2,1)S(1)}, u32[]{:S(2)}, u32[]{:S(2)}) %collective-permute-start.30) | collective-permute-done | bytes 1048608 | tf_op jit(solution)/shard_map/ppermute | solution.py:48
  551.5 3.7 fusion.6
  562.9 4.4 collective-permute-done.34
  567.6 9.1 %collective-permute-done.35 = bf16[64,1024]{1,0:T(8,128)(2,1)S(1)} collective-permute-done((bf16[64,1024]{1,0:T(8,128)(2,1)S(1)}, bf16[64,1024]{1,0:T(8,128)(2,1)S(1)}, u32[]{:S(2)}, u32[]{:S(2)}) %collective-permute-start.35) | collective-permute-done | bytes 131104 | tf_op jit(solution)/shard_map/ppermute | solution.py:48
  576.6 3.3 collective-permute-start.41
  580.6 6.7 %collective-permute-done.40 = bf16[64,1024]{1,0:T(8,128)(2,1)S(1)} collective-permute-done((bf16[64,1024]{1,0:T(8,128)(2,1)S(1)}, bf16[64,1024]{1,0:T(8,128)(2,1)S(1)}, u32[]{:S(2)}, u32[]{:S(2)}) %collective-permute-start.40) | collective-permute-done | bytes 131104 | tf_op jit(solution)/shard_map/ppermute | solution.py:48
  (331 shorter events, 147.6 us)
Async XLA Ops:
  2.6 65.3 %collective-permute-start.7 = (bf16[64,1024]{1,0:T(8,128)(2,1)}, bf16[64,1024]{1,0:T(8,128)(2,1)S(1)}, u32[]{:S(2)}, u32[]{:S(2)}) collective-permute-start(bf16[64,1024]{1,0:T(8,128)(2,1)} %bitcast.14), channel_id=1, source_target_pairs={{0,8},{2,10},{4,12},{6,14},{8,0},{10,2},{12,4},{14,6},{16,24},{18,... | collective-permute-start | bytes 393224 | tf_op jit(solution)/shard_map/ppermute | solution.py:48
  5.6 64.6 %collective-permute-start.8 = (bf16[64,1024]{1,0:T(8,128)(2,1)}, bf16[64,1024]{1,0:T(8,128)(2,1)S(1)}, u32[]{:S(2)}, u32[]{:S(2)}) collective-permute-start(bf16[64,1024]{1,0:T(8,128)(2,1)} %bitcast.14), channel_id=1, source_target_pairs={{0,16},{2,18},{4,20},{6,22},{8,24},{10,26},{12,28},{14,30},{16,0},... | collective-permute-start | bytes 393224 | tf_op jit(solution)/shard_map/ppermute | solution.py:48
  8.2 63.5 %collective-permute-start.9 = (bf16[64,1024]{1,0:T(8,128)(2,1)}, bf16[64,1024]{1,0:T(8,128)(2,1)S(1)}, u32[]{:S(2)}, u32[]{:S(2)}) collective-permute-start(bf16[64,1024]{1,0:T(8,128)(2,1)} %bitcast.14), channel_id=1, source_target_pairs={{0,24},{2,26},{4,28},{6,30},{8,16},{10,18},{12,20},{14,22},{16,8},... | collective-permute-start | bytes 393224 | tf_op jit(solution)/shard_map/ppermute | solution.py:48
  9.0 34.2 %collective-permute-start.12 = (bf16[32,288]{1,0:T(8,128)(2,1)S(1)}, bf16[32,288]{1,0:T(8,128)(2,1)S(1)}, u32[]{:S(2)}, u32[]{:S(2)}) collective-permute-start(bf16[32,288]{1,0:T(8,128)(2,1)S(1)} %convert_element_type.213), channel_id=1, source_target_pairs={{0,1},{1,0},{2,3},{3,2},{4,5},{5,4},{6,7},{7,6},{8,9},{9,8},{10,11... | collective-permute-start | bytes 55304 | tf_op jit(solution)/shard_map/ppermute | solution.py:48
  12.2 15.5 %collective-permute-start.1 = (f32[1,456]{1,0:T(1,128)S(1)}, f32[1,456]{1,0:T(1,128)S(1)}, u32[]{:S(2)}, u32[]{:S(2)}) collective-permute-start(f32[1,456]{1,0:T(1,128)S(1)} %pad_maximum_fusion.8), channel_id=1, source_target_pairs={{0,1},{1,0},{2,3},{3,2},{4,5},{5,4},{6,7},{7,6},{8,9},{9,8},{10,11... | collective-permute-start | bytes 5480 | tf_op jit(solution)/shard_map/ppermute | solution.py:48
  42.6 30.7 %collective-permute-start.19 = (bf16[64,1024]{1,0:T(8,128)(2,1)}, bf16[64,1024]{1,0:T(8,128)(2,1)S(1)}, u32[]{:S(2)}, u32[]{:S(2)}) collective-permute-start(bf16[64,1024]{1,0:T(8,128)(2,1)} %bitcast.45), channel_id=1, source_target_pairs={{0,8},{2,10},{4,12},{6,14},{8,0},{10,2},{12,4},{14,6},{16,24},{18,... | collective-permute-start | bytes 393224 | tf_op jit(solution)/shard_map/ppermute | solution.py:48
  66.7 15.1 %collective-permute-start.20 = (bf16[64,1024]{1,0:T(8,128)(2,1)}, bf16[64,1024]{1,0:T(8,128)(2,1)S(1)}, u32[]{:S(2)}, u32[]{:S(2)}) collective-permute-start(bf16[64,1024]{1,0:T(8,128)(2,1)} %bitcast.45), channel_id=1, source_target_pairs={{0,16},{2,18},{4,20},{6,22},{8,24},{10,26},{12,28},{14,30},{16,0},... | collective-permute-start | bytes 393224 | tf_op jit(solution)/shard_map/ppermute | solution.py:48
  68.0 15.3 %collective-permute-start.21 = (bf16[64,1024]{1,0:T(8,128)(2,1)}, bf16[64,1024]{1,0:T(8,128)(2,1)S(1)}, u32[]{:S(2)}, u32[]{:S(2)}) collective-permute-start(bf16[64,1024]{1,0:T(8,128)(2,1)} %bitcast.45), channel_id=1, source_target_pairs={{0,24},{2,26},{4,28},{6,30},{8,16},{10,18},{12,20},{14,22},{16,8},... | collective-permute-start | bytes 393224 | tf_op jit(solution)/shard_map/ppermute | solution.py:48
  70.2 15.6 %collective-permute-start.24 = (bf16[64,1024]{1,0:T(8,128)(2,1)}, bf16[64,1024]{1,0:T(8,128)(2,1)S(1)}, u32[]{:S(2)}, u32[]{:S(2)}) collective-permute-start(bf16[64,1024]{1,0:T(8,128)(2,1)} %convert_bitcast_fusion.1), channel_id=1, source_target_pairs={{0,8},{2,10},{4,12},{6,14},{8,0},{10,2},{12,4},{14,6},{16,24},{18,... | collective-permute-start | bytes 393224 | tf_op jit(solution)/shard_map/ppermute | solution.py:48
  71.8 15.6 %collective-permute-start.25 = (bf16[64,1024]{1,0:T(8,128)(2,1)}, bf16[64,1024]{1,0:T(8,128)(2,1)S(1)}, u32[]{:S(2)}, u32[]{:S(2)}) collective-permute-start(bf16[64,1024]{1,0:T(8,128)(2,1)} %convert_bitcast_fusion.1), channel_id=1, source_target_pairs={{0,16},{2,18},{4,20},{6,22},{8,24},{10,26},{12,28},{14,30},{16,0},... | collective-permute-start | bytes 393224 | tf_op jit(solution)/shard_map/ppermute | solution.py:48
  73.3 15.6 %collective-permute-start.26 = (bf16[64,1024]{1,0:T(8,128)(2,1)}, bf16[64,1024]{1,0:T(8,128)(2,1)S(1)}, u32[]{:S(2)}, u32[]{:S(2)}) collective-permute-start(bf16[64,1024]{1,0:T(8,128)(2,1)} %convert_bitcast_fusion.1), channel_id=1, source_target_pairs={{0,24},{2,26},{4,28},{6,30},{8,16},{10,18},{12,20},{14,22},{16,8},... | collective-permute-start | bytes 393224 | tf_op jit(solution)/shard_map/ppermute | solution.py:48
  81.8 36.9 %collective-permute-start = (bf16[512,1024]{1,0:T(8,128)(2,1)S(1)}, bf16[512,1024]{1,0:T(8,128)(2,1)}, u32[]{:S(2)}, u32[]{:S(2)}) collective-permute-start(bf16[512,1024]{1,0:T(8,128)(2,1)S(1)} %copy-done.10), channel_id=1, source_target_pairs={{0,1},{1,0},{2,3},{3,2},{4,5},{5,4},{6,7},{7,6},{8,9},{9,8},{10,11... | collective-permute-start | bytes 3145736 | tf_op jit(solution)/shard_map/ppermute | solution.py:48
  85.8 14.9 %collective-permute-start.10 = (bf16[4,64,1024]{2,1,0:T(8,128)(2,1)S(1)}, bf16[4,64,1024]{2,1,0:T(8,128)(2,1)S(1)}, u32[]{:S(2)}, u32[]{:S(2)}) collective-permute-start(bf16[4,64,1024]{2,1,0:T(8,128)(2,1)S(1)} %pad_maximum_fusion), channel_id=1, source_target_pairs={{0,4},{2,6},{4,0},{6,2},{8,12},{10,14},{12,8},{14,10},{16,20},{18,... | collective-permute-start | bytes 1572872 | tf_op jit(solution)/shard_map/ppermute | solution.py:48
  87.4 24.0 %collective-permute-start.22 = (bf16[4,64,1024]{2,1,0:T(8,128)(2,1)S(1)}, bf16[4,64,1024]{2,1,0:T(8,128)(2,1)S(1)}, u32[]{:S(2)}, u32[]{:S(2)}) collective-permute-start(bf16[4,64,1024]{2,1,0:T(8,128)(2,1)S(1)} %pad_maximum_fusion.1), channel_id=1, source_target_pairs={{0,4},{2,6},{4,0},{6,2},{8,12},{10,14},{12,8},{14,10},{16,20},{18,... | collective-permute-start | bytes 1572872 | tf_op jit(solution)/shard_map/ppermute | solution.py:48
  89.9 27.1 %collective-permute-start.27 = (bf16[4,64,1024]{2,1,0:T(8,128)(2,1)S(1)}, bf16[4,64,1024]{2,1,0:T(8,128)(2,1)S(1)}, u32[]{:S(2)}, u32[]{:S(2)}) collective-permute-start(bf16[4,64,1024]{2,1,0:T(8,128)(2,1)S(1)} %pad_maximum_fusion.2), channel_id=1, source_target_pairs={{0,4},{2,6},{4,0},{6,2},{8,12},{10,14},{12,8},{14,10},{16,20},{18,... | collective-permute-start | bytes 1572872 | tf_op jit(solution)/shard_map/ppermute | solution.py:48
  96.5 21.4 %collective-permute-start.17 = (bf16[8,2,32,288]{3,2,1,0:T(8,128)(2,1)S(1)}, bf16[8,2,32,288]{3,2,1,0:T(8,128)(2,1)S(1)}, u32[]{:S(2)}, u32[]{:S(2)}) collective-permute-start(bf16[8,2,32,288]{3,2,1,0:T(8,128)(2,1)S(1)} %get-tuple-element.139), channel_id=1, source_target_pairs={{0,2},{2,0},{4,6},{6,4},{8,10},{10,8},{12,14},{14,12},{16,18},{18,... | collective-permute-start | bytes 884744 | tf_op jit(solution)/shard_map/ppermute | solution.py:48
  101.5 22.5 %collective-permute-start.11 = (bf16[8,64,1024]{2,1,0:T(8,128)(2,1)}, bf16[8,64,1024]{2,1,0:T(8,128)(2,1)}, u32[]{:S(2)}, u32[]{:S(2)}) collective-permute-start(bf16[8,64,1024]{2,1,0:T(8,128)(2,1)} %constant_dynamic-update-slice_fusion.11.near), channel_id=1, source_target_pairs={{0,2},{2,0},{4,6},{6,4},{8,10},{10,8},{12,14},{14,12},{16,18},{18,... | collective-permute-start | bytes 3145736 | tf_op jit(solution)/shard_map/ppermute | solution.py:48
  112.2 76.5 %collective-permute-start.23 = (bf16[8,64,1024]{2,1,0:T(8,128)(2,1)}, bf16[8,64,1024]{2,1,0:T(8,128)(2,1)}, u32[]{:S(2)}, u32[]{:S(2)}) collective-permute-start(bf16[8,64,1024]{2,1,0:T(8,128)(2,1)} %constant_dynamic-update-slice_fusion.27.near), channel_id=1, source_target_pairs={{0,2},{2,0},{4,6},{6,4},{8,10},{10,8},{12,14},{14,12},{16,18},{18,... | collective-permute-start | bytes 3145736 | tf_op jit(solution)/shard_map/ppermute | solution.py:48
  117.9 135.7 %collective-permute-start.28 = (bf16[8,64,1024]{2,1,0:T(8,128)(2,1)}, bf16[8,64,1024]{2,1,0:T(8,128)(2,1)}, u32[]{:S(2)}, u32[]{:S(2)}) collective-permute-start(bf16[8,64,1024]{2,1,0:T(8,128)(2,1)} %constant_dynamic-update-slice_fusion.32.near), channel_id=1, source_target_pairs={{0,2},{2,0},{4,6},{6,4},{8,10},{10,8},{12,14},{14,12},{16,18},{18,... | collective-permute-start | bytes 3145736 | tf_op jit(solution)/shard_map/ppermute | solution.py:48
  122.4 220.6 %collective-permute-start.18 = (bf16[512,1024]{1,0:T(8,128)(2,1)}, bf16[512,1024]{1,0:T(8,128)(2,1)S(1)}, u32[]{:S(2)}, u32[]{:S(2)}) collective-permute-start(bf16[512,1024]{1,0:T(8,128)(2,1)} %param.23), channel_id=1, source_target_pairs={{0,1},{1,0},{2,3},{3,2},{4,5},{5,4},{6,7},{7,6},{8,9},{9,8},{10,11... | collective-permute-start | bytes 3145736 | tf_op jit(solution)/shard_map/ppermute | solution.py:48
  484.9 25.7 %collective-permute-start.48 = (bf16[8,64,1024]{2,1,0:T(8,128)(2,1)}, bf16[8,64,1024]{2,1,0:T(8,128)(2,1)}, u32[]{:S(2)}, u32[]{:S(2)}) collective-permute-start(bf16[8,64,1024]{2,1,0:T(8,128)(2,1)} %get-tuple-element.79), channel_id=1, source_target_pairs={{0,2},{2,0},{4,6},{6,4},{8,10},{10,8},{12,14},{14,12},{16,18},{18,... | collective-permute-start | bytes 3145736 | tf_op jit(solution)/shard_map/ppermute | solution.py:48
  484.9 28.9 %collective-permute-start.32 = (bf16[8,64,1024]{2,1,0:T(8,128)(2,1)}, bf16[8,64,1024]{2,1,0:T(8,128)(2,1)}, u32[]{:S(2)}, u32[]{:S(2)}) collective-permute-start(bf16[8,64,1024]{2,1,0:T(8,128)(2,1)} %get-tuple-element.73), channel_id=1, source_target_pairs={{0,2},{2,0},{4,6},{6,4},{8,10},{10,8},{12,14},{14,12},{16,18},{18,... | collective-permute-start | bytes 3145736 | tf_op jit(solution)/shard_map/ppermute | solution.py:48
  485.4 31.6 %collective-permute-start.37 = (bf16[8,64,1024]{2,1,0:T(8,128)(2,1)}, bf16[8,64,1024]{2,1,0:T(8,128)(2,1)}, u32[]{:S(2)}, u32[]{:S(2)}) collective-permute-start(bf16[8,64,1024]{2,1,0:T(8,128)(2,1)} %get-tuple-element.75), channel_id=1, source_target_pairs={{0,2},{2,0},{4,6},{6,4},{8,10},{10,8},{12,14},{14,12},{16,18},{18,... | collective-permute-start | bytes 3145736 | tf_op jit(solution)/shard_map/ppermute | solution.py:48
  505.6 26.3 %collective-permute-start.31 = (bf16[512,1024]{1,0:T(8,128)(2,1)}, bf16[512,1024]{1,0:T(8,128)(2,1)S(1)}, u32[]{:S(2)}, u32[]{:S(2)}) collective-permute-start(bf16[512,1024]{1,0:T(8,128)(2,1)} %copy-done.7), channel_id=1, source_target_pairs={{0,1},{1,0},{2,3},{3,2},{4,5},{5,4},{6,7},{7,6},{8,9},{9,8},{10,11... | collective-permute-start | bytes 3145736 | tf_op jit(solution)/shard_map/ppermute | solution.py:48
  508.1 43.4 %collective-permute-start.30 = (bf16[512,1024]{1,0:T(8,128)(2,1)}, bf16[512,1024]{1,0:T(8,128)(2,1)S(1)}, u32[]{:S(2)}, u32[]{:S(2)}) collective-permute-start(bf16[512,1024]{1,0:T(8,128)(2,1)} %slice.227), channel_id=1, source_target_pairs={{0,1},{1,0},{2,3},{3,2},{4,5},{5,4},{6,7},{7,6},{8,9},{9,8},{10,11... | collective-permute-start | bytes 3145736 | tf_op jit(solution)/shard_map/ppermute | solution.py:48
  513.0 42.2 %collective-permute-start.49 = (bf16[4,64,1024]{2,1,0:T(8,128)(2,1)S(1)}, bf16[4,64,1024]{2,1,0:T(8,128)(2,1)S(1)}, u32[]{:S(2)}, u32[]{:S(2)}) collective-permute-start(bf16[4,64,1024]{2,1,0:T(8,128)(2,1)S(1)} %slice.386), channel_id=1, source_target_pairs={{0,4},{2,6},{4,0},{6,2},{8,12},{10,14},{12,8},{14,10},{16,20},{18,... | collective-permute-start | bytes 1572872 | tf_op jit(solution)/shard_map/ppermute | solution.py:48
  515.6 42.3 %collective-permute-start.33 = (bf16[4,64,1024]{2,1,0:T(8,128)(2,1)S(1)}, bf16[4,64,1024]{2,1,0:T(8,128)(2,1)S(1)}, u32[]{:S(2)}, u32[]{:S(2)}) collective-permute-start(bf16[4,64,1024]{2,1,0:T(8,128)(2,1)S(1)} %slice.388), channel_id=1, source_target_pairs={{0,4},{2,6},{4,0},{6,2},{8,12},{10,14},{12,8},{14,10},{16,20},{18,... | collective-permute-start | bytes 1572872 | tf_op jit(solution)/shard_map/ppermute | solution.py:48
  518.8 42.0 %collective-permute-start.38 = (bf16[4,64,1024]{2,1,0:T(8,128)(2,1)S(1)}, bf16[4,64,1024]{2,1,0:T(8,128)(2,1)S(1)}, u32[]{:S(2)}, u32[]{:S(2)}) collective-permute-start(bf16[4,64,1024]{2,1,0:T(8,128)(2,1)S(1)} %slice.387), channel_id=1, source_target_pairs={{0,4},{2,6},{4,0},{6,2},{8,12},{10,14},{12,8},{14,10},{16,20},{18,... | collective-permute-start | bytes 1572872 | tf_op jit(solution)/shard_map/ppermute | solution.py:48
  555.5 33.4 %collective-permute-start.50 = (bf16[64,1024]{1,0:T(8,128)(2,1)S(1)}, bf16[64,1024]{1,0:T(8,128)(2,1)S(1)}, u32[]{:S(2)}, u32[]{:S(2)}) collective-permute-start(bf16[64,1024]{1,0:T(8,128)(2,1)S(1)} %get-tuple-element.128), channel_id=1, source_target_pairs={{0,8},{2,10},{4,12},{6,14},{8,0},{10,2},{12,4},{14,6},{16,24},{18,... | collective-permute-start | bytes 393224 | tf_op jit(solution)/shard_map/ppermute | solution.py:48
  555.5 33.3 %collective-permute-start.51 = (bf16[64,1024]{1,0:T(8,128)(2,1)S(1)}, bf16[64,1024]{1,0:T(8,128)(2,1)S(1)}, u32[]{:S(2)}, u32[]{:S(2)}) collective-permute-start(bf16[64,1024]{1,0:T(8,128)(2,1)S(1)} %get-tuple-element.130), channel_id=1, source_target_pairs={{0,16},{2,18},{4,20},{6,22},{8,24},{10,26},{12,28},{14,30},{16,0},... | collective-permute-start | bytes 393224 | tf_op jit(solution)/shard_map/ppermute | solution.py:48
  559.4 17.3 %collective-permute-start.35 = (bf16[64,1024]{1,0:T(8,128)(2,1)S(1)}, bf16[64,1024]{1,0:T(8,128)(2,1)S(1)}, u32[]{:S(2)}, u32[]{:S(2)}) collective-permute-start(bf16[64,1024]{1,0:T(8,128)(2,1)S(1)} %get-tuple-element.133), channel_id=1, source_target_pairs={{0,16},{2,18},{4,20},{6,22},{8,24},{10,26},{12,28},{14,30},{16,0},... | collective-permute-start | bytes 393224 | tf_op jit(solution)/shard_map/ppermute | solution.py:48
  560.8 15.9 %collective-permute-start.36 = (bf16[64,1024]{1,0:T(8,128)(2,1)S(1)}, bf16[64,1024]{1,0:T(8,128)(2,1)S(1)}, u32[]{:S(2)}, u32[]{:S(2)}) collective-permute-start(bf16[64,1024]{1,0:T(8,128)(2,1)S(1)} %get-tuple-element.132), channel_id=1, source_target_pairs={{0,24},{2,26},{4,28},{6,30},{8,16},{10,18},{12,20},{14,22},{16,8},... | collective-permute-start | bytes 393224 | tf_op jit(solution)/shard_map/ppermute | solution.py:48
  (59 other events, 515.0 us)

commit v2 on v1

--- a/solution.py
+++ b/solution.py
@@ -71,15 +71,23 @@
     return plane, swap(plane, "dp", dp, 1)
 
 
-def scatter_sum(keep, send, dp):
+def start_sum(keep, send, dp):
     high, middle = axis_parts(dp)
-    total = keep.astype(f32) + swap(send, "dp", dp, 1).astype(f32)
-    total = total.reshape((middle, high) + total.shape[1:])
+    total = keep + swap(send, "dp", dp, 1).astype(f32)
+    return total.reshape((middle, high) + total.shape[1:])
+
+
+def middle_sum(total, dp):
     line = total[0]
-    for step in range(1, middle):
+    for step in range(1, total.shape[0]):
         line = line + swap(total[step].astype(bf16), "dp", dp, step * CORES).astype(f32)
+    return line
+
+
+def high_sum(line, dp):
+    middle = axis_parts(dp)[1]
     block = line[0]
-    for step in range(1, high):
+    for step in range(1, line.shape[0]):
         block = block + swap(line[step].astype(bf16), "dp", dp, step * middle * CORES).astype(f32)
     return block
 
@@ -175,29 +183,27 @@
     )
 
 
-def assemble_kernel(dp, me, near, far, out, sems):
+def assemble_kernel(dp, me, near, far, *outs):
     half = dp // CORES
-    places = relative_places(dp)
-    copies = []
-    for place, distance in enumerate(places):
-        source = near.at[place] if place < half else far.at[place - half]
-        copies.append(pltpu.make_async_copy(source, out.at[me[0] ^ distance], sems.at[place]))
-    for copy in copies:
-        copy.start()
-    for copy in copies:
-        copy.wait()
-
-
-def assemble(near, far, dp, dp_rank):
-    any_spec = pl.BlockSpec(memory_space=pl.ANY)
+    for place, distance in enumerate(relative_places(dp)):
+        source, at = (near, place) if place < half else (far, place - half)
+        start = 0
+        for out in outs:
+            out[me[0] ^ distance] = source[at, start : start + out.shape[1], :]
+            start += out.shape[1]
+
+
+def assemble(near, far, dp, dp_rank, counts):
+    width = near.shape[2]
+    vmem = pl.BlockSpec(memory_space=pltpu.VMEM)
     return pl.pallas_call(
         functools.partial(assemble_kernel, dp),
-        in_specs=[pl.BlockSpec(memory_space=pltpu.SMEM), any_spec, any_spec],
-        out_specs=any_spec,
-        out_shape=shape(dp, *near.shape[1:], dtype=near.dtype),
-        scratch_shapes=[pltpu.SemaphoreType.DMA((dp,))],
+        in_specs=[pl.BlockSpec(memory_space=pltpu.SMEM), vmem, vmem],
+        out_specs=[vmem] * len(counts),
+        out_shape=[shape(dp, count, width, dtype=near.dtype) for count in counts],
+        compiler_params=pltpu.CompilerParams(vmem_limit_bytes=24 * 1024 * 1024),
         cost_estimate=pl.CostEstimate(flops=0, bytes_accessed=4 * near.size * 2, transcendentals=0),
-    )(dp_rank, near, far).reshape(dp * near.shape[1], near.shape[2])
+    )(dp_rank, near, far)
 
 
 def scan_kernel(
@@ -310,17 +316,18 @@
 
 def scan_back_kernel(
     dssd, mix, pre, ch, ssd, hin, step, conv, skip, hp, aux, segr, heads_of,
-    dval_o, dcommon_o, dconv_o, dheads_o, dskip_o,
-    dmix, dwin, both, dstate, carry,
+    state_in, win_in, carry_in,
+    dval_o, dcommon_o, dconv_o, dheads_o, dskip_o, dstate, dtail, carry,
+    dmix, dwin, both,
 ):
     width = dssd.shape[1]
     channels = width + 2 * N
 
     @pl.when(pl.program_id(0) == 0)
     def _():
-        dwin[CHUNK:, :] = jnp.zeros((8, channels), f32)
-        dstate[...] = jnp.zeros(dstate.shape, f32)
-        carry[...] = jnp.zeros(carry.shape, f32)
+        dwin[CHUNK:, :] = win_in[...]
+        dstate[...] = state_in[...]
+        carry[...] = carry_in[...]
         dconv_o[...] = jnp.zeros(dconv_o.shape, f32)
         dheads_o[...] = jnp.zeros(dheads_o.shape, f32)
         dskip_o[...] = jnp.zeros(dskip_o.shape, f32)
@@ -410,40 +417,101 @@
         else:
             dcommon_o[:, : 2 * N] = total
     dwin[CHUNK:, :] = dwin[0:8, :]
-
-
-def weight_grad_kernel(dp, me, lhs, rhs, keep_o, send_o, full):
-    full[...] = mm(lhs[...], rhs[...], 0, 0)
+    dtail[...] = dwin[0:8, :]
+
+
+def scatter_blocks(dp, me, full, keep_o, send_o, cols):
     half = dp // CORES
-    block = lhs.shape[1] // dp
+    block = full.shape[0] // dp
     for place, distance in enumerate(relative_places(dp)):
         start = pl.multiple_of((me[0] ^ distance) * block, block)
         part = full[pl.ds(start, block), :]
         if place < half:
-            keep_o[place] = part
+            keep_o[place, :, cols] = part
         else:
-            send_o[place - half] = part.astype(bf16)
-
-
-def weight_grad(lhs, rhs, dp, dp_rank):
-    length, width = rhs.shape
-    depth = lhs.shape[1]
-    block, half = depth // dp, dp // CORES
-    piece = pl.BlockSpec((half, block, 256), lambda i, *s: (0, 0, i))
+            send_o[place - half, :, cols] = part.astype(bf16)
+
+
+def pair_grad_kernel(dp, me, lhs0, lhs1, rhs0, rhs1, keep_o, send_o, turned, full):
+    step = pl.program_id(0)
+    per = pl.num_programs(0) // 2
+    for first, lhs, rhs in ((0, lhs0, rhs0), (per, lhs1, rhs1)):
+
+        @pl.when(step == first)
+        def _():
+            turned[...] = lhs[...].T
+
+        @pl.when((step >= first) & (step < first + per))
+        def _():
+            full[...] = mm(turned[...], rhs[...])
+
+    scatter_blocks(dp, me, full, keep_o, send_o, slice(None))
+
+
+def pair_grad(lhs0, rhs0, lhs1, rhs1, dp, dp_rank):
+    length, width = rhs0.shape
+    depth = lhs0.shape[1]
+    block, half, per = depth // dp, dp // CORES, width // 256
+    piece = pl.BlockSpec((half, block, 256), lambda i, *s: (0, i // per, i % per))
     return call(
-        functools.partial(weight_grad_kernel, dp),
-        (width // 256,),
-        [whole((length, depth)), pl.BlockSpec((length, 256), lambda i, *s: (0, i))],
+        functools.partial(pair_grad_kernel, dp),
+        (2 * per,),
+        [
+            whole((length, depth)), whole((length, depth)),
+            pl.BlockSpec((length, 256), lambda i, *s: (0, jnp.minimum(i, per - 1))),
+            pl.BlockSpec((length, 256), lambda i, *s: (0, jnp.maximum(i - per, 0))),
+        ],
         [piece, piece],
-        [shape(half, block, width), shape(half, block, width, dtype=bf16)],
-        [pltpu.VMEM((depth, 256), f32)],
-        2 * length * width * depth,
+        [shape(half, 2 * block, width), shape(half, 2 * block, width, dtype=bf16)],
+        [pltpu.VMEM((depth, length), bf16), pltpu.VMEM((depth, 256), f32)],
+        4 * length * width * depth,
         scalars=1,
-    )(dp_rank, lhs, rhs)
-
-
-def shared_grad_kernel(lhs, rhs, out):
-    out[...] = mm_right(lhs[...], rhs[...], 0, 0)
+    )(dp_rank, lhs0, lhs1, rhs0, rhs1)
+
+
+def value_grad_kernel(dp, me, lhs, dval, dcommon, keep_o, send_o, turned, full, wide):
+    step = pl.program_id(0)
+    last = pl.num_programs(0) - 1
+
+    @pl.when(step == 0)
+    def _():
+        turned[...] = lhs[...].T
+
+    @pl.when(step < last)
+    def _():
+        full[...] = mm(turned[...], dval[...])
+        cols = pl.ds(pl.multiple_of(step * 256, 256), 256)
+        scatter_blocks(dp, me, full, keep_o, send_o, cols)
+
+    @pl.when(step == last)
+    def _():
+        wide[...] = mm_right(turned[...], dcommon[...])
+        cols = slice(keep_o.shape[2] - wide.shape[1], keep_o.shape[2])
+        scatter_blocks(dp, me, wide, keep_o, send_o, cols)
+
+
+def value_grad(lhs, dval, dcommon, dp, dp_rank):
+    length, width = dval.shape
+    depth, extra = lhs.shape[1], dcommon.shape[1]
+    block, half, per = depth // dp, dp // CORES, width // 256
+    dims = (half, block, width + extra)
+    return call(
+        functools.partial(value_grad_kernel, dp),
+        (per + 1,),
+        [
+            whole((length, depth)),
+            pl.BlockSpec((length, 256), lambda i, *s: (0, jnp.minimum(i, per - 1))),
+            whole((length, extra)),
+        ],
+        [whole(dims), whole(dims)],
+        [shape(*dims), shape(*dims, dtype=bf16)],
+        [
+            pltpu.VMEM((depth, length), bf16), pltpu.VMEM((depth, 256), f32),
+            pltpu.VMEM((depth, extra), f32),
+        ],
+        2 * length * (width + 2 * extra) * depth,
+        scalars=1,
+    )(dp_rank, lhs, dval, dcommon)
 
 
 def input_grad_kernel(rank, dgate, dval, dcommon, tok, wg, wv, shw, ng_o, gain_o):
@@ -483,7 +551,6 @@
     wide = 2 * CHUNK
     band = min(2 * CHUNK, rows_here)
     per_piece = rows_here // band
-    places = jnp.array(relative_places(dp), jnp.int32)
 
     def over_tensor(value):
         pieces = [value] + [swap(value, "tensor", nt, d) for d in range(1, nt)]
@@ -494,34 +561,49 @@
         stacked = jnp.take(jnp.stack(pieces), jnp.arange(nt) ^ t_rank, axis=0)
         return stacked.reshape((nt * value.shape[0],) + value.shape[1:])
 
-    tokens_all = over_tensor(residual)
-
-    def everywhere(value):
-        pieces = jnp.stack([value] + [swap(value, "tensor", nt, d) for d in range(1, nt)])
-        pieces = jnp.take(pieces, jnp.arange(nt) ^ t_rank, axis=0)
-        both = jnp.concatenate(gather_halves(pieces, dp), axis=0)
-        spots = jnp.argsort(places ^ d_rank)
-        return jnp.take(both, spots, axis=0)
-
-    small = jnp.concatenate([conv_params.reshape(1, -1), norm_gains.reshape(1, -1)], axis=1)
-    small_all = everywhere(small).reshape(dp * nt, -1)
     kernel_rows, columns = conv_params.shape
+    gain_count = norm_gains.shape[0]
+    shared_size = shared_proj.size
+    exact = jnp.concatenate([conv_params.reshape(-1), norm_gains])
+    terms = []
+    rest = exact
+    for _ in range(3):
+        term = lax.optimization_barrier(rest.astype(bf16))
+        terms.append(term)
+        rest = rest - term.astype(f32)
+    small = jnp.concatenate([shared_proj.astype(bf16).reshape(-1)] + terms)
+    small_rows = -(-small.size // width)
+    while small_rows * nt % 16:
+        small_rows += 1
+    small = jnp.pad(small, (0, small_rows * width - small.size)).reshape(small_rows, width)
+    small_pair = over_tensor(small)
+    tokens_all = over_tensor(after(residual, small_pair))
+
+    block_rows = D // dp
+    value_shard = jnp.concatenate([inner_proj[1].astype(bf16), small_pair], axis=0)
+    near, far = gather_halves(value_shard, dp)
+    value_w, small_all = assemble(near, far, dp, dp_me, [block_rows, small_rows * nt])
+    value_w = value_w.reshape(D, width)
+    other_shard = jnp.concatenate(
+        [inner_proj[0].astype(bf16), outer_proj.T.astype(bf16)], axis=0
+    )
+    other_halves = gather_halves(after(other_shard, near), dp)
+    gate_w, outer_t = assemble(*other_halves, dp, dp_me, [block_rows, block_rows])
+    gate_w, outer_t = gate_w.reshape(D, width), outer_t.reshape(D, width)
+    cot_all = over_tensor(after(cotangent, tokens_all))
+
+    small_all = small_all.reshape(dp * nt, small_rows * width)
+    shared_full = small_all[:, :shared_size].reshape(D, -1)
+    exact_all = small_all[:, shared_size : shared_size + 3 * exact.size].astype(f32)
+    exact_all = exact_all.reshape(dp * nt, 3, exact.size)
+    exact_all = (exact_all[:, 0] + exact_all[:, 1]) + exact_all[:, 2]
     conv_full = (
-        small_all[:, : kernel_rows * columns]
+        exact_all[:, : kernel_rows * columns]
         .reshape(dp * nt, kernel_rows, columns)
         .transpose(1, 0, 2)
         .reshape(kernel_rows, -1)
     )
-    gains_full = small_all[:, kernel_rows * columns :].reshape(-1)
-    shared_full = everywhere(shared_proj.astype(bf16)).reshape(D, -1)
-
-    value_shard = inner_proj[1].astype(bf16)
-    gate_shard = inner_proj[0].astype(bf16)
-    outer_shard = outer_proj.T.astype(bf16)
-    value_w = assemble(*gather_halves(value_shard, dp), dp, dp_me)
-    gate_w = assemble(*gather_halves(gate_shard, dp), dp, dp_me)
-    outer_t = assemble(*gather_halves(outer_shard, dp), dp, dp_me)
-    cot_all = over_tensor(after(cotangent, tokens_all))
+    gains_full = exact_all[:, kernel_rows * columns :].reshape(-1)
 
     pre_gain = gains_full[:D].reshape(1, D)
     post_gain = lax.dynamic_slice_in_dim(gains_full, D + t_rank * width, width).reshape(1, width)
@@ -634,8 +716,9 @@
         2 * length * D * width,
         scalars=1,
     )(t_me, gate, scaled_grad, ssd, sums, outer_t, post_gain)
-    outer_part = scatter_sum(*weight_grad(returned, scaled, dp, dp_me), dp)
-    gate_part = scatter_sum(*weight_grad(normed, dgate, dp, dp_me), dp)
+    sums_og = start_sum(*pair_grad(returned, scaled, normed, dgate, dp, dp_me), dp)
+    dssd = after(dssd, sums_og)
+    line_og = middle_sum(sums_og, dp)
 
     branch = branch.reshape(nt, rows_here, D)
     branch_sum = branch[0].astype(f32)
@@ -645,33 +728,55 @@
     tokens = residual.astype(f32)
     block_out = (tokens + branch_sum * live_here[:, None]).astype(bf16)
 
-    back = lambda i: chunks - 1 - i
-    dval, dcommon, dconv, dheads, dskip = call(
-        scan_back_kernel,
-        (chunks,),
-        [
-            rows(CHUNK, width, back), rows(CHUNK, channels, back), rows(CHUNK, channels, back),
-            rows(CHUNK, channels, back), rows(CHUNK, width, back),
-            pl.BlockSpec((1, N, width), lambda i: (chunks - 1 - i, 0, 0)),
-            rows(CHUNK, LANES, back), whole((8, channels)), whole((1, width)),
-            whole((8, LANES)), rows(CHUNK, aux_cols, back),
-            pl.BlockSpec((1, CHUNK), lambda i: (0, chunks - 1 - i)), whole((width, LANES)),
-        ],
-        [
-            rows(CHUNK, width, back), rows(CHUNK, common_width, back), whole((8, channels)),
-            whole((8, LANES)), whole((1, width)),
-        ],
-        [
-            shape(length, width, dtype=bf16), shape(length, common_width), shape(8, channels),
-            shape(8, LANES), shape(1, width),
-        ],
-        [
-            pltpu.VMEM((CHUNK, channels), f32), pltpu.VMEM((CHUNK + 8, channels), f32),
-            pltpu.VMEM((2 * CHUNK, width), f32), pltpu.VMEM((N, width), f32),
-            pltpu.VMEM((8, LANES), f32),
-        ],
-        length * 30 * width * CHUNK,
-    )(dssd, mixed, pre, chans, ssd, entering, step_in, conv_here, skip, head_rows, aux, segr, heads_of)
+    calls = 2
+    per_call = chunks // calls
+    state = jnp.zeros((N, width), f32)
+    win = jnp.zeros((8, channels), f32)
+    carry = jnp.zeros((8, LANES), f32)
+    back_parts = []
+    for part in range(calls):
+        back = lambda i, top=chunks - 1 - part * per_call: top - i
+        here = lambda i: per_call - 1 - i
+        *results, state, win, carry = call(
+            scan_back_kernel,
+            (per_call,),
+            [
+                rows(CHUNK, width, back), rows(CHUNK, channels, back), rows(CHUNK, channels, back),
+                rows(CHUNK, channels, back), rows(CHUNK, width, back),
+                pl.BlockSpec((1, N, width), lambda i, back=back: (back(i), 0, 0)),
+                rows(CHUNK, LANES, back), whole((8, channels)), whole((1, width)),
+                whole((8, LANES)), rows(CHUNK, aux_cols, back),
+                pl.BlockSpec((1, CHUNK), lambda i, back=back: (0, back(i))),
+                whole((width, LANES)),
+                whole((N, width)), whole((8, channels)), whole((8, LANES)),
+            ],
+            [
+                rows(CHUNK, width, here), rows(CHUNK, common_width, here), whole((8, channels)),
+                whole((8, LANES)), whole((1, width)),
+                whole((N, width)), whole((8, channels)), whole((8, LANES)),
+            ],
+            [
+                shape(length // calls, width, dtype=bf16), shape(length // calls, common_width),
+                shape(8, channels), shape(8, LANES), shape(1, width),
+                shape(N, width), shape(8, channels), shape(8, LANES),
+            ],
+            [
+                pltpu.VMEM((CHUNK, channels), f32), pltpu.VMEM((CHUNK + 8, channels), f32),
+                pltpu.VMEM((2 * CHUNK, width), f32),
+            ],
+            length // calls * 30 * width * CHUNK,
+        )(
+            dssd, mixed, pre, chans, ssd, entering, step_in, conv_here, skip, head_rows, aux, segr,
+            heads_of, state, win, carry,
+        )
+        back_parts.append(results)
+        if part == 0:
+            state = after(state, line_og)
+    dval = jnp.concatenate([back_parts[1][0], back_parts[0][0]], axis=0)
+    dcommon = jnp.concatenate([back_parts[1][1], back_parts[0][1]], axis=0)
+    dconv, dheads, dskip = [back_parts[0][i] + back_parts[1][i] for i in range(2, 5)]
+    og_part = high_sum(line_og, dp)
+    outer_part, gate_part = og_part[:block_rows], og_part[block_rows:]
 
     def input_grad(count, offset, dtype):
         return call(
@@ -688,36 +793,34 @@
             scalars=1,
         )(t_me, dgate, dval, dcommon, tokens_all, gate_w, value_w, shared_here)
 
+    value_keep, value_send = value_grad(normed, dval, dcommon, dp, dp_me)
     sent, pre_grad_sent = input_grad(nt - 1, per_piece, bf16)
     sent = sent.reshape(nt - 1, rows_here, D)
-    value_part = scatter_sum(*weight_grad(normed, dval, dp, dp_me), dp)
     own, pre_grad_own = input_grad(1, 0, f32)
     normed_grad = own
     for d in range(1, nt):
         normed_grad = normed_grad + swap(sent[d - 1], "tensor", nt, d).astype(f32)
 
-    shared_grad = pl.pallas_call(
-        shared_grad_kernel,
-        out_shape=shape(D, common_width),
-        compiler_params=pltpu.CompilerParams(vmem_limit_bytes=50 * 1024 * 1024),
-        cost_estimate=pl.CostEstimate(
-            flops=4 * length * D * common_width, bytes_accessed=6 * D * common_width, transcendentals=0
-        ),
-    )(normed, dcommon)
+    value_sum = high_sum(middle_sum(start_sum(value_keep, value_send, dp), dp), dp)
+    value_part = value_sum[:, :width]
     shared_rows = shared_proj.shape[0]
-    shared_grad = lax.dynamic_update_slice(
-        jnp.pad(shared_grad[:, : 2 * N], ((0, 0), (0, H))),
-        shared_grad[:, 2 * N : 2 * N + heads_here],
-        (0, 2 * N + t_rank * heads_here),
-    )
-    shared_grad = shared_grad.reshape(dp, nt, shared_rows, 2 * N + H)
-    shared_mine = lax.dynamic_index_in_dim(shared_grad, t_rank, 1, False)
+    shared_sum = value_sum[:, width:].reshape(nt, shared_rows, common_width)
+    shared_mine = lax.dynamic_index_in_dim(shared_sum, t_rank, 0, False)
+    shared_common = shared_mine[:, : 2 * N]
+    shared_part = jnp.zeros((shared_rows, 2 * N + H), f32)
+
+    def place_heads(table, piece, rank):
+        return lax.dynamic_update_slice(
+            table, piece[:, 2 * N : 2 * N + heads_here], (0, 2 * N + rank * heads_here)
+        )
+
+    shared_part = place_heads(shared_part, shared_mine, t_rank)
     for d in range(1, nt):
-        part = lax.dynamic_index_in_dim(shared_grad, t_rank ^ d, 1, False).astype(bf16)
-        shared_mine = shared_mine + swap(part, "tensor", nt, d).astype(f32)
-    shared_mine = jnp.take(shared_mine, places ^ d_rank, axis=0)
-    half = dp // CORES
-    shared_part = scatter_sum(shared_mine[:half], shared_mine[half:].astype(bf16), dp)
+        piece = lax.dynamic_index_in_dim(shared_sum, t_rank ^ d, 0, False)
+        piece = swap(piece, "tensor", nt, d)
+        shared_common = shared_common + piece[:, : 2 * N]
+        shared_part = place_heads(shared_part, piece, t_rank ^ d)
+    shared_part = lax.dynamic_update_slice(shared_part, shared_common, (0, 0))
 
     conv_grad = lax.dynamic_update_slice(
         jnp.pad(dconv[:kernel_rows, width:], ((0, 0), (DI, 0))),
@@ -749,7 +852,6 @@
     conv_part = lax.dynamic_slice_in_dim(
         vector[0, :conv_size].reshape(kernel_rows, -1), place * columns, columns, 1
     )
-    gain_count = norm_gains.shape[0]
     gains_part = lax.dynamic_slice_in_dim(vector[0], conv_size + place * gain_count, gain_count)
     heads_part = lax.dynamic_slice_in_dim(
         vector[0, conv_size + D + DI :].reshape(3, H), t_rank * heads_here, heads_here, 1

time: 597 us -> 352 us (0.59)
  Pallas kernels: 312 us -> 124 us
  starting transfers between devices: 76.3 us -> 45.7 us
  other arithmetic: 47 us -> 35.3 us
  local copies, waits for them, and re-layouts: 42.9 us -> 34.3 us
    pallas_call x3 -> x2, Pallas kernels: 194 us -> 3.47 us  [assemble(): pl.pallas_call(functools.partial(assemble_kernel, dp), in_specs=[pl.Block...]
    ppermute x58 -> x32, starting transfers between devices: 76.3 us -> 45.7 us  [swap(): return lax.ppermute(value, axis, [(i, i ^ distance) for i in range(size)])]
    ppermute x58 -> x32, waiting for transfers between devices: 110 us -> 106 us  [swap(): return lax.ppermute(value, axis, [(i, i ^ distance) for i in range(size)])]
    pallas_call x5 -> x4, Pallas kernels: 58 us -> 60.3 us  [the longest x2 37.2 us: shards(): call(scan_back_kernel, (per_call,), [rows(CHUNK, width, back), rows(CHUNK...]
    unnamed x85 -> x103, local copies, waits for them, and re-layouts: 19.8 us -> 19.5 us
  transfers between devices with their start and end apart: 58 -> 32, of which waited for: 21 -> 19; matrix products, arithmetic and copies ran while one was open for 12% -> 13% of each run, Pallas kernels for 40% -> 16%
where the time goes in v2:
time: 352 us; the launch traced here: 347 us
  Pallas kernels  124 us (35%)
  waiting for transfers between devices  106 us (30%)
  starting transfers between devices  45.7 us (13%)
  other arithmetic  35.3 us (10%)
  local copies, waits for them, and re-layouts  34.3 us (10%)
    ppermute x32, waiting for transfers between devices, swap(): return lax.ppermute(value, axis, [(i, i ^ distance) for i in range(size)])  106 us
    ppermute x32, starting transfers between devices, swap(): return lax.ppermute(value, axis, [(i, i ^ distance) for i in range(size)])  45.7 us
    pallas_call x2, Pallas kernels, shards(): call(scan_back_kernel, (per_call,), [rows(CHUNK, width, back), rows(CHUNK...  37.2 us
    pallas_call x1, Pallas kernels, shards(): call(scan_kernel, (steps,), [rows(wide, D), whole((1, D)), whole((D, widt...  24.5 us
    unnamed x103, local copies, waits for them, and re-layouts  19.5 us
    pallas_call x2, Pallas kernels, input_grad(): call(input_grad_kernel, (count * per_piece,), [rel_rows(width, offset), r...  15.3 us
    pallas_call x1, Pallas kernels, pair_grad(): call(functools.partial(pair_grad_kernel, dp), (2 * per,), [whole((length,...  12.5 us
    pallas_call x1, Pallas kernels, value_grad(): call(functools.partial(value_grad_kernel, dp), (per + 1,), [whole((length...  10.6 us
  transfers between devices with their start and end apart: 32, of which 19 were waited for; matrix products, arithmetic and copies ran while one was open for 13% of the time, Pallas kernels for 16%

profile of v2, /device:TPU:0, one launch (start us, length us, event | category | flops | bytes accessed | tf_op | source)
XLA Modules:
  0.0 347.2 jit_solution(11645478225695913432)
XLA Ops:
  4.7 3.0 collective-permute-start
  19.9 4.1 %collective-permute-done.2 = bf16[96,1024]{1,0:T(8,128)(2,1)S(1)} collective-permute-done((bf16[96,1024]{1,0:T(8,128)(2,1)S(1)}, bf16[96,1024]{1,0:T(8,128)(2,1)S(1)}, u32[]{:S(2)}, u32[]{:S(2)}) %collective-permute-start.2) | collective-permute-done | bytes 196640 | tf_op jit(solution)/shard_map/ppermute | solution.py:48
  24.0 9.2 %collective-permute-done.3 = bf16[96,1024]{1,0:T(8,128)(2,1)S(1)} collective-permute-done((bf16[96,1024]{1,0:T(8,128)(2,1)S(1)}, bf16[96,1024]{1,0:T(8,128)(2,1)S(1)}, u32[]{:S(2)}, u32[]{:S(2)}) %collective-permute-start.3) | collective-permute-done | bytes 196640 | tf_op jit(solution)/shard_map/ppermute | solution.py:48
  38.3 11.8 %collective-permute-done.5 = bf16[4,96,1024]{2,1,0:T(8,128)(2,1)S(1)} collective-permute-done((bf16[4,96,1024]{2,1,0:T(8,128)(2,1)S(1)}, bf16[4,96,1024]{2,1,0:T(8,128)(2,1)S(1)}, u32[]{:S(2)}, u32[]{:S(2)}) %collective-permute-start.5) | collective-permute-done | bytes 786464 | tf_op jit(solution)/shard_map/ppermute | solution.py:48
  50.2 4.9 %collective-permute-start.8 = (bf16[128,1024]{1,0:T(8,128)(2,1)S(1)}, bf16[128,1024]{1,0:T(8,128)(2,1)}, u32[]{:S(2)}, u32[]{:S(2)}) collective-permute-start(bf16[128,1024]{1,0:T(8,128)(2,1)S(1)} %pad_maximum_fusion.3), channel_id=1, source_target_pairs={{0,8},{2,10},{4,12},{6,14},{8,0},{10,2},{12,4},{14,6},{16,24},{18,... | collective-permute-start | bytes 786440 | tf_op jit(solution)/shard_map/ppermute | solution.py:48
  58.5 4.2 %collective-permute-done.8 = bf16[128,1024]{1,0:T(8,128)(2,1)} collective-permute-done((bf16[128,1024]{1,0:T(8,128)(2,1)S(1)}, bf16[128,1024]{1,0:T(8,128)(2,1)}, u32[]{:S(2)}, u32[]{:S(2)}) %collective-permute-start.8) | collective-permute-done | bytes 262176 | tf_op jit(solution)/shard_map/ppermute | solution.py:48
  62.7 12.9 %collective-permute-done.9 = bf16[128,1024]{1,0:T(8,128)(2,1)} collective-permute-done((bf16[128,1024]{1,0:T(8,128)(2,1)S(1)}, bf16[128,1024]{1,0:T(8,128)(2,1)}, u32[]{:S(2)}, u32[]{:S(2)}) %collective-permute-start.9) | collective-permute-done | bytes 262176 | tf_op jit(solution)/shard_map/ppermute | solution.py:48
  78.5 4.0 %maximum_select_fusion.tok = bf16[1024,1024]{1,0:T(8,128)(2,1)} fusion(bf16[512,1024]{1,0:T(8,128)(2,1)} %collective-permute-done.1, bf16[512,1024]{1,0:T(8,128)(2,1)S(1)} %copy-done.7, pred[]{:T(512)S(6)} %eq.81), kind=kLoop, calls=%fused_computation.16 | loop fusion | flops 9437184 | bytes 4194305 | tf_op jit(solution)/shard_map/jit(_where)/select_n | solution.py:560
  88.7 7.0 %collective-permute-done.11 = bf16[4,128,1024]{2,1,0:T(8,128)(2,1)S(1)} collective-permute-done((bf16[4,128,1024]{2,1,0:T(8,128)(2,1)S(1)}, bf16[4,128,1024]{2,1,0:T(8,128)(2,1)S(1)}, u32[]{:S(2)}, u32[]{:S(2)}) %collective-permute-start.11) | collective-permute-done | bytes 1048608 | tf_op jit(solution)/shard_map/ppermute | solution.py:48
  96.8 4.1 %collective-permute-done.7 = bf16[512,1024]{1,0:T(8,128)(2,1)S(1)} collective-permute-done((bf16[512,1024]{1,0:T(8,128)(2,1)S(1)}, bf16[512,1024]{1,0:T(8,128)(2,1)S(1)}, u32[]{:S(2)}, u32[]{:S(2)}) %collective-permute-start.7) | collective-permute-done | bytes 1048608 | tf_op jit(solution)/shard_map/ppermute | solution.py:48
  108.3 24.5 %shard_map.357 = (bf16[1024,1024]{1,0:T(8,128)(2,1)S(1)}, f32[1024,1280]{1,0:T(8,128)}, f32[1024,1280]{1,0:T(8,128)}, bf16[1024,1280]{1,0:T(8,128)(2,1)}, f32[10...) custom-call(bf16[1024,1024]{1,0:T(8,128)(2,1)} %maximum_select_fusion.tok, ...), custom_call_target="tpu_custom_call" | custom-call | flops 4563402752 | bytes 48234496 | tf_op jit(solution)/shard_map/pallas_call | solution.py:652
  132.8 3.3 shard_map.358
  138.6 10.4 %shard_map.359 = (f32[1024,1024]{1,0:T(8,128)}, f32[1024,1024]{1,0:T(8,128)}, bf16[1024,1024]{1,0:T(8,128)(2,1)S(1)}, f32[1024,128]{1,0:T(8,128)S(1)}) custom-call(bf16[1024,1024]{1,0:T(8,128)(2,1)} %copy-done.5, bf16[1024,1024]{1,0:T(8,128)(2,1)} %maximum_select_fusion.1.cot, f32[1024,16]{1,0:T(8,128)S(1)} %copy.75.aux, ...), custom_call_target="tpu_custom_call" | custom-call | flops 4294967296 | bytes 22020096 | tf_op jit(solution)/shard_map/pallas_call | solution.py:674
  149.7 9.7 %collective-permute-done.13 = f32[2,1024]{0,1:T(8,128)S(1)} collective-permute-done((f32[2,1024]{0,1:T(8,128)S(1)}, f32[2,1024]{0,1:T(8,128)S(1)}, u32[]{:S(2)}, u32[]{:S(2)}) %collective-permute-start.13) | collective-permute-done | bytes 8224 | tf_op jit(solution)/shard_map/ppermute | solution.py:48
  159.4 10.2 %shard_map.360 = (bf16[1024,1024]{1,0:T(8,128)(2,1)S(1)}, bf16[1024,1024]{1,0:T(8,128)(2,1)}, bf16[1024,1024]{1,0:T(8,128)(2,1)}, bf16[1024,1024]{1,0:T(8,128)(2,1)}, f32[1,1024]{1,0:T(1,128)S(1)}) custom-call(s32[1]{0:T(128)} %bitcast.rank, f32[1024,1024]{1,0:T(8,128)} %get-tuple-element.74.gate_r, f32[1024,1024]{1,0:T(8,128)} %get-tuple-element.75.sg_r, ...), custom_call_target="tpu_custom_call" | custom-call | flops 2147483648 | bytes 16785408 | tf_op jit(solution)/shard_map/pallas_call | solution.py:703
  171.0 12.5 %shard_map.362 = (f32[8,128,1024]{2,1,0:T(8,128)}, bf16[8,128,1024]{2,1,0:T(8,128)(2,1)S(1)}) custom-call(s32[1]{0:T(128)} %bitcast.1.me, bf16[1024,1024]{1,0:T(8,128)(2,1)} %copy-done.6, bf16[1024,1024]{1,0:T(8,128)(2,1)} %copy-done.5, bf16[1024,1024]{1,0:T(8,128)(2,1)} %get-tuple-element.87.rhs0, bf16[1024,1024]{1,0:T(8,128)(2,1)} %get-tuple-element.78.rhs1.dgate), custom_call_target="tpu_custom_call" | custom-call | flops 4294967296 | bytes 12582912 | tf_op jit(solution)/shard_map/pallas_call | solution.py:456
  183.5 4.2 %collective-permute-done.15 = bf16[8,128,1024]{2,1,0:T(8,128)(2,1)S(1)} collective-permute-done((bf16[8,128,1024]{2,1,0:T(8,128)(2,1)S(1)}, bf16[8,128,1024]{2,1,0:T(8,128)(2,1)S(1)}, u32[]{:S(2)}, u32[]{:S(2)}) %collective-permute-start.15) | collective-permute-done | bytes 2097184 | tf_op jit(solution)/shard_map/ppermute | solution.py:48
  187.6 3.2 convert_add_fusion
  195.0 18.6 %shard_map.361 = (bf16[512,1024]{1,0:T(8,128)(2,1)}, f32[512,384]{1,0:T(8,128)S(1)}, f32[8,1280]{1,0:T(8,128)S(1)}, f32[8,128]{1,0:T(8,128)S(1)}, f32[1,1024]{1,...) custom-call(bf16[1024,1024]{1,0:T(8,128)(2,1)} %get-tuple-element.79.dssd, ...), custom_call_target="tpu_custom_call" | custom-call | flops 2013265920 | bytes 4907008 | tf_op jit(solution)/shard_map/pallas_call | solution.py:740
  213.5 4.9 %collective-permute-done.16 = bf16[4,128,1024]{2,1,0:T(8,128)(2,1)} collective-permute-done((bf16[4,128,1024]{2,1,0:T(8,128)(2,1)S(1)}, bf16[4,128,1024]{2,1,0:T(8,128)(2,1)}, u32[]{:S(2)}, u32[]{:S(2)}) %collective-permute-start.16) | collective-permute-done | bytes 1048608 | tf_op jit(solution)/shard_map/ppermute | solution.py:48
  218.4 3.4 fusion.45
  221.8 18.7 %shard_map.363 = (bf16[512,1024]{1,0:T(8,128)(2,1)}, f32[512,384]{1,0:T(8,128)S(1)}, f32[8,1280]{1,0:T(8,128)S(1)}, f32[8,128]{1,0:T(8,128)S(1)}, f32[1,1024]{1,...) custom-call(bf16[1024,1024]{1,0:T(8,128)(2,1)} %get-tuple-element.79.dssd, ...), custom_call_target="tpu_custom_call" | custom-call | flops 2013265920 | bytes 4907008 | tf_op jit(solution)/shard_map/pallas_call | solution.py:740
  243.4 7.6 %shard_map.365 = (bf16[512,1024]{1,0:T(8,128)(2,1)}, f32[1,1024]{1,0:T(1,128)S(1)}) custom-call(s32[1]{0:T(128)} %bitcast.rank, bf16[1024,1024]{1,0:T(8,128)(2,1)} %get-tuple-element.78.rhs1.dgate, bf16[1024,1024]{1,0:T(8,128)(2,1)} %copy-done.9, f32[1024,384]{1,0:T(8,128)S(1)} %constant_dynamic-update-slice_fusion.12.dcommon, ...), custom_call_target="tpu_custom_call" | custom-call | flops 2952790016 | bytes 2105344 | tf_op jit(solution)/shard_map/pallas_call | solution.py:782
  251.0 7.7 %shard_map.364 = (f32[512,1024]{1,0:T(8,128)}, f32[1,1024]{1,0:T(1,128)S(1)}) custom-call(s32[1]{0:T(128)} %bitcast.rank, bf16[1024,1024]{1,0:T(8,128)(2,1)} %get-tuple-element.78.rhs1.dgate, bf16[1024,1024]{1,0:T(8,128)(2,1)} %copy-done.9, f32[1024,384]{1,0:T(8,128)S(1)} %constant_dynamic-update-slice_fusion.12.dcommon, ...), custom_call_target="tpu_custom_call" | custom-call | flops 2952790016 | bytes 4202496 | tf_op jit(solution)/shard_map/pallas_call | solution.py:782
  268.6 7.0 %collective-permute-start.18 = (bf16[128,1024]{1,0:T(8,128)(2,1)S(1)}, bf16[128,1024]{1,0:T(8,128)(2,1)S(1)}, u32[]{:S(2)}, u32[]{:S(2)}) collective-permute-start(bf16[128,1024]{1,0:T(8,128)(2,1)S(1)} %get-tuple-element.134), channel_id=1, source_target_pairs={{0,8},{2,10},{4,12},{6,14},{8,0},{10,2},{12,4},{14,6},{16,24},{18,... | collective-permute-start | bytes 786440 | tf_op jit(solution)/shard_map/ppermute | solution.py:48
  279.8 10.6 %shard_map.366 = (f32[8,64,1408]{2,1,0:T(8,128)}, bf16[8,64,1408]{2,1,0:T(8,128)(2,1)}) custom-call(s32[1]{0:T(128)} %bitcast.1.me, bf16[1024,1024]{1,0:T(8,128)(2,1)} %copy-done.5, bf16[1024,1024]{1,0:T(8,128)(2,1)} %copy-done.9, f32[1024,384]{1,0:T(8,128)S(1)} %constant_dynamic-update-slice_fusion.12.dcommon), custom_call_target="tpu_custom_call" | custom-call | flops 3758096384 | bytes 8650752 | tf_op jit(solution)/shard_map/pallas_call | solution.py:498
  290.4 3.3 collective-permute-done.30
  296.4 3.4 collective-permute-start.31
  309.2 10.6 %collective-permute-done.17 = bf16[512,1024]{1,0:T(8,128)(2,1)S(1)} collective-permute-done((bf16[512,1024]{1,0:T(8,128)(2,1)}, bf16[512,1024]{1,0:T(8,128)(2,1)S(1)}, u32[]{:S(2)}, u32[]{:S(2)}) %collective-permute-start.17) | collective-permute-done | bytes 1048608 | tf_op jit(solution)/shard_map/ppermute | solution.py:48
  320.4 5.3 %collective-permute-done.22 = bf16[4,64,1408]{2,1,0:T(8,128)(2,1)S(1)} collective-permute-done((bf16[4,64,1408]{2,1,0:T(8,128)(2,1)S(1)}, bf16[4,64,1408]{2,1,0:T(8,128)(2,1)S(1)}, u32[]{:S(2)}, u32[]{:S(2)}) %collective-permute-start.22) | collective-permute-done | bytes 720928 | tf_op jit(solution)/shard_map/ppermute | solution.py:48
  330.5 3.7 %fusion.6 = (bf16[512,1024]{1,0:T(8,128)(2,1)}, bf16[512,1024]{1,0:T(8,128)(2,1)}) fusion(bf16[512,1024]{1,0:T(8,128)(2,1)S(1)} %copy-done.8, bf16[512,1024]{1,0:T(8,128)(2,1)S(1)} %copy-done.14, f32[512,1024]{1,0:T(8,128)S(1)} %copy-done.12, bf16[512,1024]{1,0:T(8,128)(2,1)S(1)} %collective-permute-done.17, f32[512]{0:T(512)S(1)} %broadcast_multiply_fusion, ...), kind=kLoop, calls=%fused_computation.11 | loop fusion | flops 8912896 | bytes 9447424 | tf_op jit(solution)/shard_map/convert_element_type | solution.py:866
  335.5 6.1 %collective-permute-done.24 = bf16[64,1408]{1,0:T(8,128)(2,1)S(1)} collective-permute-done((bf16[64,1408]{1,0:T(8,128)(2,1)S(1)}, bf16[64,1408]{1,0:T(8,128)(2,1)S(1)}, u32[]{:S(2)}, u32[]{:S(2)}) %collective-permute-start.24) | collective-permute-done | bytes 180256 | tf_op jit(solution)/shard_map/ppermute | solution.py:48
  (274 shorter events, 91.3 us)
Async XLA Ops:
  4.7 9.6 %collective-permute-start = (bf16[16,1024]{1,0:T(8,128)(2,1)S(1)}, bf16[16,1024]{1,0:T(8,128)(2,1)S(1)}, u32[]{:S(2)}, u32[]{:S(2)}) collective-permute-start(bf16[16,1024]{1,0:T(8,128)(2,1)S(1)} %reshape.209), channel_id=1, source_target_pairs={{0,1},{1,0},{2,3},{3,2},{4,5},{5,4},{6,7},{7,6},{8,9},{9,8},{10,11... | collective-permute-start | bytes 98312 | tf_op jit(solution)/shard_map/ppermute | solution.py:48
  14.4 9.6 %collective-permute-start.2 = (bf16[96,1024]{1,0:T(8,128)(2,1)S(1)}, bf16[96,1024]{1,0:T(8,128)(2,1)S(1)}, u32[]{:S(2)}, u32[]{:S(2)}) collective-permute-start(bf16[96,1024]{1,0:T(8,128)(2,1)S(1)} %get-tuple-element.145), channel_id=1, source_target_pairs={{0,8},{2,10},{4,12},{6,14},{8,0},{10,2},{12,4},{14,6},{16,24},{18,... | collective-permute-start | bytes 589832 | tf_op jit(solution)/shard_map/ppermute | solution.py:48
  16.0 17.2 %collective-permute-start.3 = (bf16[96,1024]{1,0:T(8,128)(2,1)S(1)}, bf16[96,1024]{1,0:T(8,128)(2,1)S(1)}, u32[]{:S(2)}, u32[]{:S(2)}) collective-permute-start(bf16[96,1024]{1,0:T(8,128)(2,1)S(1)} %get-tuple-element.145), channel_id=1, source_target_pairs={{0,16},{2,18},{4,20},{6,22},{8,24},{10,26},{12,28},{14,30},{16,0},... | collective-permute-start | bytes 589832 | tf_op jit(solution)/shard_map/ppermute | solution.py:48
  18.6 14.6 %collective-permute-start.4 = (bf16[96,1024]{1,0:T(8,128)(2,1)S(1)}, bf16[96,1024]{1,0:T(8,128)(2,1)S(1)}, u32[]{:S(2)}, u32[]{:S(2)}) collective-permute-start(bf16[96,1024]{1,0:T(8,128)(2,1)S(1)} %get-tuple-element.145), channel_id=1, source_target_pairs={{0,24},{2,26},{4,28},{6,30},{8,16},{10,18},{12,20},{14,22},{16,8},... | collective-permute-start | bytes 589832 | tf_op jit(solution)/shard_map/ppermute | solution.py:48
  19.5 59.0 %collective-permute-start.1 = (bf16[512,1024]{1,0:T(8,128)(2,1)S(1)}, bf16[512,1024]{1,0:T(8,128)(2,1)}, u32[]{:S(2)}, u32[]{:S(2)}) collective-permute-start(bf16[512,1024]{1,0:T(8,128)(2,1)S(1)} %copy-done.7), channel_id=1, source_target_pairs={{0,1},{1,0},{2,3},{3,2},{4,5},{5,4},{6,7},{7,6},{8,9},{9,8},{10,11... | collective-permute-start | bytes 3145736 | tf_op jit(solution)/shard_map/ppermute | solution.py:48
  34.0 16.1 %collective-permute-start.5 = (bf16[4,96,1024]{2,1,0:T(8,128)(2,1)S(1)}, bf16[4,96,1024]{2,1,0:T(8,128)(2,1)S(1)}, u32[]{:S(2)}, u32[]{:S(2)}) collective-permute-start(bf16[4,96,1024]{2,1,0:T(8,128)(2,1)S(1)} %pad_maximum_fusion.1), channel_id=1, source_target_pairs={{0,4},{2,6},{4,0},{6,2},{8,12},{10,14},{12,8},{14,10},{16,20},{18,... | collective-permute-start | bytes 2359304 | tf_op jit(solution)/shard_map/ppermute | solution.py:48
  50.2 12.6 %collective-permute-start.8 = (bf16[128,1024]{1,0:T(8,128)(2,1)S(1)}, bf16[128,1024]{1,0:T(8,128)(2,1)}, u32[]{:S(2)}, u32[]{:S(2)}) collective-permute-start(bf16[128,1024]{1,0:T(8,128)(2,1)S(1)} %pad_maximum_fusion.3), channel_id=1, source_target_pairs={{0,8},{2,10},{4,12},{6,14},{8,0},{10,2},{12,4},{14,6},{16,24},{18,... | collective-permute-start | bytes 786440 | tf_op jit(solution)/shard_map/ppermute | solution.py:48
  55.0 20.6 %collective-permute-start.9 = (bf16[128,1024]{1,0:T(8,128)(2,1)S(1)}, bf16[128,1024]{1,0:T(8,128)(2,1)}, u32[]{:S(2)}, u32[]{:S(2)}) collective-permute-start(bf16[128,1024]{1,0:T(8,128)(2,1)S(1)} %pad_maximum_fusion.3), channel_id=1, source_target_pairs={{0,16},{2,18},{4,20},{6,22},{8,24},{10,26},{12,28},{14,30},{16,0},... | collective-permute-start | bytes 786440 | tf_op jit(solution)/shard_map/ppermute | solution.py:48
  56.2 19.4 %collective-permute-start.10 = (bf16[128,1024]{1,0:T(8,128)(2,1)S(1)}, bf16[128,1024]{1,0:T(8,128)(2,1)}, u32[]{:S(2)}, u32[]{:S(2)}) collective-permute-start(bf16[128,1024]{1,0:T(8,128)(2,1)S(1)} %pad_maximum_fusion.3), channel_id=1, source_target_pairs={{0,24},{2,26},{4,28},{6,30},{8,16},{10,18},{12,20},{14,22},{16,8},... | collective-permute-start | bytes 786440 | tf_op jit(solution)/shard_map/ppermute | solution.py:48
  58.4 44.8 %collective-permute-start.6 = (bf16[8,96,1024]{2,1,0:T(8,128)(2,1)S(1)}, bf16[8,96,1024]{2,1,0:T(8,128)(2,1)S(1)}, u32[]{:S(2)}, u32[]{:S(2)}) collective-permute-start(bf16[8,96,1024]{2,1,0:T(8,128)(2,1)S(1)} %constant_dynamic-update-slice_fusion.near), channel_id=1, source_target_pairs={{0,2},{2,0},{4,6},{6,4},{8,10},{10,8},{12,14},{14,12},{16,18},{18,... | collective-permute-start | bytes 4718600 | tf_op jit(solution)/shard_map/ppermute | solution.py:48
  76.9 18.8 %collective-permute-start.11 = (bf16[4,128,1024]{2,1,0:T(8,128)(2,1)S(1)}, bf16[4,128,1024]{2,1,0:T(8,128)(2,1)S(1)}, u32[]{:S(2)}, u32[]{:S(2)}) collective-permute-start(bf16[4,128,1024]{2,1,0:T(8,128)(2,1)S(1)} %pad_maximum_fusion), channel_id=1, source_target_pairs={{0,4},{2,6},{4,0},{6,2},{8,12},{10,14},{12,8},{14,10},{16,20},{18,... | collective-permute-start | bytes 3145736 | tf_op jit(solution)/shard_map/ppermute | solution.py:48
  82.4 18.5 %collective-permute-start.7 = (bf16[512,1024]{1,0:T(8,128)(2,1)S(1)}, bf16[512,1024]{1,0:T(8,128)(2,1)S(1)}, u32[]{:S(2)}, u32[]{:S(2)}) collective-permute-start(bf16[512,1024]{1,0:T(8,128)(2,1)S(1)} %copy-done.13), channel_id=1, source_target_pairs={{0,1},{1,0},{2,3},{3,2},{4,5},{5,4},{6,7},{7,6},{8,9},{9,8},{10,11... | collective-permute-start | bytes 3145736 | tf_op jit(solution)/shard_map/ppermute | solution.py:48
  96.8 36.0 %collective-permute-start.12 = (bf16[8,128,1024]{2,1,0:T(8,128)(2,1)}, bf16[8,128,1024]{2,1,0:T(8,128)(2,1)}, u32[]{:S(2)}, u32[]{:S(2)}) collective-permute-start(bf16[8,128,1024]{2,1,0:T(8,128)(2,1)} %constant_dynamic-update-slice_fusion.5.near), channel_id=1, source_target_pairs={{0,2},{2,0},{4,6},{6,4},{8,10},{10,8},{12,14},{14,12},{16,18},{18,... | collective-permute-start | bytes 6291464 | tf_op jit(solution)/shard_map/ppermute | solution.py:48
  149.1 10.3 %collective-permute-start.13 = (f32[2,1024]{0,1:T(8,128)S(1)}, f32[2,1024]{0,1:T(8,128)S(1)}, u32[]{:S(2)}, u32[]{:S(2)}) collective-permute-start(f32[2,1024]{0,1:T(8,128)S(1)} %slice_bitcast_fusion.1), channel_id=1, source_target_pairs={{0,1},{1,0},{2,3},{3,2},{4,5},{5,4},{6,7},{7,6},{8,9},{9,8},{10,11... | collective-permute-start | bytes 24584 | tf_op jit(solution)/shard_map/ppermute | solution.py:48
  183.5 4.2 %collective-permute-start.15 = (bf16[8,128,1024]{2,1,0:T(8,128)(2,1)S(1)}, bf16[8,128,1024]{2,1,0:T(8,128)(2,1)S(1)}, u32[]{:S(2)}, u32[]{:S(2)}) collective-permute-start(bf16[8,128,1024]{2,1,0:T(8,128)(2,1)S(1)} %get-tuple-element.89), channel_id=1, source_target_pairs={{0,2},{2,0},{4,6},{6,4},{8,10},{10,8},{12,14},{14,12},{16,18},{18,... | collective-permute-start | bytes 6291464 | tf_op jit(solution)/shard_map/ppermute | solution.py:48
  193.0 25.4 %collective-permute-start.16 = (bf16[4,128,1024]{2,1,0:T(8,128)(2,1)S(1)}, bf16[4,128,1024]{2,1,0:T(8,128)(2,1)}, u32[]{:S(2)}, u32[]{:S(2)}) collective-permute-start(bf16[4,128,1024]{2,1,0:T(8,128)(2,1)S(1)} %slice.329), channel_id=1, source_target_pairs={{0,4},{2,6},{4,0},{6,2},{8,12},{10,14},{12,8},{14,10},{16,20},{18,... | collective-permute-start | bytes 3145736 | tf_op jit(solution)/shard_map/ppermute | solution.py:48
  259.4 4.3 %collective-permute-start.27 = (f32[1,14688]{1,0:T(1,128)S(1)}, f32[1,14688]{1,0:T(1,128)S(1)}, u32[]{:S(2)}, u32[]{:S(2)}) collective-permute-start(f32[1,14688]{1,0:T(1,128)S(1)} %pad_maximum_fusion.5), channel_id=1, source_target_pairs={{0,1},{1,0},{2,3},{3,2},{4,5},{5,4},{6,7},{7,6},{8,9},{9,8},{10,11... | collective-permute-start | bytes 176264 | tf_op jit(solution)/shard_map/ppermute | solution.py:48
  263.8 3.2 collective-permute-start.28
  266.2 64.2 %collective-permute-start.14 = (bf16[512,1024]{1,0:T(8,128)(2,1)}, bf16[512,1024]{1,0:T(8,128)(2,1)}, u32[]{:S(2)}, u32[]{:S(2)}) collective-permute-start(bf16[512,1024]{1,0:T(8,128)(2,1)} %slice.211), channel_id=1, source_target_pairs={{0,1},{1,0},{2,3},{3,2},{4,5},{5,4},{6,7},{7,6},{8,9},{9,8},{10,11... | collective-permute-start | bytes 3145736 | tf_op jit(solution)/shard_map/ppermute | solution.py:48
  267.0 12.1 %collective-permute-start.29 = (f32[1,14688]{1,0:T(1,128)S(1)}, f32[1,14688]{1,0:T(1,128)S(1)}, u32[]{:S(2)}, u32[]{:S(2)}) collective-permute-start(f32[1,14688]{1,0:T(1,128)S(1)} %add.319), channel_id=1, source_target_pairs={{0,4},{2,6},{4,0},{6,2},{8,12},{10,14},{12,8},{14,10},{16,20},{18,... | collective-permute-start | bytes 176264 | tf_op jit(solution)/shard_map/ppermute | solution.py:48
  268.6 25.2 %collective-permute-start.18 = (bf16[128,1024]{1,0:T(8,128)(2,1)S(1)}, bf16[128,1024]{1,0:T(8,128)(2,1)S(1)}, u32[]{:S(2)}, u32[]{:S(2)}) collective-permute-start(bf16[128,1024]{1,0:T(8,128)(2,1)S(1)} %get-tuple-element.134), channel_id=1, source_target_pairs={{0,8},{2,10},{4,12},{6,14},{8,0},{10,2},{12,4},{14,6},{16,24},{18,... | collective-permute-start | bytes 786440 | tf_op jit(solution)/shard_map/ppermute | solution.py:48
  275.6 20.8 %collective-permute-start.19 = (bf16[128,1024]{1,0:T(8,128)(2,1)S(1)}, bf16[128,1024]{1,0:T(8,128)(2,1)S(1)}, u32[]{:S(2)}, u32[]{:S(2)}) collective-permute-start(bf16[128,1024]{1,0:T(8,128)(2,1)S(1)} %get-tuple-element.136), channel_id=1, source_target_pairs={{0,16},{2,18},{4,20},{6,22},{8,24},{10,26},{12,28},{14,30},{16,0},... | collective-permute-start | bytes 786440 | tf_op jit(solution)/shard_map/ppermute | solution.py:48
  277.7 22.1 %collective-permute-start.20 = (bf16[128,1024]{1,0:T(8,128)(2,1)S(1)}, bf16[128,1024]{1,0:T(8,128)(2,1)S(1)}, u32[]{:S(2)}, u32[]{:S(2)}) collective-permute-start(bf16[128,1024]{1,0:T(8,128)(2,1)S(1)} %get-tuple-element.135), channel_id=1, source_target_pairs={{0,24},{2,26},{4,28},{6,30},{8,16},{10,18},{12,20},{14,22},{16,8},... | collective-permute-start | bytes 786440 | tf_op jit(solution)/shard_map/ppermute | solution.py:48
  279.2 14.6 %collective-permute-start.30 = (f32[1,14688]{1,0:T(1,128)S(1)}, f32[1,14688]{1,0:T(1,128)S(1)}, u32[]{:S(2)}, u32[]{:S(2)}) collective-permute-start(f32[1,14688]{1,0:T(1,128)S(1)} %add.320), channel_id=1, source_target_pairs={{0,8},{2,10},{4,12},{6,14},{8,0},{10,2},{12,4},{14,6},{16,24},{18,... | collective-permute-start | bytes 176264 | tf_op jit(solution)/shard_map/ppermute | solution.py:48
  293.8 11.7 %collective-permute-start.21 = (bf16[8,64,1408]{2,1,0:T(8,128)(2,1)}, bf16[8,64,1408]{2,1,0:T(8,128)(2,1)S(1)}, u32[]{:S(2)}, u32[]{:S(2)}) collective-permute-start(bf16[8,64,1408]{2,1,0:T(8,128)(2,1)} %get-tuple-element.100), channel_id=1, source_target_pairs={{0,2},{2,0},{4,6},{6,4},{8,10},{10,8},{12,14},{14,12},{16,18},{18,... | collective-permute-start | bytes 4325384 | tf_op jit(solution)/shard_map/ppermute | solution.py:48
  293.9 25.8 %collective-permute-start.17 = (bf16[512,1024]{1,0:T(8,128)(2,1)}, bf16[512,1024]{1,0:T(8,128)(2,1)S(1)}, u32[]{:S(2)}, u32[]{:S(2)}) collective-permute-start(bf16[512,1024]{1,0:T(8,128)(2,1)} %get-tuple-element.98), channel_id=1, source_target_pairs={{0,1},{1,0},{2,3},{3,2},{4,5},{5,4},{6,7},{7,6},{8,9},{9,8},{10,11... | collective-permute-start | bytes 3145736 | tf_op jit(solution)/shard_map/ppermute | solution.py:48
  296.4 7.4 %collective-permute-start.31 = (f32[1,14688]{1,0:T(1,128)S(1)}, f32[1,14688]{1,0:T(1,128)S(1)}, u32[]{:S(2)}, u32[]{:S(2)}) collective-permute-start(f32[1,14688]{1,0:T(1,128)S(1)} %add.321), channel_id=1, source_target_pairs={{0,16},{2,18},{4,20},{6,22},{8,24},{10,26},{12,28},{14,30},{16,0},... | collective-permute-start | bytes 176264 | tf_op jit(solution)/shard_map/ppermute | solution.py:48
  307.8 18.0 %collective-permute-start.22 = (bf16[4,64,1408]{2,1,0:T(8,128)(2,1)S(1)}, bf16[4,64,1408]{2,1,0:T(8,128)(2,1)S(1)}, u32[]{:S(2)}, u32[]{:S(2)}) collective-permute-start(bf16[4,64,1408]{2,1,0:T(8,128)(2,1)S(1)} %slice.330), channel_id=1, source_target_pairs={{0,4},{2,6},{4,0},{6,2},{8,12},{10,14},{12,8},{14,10},{16,20},{18,... | collective-permute-start | bytes 2162696 | tf_op jit(solution)/shard_map/ppermute | solution.py:48
  326.0 9.5 %collective-permute-start.23 = (bf16[64,1408]{1,0:T(8,128)(2,1)S(1)}, bf16[64,1408]{1,0:T(8,128)(2,1)S(1)}, u32[]{:S(2)}, u32[]{:S(2)}) collective-permute-start(bf16[64,1408]{1,0:T(8,128)(2,1)S(1)} %get-tuple-element.139), channel_id=1, source_target_pairs={{0,8},{2,10},{4,12},{6,14},{8,0},{10,2},{12,4},{14,6},{16,24},{18,... | collective-permute-start | bytes 540680 | tf_op jit(solution)/shard_map/ppermute | solution.py:48
  326.1 15.5 %collective-permute-start.24 = (bf16[64,1408]{1,0:T(8,128)(2,1)S(1)}, bf16[64,1408]{1,0:T(8,128)(2,1)S(1)}, u32[]{:S(2)}, u32[]{:S(2)}) collective-permute-start(bf16[64,1408]{1,0:T(8,128)(2,1)S(1)} %get-tuple-element.141), channel_id=1, source_target_pairs={{0,16},{2,18},{4,20},{6,22},{8,24},{10,26},{12,28},{14,30},{16,0},... | collective-permute-start | bytes 540680 | tf_op jit(solution)/shard_map/ppermute | solution.py:48
  328.7 12.8 %collective-permute-start.25 = (bf16[64,1408]{1,0:T(8,128)(2,1)S(1)}, bf16[64,1408]{1,0:T(8,128)(2,1)S(1)}, u32[]{:S(2)}, u32[]{:S(2)}) collective-permute-start(bf16[64,1408]{1,0:T(8,128)(2,1)S(1)} %get-tuple-element.140), channel_id=1, source_target_pairs={{0,24},{2,26},{4,28},{6,30},{8,16},{10,18},{12,20},{14,22},{16,8},... | collective-permute-start | bytes 540680 | tf_op jit(solution)/shard_map/ppermute | solution.py:48
  341.7 4.2 %collective-permute-start.26 = (f32[32,384]{1,0:T(8,128)S(1)}, f32[32,384]{1,0:T(8,128)S(1)}, u32[]{:S(2)}, u32[]{:S(2)}) collective-permute-start(f32[32,384]{1,0:T(8,128)S(1)} %get-tuple-element.146), channel_id=1, source_target_pairs={{0,1},{1,0},{2,3},{3,2},{4,5},{5,4},{6,7},{7,6},{8,9},{9,8},{10,11... | collective-permute-start | bytes 147464 | tf_op jit(solution)/shard_map/ppermute | solution.py:48
  (46 other events, 373.3 us)

commit v3 on v2

--- a/solution.py
+++ b/solution.py
@@ -58,37 +58,40 @@
     return high, middle
 
 
-def gather_halves(shard, dp):
+def gather_line(shard, dp):
     high, middle = axis_parts(dp)
     pieces = [shard[None]]
     for step in range(1, high):
         pieces.append(swap(shard, "dp", dp, step * middle * CORES)[None])
-    line = jnp.concatenate(pieces, axis=0)
+    return jnp.concatenate(pieces, axis=0)
+
+
+def gather_plane(line, dp, *first):
     lines = [line]
-    for step in range(1, middle):
-        lines.append(swap(line, "dp", dp, step * CORES))
-    plane = jnp.concatenate(lines, axis=0)
-    return plane, swap(plane, "dp", dp, 1)
+    for step in range(1, axis_parts(dp)[1]):
+        lines.append(after(swap(line, "dp", dp, step * CORES), *first))
+    return jnp.concatenate(lines, axis=0)
 
 
 def start_sum(keep, send, dp):
     high, middle = axis_parts(dp)
-    total = keep + swap(send, "dp", dp, 1).astype(f32)
-    return total.reshape((middle, high) + total.shape[1:])
-
-
-def middle_sum(total, dp):
-    line = total[0]
-    for step in range(1, total.shape[0]):
-        line = line + swap(total[step].astype(bf16), "dp", dp, step * CORES).astype(f32)
-    return line
-
-
-def high_sum(line, dp):
+    other = swap(send, "dp", dp, 1)
+    parts = [slice(step * high, (step + 1) * high) for step in range(middle)]
+    line = keep[parts[0]].astype(f32) + other[parts[0]].astype(f32)
+    rest = [(keep[at].astype(f32) + other[at].astype(f32)).astype(bf16) for at in parts[1:]]
+    return line, rest
+
+
+def middle_sum(line, rest, dp):
+    for step, part in enumerate(rest):
+        line = line + swap(part, "dp", dp, (step + 1) * CORES).astype(f32)
+    return line[0], [part.astype(bf16) for part in line[1:]]
+
+
+def high_sum(block, rest, dp):
     middle = axis_parts(dp)[1]
-    block = line[0]
-    for step in range(1, line.shape[0]):
-        block = block + swap(line[step].astype(bf16), "dp", dp, step * middle * CORES).astype(f32)
+    for step, part in enumerate(rest):
+        block = block + swap(part, "dp", dp, (step + 1) * middle * CORES).astype(f32)
     return block
 
 
@@ -111,7 +114,7 @@
     ]
 
 
-def call(kernel, grid, in_specs, out_specs, out_shape, scratch, flops, scalars=0):
+def call(kernel, grid, in_specs, out_specs, out_shape, scratch, flops, scalars=0, aliases=None):
     params = pltpu.CompilerParams(vmem_limit_bytes=50 * 1024 * 1024)
     moved = sum(2 * s.dtype.itemsize * s.size for s in jax.tree.leaves(out_shape))
     return pl.pallas_call(
@@ -125,6 +128,7 @@
         ),
         out_shape=out_shape,
         compiler_params=params,
+        input_output_aliases=aliases or {},
         cost_estimate=pl.CostEstimate(flops=int(flops), bytes_accessed=int(moved), transcendentals=0),
     )
 
@@ -206,12 +210,24 @@
     )(dp_rank, near, far)
 
 
+def pick_half(rank, first, second):
+    half = (2 * pl.program_id(0)) // pl.num_programs(0)
+    own = (half == rank[0]).astype(jnp.int32)
+    return jnp.where(jnp.broadcast_to(own, first.shape) == 1, first[...], second[...])
+
+
+def across(pair, left):
+    return jnp.concatenate(
+        [jnp.where(left, pair, 0.0), jnp.where(left, 0.0, pair)], axis=0
+    ).astype(bf16)
+
+
 def scan_kernel(
-    tok, gain, wv, shw, conv, skip, hp, aux, segr,
+    rank, tok0, tok1, gain, wv, shw, conv, skip, hp, aux, segr,
     normed_o, ch_o, pre_o, mix_o, ssd_o, hin_o, step_o,
-    win, state,
+    win, state, carried, weighted,
 ):
-    count = tok.shape[0]
+    count = tok0.shape[0]
     width = wv.shape[1]
     channels = width + 2 * N
 
@@ -220,7 +236,7 @@
         win[0:8, :] = jnp.zeros((8, channels), f32)
         state[...] = jnp.zeros(state.shape, f32)
 
-    x = tok[...].astype(f32)
+    x = pick_half(rank, tok0, tok1).astype(f32)
     inverse = lax.rsqrt(jnp.mean(x * x, axis=1, keepdims=True) + norm_epsilon)
     normed = (x * inverse * gain[...]).astype(bf16)
     normed_o[...] = normed
@@ -249,38 +265,40 @@
         at = slice(sub * CHUNK, (sub + 1) * CHUNK)
         dt = softplus(step_o[at, :])
         run = jnp.dot(tri, -(dt * hp[1:2, :]), precision=highest, preferred_element_type=f32)
-        run_t, dt_t = run.T, dt.T
+        run_t = run.T
         allowed = (table[at, SEG : SEG + 1] == segr[:, at]) & (row >= col)
         b_in = mix_o[at, width : width + N]
+        b_turned = b_in.astype(f32).T.astype(bf16)
         c_out = mix_o[at, width + N :]
         scores = mm(c_out, b_in, 1, 1)
         ending = run[CHUNK - 1 : CHUNK, :]
         entry = jnp.exp(run) * table[at, INHERIT : INHERIT + 1]
-        tail = jnp.exp(ending - run) * dt * table[at, TAIL : TAIL + 1]
+        tail = jnp.exp(ending - run) * table[at, TAIL : TAIL + 1]
         factor = jnp.exp(ending) * table[at, LINKED : LINKED + 1][CHUNK - 1 :, :]
-        entering = state[...]
-        hin_o[sub] = entering
+        hin_o[sub] = state[...]
+        carried[...] = mm_right(c_out, state[...])
         for pair in range(width // LANES):
             lanes = slice(pair * LANES, (pair + 1) * LANES)
             x_pair = mix_o[at, lanes].astype(f32)
+            stepped = (x_pair * pair_spread(dt, pair, left)).astype(bf16).astype(f32)
             mixing = []
             for head in (2 * pair, 2 * pair + 1):
                 spread = run[:, head : head + 1] - run_t[head : head + 1, :]
                 decays = jnp.exp(jnp.where(allowed, spread, -1e30))
-                mixing.append(decays * scores * dt_t[head : head + 1, :])
-            x_cross = jnp.concatenate(
-                [jnp.where(left, x_pair, 0.0), jnp.where(left, 0.0, x_pair)], axis=0
-            ).astype(bf16)
-            local = mm_left(jnp.concatenate(mixing, axis=1), x_cross)
-            before = entering[:, lanes]
-            carried = mm_right(c_out, before) * pair_spread(entry, pair, left)
-            ssd_o[at, lanes] = local + carried + skip[:, lanes] * x_pair
-            fresh = mm_right(b_in, x_pair * pair_spread(tail, pair, left), 0, 0)
-            state[:, lanes] = pair_spread(factor, pair, left) * before + fresh
-
-
-def gate_kernel(normed, cot, aux, ssd, wg, out_t, gain, gate_o, sg_o, ret_o, sums_o):
-    returned = (cot[...].astype(f32) * aux[:, LIVE : LIVE + 1]).astype(bf16)
+                mixing.append((decays * scores).astype(bf16))
+            local = mm(jnp.concatenate(mixing, axis=1), across(stepped, left))
+            ssd_o[at, lanes] = (
+                local + carried[:, lanes] * pair_spread(entry, pair, left) + skip[:, lanes] * x_pair
+            )
+            high, low = split(stepped * pair_spread(tail, pair, left))
+            weighted[0, :, lanes] = high
+            weighted[1, :, lanes] = low
+            state[:, lanes] = pair_spread(factor, pair, left) * state[:, lanes]
+        state[...] += mm(b_turned, weighted[0]) + mm(b_turned, weighted[1])
+
+
+def gate_kernel(rank, normed, cot0, cot1, aux, ssd, wg, out_t, gain, gate_o, sg_o, ret_o, sums_o):
+    returned = (pick_half(rank, cot0, cot1).astype(f32) * aux[:, LIVE : LIVE + 1]).astype(bf16)
     ret_o[...] = returned
     gate = mm(normed[...], wg[...])
     gate_o[...] = gate
@@ -316,10 +334,10 @@
 
 def scan_back_kernel(
     dssd, mix, pre, ch, ssd, hin, step, conv, skip, hp, aux, segr, heads_of,
-    state_in, win_in, carry_in,
-    dval_o, dcommon_o, dconv_o, dheads_o, dskip_o, dstate, dtail, carry,
-    dmix, dwin, both,
+    state_in, win_in, carry_in, *rest,
 ):
+    dval_o, dcommon_o, dconv_o, dheads_o, dskip_o, dstate, dtail, carry = rest[-14:-6]
+    dmix, dwin, both, flows, entries, weighted = rest[-6:]
     width = dssd.shape[1]
     channels = width + 2 * N
 
@@ -349,46 +367,42 @@
     entry = jnp.exp(run) * table[:, INHERIT : INHERIT + 1]
     tail = jnp.exp(ending - run) * table[:, TAIL : TAIL + 1]
     factor = jnp.exp(ending) * table[:, LINKED : LINKED + 1][CHUNK - 1 :, :]
+    c_turned = c_out.astype(f32).T.astype(bf16)
     pairs = jnp.zeros((CHUNK, CHUNK), f32)
-    dc = jnp.zeros((CHUNK, N), f32)
-    db = jnp.zeros((CHUNK, N), f32)
+    state_high, state_low = split(dstate[...])
+    flows[...] = mm(b_in, state_high) + mm(b_in, state_low)
     for pair in range(width // LANES):
         lanes = slice(pair * LANES, (pair + 1) * LANES)
         x_pair = mix[:, lanes].astype(f32)
         dy_low = dssd[:, lanes]
         dy = dy_low.astype(f32)
         dt_pair = pair_spread(dt, pair, left)
-        x_cross = jnp.concatenate(
-            [jnp.where(left, x_pair, 0.0), jnp.where(left, 0.0, x_pair)], axis=0
-        ).astype(bf16)
-        dy_cross = jnp.concatenate(
-            [jnp.where(left, dy, 0.0), jnp.where(left, 0.0, dy)], axis=0
-        ).astype(bf16)
-        inner = mm(x_cross, dy_low, 1, 1)
+        tail_pair = pair_spread(tail, pair, left)
+        stepped = (x_pair * dt_pair).astype(bf16).astype(f32)
+        inner = mm(across(stepped, left), dy_low, 1, 1)
         mixing = []
         for place, head in enumerate((2 * pair, 2 * pair + 1)):
             spread = run_t[head : head + 1, :] - run[:, head : head + 1]
             decays = jnp.exp(jnp.where(allowed, spread, -1e30))
-            mixing.append(decays * scores)
-            pairs = pairs + inner[place * CHUNK : (place + 1) * CHUNK] * decays * dt[:, head : head + 1]
-        d_state = dstate[:, lanes]
-        tail_pair = pair_spread(tail, pair, left)
-        flow = mm_left(jnp.concatenate(mixing, axis=1), dy_cross)
-        flow = flow + tail_pair * mm_right(b_in, d_state)
+            mixing.append((decays * scores).astype(bf16))
+            pairs = pairs + inner[place * CHUNK : (place + 1) * CHUNK] * decays
+        flow = mm(jnp.concatenate(mixing, axis=1), across(dy, left)) + tail_pair * flows[:, lanes]
         dmix[:, lanes] = dt_pair * flow + skip[:, lanes] * dy
         both[0:CHUNK, lanes] = flow * x_pair
-        both[CHUNK:, lanes] = dy * (ssd[:, lanes] - skip[:, lanes] * x_pair)
+        both[CHUNK : 2 * CHUNK, lanes] = dy * (ssd[:, lanes] - skip[:, lanes] * x_pair) - flow * stepped
         dskip_o[:, lanes] += jnp.sum(dy * x_pair, axis=0, keepdims=True)
-        entry_dy = pair_spread(entry, pair, left) * dy
-        db = db + mm_both(tail_pair * dt_pair * x_pair, d_state, 1, 1)
-        dc = dc + mm_both(entry_dy, hin[0, :, lanes], 1, 1)
-        dstate[:, lanes] = pair_spread(factor, pair, left) * d_state + mm_right(c_out, entry_dy, 0, 0)
-    dmix[:, width : width + N] = db + mm_left(pairs, c_out)
-    dmix[:, width + N :] = dc + mm_left(pairs, b_in, 0, 0)
+        high, low = split(pair_spread(entry, pair, left) * dy)
+        entries[0, :, lanes] = high
+        entries[1, :, lanes] = low
+        weighted[:, lanes] = (tail_pair * stepped).astype(bf16)
+        dstate[:, lanes] = pair_spread(factor, pair, left) * dstate[:, lanes]
+    dstate[...] += mm(c_turned, entries[0]) + mm(c_turned, entries[1])
+    dmix[:, width : width + N] = mm(weighted[...], state_high, 1, 1) + mm_left(pairs, c_out)
+    dmix[:, width + N :] = mm(entries[0], hin[0].astype(bf16), 1, 1) + mm_left(pairs, b_in, 0, 0)
 
     by_head = mm_left(both[...], heads_of[...])
     direct = by_head[0:CHUNK]
-    balance = by_head[CHUNK:] - dt * direct
+    balance = by_head[CHUNK:]
     later = allowed.astype(f32)
     log_grad = jnp.dot(later, balance, precision=highest, preferred_element_type=f32)
     log_grad = log_grad + table[:, NEXT : NEXT + 1] * carry[0:1, :]
@@ -425,48 +439,37 @@
     block = full.shape[0] // dp
     for place, distance in enumerate(relative_places(dp)):
         start = pl.multiple_of((me[0] ^ distance) * block, block)
-        part = full[pl.ds(start, block), :]
+        part = full[pl.ds(start, block), :].astype(bf16)
         if place < half:
             keep_o[place, :, cols] = part
         else:
-            send_o[place - half, :, cols] = part.astype(bf16)
-
-
-def pair_grad_kernel(dp, me, lhs0, lhs1, rhs0, rhs1, keep_o, send_o, turned, full):
-    step = pl.program_id(0)
-    per = pl.num_programs(0) // 2
-    for first, lhs, rhs in ((0, lhs0, rhs0), (per, lhs1, rhs1)):
-
-        @pl.when(step == first)
-        def _():
-            turned[...] = lhs[...].T
-
-        @pl.when((step >= first) & (step < first + per))
-        def _():
-            full[...] = mm(turned[...], rhs[...])
-
+            send_o[place - half, :, cols] = part
+
+
+def weight_grad_kernel(dp, me, lhs, rhs, keep_o, send_o, turned, full):
+    @pl.when(pl.program_id(0) == 0)
+    def _():
+        turned[...] = lhs[...].T
+
+    full[...] = mm(turned[...], rhs[...])
     scatter_blocks(dp, me, full, keep_o, send_o, slice(None))
 
 
-def pair_grad(lhs0, rhs0, lhs1, rhs1, dp, dp_rank):
-    length, width = rhs0.shape
-    depth = lhs0.shape[1]
-    block, half, per = depth // dp, dp // CORES, width // 256
-    piece = pl.BlockSpec((half, block, 256), lambda i, *s: (0, i // per, i % per))
+def weight_grad(lhs, rhs, dp, dp_rank):
+    length, width = rhs.shape
+    depth = lhs.shape[1]
+    block, half = depth // dp, dp // CORES
+    piece = pl.BlockSpec((half, block, 256), lambda i, *s: (0, 0, i))
     return call(
-        functools.partial(pair_grad_kernel, dp),
-        (2 * per,),
-        [
-            whole((length, depth)), whole((length, depth)),
-            pl.BlockSpec((length, 256), lambda i, *s: (0, jnp.minimum(i, per - 1))),
-            pl.BlockSpec((length, 256), lambda i, *s: (0, jnp.maximum(i - per, 0))),
-        ],
+        functools.partial(weight_grad_kernel, dp),
+        (width // 256,),
+        [whole((length, depth)), pl.BlockSpec((length, 256), lambda i, *s: (0, i))],
         [piece, piece],
-        [shape(half, 2 * block, width), shape(half, 2 * block, width, dtype=bf16)],
+        [shape(half, block, width, dtype=bf16)] * 2,
         [pltpu.VMEM((depth, length), bf16), pltpu.VMEM((depth, 256), f32)],
-        4 * length * width * depth,
+        2 * length * width * depth,
         scalars=1,
-    )(dp_rank, lhs0, lhs1, rhs0, rhs1)
+    )(dp_rank, lhs, rhs)
 
 
 def value_grad_kernel(dp, me, lhs, dval, dcommon, keep_o, send_o, turned, full, wide):
@@ -504,7 +507,7 @@
             whole((length, extra)),
         ],
         [whole(dims), whole(dims)],
-        [shape(*dims), shape(*dims, dtype=bf16)],
+        [shape(*dims, dtype=bf16)] * 2,
         [
             pltpu.VMEM((depth, length), bf16), pltpu.VMEM((depth, 256), f32),
             pltpu.VMEM((depth, extra), f32),
@@ -552,14 +555,17 @@
     band = min(2 * CHUNK, rows_here)
     per_piece = rows_here // band
 
-    def over_tensor(value):
-        pieces = [value] + [swap(value, "tensor", nt, d) for d in range(1, nt)]
+    def pieces_of(value):
+        return [value] + [swap(value, "tensor", nt, d) for d in range(1, nt)]
+
+    def over_tensor(value, pieces=None):
+        pieces = pieces_of(value) if pieces is None else pieces
         if nt == 2:
             first = jnp.concatenate(pieces, axis=0)
             second = jnp.concatenate(pieces[::-1], axis=0)
             return jnp.where(t_rank == 0, first, second)
         stacked = jnp.take(jnp.stack(pieces), jnp.arange(nt) ^ t_rank, axis=0)
-        return stacked.reshape((nt * value.shape[0],) + value.shape[1:])
+        return stacked.reshape((nt * stacked.shape[1],) + stacked.shape[2:])
 
     kernel_rows, columns = conv_params.shape
     gain_count = norm_gains.shape[0]
@@ -577,20 +583,27 @@
         small_rows += 1
     small = jnp.pad(small, (0, small_rows * width - small.size)).reshape(small_rows, width)
     small_pair = over_tensor(small)
-    tokens_all = over_tensor(after(residual, small_pair))
+    token_pieces = pieces_of(after(residual, small_pair))
 
     block_rows = D // dp
     value_shard = jnp.concatenate([inner_proj[1].astype(bf16), small_pair], axis=0)
-    near, far = gather_halves(value_shard, dp)
-    value_w, small_all = assemble(near, far, dp, dp_me, [block_rows, small_rows * nt])
+    value_line = gather_line(value_shard, dp)
+    near = gather_plane(value_line, dp)
+    value_w, small_all = assemble(
+        near, swap(near, "dp", dp, 1), dp, dp_me, [block_rows, small_rows * nt]
+    )
     value_w = value_w.reshape(D, width)
     other_shard = jnp.concatenate(
         [inner_proj[0].astype(bf16), outer_proj.T.astype(bf16)], axis=0
     )
-    other_halves = gather_halves(after(other_shard, near), dp)
-    gate_w, outer_t = assemble(*other_halves, dp, dp_me, [block_rows, block_rows])
-    gate_w, outer_t = gate_w.reshape(D, width), outer_t.reshape(D, width)
-    cot_all = over_tensor(after(cotangent, tokens_all))
+    other_line = gather_line(after(other_shard, value_line), dp)
+    cot_pieces = pieces_of(after(cotangent, small_pair))
+
+    def halves(pieces):
+        if nt == 2:
+            return t_me, pieces[0], pieces[1]
+        all_rows = over_tensor(None, pieces)
+        return jnp.zeros((1,), jnp.int32), all_rows[: length // 2], all_rows[length // 2 :]
 
     small_all = small_all.reshape(dp * nt, small_rows * width)
     shared_full = small_all[:, :shared_size].reshape(D, -1)
@@ -649,17 +662,19 @@
     aux_cols = aux.shape[1]
 
     steps = length // wide
+    in_half = lambda i: i % (steps // 2)
+    value_w = after(value_w, other_line, *cot_pieces[1:])
     normed, chans, pre, mixed, ssd, entering, step_in = call(
         scan_kernel,
         (steps,),
         [
-            rows(wide, D), whole((1, D)), whole((D, width)), whole((D, common_width)),
-            whole((8, channels)), whole((1, width)), whole((8, LANES)), rows(wide, aux_cols),
-            pl.BlockSpec((1, wide), lambda i: (0, i)),
+            rows(wide, D, in_half), rows(wide, D, in_half), whole((1, D)), whole((D, width)),
+            whole((D, common_width)), whole((8, channels)), whole((1, width)), whole((8, LANES)),
+            rows(wide, aux_cols), pl.BlockSpec((1, wide), lambda i, r: (0, i)),
         ],
         [
             rows(wide, D), rows(wide, channels), rows(wide, channels), rows(wide, channels),
-            rows(wide, width), pl.BlockSpec((wide // CHUNK, N, width), lambda i: (i, 0, 0)),
+            rows(wide, width), pl.BlockSpec((wide // CHUNK, N, width), lambda i, r: (i, 0, 0)),
             rows(wide, LANES),
         ],
         [
@@ -667,16 +682,26 @@
             shape(length, channels, dtype=bf16), shape(length, width),
             shape(chunks, N, width), shape(length, LANES),
         ],
-        [pltpu.VMEM((wide + 8, channels), f32), pltpu.VMEM((N, width), f32)],
+        [
+            pltpu.VMEM((wide + 8, channels), f32), pltpu.VMEM((N, width), f32),
+            pltpu.VMEM((CHUNK, width), f32), pltpu.VMEM((2, CHUNK, width), bf16),
+        ],
         length * (2 * D * (width + common_width) + 12 * width * CHUNK),
-    )(tokens_all, pre_gain, value_w, shared_here, conv_here, skip, head_rows, aux, segr)
-
+        scalars=1,
+    )(*halves(token_pieces), pre_gain, value_w, shared_here, conv_here, skip, head_rows, aux, segr)
+
+    plane = gather_plane(other_line, dp, normed)
+    gate_w, outer_t = assemble(
+        plane, swap(plane, "dp", dp, 1), dp, dp_me, [block_rows, block_rows]
+    )
+    gate_w, outer_t = gate_w.reshape(D, width), outer_t.reshape(D, width)
+    cot_rank, cot0, cot1 = halves(cot_pieces)
     gate, scaled_grad, returned, sums = call(
         gate_kernel,
         (steps,),
         [
-            rows(wide, D), rows(wide, D), rows(wide, aux_cols), rows(wide, width),
-            whole((D, width)), whole((D, width)), whole((1, width)),
+            rows(wide, D), rows(wide, D, in_half), rows(wide, D, in_half), rows(wide, aux_cols),
+            rows(wide, width), whole((D, width)), whole((D, width)), whole((1, width)),
         ],
         [rows(wide, width), rows(wide, width), rows(wide, D), rows(wide, LANES)],
         [
@@ -685,7 +710,8 @@
         ],
         [],
         4 * length * D * width,
-    )(normed, cot_all, aux, ssd, gate_w, outer_t, post_gain)
+        scalars=1,
+    )(cot_rank, normed, cot0, cot1, aux, ssd, gate_w, outer_t, post_gain)
     sums = sums[:, :2].T
     distance = 1
     while distance < nt:
@@ -716,9 +742,11 @@
         2 * length * D * width,
         scalars=1,
     )(t_me, gate, scaled_grad, ssd, sums, outer_t, post_gain)
-    sums_og = start_sum(*pair_grad(returned, scaled, normed, dgate, dp, dp_me), dp)
-    dssd = after(dssd, sums_og)
-    line_og = middle_sum(sums_og, dp)
+    outer_keep, outer_send = weight_grad(returned, scaled, dp, dp_me)
+    gate_keep, gate_send = weight_grad(normed, after(dgate, outer_send), dp, dp_me)
+    outer_line, outer_rest = start_sum(outer_keep, outer_send, dp)
+    gate_line, gate_rest = start_sum(gate_keep, gate_send, dp)
+    dssd = after(dssd, *outer_rest, *gate_rest)
 
     branch = branch.reshape(nt, rows_here, D)
     branch_sum = branch[0].astype(f32)
@@ -728,18 +756,18 @@
     tokens = residual.astype(f32)
     block_out = (tokens + branch_sum * live_here[:, None]).astype(bf16)
 
-    calls = 2
-    per_call = chunks // calls
     state = jnp.zeros((N, width), f32)
     win = jnp.zeros((8, channels), f32)
     carry = jnp.zeros((8, LANES), f32)
     back_parts = []
-    for part in range(calls):
-        back = lambda i, top=chunks - 1 - part * per_call: top - i
-        here = lambda i: per_call - 1 - i
+    filled = []
+    top = chunks
+    for part, count in enumerate((3, 3, chunks - 6)):
+        back = lambda i, top=top: top - 1 - i
+        top -= count
         *results, state, win, carry = call(
             scan_back_kernel,
-            (per_call,),
+            (count,),
             [
                 rows(CHUNK, width, back), rows(CHUNK, channels, back), rows(CHUNK, channels, back),
                 rows(CHUNK, channels, back), rows(CHUNK, width, back),
@@ -749,59 +777,69 @@
                 pl.BlockSpec((1, CHUNK), lambda i, back=back: (0, back(i))),
                 whole((width, LANES)),
                 whole((N, width)), whole((8, channels)), whole((8, LANES)),
-            ],
+            ]
+            + [pl.BlockSpec(memory_space=pl.ANY)] * len(filled),
             [
-                rows(CHUNK, width, here), rows(CHUNK, common_width, here), whole((8, channels)),
+                rows(CHUNK, width, back), rows(CHUNK, common_width, back), whole((8, channels)),
                 whole((8, LANES)), whole((1, width)),
                 whole((N, width)), whole((8, channels)), whole((8, LANES)),
             ],
             [
-                shape(length // calls, width, dtype=bf16), shape(length // calls, common_width),
+                shape(length, width, dtype=bf16), shape(length, common_width),
                 shape(8, channels), shape(8, LANES), shape(1, width),
                 shape(N, width), shape(8, channels), shape(8, LANES),
             ],
             [
                 pltpu.VMEM((CHUNK, channels), f32), pltpu.VMEM((CHUNK + 8, channels), f32),
-                pltpu.VMEM((2 * CHUNK, width), f32),
+                pltpu.VMEM((2 * CHUNK, width), f32), pltpu.VMEM((CHUNK, width), f32),
+                pltpu.VMEM((2, CHUNK, width), bf16), pltpu.VMEM((CHUNK, width), bf16),
             ],
-            length // calls * 30 * width * CHUNK,
+            count * CHUNK * 30 * width * CHUNK,
+            aliases={16: 0, 17: 1} if filled else None,
         )(
             dssd, mixed, pre, chans, ssd, entering, step_in, conv_here, skip, head_rows, aux, segr,
-            heads_of, state, win, carry,
+            heads_of, state, win, carry, *filled,
         )
-        back_parts.append(results)
+        filled = results[:2]
+        back_parts.append(results[2:])
         if part == 0:
-            state = after(state, line_og)
-    dval = jnp.concatenate([back_parts[1][0], back_parts[0][0]], axis=0)
-    dcommon = jnp.concatenate([back_parts[1][1], back_parts[0][1]], axis=0)
-    dconv, dheads, dskip = [back_parts[0][i] + back_parts[1][i] for i in range(2, 5)]
-    og_part = high_sum(line_og, dp)
-    outer_part, gate_part = og_part[:block_rows], og_part[block_rows:]
-
-    def input_grad(count, offset, dtype):
+            outer_block, outer_far = middle_sum(after(outer_line, state), outer_rest, dp)
+            state = after(state, *outer_far)
+        if part == 1:
+            gate_block, gate_far = middle_sum(after(gate_line, state), gate_rest, dp)
+            state = after(state, *gate_far)
+    dval, dcommon = filled
+    dconv, dheads, dskip = [sum(parts) for parts in zip(*back_parts)]
+    outer_part = high_sum(outer_block, outer_far, dp)
+    gate_part = high_sum(gate_block, gate_far, dp)
+
+    def input_grad(count, offset, dtype, positions, dgate):
         return call(
             input_grad_kernel,
             (count * per_piece,),
             [
                 rel_rows(width, offset), rel_rows(width, offset), rel_rows(common_width, offset),
-                rel_rows(D, offset), whole((D, width)), whole((D, width)), whole((D, common_width)),
+                plain(D), whole((D, width)), whole((D, width)), whole((D, common_width)),
             ],
             [plain(D), whole((1, D))],
             [shape(count * rows_here, D, dtype=dtype), shape(1, D)],
             [],
             4 * count * rows_here * D * (width + common_width),
             scalars=1,
-        )(t_me, dgate, dval, dcommon, tokens_all, gate_w, value_w, shared_here)
-
-    value_keep, value_send = value_grad(normed, dval, dcommon, dp, dp_me)
-    sent, pre_grad_sent = input_grad(nt - 1, per_piece, bf16)
+        )(t_me, dgate, dval, dcommon, positions, gate_w, value_w, shared_here)
+
+    value_keep, value_send = value_grad(normed, after(dval, outer_part, branch_sum), dcommon, dp, dp_me)
+    value_line, value_rest = start_sum(value_keep, value_send, dp)
+    others = token_pieces[1] if nt == 2 else jnp.concatenate(token_pieces[1:], axis=0)
+    sent, pre_grad_sent = input_grad(
+        nt - 1, per_piece, bf16, others, after(dgate, value_send, gate_part)
+    )
     sent = sent.reshape(nt - 1, rows_here, D)
-    own, pre_grad_own = input_grad(1, 0, f32)
-    normed_grad = own
-    for d in range(1, nt):
-        normed_grad = normed_grad + swap(sent[d - 1], "tensor", nt, d).astype(f32)
-
-    value_sum = high_sum(middle_sum(start_sum(value_keep, value_send, dp), dp), dp)
+    own, pre_grad_own = input_grad(1, 0, f32, residual, after(dgate, sent, *value_rest))
+    received = [swap(sent[d - 1], "tensor", nt, d) for d in range(1, nt)]
+
+    value_block, value_far = middle_sum(after(value_line, own), value_rest, dp)
+    value_sum = high_sum(value_block, value_far, dp)
     value_part = value_sum[:, :width]
     shared_rows = shared_proj.shape[0]
     shared_sum = value_sum[:, width:].reshape(nt, shared_rows, common_width)
@@ -846,7 +884,7 @@
         ],
         axis=1,
     )
-    vector = sum_everywhere(vector, dp, nt)
+    vector = sum_everywhere(after(vector, *value_far), dp, nt)
     conv_size = kernel_rows * (DI + 2 * N)
     place = d_rank * nt + t_rank
     conv_part = lax.dynamic_slice_in_dim(
@@ -857,6 +895,9 @@
         vector[0, conv_size + D + DI :].reshape(3, H), t_rank * heads_here, heads_here, 1
     )
 
+    normed_grad = own
+    for piece in received:
+        normed_grad = normed_grad + after(piece, vector).astype(f32)
     inverse = lax.rsqrt(jnp.mean(tokens * tokens, axis=1, keepdims=True) + norm_epsilon)
     normal_tokens = tokens * inverse
     normal_grad = normed_grad * pre_gain

time: 352 us -> 383 us (1.088)
  waiting for transfers between devices: 106 us -> 133 us
  local copies, waits for them, and re-layouts: 34.3 us -> 39.6 us
  other arithmetic: 35.3 us -> 39.3 us
  starting transfers between devices: 45.7 us -> 41.7 us
    ppermute x32 -> x37, waiting for transfers between devices: 106 us -> 133 us  [swap(): return lax.ppermute(value, axis, [(i, i ^ distance) for i in range(size)])]
    unnamed x103, local copies, waits for them, and re-layouts: 19.5 us -> 13.1 us
    select_n x3 -> x1, other arithmetic: 6.27 us -> 0.01 us  [over_tensor(): return jnp.where(t_rank == 0, first, second)]
    ppermute x32 -> x37, starting transfers between devices: 45.7 us -> 41.7 us  [swap(): return lax.ppermute(value, axis, [(i, i ^ distance) for i in range(size)])]
    add x7 -> x8, other arithmetic: 6.73 us -> 8.31 us  [the longest x3 5.26 us: start_sum(): line = keep[parts[0]].astype(f32) + other[parts[0]].astype(f32)]
    pallas_call x5 -> x7, Pallas kernels: 84.6 us -> 85.8 us  [the longest x3 36.3 us: shards(): call(scan_back_kernel, (count,), [rows(CHUNK, width, back), rows(CHUNK, c...]
  transfers between devices with their start and end apart: 32 -> 37, of which waited for: 19 -> 15; matrix products, arithmetic and copies ran while one was open for 13% -> 15% of each run, Pallas kernels for 16% -> 25%
where the time goes in v3:
time: 383 us; the launch traced here: 379 us
  waiting for transfers between devices  133 us (35%)
  Pallas kernels  123 us (32%)
  starting transfers between devices  41.7 us (11%)
  local copies, waits for them, and re-layouts  39.6 us (10%)
  other arithmetic  39.3 us (10%)
    ppermute x37, waiting for transfers between devices, swap(): return lax.ppermute(value, axis, [(i, i ^ distance) for i in range(size)])  133 us
    ppermute x37, starting transfers between devices, swap(): return lax.ppermute(value, axis, [(i, i ^ distance) for i in range(size)])  41.7 us
    pallas_call x3, Pallas kernels, shards(): call(scan_back_kernel, (count,), [rows(CHUNK, width, back), rows(CHUNK, c...  36.3 us
    pallas_call x1, Pallas kernels, shards(): call(scan_kernel, (steps,), [rows(wide, D, in_half), rows(wide, D, in_hal...  25 us
    pallas_call x2, Pallas kernels, input_grad(): call(input_grad_kernel, (count * per_piece,), [rel_rows(width, offset), r...  15 us
    pallas_call x2, Pallas kernels, weight_grad(): call(functools.partial(weight_grad_kernel, dp), (width // 256,), [whole((...  13.6 us
    unnamed x103, local copies, waits for them, and re-layouts  13.1 us
    pallas_call x1, Pallas kernels, shards(): call(gate_kernel, (steps,), [rows(wide, D), rows(wide, D, in_half), rows(...  10.9 us
  transfers between devices with their start and end apart: 37, of which 15 were waited for; matrix products, arithmetic and copies ran while one was open for 15% of the time, Pallas kernels for 25%

profile of v3, /device:TPU:0, one launch (start us, length us, event | category | flops | bytes accessed | tf_op | source)
XLA Modules:
  0.0 378.7 jit_solution(10754499900791743196)
XLA Ops:
  4.7 3.0 collective-permute-start
  19.5 2.6 collective-permute-start.3
  22.9 4.6 %collective-permute-done.2 = bf16[96,1024]{1,0:T(8,128)(2,1)S(1)} collective-permute-done((bf16[96,1024]{1,0:T(8,128)(2,1)S(1)}, bf16[96,1024]{1,0:T(8,128)(2,1)S(1)}, u32[]{:S(2)}, u32[]{:S(2)}) %collective-permute-start.2) | collective-permute-done | bytes 196640 | tf_op jit(solution)/shard_map/ppermute | solution.py:48
  27.5 9.2 %collective-permute-done.3 = bf16[96,1024]{1,0:T(8,128)(2,1)S(1)} collective-permute-done((bf16[96,1024]{1,0:T(8,128)(2,1)S(1)}, bf16[96,1024]{1,0:T(8,128)(2,1)S(1)}, u32[]{:S(2)}, u32[]{:S(2)}) %collective-permute-start.3) | collective-permute-done | bytes 196640 | tf_op jit(solution)/shard_map/ppermute | solution.py:48
  38.6 14.6 %collective-permute-done.5 = bf16[4,96,1024]{2,1,0:T(8,128)(2,1)S(1)} collective-permute-done((bf16[4,96,1024]{2,1,0:T(8,128)(2,1)S(1)}, bf16[4,96,1024]{2,1,0:T(8,128)(2,1)S(1)}, u32[]{:S(2)}, u32[]{:S(2)}) %collective-permute-start.5) | collective-permute-done | bytes 786464 | tf_op jit(solution)/shard_map/ppermute | solution.py:48
  53.5 4.8 %collective-permute-start.7 = (bf16[128,1024]{1,0:T(8,128)(2,1)S(1)}, bf16[128,1024]{1,0:T(8,128)(2,1)}, u32[]{:S(2)}, u32[]{:S(2)}) collective-permute-start(bf16[128,1024]{1,0:T(8,128)(2,1)S(1)} %pad_maximum_fusion.3), channel_id=1, source_target_pairs={{0,8},{2,10},{4,12},{6,14},{8,0},{10,2},{12,4},{14,6},{16,24},{18,... | collective-permute-start | bytes 786440 | tf_op jit(solution)/shard_map/ppermute | solution.py:48
  63.4 7.2 %collective-permute-done.7 = bf16[128,1024]{1,0:T(8,128)(2,1)} collective-permute-done((bf16[128,1024]{1,0:T(8,128)(2,1)S(1)}, bf16[128,1024]{1,0:T(8,128)(2,1)}, u32[]{:S(2)}, u32[]{:S(2)}) %collective-permute-start.7) | collective-permute-done | bytes 262176 | tf_op jit(solution)/shard_map/ppermute | solution.py:48
  71.2 8.6 %collective-permute-done.8 = bf16[128,1024]{1,0:T(8,128)(2,1)} collective-permute-done((bf16[128,1024]{1,0:T(8,128)(2,1)S(1)}, bf16[128,1024]{1,0:T(8,128)(2,1)}, u32[]{:S(2)}, u32[]{:S(2)}) %collective-permute-start.8) | collective-permute-done | bytes 262176 | tf_op jit(solution)/shard_map/ppermute | solution.py:48
  97.6 13.1 %collective-permute-done.1.tok1.tok = bf16[512,1024]{1,0:T(8,128)(2,1)} collective-permute-done((bf16[512,1024]{1,0:T(8,128)(2,1)S(1)}, bf16[512,1024]{1,0:T(8,128)(2,1)}, u32[]{:S(2)}, u32[]{:S(2)}) %collective-permute-start.1) | collective-permute-done | bytes 1048608 | tf_op jit(solution)/shard_map/ppermute | solution.py:48
  110.7 25.0 %shard_map.357 = (bf16[1024,1024]{1,0:T(8,128)(2,1)}, f32[1024,1280]{1,0:T(8,128)}, f32[1024,1280]{1,0:T(8,128)}, bf16[1024,1280]{1,0:T(8,128)(2,1)}, f32[1024,1...) custom-call(s32[1]{0:T(128)} %bitcast.rank, bf16[512,1024]{1,0:T(8,128)(2,1)S(1)} %copy-done.2, ...), custom_call_target="tpu_custom_call" | custom-call | flops 4563402752 | bytes 48234496 | tf_op jit(solution)/shard_map/pallas_call | solution.py:667
  137.2 4.1 %collective-permute-done.12.far = bf16[8,128,1024]{2,1,0:T(8,128)(2,1)S(1)} collective-permute-done((bf16[8,128,1024]{2,1,0:T(8,128)(2,1)S(1)}, bf16[8,128,1024]{2,1,0:T(8,128)(2,1)S(1)}, u32[]{:S(2)}, u32[]{:S(2)}) %collective-permute-start.12) | collective-permute-done | bytes 2097184 | tf_op jit(solution)/shard_map/ppermute | solution.py:48
  144.3 10.9 %shard_map.359 = (f32[1024,1024]{1,0:T(8,128)}, f32[1024,1024]{1,0:T(8,128)}, bf16[1024,1024]{1,0:T(8,128)(2,1)}, f32[1024,128]{1,0:T(8,128)S(1)}) custom-call(s32[1]{0:T(128)} %bitcast.rank, bf16[1024,1024]{1,0:T(8,128)(2,1)} %get-tuple-element.94.normed.lhs, bf16[512,1024]{1,0:T(8,128)(2,1)S(1)} %copy-done.14, ...), custom_call_target="tpu_custom_call" | custom-call | flops 4294967296 | bytes 22020096 | tf_op jit(solution)/shard_map/pallas_call | solution.py:699
  155.8 13.4 %collective-permute-done.13 = f32[2,1024]{0,1:T(8,128)S(1)} collective-permute-done((f32[2,1024]{0,1:T(8,128)S(1)}, f32[2,1024]{0,1:T(8,128)S(1)}, u32[]{:S(2)}, u32[]{:S(2)}) %collective-permute-start.13) | collective-permute-done | bytes 8224 | tf_op jit(solution)/shard_map/ppermute | solution.py:48
  169.3 10.2 %shard_map.360 = (bf16[1024,1024]{1,0:T(8,128)(2,1)S(1)}, bf16[1024,1024]{1,0:T(8,128)(2,1)}, bf16[1024,1024]{1,0:T(8,128)(2,1)}, bf16[1024,1024]{1,0:T(8,128)(2,1)}, f32[1,1024]{1,0:T(1,128)S(1)}) custom-call(s32[1]{0:T(128)} %bitcast.rank, f32[1024,1024]{1,0:T(8,128)} %get-tuple-element.99.gate_r, f32[1024,1024]{1,0:T(8,128)} %get-tuple-element.100.sg_r, ...), custom_call_target="tpu_custom_call" | custom-call | flops 2147483648 | bytes 16785408 | tf_op jit(solution)/shard_map/pallas_call | solution.py:729
  180.9 6.9 %shard_map.361 = (bf16[8,64,1024]{2,1,0:T(8,128)(2,1)S(1)}, bf16[8,64,1024]{2,1,0:T(8,128)(2,1)}) custom-call(s32[1]{0:T(128)} %bitcast.1.me, bf16[1024,1024]{1,0:T(8,128)(2,1)} %get-tuple-element.105.lhs, bf16[1024,1024]{1,0:T(8,128)(2,1)} %get-tuple-element.106.rhs), custom_call_target="tpu_custom_call" | custom-call | flops 2147483648 | bytes 4194304 | tf_op jit(solution)/shard_map/pallas_call | solution.py:463
  188.9 6.7 %shard_map.362 = (bf16[8,64,1024]{2,1,0:T(8,128)(2,1)S(1)}, bf16[8,64,1024]{2,1,0:T(8,128)(2,1)}) custom-call(s32[1]{0:T(128)} %bitcast.1.me, bf16[1024,1024]{1,0:T(8,128)(2,1)} %get-tuple-element.94.normed.lhs, bf16[1024,1024]{1,0:T(8,128)(2,1)} %get-tuple-element.139.rhs.dgate), custom_call_target="tpu_custom_call" | custom-call | flops 2147483648 | bytes 4194304 | tf_op jit(solution)/shard_map/pallas_call | solution.py:463
  202.1 13.1 %shard_map.363 = (bf16[1024,1024]{1,0:T(8,128)(2,1)}, f32[1024,384]{1,0:T(8,128)S(1)}, f32[8,1280]{1,0:T(8,128)S(1)}, f32[8,128]{1,0:T(8,128)S(1)}, f32[1,1024]{...) custom-call(bf16[1024,1024]{1,0:T(8,128)(2,1)} %get-tuple-element.112.dssd, ...), custom_call_target="tpu_custom_call" | custom-call | flops 1509949440 | bytes 8577024 | tf_op jit(solution)/shard_map/pallas_call | solution.py:768
  216.1 2.4 collective-permute-start.20
  219.9 13.0 %shard_map.364 = (bf16[1024,1024]{1,0:T(8,128)(2,1)}, f32[1024,384]{1,0:T(8,128)S(1)}, f32[8,1280]{1,0:T(8,128)S(1)}, f32[8,128]{1,0:T(8,128)S(1)}, f32[1,1024]{...) custom-call(bf16[1024,1024]{1,0:T(8,128)(2,1)} %get-tuple-element.11, ...), custom_call_target="tpu_custom_call", output_to_operand_aliasing={{0}: (16, {}), {1}: (17, {})} | custom-call | flops 1509949440 | bytes 8577024 | tf_op jit(solution)/shard_map/pallas_call | solution.py:768
  234.8 3.0 collective-permute-start.24
  237.8 10.2 %shard_map.365 = (bf16[1024,1024]{1,0:T(8,128)(2,1)}, f32[1024,384]{1,0:T(8,128)S(1)}, f32[8,1280]{1,0:T(8,128)S(1)}, f32[8,128]{1,0:T(8,128)S(1)}, f32[1,1024]{...) custom-call(bf16[1024,1024]{1,0:T(8,128)(2,1)} %get-tuple-element.11, ...), custom_call_target="tpu_custom_call", output_to_operand_aliasing={{0}: (16, {}), {1}: (17, {})} | custom-call | flops 1006632960 | bytes 8577024 | tf_op jit(solution)/shard_map/pallas_call | solution.py:768
  250.6 9.9 %shard_map.366 = (bf16[8,64,1408]{2,1,0:T(8,128)(2,1)S(1)}, bf16[8,64,1408]{2,1,0:T(8,128)(2,1)}) custom-call(s32[1]{0:T(128)} %bitcast.1.me, bf16[1024,1024]{1,0:T(8,128)(2,1)} %get-tuple-element.94.normed.lhs, bf16[1024,1024]{1,0:T(8,128)(2,1)} %get-tuple-element.133.dval, f32[1024,384]{1,0:T(8,128)} %copy-done), custom_call_target="tpu_custom_call" | custom-call | flops 3758096384 | bytes 5767168 | tf_op jit(solution)/shard_map/pallas_call | solution.py:501
  271.4 7.6 %shard_map.368 = (bf16[512,1024]{1,0:T(8,128)(2,1)}, f32[1,1024]{1,0:T(1,128)S(1)}) custom-call(s32[1]{0:T(128)} %bitcast.rank, bf16[1024,1024]{1,0:T(8,128)(2,1)} %get-tuple-element.139.rhs.dgate, bf16[1024,1024]{1,0:T(8,128)(2,1)} %get-tuple-element.133.dval, f32[1024,384]{1,0:T(8,128)} %copy-done, bf16[512,1024]{1,0:T(8,128)(2,1)} %collective-permute-done.1.tok1.tok, ...), custom_call_target="tpu_custom_call" | custom-call | flops 2952790016 | bytes 2105344 | tf_op jit(solution)/shard_map/pallas_call | solution.py:817
  282.3 7.4 %shard_map.367 = (f32[512,1024]{1,0:T(8,128)}, f32[1,1024]{1,0:T(1,128)S(1)}) custom-call(s32[1]{0:T(128)} %bitcast.rank, bf16[1024,1024]{1,0:T(8,128)(2,1)} %get-tuple-element.139.rhs.dgate, bf16[1024,1024]{1,0:T(8,128)(2,1)} %get-tuple-element.133.dval, f32[1024,384]{1,0:T(8,128)S(1)} %copy-done.1, bf16[512,1024]{1,0:T(8,128)(2,1)S(1)} %copy-done.2, ...), custom_call_target="tpu_custom_call" | custom-call | flops 2952790016 | bytes 4202496 | tf_op jit(solution)/shard_map/pallas_call | solution.py:817
  289.9 9.5 %collective-permute-done.27 = bf16[4,64,1408]{2,1,0:T(8,128)(2,1)S(1)} collective-permute-done((bf16[4,64,1408]{2,1,0:T(8,128)(2,1)S(1)}, bf16[4,64,1408]{2,1,0:T(8,128)(2,1)S(1)}, u32[]{:S(2)}, u32[]{:S(2)}) %collective-permute-start.27) | collective-permute-done | bytes 720928 | tf_op jit(solution)/shard_map/ppermute | solution.py:48
  302.1 3.6 collective-permute-done.28
  306.2 3.0 collective-permute-start.34
  317.0 5.6 %collective-permute-done.34 = bf16[64,1408]{1,0:T(8,128)(2,1)} collective-permute-done((bf16[64,1408]{1,0:T(8,128)(2,1)}, bf16[64,1408]{1,0:T(8,128)(2,1)}, u32[]{:S(2)}, u32[]{:S(2)}) %collective-permute-start.34) | collective-permute-done | bytes 180256 | tf_op jit(solution)/shard_map/ppermute | solution.py:48
  326.9 34.7 %collective-permute-done.36 = f32[32,384]{1,0:T(8,128)S(1)} collective-permute-done((f32[32,384]{1,0:T(8,128)}, f32[32,384]{1,0:T(8,128)S(1)}, u32[]{:S(2)}, u32[]{:S(2)}) %collective-permute-start.36) | collective-permute-done | bytes 49184 | tf_op jit(solution)/shard_map/ppermute | solution.py:48
  365.5 3.3 collective-permute-done.32
  370.5 2.6 fusion.2
  374.5 4.0 %fusion.6 = (bf16[512,1024]{1,0:T(8,128)(2,1)}, bf16[512,1024]{1,0:T(8,128)(2,1)}) fusion(bf16[512,1024]{1,0:T(8,128)(2,1)S(1)} %copy-done.2, bf16[512,1024]{1,0:T(8,128)(2,1)S(1)} %copy-done.15, f32[512,1024]{1,0:T(8,128)S(1)} %copy-done.18, bf16[512,1024]{1,0:T(8,128)(2,1)} %collective-permute-done.26, f32[512]{0:T(512)S(1)} %broadcast_multiply_fusion, ...), kind=kLoop, calls=%fused_computation.9 | loop fusion | flops 8912896 | bytes 9447424 | tf_op jit(solution)/shard_map/convert_element_type | solution.py:907
  (282 shorter events, 99.1 us)
Async XLA Ops:
  4.7 13.2 %collective-permute-start = (bf16[16,1024]{1,0:T(8,128)(2,1)S(1)}, bf16[16,1024]{1,0:T(8,128)(2,1)S(1)}, u32[]{:S(2)}, u32[]{:S(2)}) collective-permute-start(bf16[16,1024]{1,0:T(8,128)(2,1)S(1)} %reshape.203), channel_id=1, source_target_pairs={{0,1},{1,0},{2,3},{3,2},{4,5},{5,4},{6,7},{7,6},{8,9},{9,8},{10,11... | collective-permute-start | bytes 98312 | tf_op jit(solution)/shard_map/ppermute | solution.py:48
  17.9 9.6 %collective-permute-start.2 = (bf16[96,1024]{1,0:T(8,128)(2,1)S(1)}, bf16[96,1024]{1,0:T(8,128)(2,1)S(1)}, u32[]{:S(2)}, u32[]{:S(2)}) collective-permute-start(bf16[96,1024]{1,0:T(8,128)(2,1)S(1)} %get-tuple-element.203), channel_id=1, source_target_pairs={{0,8},{2,10},{4,12},{6,14},{8,0},{10,2},{12,4},{14,6},{16,24},{18,... | collective-permute-start | bytes 589832 | tf_op jit(solution)/shard_map/ppermute | solution.py:48
  19.5 17.2 %collective-permute-start.3 = (bf16[96,1024]{1,0:T(8,128)(2,1)S(1)}, bf16[96,1024]{1,0:T(8,128)(2,1)S(1)}, u32[]{:S(2)}, u32[]{:S(2)}) collective-permute-start(bf16[96,1024]{1,0:T(8,128)(2,1)S(1)} %get-tuple-element.203), channel_id=1, source_target_pairs={{0,16},{2,18},{4,20},{6,22},{8,24},{10,26},{12,28},{14,30},{16,0},... | collective-permute-start | bytes 589832 | tf_op jit(solution)/shard_map/ppermute | solution.py:48
  22.1 14.6 %collective-permute-start.4 = (bf16[96,1024]{1,0:T(8,128)(2,1)S(1)}, bf16[96,1024]{1,0:T(8,128)(2,1)S(1)}, u32[]{:S(2)}, u32[]{:S(2)}) collective-permute-start(bf16[96,1024]{1,0:T(8,128)(2,1)S(1)} %get-tuple-element.203), channel_id=1, source_target_pairs={{0,24},{2,26},{4,28},{6,30},{8,16},{10,18},{12,20},{14,22},{16,8},... | collective-permute-start | bytes 589832 | tf_op jit(solution)/shard_map/ppermute | solution.py:48
  36.9 16.3 %collective-permute-start.5 = (bf16[4,96,1024]{2,1,0:T(8,128)(2,1)S(1)}, bf16[4,96,1024]{2,1,0:T(8,128)(2,1)S(1)}, u32[]{:S(2)}, u32[]{:S(2)}) collective-permute-start(bf16[4,96,1024]{2,1,0:T(8,128)(2,1)S(1)} %pad_maximum_fusion.1), channel_id=1, source_target_pairs={{0,4},{2,6},{4,0},{6,2},{8,12},{10,14},{12,8},{14,10},{16,20},{18,... | collective-permute-start | bytes 2359304 | tf_op jit(solution)/shard_map/ppermute | solution.py:48
  53.2 33.2 %collective-permute-start.6 = (bf16[8,96,1024]{2,1,0:T(8,128)(2,1)S(1)}, bf16[8,96,1024]{2,1,0:T(8,128)(2,1)}, u32[]{:S(2)}, u32[]{:S(2)}) collective-permute-start(bf16[8,96,1024]{2,1,0:T(8,128)(2,1)S(1)} %constant_dynamic-update-slice_fusion.near), channel_id=1, source_target_pairs={{0,2},{2,0},{4,6},{6,4},{8,10},{10,8},{12,14},{14,12},{16,18},{18,... | collective-permute-start | bytes 4718600 | tf_op jit(solution)/shard_map/ppermute | solution.py:48
  53.5 17.1 %collective-permute-start.7 = (bf16[128,1024]{1,0:T(8,128)(2,1)S(1)}, bf16[128,1024]{1,0:T(8,128)(2,1)}, u32[]{:S(2)}, u32[]{:S(2)}) collective-permute-start(bf16[128,1024]{1,0:T(8,128)(2,1)S(1)} %pad_maximum_fusion.3), channel_id=1, source_target_pairs={{0,8},{2,10},{4,12},{6,14},{8,0},{10,2},{12,4},{14,6},{16,24},{18,... | collective-permute-start | bytes 786440 | tf_op jit(solution)/shard_map/ppermute | solution.py:48
  58.3 21.4 %collective-permute-start.8 = (bf16[128,1024]{1,0:T(8,128)(2,1)S(1)}, bf16[128,1024]{1,0:T(8,128)(2,1)}, u32[]{:S(2)}, u32[]{:S(2)}) collective-permute-start(bf16[128,1024]{1,0:T(8,128)(2,1)S(1)} %pad_maximum_fusion.3), channel_id=1, source_target_pairs={{0,16},{2,18},{4,20},{6,22},{8,24},{10,26},{12,28},{14,30},{16,0},... | collective-permute-start | bytes 786440 | tf_op jit(solution)/shard_map/ppermute | solution.py:48
  59.5 20.2 %collective-permute-start.9 = (bf16[128,1024]{1,0:T(8,128)(2,1)S(1)}, bf16[128,1024]{1,0:T(8,128)(2,1)}, u32[]{:S(2)}, u32[]{:S(2)}) collective-permute-start(bf16[128,1024]{1,0:T(8,128)(2,1)S(1)} %pad_maximum_fusion.3), channel_id=1, source_target_pairs={{0,24},{2,26},{4,28},{6,30},{8,16},{10,18},{12,20},{14,22},{16,8},... | collective-permute-start | bytes 786440 | tf_op jit(solution)/shard_map/ppermute | solution.py:48
  62.9 34.4 %collective-permute-start.10 = (bf16[512,1024]{1,0:T(8,128)(2,1)}, bf16[512,1024]{1,0:T(8,128)(2,1)}, u32[]{:S(2)}, u32[]{:S(2)}) collective-permute-start(bf16[512,1024]{1,0:T(8,128)(2,1)} %cot0), channel_id=1, source_target_pairs={{0,1},{1,0},{2,3},{3,2},{4,5},{5,4},{6,7},{7,6},{8,9},{9,8},{10,11... | collective-permute-start | bytes 3145736 | tf_op jit(solution)/shard_map/ppermute | solution.py:48
  70.6 40.0 %collective-permute-start.1 = (bf16[512,1024]{1,0:T(8,128)(2,1)S(1)}, bf16[512,1024]{1,0:T(8,128)(2,1)}, u32[]{:S(2)}, u32[]{:S(2)}) collective-permute-start(bf16[512,1024]{1,0:T(8,128)(2,1)S(1)} %copy-done.2), channel_id=1, source_target_pairs={{0,1},{1,0},{2,3},{3,2},{4,5},{5,4},{6,7},{7,6},{8,9},{9,8},{10,11... | collective-permute-start | bytes 3145736 | tf_op jit(solution)/shard_map/ppermute | solution.py:48
  81.9 53.7 %collective-permute-start.11 = (bf16[4,128,1024]{2,1,0:T(8,128)(2,1)}, bf16[4,128,1024]{2,1,0:T(8,128)(2,1)}, u32[]{:S(2)}, u32[]{:S(2)}) collective-permute-start(bf16[4,128,1024]{2,1,0:T(8,128)(2,1)} %pad_maximum_fusion), channel_id=1, source_target_pairs={{0,4},{2,6},{4,0},{6,2},{8,12},{10,14},{12,8},{14,10},{16,20},{18,... | collective-permute-start | bytes 3145736 | tf_op jit(solution)/shard_map/ppermute | solution.py:48
  155.2 14.0 %collective-permute-start.13 = (f32[2,1024]{0,1:T(8,128)S(1)}, f32[2,1024]{0,1:T(8,128)S(1)}, u32[]{:S(2)}, u32[]{:S(2)}) collective-permute-start(f32[2,1024]{0,1:T(8,128)S(1)} %slice_bitcast_fusion), channel_id=1, source_target_pairs={{0,1},{1,0},{2,3},{3,2},{4,5},{5,4},{6,7},{7,6},{8,9},{9,8},{10,11... | collective-permute-start | bytes 24584 | tf_op jit(solution)/shard_map/ppermute | solution.py:48
  188.9 7.4 %collective-permute-start.15 = (bf16[8,64,1024]{2,1,0:T(8,128)(2,1)}, bf16[8,64,1024]{2,1,0:T(8,128)(2,1)}, u32[]{:S(2)}, u32[]{:S(2)}) collective-permute-start(bf16[8,64,1024]{2,1,0:T(8,128)(2,1)} %get-tuple-element.108), channel_id=1, source_target_pairs={{0,2},{2,0},{4,6},{6,4},{8,10},{10,8},{12,14},{14,12},{16,18},{18,... | collective-permute-start | bytes 3145736 | tf_op jit(solution)/shard_map/ppermute | solution.py:48
  198.2 17.0 %collective-permute-start.17 = (bf16[4,64,1024]{2,1,0:T(8,128)(2,1)S(1)}, bf16[4,64,1024]{2,1,0:T(8,128)(2,1)S(1)}, u32[]{:S(2)}, u32[]{:S(2)}) collective-permute-start(bf16[4,64,1024]{2,1,0:T(8,128)(2,1)S(1)} %get-tuple-element.188), channel_id=1, source_target_pairs={{0,4},{2,6},{4,0},{6,2},{8,12},{10,14},{12,8},{14,10},{16,20},{18,... | collective-permute-start | bytes 1572872 | tf_op jit(solution)/shard_map/ppermute | solution.py:48
  201.5 31.4 %collective-permute-start.18 = (bf16[4,64,1024]{2,1,0:T(8,128)(2,1)S(1)}, bf16[4,64,1024]{2,1,0:T(8,128)(2,1)S(1)}, u32[]{:S(2)}, u32[]{:S(2)}) collective-permute-start(bf16[4,64,1024]{2,1,0:T(8,128)(2,1)S(1)} %get-tuple-element.186), channel_id=1, source_target_pairs={{0,4},{2,6},{4,0},{6,2},{8,12},{10,14},{12,8},{14,10},{16,20},{18,... | collective-permute-start | bytes 1572872 | tf_op jit(solution)/shard_map/ppermute | solution.py:48
  215.4 32.6 %collective-permute-start.19 = (bf16[64,1024]{1,0:T(8,128)(2,1)S(1)}, bf16[64,1024]{1,0:T(8,128)(2,1)S(1)}, u32[]{:S(2)}, u32[]{:S(2)}) collective-permute-start(bf16[64,1024]{1,0:T(8,128)(2,1)S(1)} %get-tuple-element.199), channel_id=1, source_target_pairs={{0,8},{2,10},{4,12},{6,14},{8,0},{10,2},{12,4},{14,6},{16,24},{18,... | collective-permute-start | bytes 393224 | tf_op jit(solution)/shard_map/ppermute | solution.py:48
  216.1 33.4 %collective-permute-start.20 = (bf16[64,1024]{1,0:T(8,128)(2,1)S(1)}, bf16[64,1024]{1,0:T(8,128)(2,1)S(1)}, u32[]{:S(2)}, u32[]{:S(2)}) collective-permute-start(bf16[64,1024]{1,0:T(8,128)(2,1)S(1)} %get-tuple-element.198), channel_id=1, source_target_pairs={{0,16},{2,18},{4,20},{6,22},{8,24},{10,26},{12,28},{14,30},{16,0},... | collective-permute-start | bytes 393224 | tf_op jit(solution)/shard_map/ppermute | solution.py:48
  218.5 31.0 %collective-permute-start.21 = (bf16[64,1024]{1,0:T(8,128)(2,1)S(1)}, bf16[64,1024]{1,0:T(8,128)(2,1)S(1)}, u32[]{:S(2)}, u32[]{:S(2)}) collective-permute-start(bf16[64,1024]{1,0:T(8,128)(2,1)S(1)} %get-tuple-element.197), channel_id=1, source_target_pairs={{0,24},{2,26},{4,28},{6,30},{8,16},{10,18},{12,20},{14,22},{16,8},... | collective-permute-start | bytes 393224 | tf_op jit(solution)/shard_map/ppermute | solution.py:48
  234.8 34.7 %collective-permute-start.23 = (bf16[64,1024]{1,0:T(8,128)(2,1)}, bf16[64,1024]{1,0:T(8,128)(2,1)S(1)}, u32[]{:S(2)}, u32[]{:S(2)}) collective-permute-start(bf16[64,1024]{1,0:T(8,128)(2,1)} %get-tuple-element.196), channel_id=1, source_target_pairs={{0,8},{2,10},{4,12},{6,14},{8,0},{10,2},{12,4},{14,6},{16,24},{18,... | collective-permute-start | bytes 393224 | tf_op jit(solution)/shard_map/ppermute | solution.py:48
  234.8 34.7 %collective-permute-start.24 = (bf16[64,1024]{1,0:T(8,128)(2,1)}, bf16[64,1024]{1,0:T(8,128)(2,1)S(1)}, u32[]{:S(2)}, u32[]{:S(2)}) collective-permute-start(bf16[64,1024]{1,0:T(8,128)(2,1)} %get-tuple-element.195), channel_id=1, source_target_pairs={{0,16},{2,18},{4,20},{6,22},{8,24},{10,26},{12,28},{14,30},{16,0},... | collective-permute-start | bytes 393224 | tf_op jit(solution)/shard_map/ppermute | solution.py:48
  248.0 21.5 %collective-permute-start.25 = (bf16[64,1024]{1,0:T(8,128)(2,1)}, bf16[64,1024]{1,0:T(8,128)(2,1)}, u32[]{:S(2)}, u32[]{:S(2)}) collective-permute-start(bf16[64,1024]{1,0:T(8,128)(2,1)} %get-tuple-element.194), channel_id=1, source_target_pairs={{0,24},{2,26},{4,28},{6,30},{8,16},{10,18},{12,20},{14,22},{16,8},... | collective-permute-start | bytes 393224 | tf_op jit(solution)/shard_map/ppermute | solution.py:48
  260.5 18.5 %collective-permute-start.22 = (bf16[8,64,1408]{2,1,0:T(8,128)(2,1)}, bf16[8,64,1408]{2,1,0:T(8,128)(2,1)}, u32[]{:S(2)}, u32[]{:S(2)}) collective-permute-start(bf16[8,64,1408]{2,1,0:T(8,128)(2,1)} %get-tuple-element.136), channel_id=1, source_target_pairs={{0,2},{2,0},{4,6},{6,4},{8,10},{10,8},{12,14},{14,12},{16,18},{18,... | collective-permute-start | bytes 4325384 | tf_op jit(solution)/shard_map/ppermute | solution.py:48
  280.8 18.6 %collective-permute-start.27 = (bf16[4,64,1408]{2,1,0:T(8,128)(2,1)S(1)}, bf16[4,64,1408]{2,1,0:T(8,128)(2,1)S(1)}, u32[]{:S(2)}, u32[]{:S(2)}) collective-permute-start(bf16[4,64,1408]{2,1,0:T(8,128)(2,1)S(1)} %get-tuple-element.184), channel_id=1, source_target_pairs={{0,4},{2,6},{4,0},{6,2},{8,12},{10,14},{12,8},{14,10},{16,20},{18,... | collective-permute-start | bytes 2162696 | tf_op jit(solution)/shard_map/ppermute | solution.py:48
  306.1 10.9 %collective-permute-start.33 = (bf16[64,1408]{1,0:T(8,128)(2,1)}, bf16[64,1408]{1,0:T(8,128)(2,1)}, u32[]{:S(2)}, u32[]{:S(2)}) collective-permute-start(bf16[64,1408]{1,0:T(8,128)(2,1)} %get-tuple-element.193), channel_id=1, source_target_pairs={{0,8},{2,10},{4,12},{6,14},{8,0},{10,2},{12,4},{14,6},{16,24},{18,... | collective-permute-start | bytes 540680 | tf_op jit(solution)/shard_map/ppermute | solution.py:48
  306.2 16.4 %collective-permute-start.34 = (bf16[64,1408]{1,0:T(8,128)(2,1)}, bf16[64,1408]{1,0:T(8,128)(2,1)}, u32[]{:S(2)}, u32[]{:S(2)}) collective-permute-start(bf16[64,1408]{1,0:T(8,128)(2,1)} %get-tuple-element.192), channel_id=1, source_target_pairs={{0,16},{2,18},{4,20},{6,22},{8,24},{10,26},{12,28},{14,30},{16,0},... | collective-permute-start | bytes 540680 | tf_op jit(solution)/shard_map/ppermute | solution.py:48
  309.2 13.5 %collective-permute-start.35 = (bf16[64,1408]{1,0:T(8,128)(2,1)}, bf16[64,1408]{1,0:T(8,128)(2,1)}, u32[]{:S(2)}, u32[]{:S(2)}) collective-permute-start(bf16[64,1408]{1,0:T(8,128)(2,1)} %get-tuple-element.191), channel_id=1, source_target_pairs={{0,24},{2,26},{4,28},{6,30},{8,16},{10,18},{12,20},{14,22},{16,8},... | collective-permute-start | bytes 540680 | tf_op jit(solution)/shard_map/ppermute | solution.py:48
  313.4 61.2 %collective-permute-start.14 = (bf16[512,1024]{1,0:T(8,128)(2,1)}, bf16[512,1024]{1,0:T(8,128)(2,1)}, u32[]{:S(2)}, u32[]{:S(2)}) collective-permute-start(bf16[512,1024]{1,0:T(8,128)(2,1)} %slice.214), channel_id=1, source_target_pairs={{0,1},{1,0},{2,3},{3,2},{4,5},{5,4},{6,7},{7,6},{8,9},{9,8},{10,11... | collective-permute-start | bytes 3145736 | tf_op jit(solution)/shard_map/ppermute | solution.py:48
  314.9 54.1 %collective-permute-start.26 = (bf16[512,1024]{1,0:T(8,128)(2,1)}, bf16[512,1024]{1,0:T(8,128)(2,1)}, u32[]{:S(2)}, u32[]{:S(2)}) collective-permute-start(bf16[512,1024]{1,0:T(8,128)(2,1)} %get-tuple-element.140), channel_id=1, source_target_pairs={{0,1},{1,0},{2,3},{3,2},{4,5},{5,4},{6,7},{7,6},{8,9},{9,8},{10,11... | collective-permute-start | bytes 3145736 | tf_op jit(solution)/shard_map/ppermute | solution.py:48
  317.0 45.6 %collective-permute-start.31 = (f32[1,14688]{1,0:T(1,128)}, f32[1,14688]{1,0:T(1,128)}, u32[]{:S(2)}, u32[]{:S(2)}) collective-permute-start(f32[1,14688]{1,0:T(1,128)} %add.339), channel_id=1, source_target_pairs={{0,8},{2,10},{4,12},{6,14},{8,0},{10,2},{12,4},{14,6},{16,24},{18,... | collective-permute-start | bytes 176264 | tf_op jit(solution)/shard_map/ppermute | solution.py:48
  324.6 37.0 %collective-permute-start.36 = (f32[32,384]{1,0:T(8,128)}, f32[32,384]{1,0:T(8,128)S(1)}, u32[]{:S(2)}, u32[]{:S(2)}) collective-permute-start(f32[32,384]{1,0:T(8,128)} %get-tuple-element.204), channel_id=1, source_target_pairs={{0,1},{1,0},{2,3},{3,2},{4,5},{5,4},{6,7},{7,6},{8,9},{9,8},{10,11... | collective-permute-start | bytes 147464 | tf_op jit(solution)/shard_map/ppermute | solution.py:48
  363.5 5.3 %collective-permute-start.32 = (f32[1,14688]{1,0:T(1,128)S(1)}, f32[1,14688]{1,0:T(1,128)S(1)}, u32[]{:S(2)}, u32[]{:S(2)}) collective-permute-start(f32[1,14688]{1,0:T(1,128)S(1)} %add.340), channel_id=1, source_target_pairs={{0,16},{2,18},{4,20},{6,22},{8,24},{10,26},{12,28},{14,30},{16,0},... | collective-permute-start | bytes 176264 | tf_op jit(solution)/shard_map/ppermute | solution.py:48
  (52 other events, 565.2 us)

commit v4 on v3

--- a/solution.py
+++ b/solution.py
@@ -48,8 +48,8 @@
     return lax.ppermute(value, axis, [(i, i ^ distance) for i in range(size)])
 
 
-def after(value, *others):
-    return lax.optimization_barrier((value,) + others)[0]
+def tie(*values):
+    return lax.optimization_barrier(values)
 
 
 def axis_parts(dp):
@@ -66,11 +66,8 @@
     return jnp.concatenate(pieces, axis=0)
 
 
-def gather_plane(line, dp, *first):
-    lines = [line]
-    for step in range(1, axis_parts(dp)[1]):
-        lines.append(after(swap(line, "dp", dp, step * CORES), *first))
-    return jnp.concatenate(lines, axis=0)
+def plane_parts(line, dp):
+    return [swap(line, "dp", dp, step * CORES) for step in range(1, axis_parts(dp)[1])]
 
 
 def start_sum(keep, send, dp):
@@ -82,29 +79,30 @@
     return line, rest
 
 
-def middle_sum(line, rest, dp):
-    for step, part in enumerate(rest):
-        line = line + swap(part, "dp", dp, (step + 1) * CORES).astype(f32)
+def middle_swaps(rest, dp):
+    return [swap(part, "dp", dp, (step + 1) * CORES) for step, part in enumerate(rest)]
+
+
+def middle_sum(line, received):
+    for part in received:
+        line = line + part.astype(f32)
     return line[0], [part.astype(bf16) for part in line[1:]]
 
 
-def high_sum(block, rest, dp):
+def high_swaps(rest, dp):
     middle = axis_parts(dp)[1]
-    for step, part in enumerate(rest):
-        block = block + swap(part, "dp", dp, (step + 1) * middle * CORES).astype(f32)
+    return [swap(part, "dp", dp, (step + 1) * middle * CORES) for step, part in enumerate(rest)]
+
+
+def high_sum(block, received):
+    for part in received:
+        block = block + part.astype(f32)
     return block
 
 
-def sum_everywhere(value, dp, nt):
-    distance = 1
-    while distance < nt:
-        value = value + swap(value, "tensor", nt, distance)
-        distance *= 2
-    distance = 1
-    while distance < dp:
-        value = value + swap(value, "dp", dp, distance)
-        distance *= 2
-    return value
+def sum_stages(dp, nt):
+    stages = [("tensor", nt, 1 << bit) for bit in range((nt - 1).bit_length())]
+    return stages + [("dp", dp, 1 << bit) for bit in range((dp - 1).bit_length())]
 
 
 def relative_places(dp):
@@ -114,8 +112,8 @@
     ]
 
 
-def call(kernel, grid, in_specs, out_specs, out_shape, scratch, flops, scalars=0, aliases=None):
-    params = pltpu.CompilerParams(vmem_limit_bytes=50 * 1024 * 1024)
+def call(kernel, grid, in_specs, out_specs, out_shape, scratch, flops, mib, scalars=0, aliases=None):
+    params = pltpu.CompilerParams(vmem_limit_bytes=mib * 1024 * 1024)
     moved = sum(2 * s.dtype.itemsize * s.size for s in jax.tree.leaves(out_shape))
     return pl.pallas_call(
         kernel,
@@ -134,6 +132,10 @@
 
 
 def whole(shape):
+    return pl.BlockSpec(shape, lambda *i: (0,) * len(shape), pipeline_mode=pl.Buffered(1))
+
+
+def result(shape):
     return pl.BlockSpec(shape, lambda *i: (0,) * len(shape))
 
 
@@ -187,27 +189,37 @@
     )
 
 
-def assemble_kernel(dp, me, near, far, *outs):
+def assemble_kernel(dp, parts, me, *refs):
     half = dp // CORES
+    sources, outs = refs[: 2 * parts], refs[2 * parts :]
     for place, distance in enumerate(relative_places(dp)):
-        source, at = (near, place) if place < half else (far, place - half)
-        start = 0
-        for out in outs:
-            out[me[0] ^ distance] = source[at, start : start + out.shape[1], :]
-            start += out.shape[1]
-
-
-def assemble(near, far, dp, dp_rank, counts):
-    width = near.shape[2]
+        base = 0
+        for part in range(parts):
+            source, at = (sources[part], place) if place < half else (sources[parts + part], place - half)
+            end = base + source.shape[1]
+            start = 0
+            for out in outs:
+                low, high = max(base, start), min(end, start + out.shape[1])
+                if low < high:
+                    out[me[0] ^ distance, low - start : high - start, :] = source[
+                        at, low - base : high - base, :
+                    ]
+                start += out.shape[1]
+            base = end
+
+
+def assemble(nears, fars, dp, dp_rank, counts):
+    width, dtype = nears[0].shape[2], nears[0].dtype
     vmem = pl.BlockSpec(memory_space=pltpu.VMEM)
+    moved = sum(4 * near.size * near.dtype.itemsize for near in nears)
     return pl.pallas_call(
-        functools.partial(assemble_kernel, dp),
-        in_specs=[pl.BlockSpec(memory_space=pltpu.SMEM), vmem, vmem],
+        functools.partial(assemble_kernel, dp, len(nears)),
+        in_specs=[pl.BlockSpec(memory_space=pltpu.SMEM)] + [vmem] * (2 * len(nears)),
         out_specs=[vmem] * len(counts),
-        out_shape=[shape(dp, count, width, dtype=near.dtype) for count in counts],
-        compiler_params=pltpu.CompilerParams(vmem_limit_bytes=24 * 1024 * 1024),
-        cost_estimate=pl.CostEstimate(flops=0, bytes_accessed=4 * near.size * 2, transcendentals=0),
-    )(dp_rank, near, far)
+        out_shape=[shape(dp, count, width, dtype=dtype) for count in counts],
+        compiler_params=pltpu.CompilerParams(vmem_limit_bytes=16 * 1024 * 1024),
+        cost_estimate=pl.CostEstimate(flops=0, bytes_accessed=moved, transcendentals=0),
+    )(dp_rank, *nears, *fars)
 
 
 def pick_half(rank, first, second):
@@ -307,18 +319,21 @@
     gated = ssd[...] * (gate * jax.nn.sigmoid(gate))
     squares = jnp.sum(gated * gated, axis=1, keepdims=True)
     crossed = jnp.sum(scaled_grad * gain[...] * gated, axis=1, keepdims=True)
-    lane = lax.broadcasted_iota(jnp.int32, sums_o.shape, 1)
-    sums_o[...] = jnp.where(lane == 0, squares, jnp.where(lane == 1, crossed, 0.0))
+    lane = lax.broadcasted_iota(jnp.int32, (squares.shape[0], LANES), 1)
+    table = jnp.where(lane == 0, squares, jnp.where(lane == 1, crossed, 0.0))
+    sums_o[...] = table.T[:8, :]
 
 
 def norm_kernel(
-    rank, gate_r, sg_r, ssd_r, sums, out_t, gain, branch_o, scaled_o, dssd_o, dgate_o, gain_o
+    rank, gate_r, sg_r, ssd_r, sums_r, out_t, gain, branch_o, scaled_o, dssd_o, dgate_o, gain_o
 ):
     @pl.when(pl.program_id(0) == 0)
     def _():
         gain_o[...] = jnp.zeros(gain_o.shape, f32)
 
     gate, ssd, scaled_grad = gate_r[...], ssd_r[...], sg_r[...]
+    table = jnp.concatenate([sums_r[...], jnp.zeros((LANES - 8, sums_r.shape[1]), f32)], axis=0)
+    sums = table.T
     scale = lax.rsqrt(sums[:, 0:1] / DI + norm_epsilon)
     sig = jax.nn.sigmoid(gate)
     silu = gate * sig
@@ -336,8 +351,8 @@
     dssd, mix, pre, ch, ssd, hin, step, conv, skip, hp, aux, segr, heads_of,
     state_in, win_in, carry_in, *rest,
 ):
-    dval_o, dcommon_o, dconv_o, dheads_o, dskip_o, dstate, dtail, carry = rest[-14:-6]
-    dmix, dwin, both, flows, entries, weighted = rest[-6:]
+    dval_o, dcommon_o, dconv_o, dheads_o, dstate, dtail, carry = rest[-14:-7]
+    dmix, dwin, both, flows, entries, weighted, dskip = rest[-7:]
     width = dssd.shape[1]
     channels = width + 2 * N
 
@@ -348,7 +363,7 @@
         carry[...] = carry_in[...]
         dconv_o[...] = jnp.zeros(dconv_o.shape, f32)
         dheads_o[...] = jnp.zeros(dheads_o.shape, f32)
-        dskip_o[...] = jnp.zeros(dskip_o.shape, f32)
+        dskip[...] = jnp.zeros(dskip.shape, f32)
 
     row, col = iota(0), iota(1)
     left = col < 64
@@ -390,7 +405,7 @@
         dmix[:, lanes] = dt_pair * flow + skip[:, lanes] * dy
         both[0:CHUNK, lanes] = flow * x_pair
         both[CHUNK : 2 * CHUNK, lanes] = dy * (ssd[:, lanes] - skip[:, lanes] * x_pair) - flow * stepped
-        dskip_o[:, lanes] += jnp.sum(dy * x_pair, axis=0, keepdims=True)
+        dskip[0:1, lanes] += jnp.sum(dy * x_pair, axis=0, keepdims=True)
         high, low = split(pair_spread(entry, pair, left) * dy)
         entries[0, :, lanes] = high
         entries[1, :, lanes] = low
@@ -433,6 +448,10 @@
     dwin[CHUNK:, :] = dwin[0:8, :]
     dtail[...] = dwin[0:8, :]
 
+    @pl.when(pl.program_id(0) == pl.num_programs(0) - 1)
+    def _():
+        dheads_o[2:3, :] = mm_left(dskip[...], heads_of[...])[0:1, :]
+
 
 def scatter_blocks(dp, me, full, keep_o, send_o, cols):
     half = dp // CORES
@@ -455,19 +474,20 @@
     scatter_blocks(dp, me, full, keep_o, send_o, slice(None))
 
 
-def weight_grad(lhs, rhs, dp, dp_rank):
-    length, width = rhs.shape
+def weight_grad(lhs, rhs, dp, dp_rank, skipped=0):
+    length, width = rhs.shape[0], rhs.shape[1] - 256 * skipped
     depth = lhs.shape[1]
     block, half = depth // dp, dp // CORES
     piece = pl.BlockSpec((half, block, 256), lambda i, *s: (0, 0, i))
     return call(
         functools.partial(weight_grad_kernel, dp),
         (width // 256,),
-        [whole((length, depth)), pl.BlockSpec((length, 256), lambda i, *s: (0, i))],
+        [whole((length, depth)), pl.BlockSpec((length, 256), lambda i, *s: (0, i + skipped))],
         [piece, piece],
         [shape(half, block, width, dtype=bf16)] * 2,
         [pltpu.VMEM((depth, length), bf16), pltpu.VMEM((depth, 256), f32)],
         2 * length * width * depth,
+        16,
         scalars=1,
     )(dp_rank, lhs, rhs)
 
@@ -494,7 +514,7 @@
 
 
 def value_grad(lhs, dval, dcommon, dp, dp_rank):
-    length, width = dval.shape
+    length, width = dval.shape[0], 256
     depth, extra = lhs.shape[1], dcommon.shape[1]
     block, half, per = depth // dp, dp // CORES, width // 256
     dims = (half, block, width + extra)
@@ -506,13 +526,14 @@
             pl.BlockSpec((length, 256), lambda i, *s: (0, jnp.minimum(i, per - 1))),
             whole((length, extra)),
         ],
-        [whole(dims), whole(dims)],
+        [result(dims), result(dims)],
         [shape(*dims, dtype=bf16)] * 2,
         [
             pltpu.VMEM((depth, length), bf16), pltpu.VMEM((depth, 256), f32),
             pltpu.VMEM((depth, extra), f32),
         ],
         2 * length * (width + 2 * extra) * depth,
+        24,
         scalars=1,
     )(dp_rank, lhs, dval, dcommon)
 
@@ -583,21 +604,33 @@
         small_rows += 1
     small = jnp.pad(small, (0, small_rows * width - small.size)).reshape(small_rows, width)
     small_pair = over_tensor(small)
-    token_pieces = pieces_of(after(residual, small_pair))
+    residual_now, small_pair = tie(residual, small_pair)
+    token_pieces = pieces_of(residual_now)
 
     block_rows = D // dp
     value_shard = jnp.concatenate([inner_proj[1].astype(bf16), small_pair], axis=0)
-    value_line = gather_line(value_shard, dp)
-    near = gather_plane(value_line, dp)
-    value_w, small_all = assemble(
-        near, swap(near, "dp", dp, 1), dp, dp_me, [block_rows, small_rows * nt]
-    )
-    value_w = value_w.reshape(D, width)
+    cut = -(-value_shard.shape[0] // 32) * 16
+    first_line = gather_line(value_shard[:cut], dp)
+    second_shard, first_line = tie(value_shard[cut:], first_line)
+    second_line = gather_line(second_shard, dp)
+    second_line, ids = tie(second_line, sequence_ids)
+    first_near = jnp.concatenate([first_line] + plane_parts(first_line, dp), axis=0)
     other_shard = jnp.concatenate(
         [inner_proj[0].astype(bf16), outer_proj.T.astype(bf16)], axis=0
     )
-    other_line = gather_line(after(other_shard, value_line), dp)
-    cot_pieces = pieces_of(after(cotangent, small_pair))
+    other_shard, second_line = tie(other_shard, second_line)
+    other_line = gather_line(other_shard, dp)
+    second_line, *parts = tie(second_line, *plane_parts(second_line, dp), *token_pieces)
+    parts, token_pieces = parts[:-nt], parts[-nt:]
+    second_near = jnp.concatenate([second_line] + parts, axis=0)
+    cotangent_now, *token_pieces = tie(cotangent, *token_pieces)
+    cot_pieces = pieces_of(cotangent_now)
+    value_w, small_all = assemble(
+        [first_near, second_near],
+        [swap(first_near, "dp", dp, 1), swap(second_near, "dp", dp, 1)],
+        dp, dp_me, [block_rows, small_rows * nt],
+    )
+    value_w = value_w.reshape(D, width)
 
     def halves(pieces):
         if nt == 2:
@@ -640,7 +673,6 @@
         jnp.arange(width)[:, None] // head_size == jnp.arange(LANES)[None, :]
     ).astype(bf16)
 
-    ids = sequence_ids
     blocked = ids.reshape(chunks, CHUNK)
     ends, firsts = blocked[:, -1], blocked[:, 0]
     none = jnp.full((1,), -1, jnp.int32)
@@ -663,7 +695,8 @@
 
     steps = length // wide
     in_half = lambda i: i % (steps // 2)
-    value_w = after(value_w, other_line, *cot_pieces[1:])
+    value_w, other_line, *cot_pieces = tie(value_w, other_line, *cot_pieces)
+    plane = plane_parts(other_line, dp)
     normed, chans, pre, mixed, ssd, entering, step_in = call(
         scan_kernel,
         (steps,),
@@ -687,12 +720,14 @@
             pltpu.VMEM((CHUNK, width), f32), pltpu.VMEM((2, CHUNK, width), bf16),
         ],
         length * (2 * D * (width + common_width) + 12 * width * CHUNK),
+        30,
         scalars=1,
     )(*halves(token_pieces), pre_gain, value_w, shared_here, conv_here, skip, head_rows, aux, segr)
 
-    plane = gather_plane(other_line, dp, normed)
+    normed, *plane = tie(normed, *plane)
+    plane = jnp.concatenate([other_line] + plane, axis=0)
     gate_w, outer_t = assemble(
-        plane, swap(plane, "dp", dp, 1), dp, dp_me, [block_rows, block_rows]
+        [plane], [swap(plane, "dp", dp, 1)], dp, dp_me, [block_rows, block_rows]
     )
     gate_w, outer_t = gate_w.reshape(D, width), outer_t.reshape(D, width)
     cot_rank, cot0, cot1 = halves(cot_pieces)
@@ -703,21 +738,20 @@
             rows(wide, D), rows(wide, D, in_half), rows(wide, D, in_half), rows(wide, aux_cols),
             rows(wide, width), whole((D, width)), whole((D, width)), whole((1, width)),
         ],
-        [rows(wide, width), rows(wide, width), rows(wide, D), rows(wide, LANES)],
+        [rows(wide, width), rows(wide, width), rows(wide, D), pl.BlockSpec((8, wide), lambda i, r: (0, i))],
         [
             shape(length, width), shape(length, width), shape(length, D, dtype=bf16),
-            shape(length, LANES),
+            shape(8, length),
         ],
         [],
         4 * length * D * width,
+        24,
         scalars=1,
     )(cot_rank, normed, cot0, cot1, aux, ssd, gate_w, outer_t, post_gain)
-    sums = sums[:, :2].T
     distance = 1
     while distance < nt:
         sums = sums + swap(sums, "tensor", nt, distance)
         distance *= 2
-    sums = sums.T
 
     def relative(block, rank):
         return (rank ^ (block // per_piece)) * per_piece + block % per_piece
@@ -730,31 +764,31 @@
         norm_kernel,
         (length // band,),
         [
-            rel_rows(width), rel_rows(width), rel_rows(width), rel_rows(2),
+            rel_rows(width), rel_rows(width), rel_rows(width),
+            pl.BlockSpec((8, band), lambda i, r: (0, relative(i, r[0]))),
             whole((D, width)), whole((1, width)),
         ],
-        [plain(D), rel_rows(width), rel_rows(width), rel_rows(width), whole((1, width))],
+        [plain(D), rel_rows(width), rel_rows(width), rel_rows(width), result((1, width))],
         [
             shape(length, D, dtype=bf16), shape(length, width, dtype=bf16),
             shape(length, width, dtype=bf16), shape(length, width, dtype=bf16), shape(1, width),
         ],
         [],
         2 * length * D * width,
+        24,
         scalars=1,
     )(t_me, gate, scaled_grad, ssd, sums, outer_t, post_gain)
     outer_keep, outer_send = weight_grad(returned, scaled, dp, dp_me)
-    gate_keep, gate_send = weight_grad(normed, after(dgate, outer_send), dp, dp_me)
+    dgate, outer_send = tie(dgate, outer_send)
+    gate_keep, gate_send = weight_grad(normed, dgate, dp, dp_me)
     outer_line, outer_rest = start_sum(outer_keep, outer_send, dp)
     gate_line, gate_rest = start_sum(gate_keep, gate_send, dp)
-    dssd = after(dssd, *outer_rest, *gate_rest)
-
     branch = branch.reshape(nt, rows_here, D)
-    branch_sum = branch[0].astype(f32)
-    for d in range(1, nt):
-        branch_sum = branch_sum + swap(branch[d], "tensor", nt, d).astype(f32)
-    live_here = lax.dynamic_slice_in_dim(aux[:, LIVE], t_rank * rows_here, rows_here)
-    tokens = residual.astype(f32)
-    block_out = (tokens + branch_sum * live_here[:, None]).astype(bf16)
+    branch_received = [swap(branch[d], "tensor", nt, d) for d in range(1, nt)]
+    dssd, *rests = tie(dssd, *outer_rest, *gate_rest)
+    outer_rest, gate_rest = rests[: len(outer_rest)], rests[len(outer_rest) :]
+    outer_received = middle_swaps(outer_rest, dp)
+    gate_received = middle_swaps(gate_rest, dp)
 
     state = jnp.zeros((N, width), f32)
     win = jnp.zeros((8, channels), f32)
@@ -780,21 +814,23 @@
             ]
             + [pl.BlockSpec(memory_space=pl.ANY)] * len(filled),
             [
-                rows(CHUNK, width, back), rows(CHUNK, common_width, back), whole((8, channels)),
-                whole((8, LANES)), whole((1, width)),
-                whole((N, width)), whole((8, channels)), whole((8, LANES)),
+                rows(CHUNK, width, back), rows(CHUNK, common_width, back), result((8, channels)),
+                result((8, LANES)),
+                result((N, width)), result((8, channels)), result((8, LANES)),
             ],
             [
                 shape(length, width, dtype=bf16), shape(length, common_width),
-                shape(8, channels), shape(8, LANES), shape(1, width),
+                shape(8, channels), shape(8, LANES),
                 shape(N, width), shape(8, channels), shape(8, LANES),
             ],
             [
                 pltpu.VMEM((CHUNK, channels), f32), pltpu.VMEM((CHUNK + 8, channels), f32),
                 pltpu.VMEM((2 * CHUNK, width), f32), pltpu.VMEM((CHUNK, width), f32),
                 pltpu.VMEM((2, CHUNK, width), bf16), pltpu.VMEM((CHUNK, width), bf16),
+                pltpu.VMEM((8, width), f32),
             ],
             count * CHUNK * 30 * width * CHUNK,
+            24,
             aliases={16: 0, 17: 1} if filled else None,
         )(
             dssd, mixed, pre, chans, ssd, entering, step_in, conv_here, skip, head_rows, aux, segr,
@@ -803,15 +839,24 @@
         filled = results[:2]
         back_parts.append(results[2:])
         if part == 0:
-            outer_block, outer_far = middle_sum(after(outer_line, state), outer_rest, dp)
-            state = after(state, *outer_far)
+            state, outer_line, *outer_received = tie(state, outer_line, *outer_received)
+            outer_block, outer_far = middle_sum(outer_line, outer_received)
+            outer_far = high_swaps(outer_far, dp)
         if part == 1:
-            gate_block, gate_far = middle_sum(after(gate_line, state), gate_rest, dp)
-            state = after(state, *gate_far)
+            state, gate_line, *rests = tie(state, gate_line, *gate_received, *branch_received)
+            gate_received, branch_received = rests[: len(gate_received)], rests[len(gate_received) :]
+            gate_block, gate_far = middle_sum(gate_line, gate_received)
+            gate_far = high_swaps(gate_far, dp)
     dval, dcommon = filled
-    dconv, dheads, dskip = [sum(parts) for parts in zip(*back_parts)]
-    outer_part = high_sum(outer_block, outer_far, dp)
-    gate_part = high_sum(gate_block, gate_far, dp)
+    dval, *outer_far = tie(dval, *outer_far)
+    outer_part = high_sum(outer_block, outer_far)
+
+    branch_sum = branch[0].astype(f32)
+    for piece in branch_received:
+        branch_sum = branch_sum + piece.astype(f32)
+    live_here = lax.dynamic_slice_in_dim(aux[:, LIVE], t_rank * rows_here, rows_here)
+    tokens = residual.astype(f32)
+    block_out = (tokens + branch_sum * live_here[:, None]).astype(bf16)
 
     def input_grad(count, offset, dtype, positions, dgate):
         return call(
@@ -821,28 +866,51 @@
                 rel_rows(width, offset), rel_rows(width, offset), rel_rows(common_width, offset),
                 plain(D), whole((D, width)), whole((D, width)), whole((D, common_width)),
             ],
-            [plain(D), whole((1, D))],
+            [plain(D), result((1, D))],
             [shape(count * rows_here, D, dtype=dtype), shape(1, D)],
             [],
             4 * count * rows_here * D * (width + common_width),
+            24,
             scalars=1,
         )(t_me, dgate, dval, dcommon, positions, gate_w, value_w, shared_here)
 
-    value_keep, value_send = value_grad(normed, after(dval, outer_part, branch_sum), dcommon, dp, dp_me)
-    value_line, value_rest = start_sum(value_keep, value_send, dp)
+    sums_keep = [value_grad(normed, dval, dcommon, dp, dp_me)]
+    if width > 256:
+        dval_now, first_send = tie(dval, sums_keep[0][1])
+        sums_keep[0] = (sums_keep[0][0], first_send)
+        sums_keep.append(weight_grad(normed, dval_now, dp, dp_me, skipped=1))
+    lines, parts = [], []
+    for keep, send in sums_keep:
+        line, part = start_sum(keep, send, dp)
+        lines.append(line)
+        parts.append(part)
+    steps_each = len(parts[0])
+    dgate, *flat = tie(dgate, *[item for part in parts for item in part])
+    parts = [flat[at : at + steps_each] for at in range(0, len(flat), steps_each)]
+    crossing = [middle_swaps(part, dp) for part in parts]
     others = token_pieces[1] if nt == 2 else jnp.concatenate(token_pieces[1:], axis=0)
-    sent, pre_grad_sent = input_grad(
-        nt - 1, per_piece, bf16, others, after(dgate, value_send, gate_part)
-    )
-    sent = sent.reshape(nt - 1, rows_here, D)
-    own, pre_grad_own = input_grad(1, 0, f32, residual, after(dgate, sent, *value_rest))
-    received = [swap(sent[d - 1], "tensor", nt, d) for d in range(1, nt)]
-
-    value_block, value_far = middle_sum(after(value_line, own), value_rest, dp)
-    value_sum = high_sum(value_block, value_far, dp)
-    value_part = value_sum[:, :width]
+    sent, pre_grad_sent = input_grad(nt - 1, per_piece, bf16, others, dgate)
+    sent = sent.reshape(nt - 1, 2, rows_here // 2, D)
+    received = [
+        [swap(sent[d - 1, part], "tensor", nt, d) for d in range(1, nt)] for part in range(2)
+    ]
+    dgate, pre_grad_sent, *rests = tie(dgate, pre_grad_sent, *gate_far, *crossing[0])
+    gate_far, crossing[0] = rests[: len(gate_far)], rests[len(gate_far) :]
+    gate_part = high_sum(gate_block, gate_far)
+    block, far = middle_sum(lines[0], crossing[0])
+    fars = [high_swaps(far, dp)]
+    blocks = [block]
+    own, pre_grad_own = input_grad(1, 0, f32, residual, dgate)
+    if len(parts) > 1:
+        pre_grad_own, *crossing[1] = tie(pre_grad_own, *crossing[1])
+        block, far = middle_sum(lines[1], crossing[1])
+        fars.append(high_swaps(far, dp))
+        blocks.append(block)
+    pre_grad_own, *rests = tie(pre_grad_own, *received[0], *fars[0])
+    received[0], fars[0] = rests[: nt - 1], rests[nt - 1 :]
+    value_sums = [high_sum(blocks[0], fars[0])]
     shared_rows = shared_proj.shape[0]
-    shared_sum = value_sum[:, width:].reshape(nt, shared_rows, common_width)
+    shared_sum = value_sums[0][:, 256:].reshape(nt, shared_rows, common_width)
     shared_mine = lax.dynamic_index_in_dim(shared_sum, t_rank, 0, False)
     shared_common = shared_mine[:, : 2 * N]
     shared_part = jnp.zeros((shared_rows, 2 * N + H), f32)
@@ -860,6 +928,8 @@
         shared_part = place_heads(shared_part, piece, t_rank ^ d)
     shared_part = lax.dynamic_update_slice(shared_part, shared_common, (0, 0))
 
+    pre_grad_own, *summed = tie(pre_grad_own, *[item for part in back_parts for item in part])
+    dconv, dheads = [sum(summed[at::2]) for at in range(2)]
     conv_grad = lax.dynamic_update_slice(
         jnp.pad(dconv[:kernel_rows, width:], ((0, 0), (DI, 0))),
         dconv[:kernel_rows, :width],
@@ -868,13 +938,7 @@
     post_all = lax.dynamic_update_slice(
         jnp.zeros((1, DI), f32), post_grad, (0, t_rank * width)
     )
-    head_grad = jnp.stack(
-        [
-            dheads[0, :heads_here],
-            dheads[1, :heads_here],
-            jnp.sum(dskip.reshape(heads_here, head_size), axis=1),
-        ]
-    )
+    head_grad = dheads[:3, :heads_here]
     head_all = lax.dynamic_update_slice(
         jnp.zeros((3, H), f32), head_grad, (0, t_rank * heads_here)
     )
@@ -884,7 +948,14 @@
         ],
         axis=1,
     )
-    vector = sum_everywhere(after(vector, *value_far), dp, nt)
+    for stage, (axis, size, distance) in enumerate(sum_stages(dp, nt)):
+        vector = vector + swap(vector, axis, size, distance)
+        if stage == 1 and len(parts) > 1:
+            vector, *fars[1] = tie(vector, *fars[1])
+            value_sums.append(high_sum(blocks[1], fars[1]))
+        if stage == 2:
+            vector, *received[1] = tie(vector, *received[1])
+    value_part = jnp.concatenate([value_sums[0][:, :256]] + value_sums[1:], axis=1)
     conv_size = kernel_rows * (DI + 2 * N)
     place = d_rank * nt + t_rank
     conv_part = lax.dynamic_slice_in_dim(
@@ -896,8 +967,8 @@
     )
 
     normed_grad = own
-    for piece in received:
-        normed_grad = normed_grad + after(piece, vector).astype(f32)
+    for low, high in zip(*received):
+        normed_grad = normed_grad + jnp.concatenate([low, high], axis=0).astype(f32)
     inverse = lax.rsqrt(jnp.mean(tokens * tokens, axis=1, keepdims=True) + norm_epsilon)
     normal_tokens = tokens * inverse
     normal_grad = normed_grad * pre_gain

time: 383 us -> 275 us (0.72)
  waiting for transfers between devices: 133 us -> 39.6 us
  Pallas kernels: 123 us -> 94.3 us
  starting transfers between devices: 41.7 us -> 56 us
  local copies, waits for them, and re-layouts: 39.6 us -> 44.5 us
  other arithmetic: 39.3 us -> 34.6 us
    ppermute x37 -> x48, waiting for transfers between devices: 133 us -> 39.6 us  [swap(): return lax.ppermute(value, axis, [(i, i ^ distance) for i in range(size)])]
    unnamed x103 -> x129, local copies, waits for them, and re-layouts: 13.1 us -> 27.8 us
    ppermute x37 -> x48, starting transfers between devices: 41.7 us -> 56 us  [swap(): return lax.ppermute(value, axis, [(i, i ^ distance) for i in range(size)])]
    pallas_call x2, Pallas kernels: 15 us -> 7.42 us  [input_grad(): call(input_grad_kernel, (count * per_piece,), [rel_rows(width, offset), r...]
    pallas_call x1, Pallas kernels: 9.9 us -> 4 us  [value_grad(): call(functools.partial(value_grad_kernel, dp), (per + 1,), [whole((length...]
    pallas_call x3, Pallas kernels: 36.3 us -> 31.6 us  [shards(): call(scan_back_kernel, (count,), [rows(CHUNK, width, back), rows(CHUNK, c...]
    pallas_call x2 -> x3, Pallas kernels: 13.6 us -> 12.4 us  [weight_grad(): call(functools.partial(weight_grad_kernel, dp), (width // 256,), [whole((...]
  transfers between devices with their start and end apart: 37 -> 48, of which waited for: 15 -> 17; matrix products, arithmetic and copies ran while one was open for 15% -> 18% of each run, Pallas kernels for 25% -> 23%
where the time goes in v4:
time: 275 us; the launch traced here: 271 us
  Pallas kernels  94.3 us (34%)
  starting transfers between devices  56 us (20%)
  local copies, waits for them, and re-layouts  44.5 us (16%)
  waiting for transfers between devices  39.6 us (14%)
  other arithmetic  34.6 us (13%)
    ppermute x48, starting transfers between devices, swap(): return lax.ppermute(value, axis, [(i, i ^ distance) for i in range(size)])  56 us
    ppermute x48, waiting for transfers between devices, swap(): return lax.ppermute(value, axis, [(i, i ^ distance) for i in range(size)])  39.6 us
    pallas_call x3, Pallas kernels, shards(): call(scan_back_kernel, (count,), [rows(CHUNK, width, back), rows(CHUNK, c...  31.6 us
    unnamed x129, local copies, waits for them, and re-layouts  27.8 us
    pallas_call x1, Pallas kernels, shards(): call(scan_kernel, (steps,), [rows(wide, D, in_half), rows(wide, D, in_hal...  23 us
    pallas_call x3, Pallas kernels, weight_grad(): call(functools.partial(weight_grad_kernel, dp), (width // 256,), [whole((...  12.4 us
    pallas_call x1, Pallas kernels, shards(): call(gate_kernel, (steps,), [rows(wide, D), rows(wide, D, in_half), rows(...  7.66 us
    pallas_call x2, Pallas kernels, input_grad(): call(input_grad_kernel, (count * per_piece,), [rel_rows(width, offset), r...  7.42 us
  transfers between devices with their start and end apart: 48, of which 17 were waited for; matrix products, arithmetic and copies ran while one was open for 18% of the time, Pallas kernels for 23%

profile of v4, /device:TPU:0, one launch (start us, length us, event | category | flops | bytes accessed | tf_op | source)
XLA Modules:
  0.0 271.2 jit_solution(14683888042914280260)
XLA Ops:
  1.9 3.1 %collective-permute-start.1 = (bf16[48,1024]{1,0:T(8,128)(2,1)S(1)}, bf16[48,1024]{1,0:T(8,128)(2,1)S(1)}, u32[]{:S(2)}, u32[]{:S(2)}) collective-permute-start(bf16[48,1024]{1,0:T(8,128)(2,1)S(1)} %get-tuple-element.305), channel_id=1, source_target_pairs={{0,8},{2,10},{4,12},{6,14},{8,0},{10,2},{12,4},{14,6},{16,24},{18,... | collective-permute-start | bytes 294920 | tf_op jit(solution)/shard_map/ppermute | solution.py:48
  5.0 2.6 collective-permute-start.2
  23.3 3.0 %collective-permute-done.5 = bf16[48,1024]{1,0:T(8,128)(2,1)S(1)} collective-permute-done((bf16[48,1024]{1,0:T(8,128)(2,1)S(1)}, bf16[48,1024]{1,0:T(8,128)(2,1)S(1)}, u32[]{:S(2)}, u32[]{:S(2)}) %collective-permute-start.5) | collective-permute-done | bytes 98336 | tf_op jit(solution)/shard_map/ppermute | solution.py:48
  33.7 5.0 %collective-permute-done.7 = bf16[4,48,1024]{2,1,0:T(8,128)(2,1)S(1)} collective-permute-done((bf16[4,48,1024]{2,1,0:T(8,128)(2,1)S(1)}, bf16[4,48,1024]{2,1,0:T(8,128)(2,1)S(1)}, u32[]{:S(2)}, u32[]{:S(2)}) %collective-permute-start.7) | collective-permute-done | bytes 393248 | tf_op jit(solution)/shard_map/ppermute | solution.py:48
  43.0 6.7 %collective-permute-done.13 = bf16[128,1024]{1,0:T(8,128)(2,1)} collective-permute-done((bf16[128,1024]{1,0:T(8,128)(2,1)}, bf16[128,1024]{1,0:T(8,128)(2,1)}, u32[]{:S(2)}, u32[]{:S(2)}) %collective-permute-start.13) | collective-permute-done | bytes 262176 | tf_op jit(solution)/shard_map/ppermute | solution.py:48
  49.7 2.3 pad_maximum_fusion
  60.0 7.0 %collective-permute-done.15.cot1 = bf16[512,1024]{1,0:T(8,128)(2,1)} collective-permute-done((bf16[512,1024]{1,0:T(8,128)(2,1)}, bf16[512,1024]{1,0:T(8,128)(2,1)}, u32[]{:S(2)}, u32[]{:S(2)}) %collective-permute-start.15) | collective-permute-done | bytes 1048608 | tf_op jit(solution)/shard_map/ppermute | solution.py:48
  71.4 23.0 %shard_map.357 = (bf16[1024,1024]{1,0:T(8,128)(2,1)S(1)}, f32[1024,1280]{1,0:T(8,128)S(1)}, f32[1024,1280]{1,0:T(8,128)}, bf16[1024,1280]{1,0:T(8,128)(2,1)S(1)}...) custom-call(s32[1]{0:T(128)} %bitcast.rank, bf16[512,1024]{1,0:T(8,128)(2,1)S(1)} %copy-done.10, ...), custom_call_target="tpu_custom_call" | custom-call | flops 4563402752 | bytes 48234496 | tf_op jit(solution)/shard_map/pallas_call | solution.py:700
  94.4 2.3 copy-done.2
  98.8 4.1 %collective-permute-done.17.refs_1_ = bf16[8,128,1024]{2,1,0:T(8,128)(2,1)S(1)} collective-permute-done((bf16[8,128,1024]{2,1,0:T(8,128)(2,1)S(1)}, bf16[8,128,1024]{2,1,0:T(8,128)(2,1)S(1)}, u32[]{:S(2)}, u32[]{:S(2)}) %collective-permute-start.17) | collective-permute-done | bytes 2097184 | tf_op jit(solution)/shard_map/ppermute | solution.py:48
  103.3 7.7 %shard_map.359 = (f32[1024,1024]{1,0:T(8,128)S(1)}, f32[1024,1024]{1,0:T(8,128)S(1)}, bf16[1024,1024]{1,0:T(8,128)(2,1)S(1)}, f32[8,1024]{1,0:T(8,128)S(1)}) custom-call(s32[1]{0:T(128)} %bitcast.rank, bf16[1024,1024]{1,0:T(8,128)(2,1)S(1)} %get-tuple-element.158.normed.lhs, bf16[512,1024]{1,0:T(8,128)(2,1)S(1)} %copy-done.27, ...), custom_call_target="tpu_custom_call" | custom-call | flops 4294967296 | bytes 21037056 | tf_op jit(solution)/shard_map/pallas_call | solution.py:734
  114.3 2.5 collective-permute-done.18
  116.9 2.2 copy-done.24
  119.0 6.6 %shard_map.360 = (bf16[1024,1024]{1,0:T(8,128)(2,1)S(1)}, bf16[1024,1024]{1,0:T(8,128)(2,1)S(1)}, bf16[1024,1024]{1,0:T(8,128)(2,1)S(1)}, bf16[1024,1024]{1,0:T(8,128)(2,1)S(1)}, f32[1,1024]{1,0:T(1,128)S(1)}) custom-call(s32[1]{0:T(128)} %bitcast.rank, f32[1024,1024]{1,0:T(8,128)S(1)} %get-tuple-element.165.gate_r, f32[1024,1024]{1,0:T(8,128)S(1)} %copy-done.24, ...), custom_call_target="tpu_custom_call" | custom-call | flops 2147483648 | bytes 16785408 | tf_op jit(solution)/shard_map/pallas_call | solution.py:763
  125.7 4.5 %shard_map.361 = (bf16[8,64,1024]{2,1,0:T(8,128)(2,1)S(1)}, bf16[8,64,1024]{2,1,0:T(8,128)(2,1)S(1)}) custom-call(s32[1]{0:T(128)} %bitcast.12.me, bf16[1024,1024]{1,0:T(8,128)(2,1)S(1)} %get-tuple-element.170.lhs, bf16[1024,1024]{1,0:T(8,128)(2,1)S(1)} %get-tuple-element.171.rhs), custom_call_target="tpu_custom_call" | custom-call | flops 2147483648 | bytes 4194304 | tf_op jit(solution)/shard_map/pallas_call | solution.py:482
  130.2 4.3 %shard_map.362 = (bf16[8,64,1024]{2,1,0:T(8,128)(2,1)S(1)}, bf16[8,64,1024]{2,1,0:T(8,128)(2,1)S(1)}) custom-call(s32[1]{0:T(128)} %bitcast.12.me, bf16[1024,1024]{1,0:T(8,128)(2,1)S(1)} %get-tuple-element.158.normed.lhs, bf16[1024,1024]{1,0:T(8,128)(2,1)S(1)} %get-tuple-element.216.rhs.dgate), custom_call_target="tpu_custom_call" | custom-call | flops 2147483648 | bytes 4194304 | tf_op jit(solution)/shard_map/pallas_call | solution.py:482
  148.7 2.5 copy-done.3
  151.2 2.5 copy-done.4
  153.7 2.2 copy-done.6
  158.5 11.4 %shard_map.363 = (bf16[1024,1024]{1,0:T(8,128)(2,1)S(1)}, f32[1024,384]{1,0:T(8,128)S(1)}, f32[8,1280]{1,0:T(8,128)S(1)}, f32[8,128]{1,0:T(8,128)S(1)}, f32[128,...) custom-call(bf16[1024,1024]{1,0:T(8,128)(2,1)S(1)} %copy-done.8, ...), custom_call_target="tpu_custom_call" | custom-call | flops 1509949440 | bytes 8568832 | tf_op jit(solution)/shard_map/pallas_call | solution.py:802
  173.0 2.4 collective-permute-start.25
  175.7 11.6 %shard_map.364 = (bf16[1024,1024]{1,0:T(8,128)(2,1)S(1)}, f32[1024,384]{1,0:T(8,128)S(1)}, f32[8,1280]{1,0:T(8,128)S(1)}, f32[8,128]{1,0:T(8,128)S(1)}, f32[128,...) custom-call(bf16[1024,1024]{1,0:T(8,128)(2,1)S(1)} %copy-done.8, ...), custom_call_target="tpu_custom_call", output_to_operand_aliasing={{0}: (16, {}), {1}: (17, {})} | custom-call | flops 1509949440 | bytes 8568832 | tf_op jit(solution)/shard_map/pallas_call | solution.py:802
  187.4 8.5 %shard_map.365 = (bf16[1024,1024]{1,0:T(8,128)(2,1)S(1)}, f32[1024,384]{1,0:T(8,128)S(1)}, f32[8,1280]{1,0:T(8,128)S(1)}, f32[8,128]{1,0:T(8,128)S(1)}, f32[128,...) custom-call(bf16[1024,1024]{1,0:T(8,128)(2,1)S(1)} %copy-done.8, ...), custom_call_target="tpu_custom_call", output_to_operand_aliasing={{0}: (16, {}), {1}: (17, {})} | custom-call | flops 1006632960 | bytes 8568832 | tf_op jit(solution)/shard_map/pallas_call | solution.py:802
  195.9 4.0 %shard_map.366 = (bf16[8,64,640]{2,1,0:T(8,128)(2,1)S(1)}, bf16[8,64,640]{2,1,0:T(8,128)(2,1)S(1)}) custom-call(s32[1]{0:T(128)} %bitcast.12.me, bf16[1024,1024]{1,0:T(8,128)(2,1)S(1)} %copy-done.34, bf16[1024,1024]{1,0:T(8,128)(2,1)S(1)} %get-tuple-element.208.dval.rhs, f32[1024,384]{1,0:T(8,128)S(1)} %get-tuple-element.204.dcommon), custom_call_target="tpu_custom_call" | custom-call | flops 2147483648 | bytes 2621440 | tf_op jit(solution)/shard_map/pallas_call | solution.py:521
  200.0 3.6 %shard_map.367 = (bf16[8,64,768]{2,1,0:T(8,128)(2,1)S(1)}, bf16[8,64,768]{2,1,0:T(8,128)(2,1)S(1)}) custom-call(s32[1]{0:T(128)} %bitcast.12.me, bf16[1024,1024]{1,0:T(8,128)(2,1)S(1)} %copy-done.34, bf16[1024,1024]{1,0:T(8,128)(2,1)S(1)} %get-tuple-element.208.dval.rhs), custom_call_target="tpu_custom_call" | custom-call | flops 1610612736 | bytes 3145728 | tf_op jit(solution)/shard_map/pallas_call | solution.py:482
  205.3 3.3 %collective-permute-start.30 = (bf16[64,1024]{1,0:T(8,128)(2,1)S(1)}, bf16[64,1024]{1,0:T(8,128)(2,1)S(1)}, u32[]{:S(2)}, u32[]{:S(2)}) collective-permute-start(bf16[64,1024]{1,0:T(8,128)(2,1)S(1)} %get-tuple-element.293), channel_id=1, source_target_pairs={{0,16},{2,18},{4,20},{6,22},{8,24},{10,26},{12,28},{14,30},{16,0},... | collective-permute-start | bytes 393224 | tf_op jit(solution)/shard_map/ppermute | solution.py:48
  211.4 3.7 %shard_map.368 = (bf16[512,1024]{1,0:T(8,128)(2,1)S(1)}, f32[1,1024]{1,0:T(1,128)S(1)}) custom-call(s32[1]{0:T(128)} %bitcast.rank, bf16[1024,1024]{1,0:T(8,128)(2,1)S(1)} %copy-done.18, bf16[1024,1024]{1,0:T(8,128)(2,1)S(1)} %get-tuple-element.208.dval.rhs, f32[1024,384]{1,0:T(8,128)S(1)} %get-tuple-element.204.dcommon, bf16[512,1024]{1,0:T(8,128)(2,1)S(1)} %copy-done.31, ...), custom_call_target="tpu_custom_call" | custom-call | flops 2952790016 | bytes 2105344 | tf_op jit(solution)/shard_map/pallas_call | solution.py:862
  222.2 3.8 %collective-permute-start.36 = (bf16[64,640]{1,0:T(8,128)(2,1)S(1)}, bf16[64,640]{1,0:T(8,128)(2,1)S(1)}, u32[]{:S(2)}, u32[]{:S(2)}) collective-permute-start(bf16[64,640]{1,0:T(8,128)(2,1)S(1)} %get-tuple-element.302), channel_id=1, source_target_pairs={{0,16},{2,18},{4,20},{6,22},{8,24},{10,26},{12,28},{14,30},{16,0},... | collective-permute-start | bytes 245768 | tf_op jit(solution)/shard_map/ppermute | solution.py:48
  226.0 3.7 %shard_map.369 = (f32[512,1024]{1,0:T(8,128)S(1)}, f32[1,1024]{1,0:T(1,128)S(1)}) custom-call(s32[1]{0:T(128)} %bitcast.rank, bf16[1024,1024]{1,0:T(8,128)(2,1)S(1)} %copy-done.18, bf16[1024,1024]{1,0:T(8,128)(2,1)S(1)} %get-tuple-element.208.dval.rhs, f32[1024,384]{1,0:T(8,128)S(1)} %get-tuple-element.204.dcommon, bf16[512,1024]{1,0:T(8,128)(2,1)S(1)} %copy-done.11, ...), custom_call_target="tpu_custom_call" | custom-call | flops 2952790016 | bytes 4202496 | tf_op jit(solution)/shard_map/pallas_call | solution.py:862
  232.8 3.2 %collective-permute-start.41 = (bf16[64,768]{1,0:T(8,128)(2,1)}, bf16[64,768]{1,0:T(8,128)(2,1)}, u32[]{:S(2)}, u32[]{:S(2)}) collective-permute-start(bf16[64,768]{1,0:T(8,128)(2,1)} %get-tuple-element.299), channel_id=1, source_target_pairs={{0,16},{2,18},{4,20},{6,22},{8,24},{10,26},{12,28},{14,30},{16,0},... | collective-permute-start | bytes 294920 | tf_op jit(solution)/shard_map/ppermute | solution.py:48
  260.9 2.3 collective-permute-done.46
  264.4 3.7 %fusion.6 = (bf16[512,1024]{1,0:T(8,128)(2,1)}, bf16[512,1024]{1,0:T(8,128)(2,1)}) fusion(bf16[512,1024]{1,0:T(8,128)(2,1)S(1)} %copy-done.11, bf16[512,1024]{1,0:T(8,128)(2,1)S(1)} %copy-done.28, f32[512,1024]{1,0:T(8,128)S(1)} %get-tuple-element.217, f32[512]{0:T(512)S(1)} %broadcast_multiply_fusion, f32[1024]{0:T(1024)S(1)} %get-tuple-element.311, ...), kind=kLoop, calls=%fused_computation.9 | loop fusion | flops 10485760 | bytes 9447424 | tf_op jit(solution)/shard_map/convert_element_type | solution.py:978
  (334 shorter events, 109.7 us)
Async XLA Ops:
  1.9 15.5 %collective-permute-start.1 = (bf16[48,1024]{1,0:T(8,128)(2,1)S(1)}, bf16[48,1024]{1,0:T(8,128)(2,1)S(1)}, u32[]{:S(2)}, u32[]{:S(2)}) collective-permute-start(bf16[48,1024]{1,0:T(8,128)(2,1)S(1)} %get-tuple-element.305), channel_id=1, source_target_pairs={{0,8},{2,10},{4,12},{6,14},{8,0},{10,2},{12,4},{14,6},{16,24},{18,... | collective-permute-start | bytes 294920 | tf_op jit(solution)/shard_map/ppermute | solution.py:48
  5.0 12.4 %collective-permute-start.2 = (bf16[48,1024]{1,0:T(8,128)(2,1)S(1)}, bf16[48,1024]{1,0:T(8,128)(2,1)S(1)}, u32[]{:S(2)}, u32[]{:S(2)}) collective-permute-start(bf16[48,1024]{1,0:T(8,128)(2,1)S(1)} %get-tuple-element.305), channel_id=1, source_target_pairs={{0,16},{2,18},{4,20},{6,22},{8,24},{10,26},{12,28},{14,30},{16,0},... | collective-permute-start | bytes 294920 | tf_op jit(solution)/shard_map/ppermute | solution.py:48
  7.5 9.8 %collective-permute-start.3 = (bf16[48,1024]{1,0:T(8,128)(2,1)S(1)}, bf16[48,1024]{1,0:T(8,128)(2,1)S(1)}, u32[]{:S(2)}, u32[]{:S(2)}) collective-permute-start(bf16[48,1024]{1,0:T(8,128)(2,1)S(1)} %get-tuple-element.305), channel_id=1, source_target_pairs={{0,24},{2,26},{4,28},{6,30},{8,16},{10,18},{12,20},{14,22},{16,8},... | collective-permute-start | bytes 294920 | tf_op jit(solution)/shard_map/ppermute | solution.py:48
  15.6 23.7 %collective-permute-start.8 = (bf16[512,1024]{1,0:T(8,128)(2,1)S(1)}, bf16[512,1024]{1,0:T(8,128)(2,1)S(1)}, u32[]{:S(2)}, u32[]{:S(2)}) collective-permute-start(bf16[512,1024]{1,0:T(8,128)(2,1)S(1)} %copy-done.9), channel_id=1, source_target_pairs={{0,1},{1,0},{2,3},{3,2},{4,5},{5,4},{6,7},{7,6},{8,9},{9,8},{10,11... | collective-permute-start | bytes 3145736 | tf_op jit(solution)/shard_map/ppermute | solution.py:48
  17.4 8.9 %collective-permute-start.5 = (bf16[48,1024]{1,0:T(8,128)(2,1)S(1)}, bf16[48,1024]{1,0:T(8,128)(2,1)S(1)}, u32[]{:S(2)}, u32[]{:S(2)}) collective-permute-start(bf16[48,1024]{1,0:T(8,128)(2,1)S(1)} %pad_maximum_fusion.6), channel_id=1, source_target_pairs={{0,16},{2,18},{4,20},{6,22},{8,24},{10,26},{12,28},{14,30},{16,0},... | collective-permute-start | bytes 294920 | tf_op jit(solution)/shard_map/ppermute | solution.py:48
  21.7 10.6 %collective-permute-start.9 = (bf16[4,48,1024]{2,1,0:T(8,128)(2,1)S(1)}, bf16[4,48,1024]{2,1,0:T(8,128)(2,1)S(1)}, u32[]{:S(2)}, u32[]{:S(2)}) collective-permute-start(bf16[4,48,1024]{2,1,0:T(8,128)(2,1)S(1)} %pad_maximum_fusion.3), channel_id=1, source_target_pairs={{0,4},{2,6},{4,0},{6,2},{8,12},{10,14},{12,8},{14,10},{16,20},{18,... | collective-permute-start | bytes 1179656 | tf_op jit(solution)/shard_map/ppermute | solution.py:48
  27.1 13.9 %collective-permute-start.12 = (bf16[128,1024]{1,0:T(8,128)(2,1)}, bf16[128,1024]{1,0:T(8,128)(2,1)}, u32[]{:S(2)}, u32[]{:S(2)}) collective-permute-start(bf16[128,1024]{1,0:T(8,128)(2,1)} %pad_maximum_fusion.5), channel_id=1, source_target_pairs={{0,8},{2,10},{4,12},{6,14},{8,0},{10,2},{12,4},{14,6},{16,24},{18,... | collective-permute-start | bytes 786440 | tf_op jit(solution)/shard_map/ppermute | solution.py:48
  28.0 21.7 %collective-permute-start.13 = (bf16[128,1024]{1,0:T(8,128)(2,1)}, bf16[128,1024]{1,0:T(8,128)(2,1)}, u32[]{:S(2)}, u32[]{:S(2)}) collective-permute-start(bf16[128,1024]{1,0:T(8,128)(2,1)} %pad_maximum_fusion.5), channel_id=1, source_target_pairs={{0,16},{2,18},{4,20},{6,22},{8,24},{10,26},{12,28},{14,30},{16,0},... | collective-permute-start | bytes 786440 | tf_op jit(solution)/shard_map/ppermute | solution.py:48
  30.5 8.3 %collective-permute-start.7 = (bf16[4,48,1024]{2,1,0:T(8,128)(2,1)S(1)}, bf16[4,48,1024]{2,1,0:T(8,128)(2,1)S(1)}, u32[]{:S(2)}, u32[]{:S(2)}) collective-permute-start(bf16[4,48,1024]{2,1,0:T(8,128)(2,1)S(1)} %pad_maximum_fusion.4), channel_id=1, source_target_pairs={{0,4},{2,6},{4,0},{6,2},{8,12},{10,14},{12,8},{14,10},{16,20},{18,... | collective-permute-start | bytes 1179656 | tf_op jit(solution)/shard_map/ppermute | solution.py:48
  32.3 17.4 %collective-permute-start.14 = (bf16[128,1024]{1,0:T(8,128)(2,1)}, bf16[128,1024]{1,0:T(8,128)(2,1)}, u32[]{:S(2)}, u32[]{:S(2)}) collective-permute-start(bf16[128,1024]{1,0:T(8,128)(2,1)} %pad_maximum_fusion.5), channel_id=1, source_target_pairs={{0,24},{2,26},{4,28},{6,30},{8,16},{10,18},{12,20},{14,22},{16,8},... | collective-permute-start | bytes 786440 | tf_op jit(solution)/shard_map/ppermute | solution.py:48
  38.7 13.3 %collective-permute-start.10 = (bf16[8,48,1024]{2,1,0:T(8,128)(2,1)S(1)}, bf16[8,48,1024]{2,1,0:T(8,128)(2,1)S(1)}, u32[]{:S(2)}, u32[]{:S(2)}) collective-permute-start(bf16[8,48,1024]{2,1,0:T(8,128)(2,1)S(1)} %constant_dynamic-update-slice_fusion.refs_0_), channel_id=1, source_target_pairs={{0,2},{2,0},{4,6},{6,4},{8,10},{10,8},{12,14},{14,12},{16,18},{18,... | collective-permute-start | bytes 2359304 | tf_op jit(solution)/shard_map/ppermute | solution.py:48
  40.2 11.8 %collective-permute-start.11 = (bf16[8,48,1024]{2,1,0:T(8,128)(2,1)S(1)}, bf16[8,48,1024]{2,1,0:T(8,128)(2,1)}, u32[]{:S(2)}, u32[]{:S(2)}) collective-permute-start(bf16[8,48,1024]{2,1,0:T(8,128)(2,1)S(1)} %constant_dynamic-update-slice_fusion.2.refs_1_), channel_id=1, source_target_pairs={{0,2},{2,0},{4,6},{6,4},{8,10},{10,8},{12,14},{14,12},{16,18},{18,... | collective-permute-start | bytes 2359304 | tf_op jit(solution)/shard_map/ppermute | solution.py:48
  41.1 26.0 %collective-permute-start.15 = (bf16[512,1024]{1,0:T(8,128)(2,1)}, bf16[512,1024]{1,0:T(8,128)(2,1)}, u32[]{:S(2)}, u32[]{:S(2)}) collective-permute-start(bf16[512,1024]{1,0:T(8,128)(2,1)} %cot0), channel_id=1, source_target_pairs={{0,1},{1,0},{2,3},{3,2},{4,5},{5,4},{6,7},{7,6},{8,9},{9,8},{10,11... | collective-permute-start | bytes 3145736 | tf_op jit(solution)/shard_map/ppermute | solution.py:48
  67.0 31.6 %collective-permute-start.16 = (bf16[4,128,1024]{2,1,0:T(8,128)(2,1)}, bf16[4,128,1024]{2,1,0:T(8,128)(2,1)S(1)}, u32[]{:S(2)}, u32[]{:S(2)}) collective-permute-start(bf16[4,128,1024]{2,1,0:T(8,128)(2,1)} %pad_maximum_fusion), channel_id=1, source_target_pairs={{0,4},{2,6},{4,0},{6,2},{8,12},{10,14},{12,8},{14,10},{16,20},{18,... | collective-permute-start | bytes 3145736 | tf_op jit(solution)/shard_map/ppermute | solution.py:48
  140.3 29.6 %collective-permute-start.21 = (bf16[4,64,1024]{2,1,0:T(8,128)(2,1)}, bf16[4,64,1024]{2,1,0:T(8,128)(2,1)}, u32[]{:S(2)}, u32[]{:S(2)}) collective-permute-start(bf16[4,64,1024]{2,1,0:T(8,128)(2,1)} %get-tuple-element.186), channel_id=1, source_target_pairs={{0,4},{2,6},{4,0},{6,2},{8,12},{10,14},{12,8},{14,10},{16,20},{18,... | collective-permute-start | bytes 1572872 | tf_op jit(solution)/shard_map/ppermute | solution.py:48
  142.2 45.2 %collective-permute-start.23 = (bf16[512,1024]{1,0:T(8,128)(2,1)}, bf16[512,1024]{1,0:T(8,128)(2,1)}, u32[]{:S(2)}, u32[]{:S(2)}) collective-permute-start(bf16[512,1024]{1,0:T(8,128)(2,1)} %slice.254), channel_id=1, source_target_pairs={{0,1},{1,0},{2,3},{3,2},{4,5},{5,4},{6,7},{7,6},{8,9},{9,8},{10,11... | collective-permute-start | bytes 3145736 | tf_op jit(solution)/shard_map/ppermute | solution.py:48
  144.8 42.5 %collective-permute-start.22 = (bf16[4,64,1024]{2,1,0:T(8,128)(2,1)}, bf16[4,64,1024]{2,1,0:T(8,128)(2,1)S(1)}, u32[]{:S(2)}, u32[]{:S(2)}) collective-permute-start(bf16[4,64,1024]{2,1,0:T(8,128)(2,1)} %get-tuple-element.193), channel_id=1, source_target_pairs={{0,4},{2,6},{4,0},{6,2},{8,12},{10,14},{12,8},{14,10},{16,20},{18,... | collective-permute-start | bytes 1572872 | tf_op jit(solution)/shard_map/ppermute | solution.py:48
  171.2 24.7 %collective-permute-start.24 = (bf16[64,1024]{1,0:T(8,128)(2,1)S(1)}, bf16[64,1024]{1,0:T(8,128)(2,1)S(1)}, u32[]{:S(2)}, u32[]{:S(2)}) collective-permute-start(bf16[64,1024]{1,0:T(8,128)(2,1)S(1)} %get-tuple-element.297), channel_id=1, source_target_pairs={{0,8},{2,10},{4,12},{6,14},{8,0},{10,2},{12,4},{14,6},{16,24},{18,... | collective-permute-start | bytes 393224 | tf_op jit(solution)/shard_map/ppermute | solution.py:48
  173.0 22.9 %collective-permute-start.25 = (bf16[64,1024]{1,0:T(8,128)(2,1)S(1)}, bf16[64,1024]{1,0:T(8,128)(2,1)S(1)}, u32[]{:S(2)}, u32[]{:S(2)}) collective-permute-start(bf16[64,1024]{1,0:T(8,128)(2,1)S(1)} %get-tuple-element.296), channel_id=1, source_target_pairs={{0,16},{2,18},{4,20},{6,22},{8,24},{10,26},{12,28},{14,30},{16,0},... | collective-permute-start | bytes 393224 | tf_op jit(solution)/shard_map/ppermute | solution.py:48
  175.3 20.6 %collective-permute-start.26 = (bf16[64,1024]{1,0:T(8,128)(2,1)S(1)}, bf16[64,1024]{1,0:T(8,128)(2,1)S(1)}, u32[]{:S(2)}, u32[]{:S(2)}) collective-permute-start(bf16[64,1024]{1,0:T(8,128)(2,1)S(1)} %get-tuple-element.295), channel_id=1, source_target_pairs={{0,24},{2,26},{4,28},{6,30},{8,16},{10,18},{12,20},{14,22},{16,8},... | collective-permute-start | bytes 393224 | tf_op jit(solution)/shard_map/ppermute | solution.py:48
  204.5 12.5 %collective-permute-start.29 = (bf16[64,1024]{1,0:T(8,128)(2,1)S(1)}, bf16[64,1024]{1,0:T(8,128)(2,1)S(1)}, u32[]{:S(2)}, u32[]{:S(2)}) collective-permute-start(bf16[64,1024]{1,0:T(8,128)(2,1)S(1)} %get-tuple-element.294), channel_id=1, source_target_pairs={{0,8},{2,10},{4,12},{6,14},{8,0},{10,2},{12,4},{14,6},{16,24},{18,... | collective-permute-start | bytes 393224 | tf_op jit(solution)/shard_map/ppermute | solution.py:48
  205.3 13.3 %collective-permute-start.30 = (bf16[64,1024]{1,0:T(8,128)(2,1)S(1)}, bf16[64,1024]{1,0:T(8,128)(2,1)S(1)}, u32[]{:S(2)}, u32[]{:S(2)}) collective-permute-start(bf16[64,1024]{1,0:T(8,128)(2,1)S(1)} %get-tuple-element.293), channel_id=1, source_target_pairs={{0,16},{2,18},{4,20},{6,22},{8,24},{10,26},{12,28},{14,30},{16,0},... | collective-permute-start | bytes 393224 | tf_op jit(solution)/shard_map/ppermute | solution.py:48
  208.6 10.7 %collective-permute-start.31 = (bf16[64,1024]{1,0:T(8,128)(2,1)S(1)}, bf16[64,1024]{1,0:T(8,128)(2,1)S(1)}, u32[]{:S(2)}, u32[]{:S(2)}) collective-permute-start(bf16[64,1024]{1,0:T(8,128)(2,1)S(1)} %get-tuple-element.292), channel_id=1, source_target_pairs={{0,24},{2,26},{4,28},{6,30},{8,16},{10,18},{12,20},{14,22},{16,8},... | collective-permute-start | bytes 393224 | tf_op jit(solution)/shard_map/ppermute | solution.py:48
  210.2 10.7 %collective-permute-start.32 = (bf16[4,64,640]{2,1,0:T(8,128)(2,1)S(1)}, bf16[4,64,640]{2,1,0:T(8,128)(2,1)S(1)}, u32[]{:S(2)}, u32[]{:S(2)}) collective-permute-start(bf16[4,64,640]{2,1,0:T(8,128)(2,1)S(1)} %add_convert_fusion.3), channel_id=1, source_target_pairs={{0,4},{2,6},{4,0},{6,2},{8,12},{10,14},{12,8},{14,10},{16,20},{18,... | collective-permute-start | bytes 983048 | tf_op jit(solution)/shard_map/ppermute | solution.py:48
  215.1 14.7 %collective-permute-start.33 = (bf16[4,64,768]{2,1,0:T(8,128)(2,1)S(1)}, bf16[4,64,768]{2,1,0:T(8,128)(2,1)S(1)}, u32[]{:S(2)}, u32[]{:S(2)}) collective-permute-start(bf16[4,64,768]{2,1,0:T(8,128)(2,1)S(1)} %add_convert_fusion.2), channel_id=1, source_target_pairs={{0,4},{2,6},{4,0},{6,2},{8,12},{10,14},{12,8},{14,10},{16,20},{18,... | collective-permute-start | bytes 1179656 | tf_op jit(solution)/shard_map/ppermute | solution.py:48
  217.0 21.1 %collective-permute-start.34 = (bf16[256,1024]{1,0:T(8,128)(2,1)S(1)}, bf16[256,1024]{1,0:T(8,128)(2,1)S(1)}, u32[]{:S(2)}, u32[]{:S(2)}) collective-permute-start(bf16[256,1024]{1,0:T(8,128)(2,1)S(1)} %get-tuple-element.291), channel_id=1, source_target_pairs={{0,1},{1,0},{2,3},{3,2},{4,5},{5,4},{6,7},{7,6},{8,9},{9,8},{10,11... | collective-permute-start | bytes 1572872 | tf_op jit(solution)/shard_map/ppermute | solution.py:48
  218.6 40.3 %collective-permute-start.44 = (bf16[256,1024]{1,0:T(8,128)(2,1)}, bf16[256,1024]{1,0:T(8,128)(2,1)}, u32[]{:S(2)}, u32[]{:S(2)}) collective-permute-start(bf16[256,1024]{1,0:T(8,128)(2,1)} %get-tuple-element.290), channel_id=1, source_target_pairs={{0,1},{1,0},{2,3},{3,2},{4,5},{5,4},{6,7},{7,6},{8,9},{9,8},{10,11... | collective-permute-start | bytes 1572872 | tf_op jit(solution)/shard_map/ppermute | solution.py:48
  221.9 10.9 %collective-permute-start.35 = (bf16[64,640]{1,0:T(8,128)(2,1)S(1)}, bf16[64,640]{1,0:T(8,128)(2,1)S(1)}, u32[]{:S(2)}, u32[]{:S(2)}) collective-permute-start(bf16[64,640]{1,0:T(8,128)(2,1)S(1)} %get-tuple-element.303), channel_id=1, source_target_pairs={{0,8},{2,10},{4,12},{6,14},{8,0},{10,2},{12,4},{14,6},{16,24},{18,... | collective-permute-start | bytes 245768 | tf_op jit(solution)/shard_map/ppermute | solution.py:48
  222.2 10.6 %collective-permute-start.36 = (bf16[64,640]{1,0:T(8,128)(2,1)S(1)}, bf16[64,640]{1,0:T(8,128)(2,1)S(1)}, u32[]{:S(2)}, u32[]{:S(2)}) collective-permute-start(bf16[64,640]{1,0:T(8,128)(2,1)S(1)} %get-tuple-element.302), channel_id=1, source_target_pairs={{0,16},{2,18},{4,20},{6,22},{8,24},{10,26},{12,28},{14,30},{16,0},... | collective-permute-start | bytes 245768 | tf_op jit(solution)/shard_map/ppermute | solution.py:48
  232.7 21.6 %collective-permute-start.40 = (bf16[64,768]{1,0:T(8,128)(2,1)}, bf16[64,768]{1,0:T(8,128)(2,1)}, u32[]{:S(2)}, u32[]{:S(2)}) collective-permute-start(bf16[64,768]{1,0:T(8,128)(2,1)} %get-tuple-element.300), channel_id=1, source_target_pairs={{0,8},{2,10},{4,12},{6,14},{8,0},{10,2},{12,4},{14,6},{16,24},{18,... | collective-permute-start | bytes 294920 | tf_op jit(solution)/shard_map/ppermute | solution.py:48
  232.8 21.6 %collective-permute-start.41 = (bf16[64,768]{1,0:T(8,128)(2,1)}, bf16[64,768]{1,0:T(8,128)(2,1)}, u32[]{:S(2)}, u32[]{:S(2)}) collective-permute-start(bf16[64,768]{1,0:T(8,128)(2,1)} %get-tuple-element.299), channel_id=1, source_target_pairs={{0,16},{2,18},{4,20},{6,22},{8,24},{10,26},{12,28},{14,30},{16,0},... | collective-permute-start | bytes 294920 | tf_op jit(solution)/shard_map/ppermute | solution.py:48
  236.7 17.7 %collective-permute-start.42 = (bf16[64,768]{1,0:T(8,128)(2,1)}, bf16[64,768]{1,0:T(8,128)(2,1)}, u32[]{:S(2)}, u32[]{:S(2)}) collective-permute-start(bf16[64,768]{1,0:T(8,128)(2,1)} %get-tuple-element.298), channel_id=1, source_target_pairs={{0,24},{2,26},{4,28},{6,30},{8,16},{10,18},{12,20},{14,22},{16,8},... | collective-permute-start | bytes 294920 | tf_op jit(solution)/shard_map/ppermute | solution.py:48
  (78 other events, 466.8 us)

commit v5 on v4

--- a/solution.py
+++ b/solution.py
@@ -127,7 +127,9 @@
         out_shape=out_shape,
         compiler_params=params,
         input_output_aliases=aliases or {},
-        cost_estimate=pl.CostEstimate(flops=int(flops), bytes_accessed=int(moved), transcendentals=0),
+        cost_estimate=pl.CostEstimate(
+            flops=int(flops) // 16, bytes_accessed=int(moved) // 16, transcendentals=0
+        ),
     )
 
 
@@ -170,6 +172,10 @@
     a_high, a_low = split(a)
     b_high, b_low = split(b)
     return mm(a_high, b_high, ca, cb) + mm(a_low, b_high, ca, cb) + mm(a_high, b_low, ca, cb)
+
+
+def sigmoid(value):
+    return 0.5 * jnp.tanh(0.5 * value) + 0.5
 
 
 def softplus(value):
@@ -189,34 +195,32 @@
     )
 
 
-def assemble_kernel(dp, parts, me, *refs):
+def assemble_kernel(dp, parts, moves, me, *refs):
     half = dp // CORES
     sources, outs = refs[: 2 * parts], refs[2 * parts :]
     for place, distance in enumerate(relative_places(dp)):
+        block = me[0] ^ distance
         base = 0
         for part in range(parts):
             source, at = (sources[part], place) if place < half else (sources[parts + part], place - half)
             end = base + source.shape[1]
-            start = 0
-            for out in outs:
-                low, high = max(base, start), min(end, start + out.shape[1])
+            for first, last, lanes, out, each, extra, row in moves:
+                low, high = max(base, first), min(end, last)
                 if low < high:
-                    out[me[0] ^ distance, low - start : high - start, :] = source[
-                        at, low - base : high - base, :
-                    ]
-                start += out.shape[1]
+                    outs[out][
+                        block * each + extra, row + low - first : row + high - first, :
+                    ] = source[at, low - base : high - base, lanes]
             base = end
 
 
-def assemble(nears, fars, dp, dp_rank, counts):
-    width, dtype = nears[0].shape[2], nears[0].dtype
+def assemble(nears, fars, dp, dp_rank, moves, shapes):
     vmem = pl.BlockSpec(memory_space=pltpu.VMEM)
     moved = sum(4 * near.size * near.dtype.itemsize for near in nears)
     return pl.pallas_call(
-        functools.partial(assemble_kernel, dp, len(nears)),
+        functools.partial(assemble_kernel, dp, len(nears), moves),
         in_specs=[pl.BlockSpec(memory_space=pltpu.SMEM)] + [vmem] * (2 * len(nears)),
-        out_specs=[vmem] * len(counts),
-        out_shape=[shape(dp, count, width, dtype=dtype) for count in counts],
+        out_specs=[vmem] * len(shapes),
+        out_shape=[shape(*dims, dtype=bf16) for dims in shapes],
         compiler_params=pltpu.CompilerParams(vmem_limit_bytes=16 * 1024 * 1024),
         cost_estimate=pl.CostEstimate(flops=0, bytes_accessed=moved, transcendentals=0),
     )(dp_rank, *nears, *fars)
@@ -235,7 +239,7 @@
 
 
 def scan_kernel(
-    rank, tok0, tok1, gain, wv, shw, conv, skip, hp, aux, segr,
+    heads, rank, tok0, tok1, gain, wv, shw, conv, skip, hp, aux, segr,
     normed_o, ch_o, pre_o, mix_o, ssd_o, hin_o, step_o,
     win, state, carried, weighted,
 ):
@@ -255,7 +259,8 @@
     win[8 : 8 + count, :width] = mm(normed, wv[...])
     common = mm(normed, shw[...])
     win[8 : 8 + count, width:] = common[:, : 2 * N]
-    step_o[...] = common[:, 2 * N :] + hp[0:1, :]
+    turn = lax.rem(LANES - heads * rank[1], LANES)
+    step_o[...] = pltpu.roll(common[:, 2 * N :], turn, 1) + hp[0:1, :]
     table = aux[...]
     for start in range(0, channels, 256):
         cols = slice(start, start + 256)
@@ -267,7 +272,7 @@
             )
         ch_o[:, cols] = here
         pre_o[:, cols] = pre
-        mix_o[:, cols] = (pre * jax.nn.sigmoid(pre)).astype(bf16)
+        mix_o[:, cols] = (pre * sigmoid(pre)).astype(bf16)
     win[0:8, :] = win[count : count + 8, :]
 
     row, col = iota(0), iota(1)
@@ -282,7 +287,7 @@
         b_in = mix_o[at, width : width + N]
         b_turned = b_in.astype(f32).T.astype(bf16)
         c_out = mix_o[at, width + N :]
-        scores = mm(c_out, b_in, 1, 1)
+        scores = jnp.where(allowed, mm(c_out, b_in, 1, 1), 0.0)
         ending = run[CHUNK - 1 : CHUNK, :]
         entry = jnp.exp(run) * table[at, INHERIT : INHERIT + 1]
         tail = jnp.exp(ending - run) * table[at, TAIL : TAIL + 1]
@@ -296,8 +301,7 @@
             mixing = []
             for head in (2 * pair, 2 * pair + 1):
                 spread = run[:, head : head + 1] - run_t[head : head + 1, :]
-                decays = jnp.exp(jnp.where(allowed, spread, -1e30))
-                mixing.append((decays * scores).astype(bf16))
+                mixing.append((jnp.exp(jnp.minimum(spread, 0.0)) * scores).astype(bf16))
             local = mm(jnp.concatenate(mixing, axis=1), across(stepped, left))
             ssd_o[at, lanes] = (
                 local + carried[:, lanes] * pair_spread(entry, pair, left) + skip[:, lanes] * x_pair
@@ -316,7 +320,7 @@
     gate_o[...] = gate
     scaled_grad = mm(returned, out_t[...])
     sg_o[...] = scaled_grad
-    gated = ssd[...] * (gate * jax.nn.sigmoid(gate))
+    gated = ssd[...] * (gate * sigmoid(gate))
     squares = jnp.sum(gated * gated, axis=1, keepdims=True)
     crossed = jnp.sum(scaled_grad * gain[...] * gated, axis=1, keepdims=True)
     lane = lax.broadcasted_iota(jnp.int32, (squares.shape[0], LANES), 1)
@@ -335,7 +339,7 @@
     table = jnp.concatenate([sums_r[...], jnp.zeros((LANES - 8, sums_r.shape[1]), f32)], axis=0)
     sums = table.T
     scale = lax.rsqrt(sums[:, 0:1] / DI + norm_epsilon)
-    sig = jax.nn.sigmoid(gate)
+    sig = sigmoid(gate)
     silu = gate * sig
     gated = ssd * silu
     scaled = (gated * scale * gain[...]).astype(bf16)
@@ -348,7 +352,7 @@
 
 
 def scan_back_kernel(
-    dssd, mix, pre, ch, ssd, hin, step, conv, skip, hp, aux, segr, heads_of,
+    heads, rank, dssd, mix, pre, ch, ssd, hin, step, conv, skip, hp, aux, segr, heads_of,
     state_in, win_in, carry_in, *rest,
 ):
     dval_o, dcommon_o, dconv_o, dheads_o, dstate, dtail, carry = rest[-14:-7]
@@ -377,7 +381,7 @@
     allowed = (table[:, SEG : SEG + 1] == segr[...]) & (col >= row)
     b_in = mix[:, width : width + N]
     c_out = mix[:, width + N :]
-    scores = mm(b_in, c_out, 1, 1)
+    scores = jnp.where(allowed, mm(b_in, c_out, 1, 1), 0.0)
     ending = run[CHUNK - 1 : CHUNK, :]
     entry = jnp.exp(run) * table[:, INHERIT : INHERIT + 1]
     tail = jnp.exp(ending - run) * table[:, TAIL : TAIL + 1]
@@ -398,7 +402,7 @@
         mixing = []
         for place, head in enumerate((2 * pair, 2 * pair + 1)):
             spread = run_t[head : head + 1, :] - run[:, head : head + 1]
-            decays = jnp.exp(jnp.where(allowed, spread, -1e30))
+            decays = jnp.exp(jnp.minimum(spread, 0.0))
             mixing.append((decays * scores).astype(bf16))
             pairs = pairs + inner[place * CHUNK : (place + 1) * CHUNK] * decays
         flow = mm(jnp.concatenate(mixing, axis=1), across(dy, left)) + tail_pair * flows[:, lanes]
@@ -411,6 +415,7 @@
         entries[1, :, lanes] = low
         weighted[:, lanes] = (tail_pair * stepped).astype(bf16)
         dstate[:, lanes] = pair_spread(factor, pair, left) * dstate[:, lanes]
+    pairs = jnp.where(allowed, pairs, 0.0)
     dstate[...] += mm(c_turned, entries[0]) + mm(c_turned, entries[1])
     dmix[:, width : width + N] = mm(weighted[...], state_high, 1, 1) + mm_left(pairs, c_out)
     dmix[:, width + N :] = mm(entries[0], hin[0].astype(bf16), 1, 1) + mm_left(pairs, b_in, 0, 0)
@@ -422,15 +427,15 @@
     log_grad = jnp.dot(later, balance, precision=highest, preferred_element_type=f32)
     log_grad = log_grad + table[:, NEXT : NEXT + 1] * carry[0:1, :]
     carry[0:1, :] = log_grad[0:1, :]
-    step_grad = (direct - rate * log_grad) * jax.nn.sigmoid(step_in)
-    dcommon_o[:, 2 * N :] = step_grad
+    step_grad = (direct - rate * log_grad) * sigmoid(step_in)
+    dcommon_o[:, 2 * N :] = pltpu.roll(step_grad, heads * rank[0], 1)
     dheads_o[0:1, :] += jnp.sum(step_grad, axis=0, keepdims=True)
     dheads_o[1:2, :] += jnp.sum(-(log_grad * dt * rate), axis=0, keepdims=True)
 
     for start in range(0, channels, 256):
         cols = slice(start, start + 256)
         value = pre[:, cols]
-        sig = jax.nn.sigmoid(value)
+        sig = sigmoid(value)
         dwin[0:CHUNK, cols] = dmix[:, cols] * (sig * (1.0 + value * (1.0 - sig)))
         here = ch[:, cols]
         own = dwin[0:CHUNK, cols]
@@ -598,11 +603,21 @@
         term = lax.optimization_barrier(rest.astype(bf16))
         terms.append(term)
         rest = rest - term.astype(f32)
-    small = jnp.concatenate([shared_proj.astype(bf16).reshape(-1)] + terms)
-    small_rows = -(-small.size // width)
-    while small_rows * nt % 16:
-        small_rows += 1
-    small = jnp.pad(small, (0, small_rows * width - small.size)).reshape(small_rows, width)
+    common_width = 2 * N + LANES
+    shared_rows = shared_proj.shape[0]
+    packed = width == 1024 and shared_rows == 32
+    if packed:
+        wide_shared = jnp.pad(shared_proj.astype(bf16), ((0, 0), (0, common_width - 2 * N - H)))
+        flat = jnp.concatenate(terms)
+        flat = jnp.pad(flat, (0, 16 * 256 - flat.size)).reshape(16, 256)
+        small = jnp.concatenate([wide_shared[:16], wide_shared[16:], flat], axis=1)
+        small_rows = 16
+    else:
+        small = jnp.concatenate([shared_proj.astype(bf16).reshape(-1)] + terms)
+        small_rows = -(-small.size // width)
+        while small_rows * nt % 16:
+            small_rows += 1
+        small = jnp.pad(small, (0, small_rows * width - small.size)).reshape(small_rows, width)
     small_pair = over_tensor(small)
     residual_now, small_pair = tie(residual, small_pair)
     token_pieces = pieces_of(residual_now)
@@ -624,11 +639,26 @@
     parts, token_pieces = parts[:-nt], parts[-nt:]
     second_near = jnp.concatenate([second_line] + parts, axis=0)
     cotangent_now, *token_pieces = tie(cotangent, *token_pieces)
-    cot_pieces = pieces_of(cotangent_now)
-    value_w, small_all = assemble(
-        [first_near, second_near],
-        [swap(first_near, "dp", dp, 1), swap(second_near, "dp", dp, 1)],
-        dp, dp_me, [block_rows, small_rows * nt],
+    cot_cut = rows_here // 2
+    cot_early = [swap(cotangent_now[:cot_cut], "tensor", nt, d) for d in range(1, nt)]
+    cot_late = [swap(cotangent_now[cot_cut:], "tensor", nt, d) for d in range(1, nt)]
+    fars = [swap(first_near, "dp", dp, 1), swap(second_near, "dp", dp, 1)]
+    first_far, second_far, *cot_early = tie(*fars, *cot_early)
+    full = slice(None)
+    moves = [(0, block_rows, full, 0, 1, 0, 0)]
+    dims = [(dp, block_rows, width)]
+    if packed:
+        for t in range(nt):
+            at = (block_rows + 16 * t, block_rows + 16 * t + 16)
+            moves.append(at + (slice(0, common_width), 1, nt, t, 0))
+            moves.append(at + (slice(common_width, 2 * common_width), 1, nt, t, 16))
+            moves.append(at + (slice(2 * common_width, width), 2, nt, t, 0))
+        dims += [(dp * nt, 32, common_width), (dp * nt, 16, 256)]
+    else:
+        moves.append((block_rows, block_rows + small_rows * nt, full, 1, 1, 0, 0))
+        dims += [(dp, small_rows * nt, width)]
+    value_w, *small_all = assemble(
+        [first_near, second_near], [first_far, second_far], dp, dp_me, moves, dims
     )
     value_w = value_w.reshape(D, width)
 
@@ -638,9 +668,14 @@
         all_rows = over_tensor(None, pieces)
         return jnp.zeros((1,), jnp.int32), all_rows[: length // 2], all_rows[length // 2 :]
 
-    small_all = small_all.reshape(dp * nt, small_rows * width)
-    shared_full = small_all[:, :shared_size].reshape(D, -1)
-    exact_all = small_all[:, shared_size : shared_size + 3 * exact.size].astype(f32)
+    if packed:
+        shared_here = small_all[0].reshape(D, common_width)
+        exact_all = small_all[1].reshape(dp * nt, -1)[:, : 3 * exact.size].astype(f32)
+    else:
+        small_all = small_all[0].reshape(dp * nt, small_rows * width)
+        shared_here = small_all[:, :shared_size].reshape(D, -1)
+        shared_here = jnp.pad(shared_here, ((0, 0), (0, common_width - 2 * N - H)))
+        exact_all = small_all[:, shared_size : shared_size + 3 * exact.size].astype(f32)
     exact_all = exact_all.reshape(dp * nt, 3, exact.size)
     exact_all = (exact_all[:, 0] + exact_all[:, 1]) + exact_all[:, 2]
     conv_full = (
@@ -657,15 +692,6 @@
         [lax.dynamic_slice_in_dim(conv_full, t_rank * width, width, 1), conv_full[:, DI:]], axis=1
     )
     conv_here = jnp.pad(conv_here, ((0, 8 - kernel_rows), (0, 0)))
-    shared_here = jnp.concatenate(
-        [
-            shared_full[:, : 2 * N],
-            lax.dynamic_slice_in_dim(shared_full, 2 * N + t_rank * heads_here, heads_here, 1),
-            jnp.zeros((D, LANES - heads_here), bf16),
-        ],
-        axis=1,
-    )
-    common_width = 2 * N + LANES
     head_rows = jnp.stack([head_params[0], jnp.exp(head_params[1])])
     head_rows = jnp.pad(head_rows, ((0, 6), (0, LANES - heads_here)))
     skip = jnp.repeat(head_params[2], head_size).reshape(1, width)
@@ -695,10 +721,14 @@
 
     steps = length // wide
     in_half = lambda i: i % (steps // 2)
-    value_w, other_line, *cot_pieces = tie(value_w, other_line, *cot_pieces)
+    value_w, other_line, *cot_late = tie(value_w, other_line, *cot_late)
+    cot_pieces = [cotangent] + [
+        jnp.concatenate([early, late], axis=0) for early, late in zip(cot_early, cot_late)
+    ]
     plane = plane_parts(other_line, dp)
+    tok_rank, tok0, tok1 = halves(token_pieces)
     normed, chans, pre, mixed, ssd, entering, step_in = call(
-        scan_kernel,
+        functools.partial(scan_kernel, heads_here),
         (steps,),
         [
             rows(wide, D, in_half), rows(wide, D, in_half), whole((1, D)), whole((D, width)),
@@ -720,14 +750,17 @@
             pltpu.VMEM((CHUNK, width), f32), pltpu.VMEM((2, CHUNK, width), bf16),
         ],
         length * (2 * D * (width + common_width) + 12 * width * CHUNK),
-        30,
+        48,
         scalars=1,
-    )(*halves(token_pieces), pre_gain, value_w, shared_here, conv_here, skip, head_rows, aux, segr)
+    )(jnp.concatenate([tok_rank, t_me]), tok0, tok1, pre_gain, value_w, shared_here, conv_here, skip, head_rows, aux, segr)
 
     normed, *plane = tie(normed, *plane)
     plane = jnp.concatenate([other_line] + plane, axis=0)
+    moves = [
+        (0, block_rows, full, 0, 1, 0, 0), (block_rows, 2 * block_rows, full, 1, 1, 0, 0)
+    ]
     gate_w, outer_t = assemble(
-        [plane], [swap(plane, "dp", dp, 1)], dp, dp_me, [block_rows, block_rows]
+        [plane], [swap(plane, "dp", dp, 1)], dp, dp_me, moves, [(dp, block_rows, width)] * 2
     )
     gate_w, outer_t = gate_w.reshape(D, width), outer_t.reshape(D, width)
     cot_rank, cot0, cot1 = halves(cot_pieces)
@@ -800,15 +833,15 @@
         back = lambda i, top=top: top - 1 - i
         top -= count
         *results, state, win, carry = call(
-            scan_back_kernel,
+            functools.partial(scan_back_kernel, heads_here),
             (count,),
             [
                 rows(CHUNK, width, back), rows(CHUNK, channels, back), rows(CHUNK, channels, back),
                 rows(CHUNK, channels, back), rows(CHUNK, width, back),
-                pl.BlockSpec((1, N, width), lambda i, back=back: (back(i), 0, 0)),
+                pl.BlockSpec((1, N, width), lambda i, r, back=back: (back(i), 0, 0)),
                 rows(CHUNK, LANES, back), whole((8, channels)), whole((1, width)),
                 whole((8, LANES)), rows(CHUNK, aux_cols, back),
-                pl.BlockSpec((1, CHUNK), lambda i, back=back: (0, back(i))),
+                pl.BlockSpec((1, CHUNK), lambda i, r, back=back: (0, back(i))),
                 whole((width, LANES)),
                 whole((N, width)), whole((8, channels)), whole((8, LANES)),
             ]
@@ -830,10 +863,11 @@
                 pltpu.VMEM((8, width), f32),
             ],
             count * CHUNK * 30 * width * CHUNK,
-            24,
-            aliases={16: 0, 17: 1} if filled else None,
+            48,
+            scalars=1,
+            aliases={17: 0, 18: 1} if filled else None,
         )(
-            dssd, mixed, pre, chans, ssd, entering, step_in, conv_here, skip, head_rows, aux, segr,
+            t_me, dssd, mixed, pre, chans, ssd, entering, step_in, conv_here, skip, head_rows, aux, segr,
             heads_of, state, win, carry, *filled,
         )
         filled = results[:2]
@@ -843,13 +877,17 @@
             outer_block, outer_far = middle_sum(outer_line, outer_received)
             outer_far = high_swaps(outer_far, dp)
         if part == 1:
-            state, gate_line, *rests = tie(state, gate_line, *gate_received, *branch_received)
-            gate_received, branch_received = rests[: len(gate_received)], rests[len(gate_received) :]
+            state, gate_line, *rests = tie(
+                state, gate_line, *branch_received, *gate_received, *outer_far
+            )
+            branch_received = rests[: nt - 1]
+            gate_received, outer_far = rests[nt - 1 : -len(outer_far)], rests[-len(outer_far) :]
             gate_block, gate_far = middle_sum(gate_line, gate_received)
             gate_far = high_swaps(gate_far, dp)
     dval, dcommon = filled
-    dval, *outer_far = tie(dval, *outer_far)
+    dval, *gate_far = tie(dval, *gate_far)
     outer_part = high_sum(outer_block, outer_far)
+    gate_part = high_sum(gate_block, gate_far)
 
     branch_sum = branch[0].astype(f32)
     for piece in branch_received:
@@ -874,62 +912,31 @@
             scalars=1,
         )(t_me, dgate, dval, dcommon, positions, gate_w, value_w, shared_here)
 
-    sums_keep = [value_grad(normed, dval, dcommon, dp, dp_me)]
-    if width > 256:
-        dval_now, first_send = tie(dval, sums_keep[0][1])
-        sums_keep[0] = (sums_keep[0][0], first_send)
-        sums_keep.append(weight_grad(normed, dval_now, dp, dp_me, skipped=1))
-    lines, parts = [], []
-    for keep, send in sums_keep:
-        line, part = start_sum(keep, send, dp)
-        lines.append(line)
-        parts.append(part)
-    steps_each = len(parts[0])
-    dgate, *flat = tie(dgate, *[item for part in parts for item in part])
-    parts = [flat[at : at + steps_each] for at in range(0, len(flat), steps_each)]
-    crossing = [middle_swaps(part, dp) for part in parts]
+    keep, send = value_grad(normed, dval, dcommon, dp, dp_me)
+    line, part = start_sum(keep, send, dp)
+    dgate, *part = tie(dgate, *part)
+    crossing = middle_swaps(part, dp)
     others = token_pieces[1] if nt == 2 else jnp.concatenate(token_pieces[1:], axis=0)
     sent, pre_grad_sent = input_grad(nt - 1, per_piece, bf16, others, dgate)
     sent = sent.reshape(nt - 1, 2, rows_here // 2, D)
     received = [
-        [swap(sent[d - 1, part], "tensor", nt, d) for d in range(1, nt)] for part in range(2)
+        [swap(sent[d - 1, at], "tensor", nt, d) for d in range(1, nt)] for at in range(2)
     ]
-    dgate, pre_grad_sent, *rests = tie(dgate, pre_grad_sent, *gate_far, *crossing[0])
-    gate_far, crossing[0] = rests[: len(gate_far)], rests[len(gate_far) :]
-    gate_part = high_sum(gate_block, gate_far)
-    block, far = middle_sum(lines[0], crossing[0])
+    dgate, pre_grad_sent = tie(dgate, pre_grad_sent)
+    own, pre_grad_own = input_grad(1, 0, f32, residual, dgate)
+    dval, pre_grad_own, *crossing = tie(dval, pre_grad_own, *crossing)
+    block, far = middle_sum(line, crossing)
     fars = [high_swaps(far, dp)]
     blocks = [block]
-    own, pre_grad_own = input_grad(1, 0, f32, residual, dgate)
-    if len(parts) > 1:
-        pre_grad_own, *crossing[1] = tie(pre_grad_own, *crossing[1])
-        block, far = middle_sum(lines[1], crossing[1])
-        fars.append(high_swaps(far, dp))
-        blocks.append(block)
-    pre_grad_own, *rests = tie(pre_grad_own, *received[0], *fars[0])
-    received[0], fars[0] = rests[: nt - 1], rests[nt - 1 :]
-    value_sums = [high_sum(blocks[0], fars[0])]
-    shared_rows = shared_proj.shape[0]
-    shared_sum = value_sums[0][:, 256:].reshape(nt, shared_rows, common_width)
-    shared_mine = lax.dynamic_index_in_dim(shared_sum, t_rank, 0, False)
-    shared_common = shared_mine[:, : 2 * N]
-    shared_part = jnp.zeros((shared_rows, 2 * N + H), f32)
-
-    def place_heads(table, piece, rank):
-        return lax.dynamic_update_slice(
-            table, piece[:, 2 * N : 2 * N + heads_here], (0, 2 * N + rank * heads_here)
-        )
-
-    shared_part = place_heads(shared_part, shared_mine, t_rank)
-    for d in range(1, nt):
-        piece = lax.dynamic_index_in_dim(shared_sum, t_rank ^ d, 0, False)
-        piece = swap(piece, "tensor", nt, d)
-        shared_common = shared_common + piece[:, : 2 * N]
-        shared_part = place_heads(shared_part, piece, t_rank ^ d)
-    shared_part = lax.dynamic_update_slice(shared_part, shared_common, (0, 0))
-
-    pre_grad_own, *summed = tie(pre_grad_own, *[item for part in back_parts for item in part])
-    dconv, dheads = [sum(summed[at::2]) for at in range(2)]
+    small_grads = [item for each in back_parts for item in each]
+    two = width > 256
+    if two:
+        keep, send = weight_grad(normed, dval, dp, dp_me, skipped=1)
+        line, part = start_sum(keep, send, dp)
+        pre_grad_own, *rests = tie(pre_grad_own, *received[0], *part)
+        received[0], part = rests[: nt - 1], rests[nt - 1 :]
+        crossing = middle_swaps(part, dp)
+    dconv, dheads = [sum(small_grads[at::2]) for at in range(2)]
     conv_grad = lax.dynamic_update_slice(
         jnp.pad(dconv[:kernel_rows, width:], ((0, 0), (DI, 0))),
         dconv[:kernel_rows, :width],
@@ -950,11 +957,20 @@
     )
     for stage, (axis, size, distance) in enumerate(sum_stages(dp, nt)):
         vector = vector + swap(vector, axis, size, distance)
-        if stage == 1 and len(parts) > 1:
-            vector, *fars[1] = tie(vector, *fars[1])
-            value_sums.append(high_sum(blocks[1], fars[1]))
-        if stage == 2:
-            vector, *received[1] = tie(vector, *received[1])
+        if stage == 0:
+            vector, *fars[0] = tie(vector, *fars[0])
+            value_sums = [high_sum(blocks[0], fars[0])]
+        if stage == 1 and two:
+            vector, *rests = tie(vector, *received[1], *crossing)
+            received[1], crossing = rests[: nt - 1], rests[nt - 1 :]
+            block, far = middle_sum(line, crossing)
+            value_sums.append(high_sum(block, high_swaps(far, dp)))
+    shared_sum = value_sums[0][:, 256:].reshape(nt, shared_rows, common_width)
+    shared_mine = lax.dynamic_index_in_dim(shared_sum, t_rank, 0, False)
+    for d in range(1, nt):
+        piece = lax.dynamic_index_in_dim(shared_sum, t_rank ^ d, 0, False)
+        shared_mine = shared_mine + swap(piece, "tensor", nt, d)
+    shared_part = shared_mine[:, : 2 * N + H]
     value_part = jnp.concatenate([value_sums[0][:, :256]] + value_sums[1:], axis=1)
     conv_size = kernel_rows * (DI + 2 * N)
     place = d_rank * nt + t_rank

time: 275 us -> 291 us (1.058)
  waiting for transfers between devices: 39.6 us -> 64.7 us
  local copies, waits for them, and re-layouts: 44.5 us -> 28.7 us
  Pallas kernels: 94.3 us -> 104 us
  other arithmetic: 34.6 us -> 27.1 us
  starting transfers between devices: 56 us -> 60 us
    ppermute x48 -> x49, waiting for transfers between devices: 39.6 us -> 64.7 us  [swap(): return lax.ppermute(value, axis, [(i, i ^ distance) for i in range(size)])]
    pallas_call x6, Pallas kernels: 56.2 us -> 66.5 us  [the longest x3 37.8 us: shards(): call(functools.partial(scan_back_kernel, heads_here), (count,), [rows(CHU...]
    unnamed x129 -> x128, local copies, waits for them, and re-layouts: 27.8 us -> 21.3 us
    ppermute x48 -> x49, starting transfers between devices: 56 us -> 60 us  [swap(): return lax.ppermute(value, axis, [(i, i ^ distance) for i in range(size)])]
    reshape x4 -> x1, local copies, waits for them, and re-layouts: 3.38 us -> 0.01 us  [shards(): flat = jnp.pad(flat, (0, 16 * 256 - flat.size)).reshape(16, 256)]
  transfers between devices with their start and end apart: 48 -> 49, of which waited for: 17 -> 20; matrix products, arithmetic and copies ran while one was open for 18% -> 10% of each run, Pallas kernels for 23% -> 26%
where the time goes in v5:
time: 291 us; the launch traced here: 287 us
  Pallas kernels  104 us (36%)
  waiting for transfers between devices  64.7 us (22%)
  starting transfers between devices  60 us (21%)
  local copies, waits for them, and re-layouts  28.7 us (10%)
  other arithmetic  27.1 us (9%)
    ppermute x49, waiting for transfers between devices, swap(): return lax.ppermute(value, axis, [(i, i ^ distance) for i in range(size)])  64.7 us
    ppermute x49, starting transfers between devices, swap(): return lax.ppermute(value, axis, [(i, i ^ distance) for i in range(size)])  60 us
    pallas_call x3, Pallas kernels, shards(): call(functools.partial(scan_back_kernel, heads_here), (count,), [rows(CHU...  37.8 us
    pallas_call x1, Pallas kernels, shards(): call(functools.partial(scan_kernel, heads_here), (steps,), [rows(wide, D,...  26.4 us
    unnamed x128, local copies, waits for them, and re-layouts  21.3 us
    pallas_call x3, Pallas kernels, weight_grad(): call(functools.partial(weight_grad_kernel, dp), (width // 256,), [whole((...  12.3 us
    pallas_call x2, Pallas kernels, input_grad(): call(input_grad_kernel, (count * per_piece,), [rel_rows(width, offset), r...  7.44 us
    pallas_call x1, Pallas kernels, shards(): call(norm_kernel, (length // band,), [rel_rows(width), rel_rows(width), r...  6.63 us
  transfers between devices with their start and end apart: 49, of which 20 were waited for; matrix products, arithmetic and copies ran while one was open for 10% of the time, Pallas kernels for 26%

profile of v5, /device:TPU:0, one launch (start us, length us, event | category | flops | bytes accessed | tf_op | source)
XLA Modules:
  0.0 287.0 jit_solution(10314613048599843010)
XLA Ops:
  1.9 3.1 %collective-permute-start.1 = (bf16[48,1024]{1,0:T(8,128)(2,1)S(1)}, bf16[48,1024]{1,0:T(8,128)(2,1)S(1)}, u32[]{:S(2)}, u32[]{:S(2)}) collective-permute-start(bf16[48,1024]{1,0:T(8,128)(2,1)S(1)} %get-tuple-element.291), channel_id=1, source_target_pairs={{0,8},{2,10},{4,12},{6,14},{8,0},{10,2},{12,4},{14,6},{16,24},{18,... | collective-permute-start | bytes 294920 | tf_op jit(solution)/shard_map/ppermute | solution.py:48
  5.0 2.6 collective-permute-start.2
  23.9 2.3 collective-permute-done.5
  33.1 5.6 %collective-permute-done.7 = bf16[4,48,1024]{2,1,0:T(8,128)(2,1)S(1)} collective-permute-done((bf16[4,48,1024]{2,1,0:T(8,128)(2,1)S(1)}, bf16[4,48,1024]{2,1,0:T(8,128)(2,1)S(1)}, u32[]{:S(2)}, u32[]{:S(2)}) %collective-permute-start.7) | collective-permute-done | bytes 393248 | tf_op jit(solution)/shard_map/ppermute | solution.py:48
  44.8 3.6 %collective-permute-start.15 = (bf16[128,1024]{1,0:T(8,128)(2,1)S(1)}, bf16[128,1024]{1,0:T(8,128)(2,1)S(1)}, u32[]{:S(2)}, u32[]{:S(2)}) collective-permute-start(bf16[128,1024]{1,0:T(8,128)(2,1)S(1)} %pad_maximum_fusion.6), channel_id=1, source_target_pairs={{0,24},{2,26},{4,28},{6,30},{8,16},{10,18},{12,20},{14,22},{16,8},... | collective-permute-start | bytes 786440 | tf_op jit(solution)/shard_map/ppermute | solution.py:48
  49.0 6.2 %collective-permute-done.15 = bf16[128,1024]{1,0:T(8,128)(2,1)S(1)} collective-permute-done((bf16[128,1024]{1,0:T(8,128)(2,1)S(1)}, bf16[128,1024]{1,0:T(8,128)(2,1)S(1)}, u32[]{:S(2)}, u32[]{:S(2)}) %collective-permute-start.15) | collective-permute-done | bytes 262176 | tf_op jit(solution)/shard_map/ppermute | solution.py:48
  62.1 6.5 %collective-permute-done.16 = bf16[256,1024]{1,0:T(8,128)(2,1)} collective-permute-done((bf16[256,1024]{1,0:T(8,128)(2,1)}, bf16[256,1024]{1,0:T(8,128)(2,1)}, u32[]{:S(2)}, u32[]{:S(2)}) %collective-permute-start.16) | collective-permute-done | bytes 524320 | tf_op jit(solution)/shard_map/ppermute | solution.py:48
  73.3 26.4 %shard_map.357 = (bf16[1024,1024]{1,0:T(8,128)(2,1)S(1)}, f32[1024,1280]{1,0:T(8,128)}, f32[1024,1280]{1,0:T(8,128)}, bf16[1024,1280]{1,0:T(8,128)(2,1)}, f32[10...) custom-call(s32[2]{0:T(128)S(1)} %pad_add_fusion.rank, bf16[512,1024]{1,0:T(8,128)(2,1)S(1)} %copy-done.5, ...), custom_call_target="tpu_custom_call" | custom-call | flops 285212672 | bytes 3014656 | tf_op jit(solution)/shard_map/pallas_call | solution.py:730
  104.4 2.9 collective-permute-done.18.refs_1_
  107.6 6.6 %shard_map.359 = (f32[1024,1024]{1,0:T(8,128)S(1)}, f32[1024,1024]{1,0:T(8,128)S(1)}, bf16[1024,1024]{1,0:T(8,128)(2,1)S(1)}, f32[8,1024]{1,0:T(8,128)S(1)}) custom-call(s32[1]{0:T(128)} %bitcast.rank, bf16[1024,1024]{1,0:T(8,128)(2,1)S(1)} %get-tuple-element.153.normed.lhs, bf16[512,1024]{1,0:T(8,128)(2,1)S(1)} %copy-done.15, ...), custom_call_target="tpu_custom_call" | custom-call | flops 268435456 | bytes 1314816 | tf_op jit(solution)/shard_map/pallas_call | solution.py:767
  116.0 2.2 collective-permute-done.19
  118.1 6.6 %shard_map.360 = (bf16[1024,1024]{1,0:T(8,128)(2,1)S(1)}, bf16[1024,1024]{1,0:T(8,128)(2,1)S(1)}, bf16[1024,1024]{1,0:T(8,128)(2,1)S(1)}, bf16[1024,1024]{1,0:T(8,128)(2,1)S(1)}, f32[1,1024]{1,0:T(1,128)S(1)}) custom-call(s32[1]{0:T(128)} %bitcast.rank, f32[1024,1024]{1,0:T(8,128)S(1)} %get-tuple-element.160.gate_r, ...), custom_call_target="tpu_custom_call" | custom-call | flops 134217728 | bytes 1049088 | tf_op jit(solution)/shard_map/pallas_call | solution.py:796
  124.8 4.3 %shard_map.361 = (bf16[8,64,1024]{2,1,0:T(8,128)(2,1)S(1)}, bf16[8,64,1024]{2,1,0:T(8,128)(2,1)S(1)}) custom-call(s32[1]{0:T(128)} %bitcast.12.me, bf16[1024,1024]{1,0:T(8,128)(2,1)S(1)} %get-tuple-element.165.lhs, bf16[1024,1024]{1,0:T(8,128)(2,1)S(1)} %get-tuple-element.166.rhs), custom_call_target="tpu_custom_call" | custom-call | flops 134217728 | bytes 262144 | tf_op jit(solution)/shard_map/pallas_call | solution.py:487
  129.1 4.5 %shard_map.362 = (bf16[8,64,1024]{2,1,0:T(8,128)(2,1)S(1)}, bf16[8,64,1024]{2,1,0:T(8,128)(2,1)S(1)}) custom-call(s32[1]{0:T(128)} %bitcast.12.me, bf16[1024,1024]{1,0:T(8,128)(2,1)S(1)} %get-tuple-element.153.normed.lhs, bf16[1024,1024]{1,0:T(8,128)(2,1)S(1)} %get-tuple-element.206.rhs.dgate), custom_call_target="tpu_custom_call" | custom-call | flops 134217728 | bytes 262144 | tf_op jit(solution)/shard_map/pallas_call | solution.py:487
  142.6 13.5 %shard_map.363 = (bf16[1024,1024]{1,0:T(8,128)(2,1)S(1)}, f32[1024,384]{1,0:T(8,128)S(1)}, f32[8,1280]{1,0:T(8,128)S(1)}, f32[8,128]{1,0:T(8,128)S(1)}, f32[128,...) custom-call(s32[1]{0:T(128)} %bitcast.rank, bf16[1024,1024]{1,0:T(8,128)(2,1)} %copy-done.8, ...), custom_call_target="tpu_custom_call" | custom-call | flops 94371840 | bytes 535552 | tf_op jit(solution)/shard_map/pallas_call | solution.py:835
  161.8 13.5 %shard_map.364 = (bf16[1024,1024]{1,0:T(8,128)(2,1)S(1)}, f32[1024,384]{1,0:T(8,128)S(1)}, f32[8,1280]{1,0:T(8,128)S(1)}, f32[8,128]{1,0:T(8,128)S(1)}, f32[128,...) custom-call(s32[1]{0:T(128)} %bitcast.rank, ...), custom_call_target="tpu_custom_call", output_to_operand_aliasing={{0}: (17, {}), {1}: (18, {})} | custom-call | flops 94371840 | bytes 535552 | tf_op jit(solution)/shard_map/pallas_call | solution.py:835
  178.2 3.0 %collective-permute-start.29 = (bf16[64,1024]{1,0:T(8,128)(2,1)S(1)}, bf16[64,1024]{1,0:T(8,128)(2,1)S(1)}, u32[]{:S(2)}, u32[]{:S(2)}) collective-permute-start(bf16[64,1024]{1,0:T(8,128)(2,1)S(1)} %get-tuple-element.279), channel_id=1, source_target_pairs={{0,16},{2,18},{4,20},{6,22},{8,24},{10,26},{12,28},{14,30},{16,0},... | collective-permute-start | bytes 393224 | tf_op jit(solution)/shard_map/ppermute | solution.py:48
  182.1 10.8 %shard_map.365 = (bf16[1024,1024]{1,0:T(8,128)(2,1)S(1)}, f32[1024,384]{1,0:T(8,128)S(1)}, f32[8,1280]{1,0:T(8,128)S(1)}, f32[8,128]{1,0:T(8,128)S(1)}, f32[128,...) custom-call(s32[1]{0:T(128)} %bitcast.rank, ...), custom_call_target="tpu_custom_call", output_to_operand_aliasing={{0}: (17, {}), {1}: (18, {})} | custom-call | flops 62914560 | bytes 535552 | tf_op jit(solution)/shard_map/pallas_call | solution.py:835
  193.0 4.8 %shard_map.366 = (bf16[8,64,640]{2,1,0:T(8,128)(2,1)S(1)}, bf16[8,64,640]{2,1,0:T(8,128)(2,1)}) custom-call(s32[1]{0:T(128)} %bitcast.12.me, bf16[1024,1024]{1,0:T(8,128)(2,1)S(1)} %get-tuple-element.153.normed.lhs, bf16[1024,1024]{1,0:T(8,128)(2,1)S(1)} %get-tuple-element.212.dval.rhs, f32[1024,384]{1,0:T(8,128)S(1)} %get-tuple-element.201.dcommon), custom_call_target="tpu_custom_call" | custom-call | flops 134217728 | bytes 163840 | tf_op jit(solution)/shard_map/pallas_call | solution.py:526
  198.8 2.3 collective-permute-done.31
  212.4 3.7 %shard_map.367 = (bf16[512,1024]{1,0:T(8,128)(2,1)S(1)}, f32[1,1024]{1,0:T(1,128)S(1)}) custom-call(s32[1]{0:T(128)} %bitcast.rank, bf16[1024,1024]{1,0:T(8,128)(2,1)S(1)} %copy-done.12, bf16[1024,1024]{1,0:T(8,128)(2,1)S(1)} %get-tuple-element.212.dval.rhs, f32[1024,384]{1,0:T(8,128)S(1)} %copy-done.2, bf16[512,1024]{1,0:T(8,128)(2,1)S(1)} %copy-done.22, ...), custom_call_target="tpu_custom_call" | custom-call | flops 184549376 | bytes 131584 | tf_op jit(solution)/shard_map/pallas_call | solution.py:900
  216.1 3.7 %shard_map.368 = (f32[512,1024]{1,0:T(8,128)S(1)}, f32[1,1024]{1,0:T(1,128)S(1)}) custom-call(s32[1]{0:T(128)} %bitcast.rank, bf16[1024,1024]{1,0:T(8,128)(2,1)S(1)} %copy-done.12, bf16[1024,1024]{1,0:T(8,128)(2,1)S(1)} %get-tuple-element.212.dval.rhs, f32[1024,384]{1,0:T(8,128)S(1)} %copy-done.2, bf16[512,1024]{1,0:T(8,128)(2,1)S(1)} %copy-done.5, ...), custom_call_target="tpu_custom_call" | custom-call | flops 184549376 | bytes 262656 | tf_op jit(solution)/shard_map/pallas_call | solution.py:900
  219.9 3.5 %shard_map.369 = (bf16[8,64,768]{2,1,0:T(8,128)(2,1)S(1)}, bf16[8,64,768]{2,1,0:T(8,128)(2,1)S(1)}) custom-call(s32[1]{0:T(128)} %bitcast.12.me, bf16[1024,1024]{1,0:T(8,128)(2,1)S(1)} %copy-done.4, bf16[1024,1024]{1,0:T(8,128)(2,1)S(1)} %get-tuple-element.212.dval.rhs), custom_call_target="tpu_custom_call" | custom-call | flops 100663296 | bytes 196608 | tf_op jit(solution)/shard_map/pallas_call | solution.py:487
  229.2 11.3 %collective-permute-done.33 = bf16[256,1024]{1,0:T(8,128)(2,1)S(1)} collective-permute-done((bf16[256,1024]{1,0:T(8,128)(2,1)S(1)}, bf16[256,1024]{1,0:T(8,128)(2,1)S(1)}, u32[]{:S(2)}, u32[]{:S(2)}) %collective-permute-start.33) | collective-permute-done | bytes 524320 | tf_op jit(solution)/shard_map/ppermute | solution.py:48
  241.3 3.8 %collective-permute-start.37 = (bf16[64,640]{1,0:T(8,128)(2,1)S(1)}, bf16[64,640]{1,0:T(8,128)(2,1)S(1)}, u32[]{:S(2)}, u32[]{:S(2)}) collective-permute-start(bf16[64,640]{1,0:T(8,128)(2,1)S(1)} %get-tuple-element.288), channel_id=1, source_target_pairs={{0,16},{2,18},{4,20},{6,22},{8,24},{10,26},{12,28},{14,30},{16,0},... | collective-permute-start | bytes 245768 | tf_op jit(solution)/shard_map/ppermute | solution.py:48
  245.5 7.1 %collective-permute-done.35 = f32[1,14688]{1,0:T(1,128)S(1)} collective-permute-done((f32[1,14688]{1,0:T(1,128)S(1)}, f32[1,14688]{1,0:T(1,128)S(1)}, u32[]{:S(2)}, u32[]{:S(2)}) %collective-permute-start.35) | collective-permute-done | bytes 58784 | tf_op jit(solution)/shard_map/ppermute | solution.py:48
  255.9 2.6 collective-permute-done.45
  259.3 4.0 %collective-permute-done.41 = bf16[4,64,768]{2,1,0:T(8,128)(2,1)S(1)} collective-permute-done((bf16[4,64,768]{2,1,0:T(8,128)(2,1)S(1)}, bf16[4,64,768]{2,1,0:T(8,128)(2,1)S(1)}, u32[]{:S(2)}, u32[]{:S(2)}) %collective-permute-start.41) | collective-permute-done | bytes 393248 | tf_op jit(solution)/shard_map/ppermute | solution.py:48
  265.1 3.8 %collective-permute-start.43 = (bf16[64,768]{1,0:T(8,128)(2,1)S(1)}, bf16[64,768]{1,0:T(8,128)(2,1)S(1)}, u32[]{:S(2)}, u32[]{:S(2)}) collective-permute-start(bf16[64,768]{1,0:T(8,128)(2,1)S(1)} %get-tuple-element.286), channel_id=1, source_target_pairs={{0,16},{2,18},{4,20},{6,22},{8,24},{10,26},{12,28},{14,30},{16,0},... | collective-permute-start | bytes 294920 | tf_op jit(solution)/shard_map/ppermute | solution.py:48
  271.6 2.7 fusion.6
  275.6 3.0 %collective-permute-done.47 = f32[1,14688]{1,0:T(1,128)S(1)} collective-permute-done((f32[1,14688]{1,0:T(1,128)S(1)}, f32[1,14688]{1,0:T(1,128)S(1)}, u32[]{:S(2)}, u32[]{:S(2)}) %collective-permute-start.47) | collective-permute-done | bytes 58784 | tf_op jit(solution)/shard_map/ppermute | solution.py:48
  278.7 2.3 collective-permute-start.48
  (326 shorter events, 102.1 us)
Async XLA Ops:
  1.9 15.4 %collective-permute-start.1 = (bf16[48,1024]{1,0:T(8,128)(2,1)S(1)}, bf16[48,1024]{1,0:T(8,128)(2,1)S(1)}, u32[]{:S(2)}, u32[]{:S(2)}) collective-permute-start(bf16[48,1024]{1,0:T(8,128)(2,1)S(1)} %get-tuple-element.291), channel_id=1, source_target_pairs={{0,8},{2,10},{4,12},{6,14},{8,0},{10,2},{12,4},{14,6},{16,24},{18,... | collective-permute-start | bytes 294920 | tf_op jit(solution)/shard_map/ppermute | solution.py:48
  5.0 12.3 %collective-permute-start.2 = (bf16[48,1024]{1,0:T(8,128)(2,1)S(1)}, bf16[48,1024]{1,0:T(8,128)(2,1)S(1)}, u32[]{:S(2)}, u32[]{:S(2)}) collective-permute-start(bf16[48,1024]{1,0:T(8,128)(2,1)S(1)} %get-tuple-element.291), channel_id=1, source_target_pairs={{0,16},{2,18},{4,20},{6,22},{8,24},{10,26},{12,28},{14,30},{16,0},... | collective-permute-start | bytes 294920 | tf_op jit(solution)/shard_map/ppermute | solution.py:48
  7.5 9.7 %collective-permute-start.3 = (bf16[48,1024]{1,0:T(8,128)(2,1)S(1)}, bf16[48,1024]{1,0:T(8,128)(2,1)S(1)}, u32[]{:S(2)}, u32[]{:S(2)}) collective-permute-start(bf16[48,1024]{1,0:T(8,128)(2,1)S(1)} %get-tuple-element.291), channel_id=1, source_target_pairs={{0,24},{2,26},{4,28},{6,30},{8,16},{10,18},{12,20},{14,22},{16,8},... | collective-permute-start | bytes 294920 | tf_op jit(solution)/shard_map/ppermute | solution.py:48
  15.5 23.5 %collective-permute-start.8 = (bf16[512,1024]{1,0:T(8,128)(2,1)S(1)}, bf16[512,1024]{1,0:T(8,128)(2,1)S(1)}, u32[]{:S(2)}, u32[]{:S(2)}) collective-permute-start(bf16[512,1024]{1,0:T(8,128)(2,1)S(1)} %copy-done.5), channel_id=1, source_target_pairs={{0,1},{1,0},{2,3},{3,2},{4,5},{5,4},{6,7},{7,6},{8,9},{9,8},{10,11... | collective-permute-start | bytes 3145736 | tf_op jit(solution)/shard_map/ppermute | solution.py:48
  21.6 10.7 %collective-permute-start.9 = (bf16[4,48,1024]{2,1,0:T(8,128)(2,1)S(1)}, bf16[4,48,1024]{2,1,0:T(8,128)(2,1)S(1)}, u32[]{:S(2)}, u32[]{:S(2)}) collective-permute-start(bf16[4,48,1024]{2,1,0:T(8,128)(2,1)S(1)} %pad_maximum_fusion.4), channel_id=1, source_target_pairs={{0,4},{2,6},{4,0},{6,2},{8,12},{10,14},{12,8},{14,10},{16,20},{18,... | collective-permute-start | bytes 1179656 | tf_op jit(solution)/shard_map/ppermute | solution.py:48
  27.0 17.4 %collective-permute-start.13 = (bf16[128,1024]{1,0:T(8,128)(2,1)S(1)}, bf16[128,1024]{1,0:T(8,128)(2,1)S(1)}, u32[]{:S(2)}, u32[]{:S(2)}) collective-permute-start(bf16[128,1024]{1,0:T(8,128)(2,1)S(1)} %pad_maximum_fusion.6), channel_id=1, source_target_pairs={{0,8},{2,10},{4,12},{6,14},{8,0},{10,2},{12,4},{14,6},{16,24},{18,... | collective-permute-start | bytes 786440 | tf_op jit(solution)/shard_map/ppermute | solution.py:48
  27.9 16.9 %collective-permute-start.14 = (bf16[128,1024]{1,0:T(8,128)(2,1)S(1)}, bf16[128,1024]{1,0:T(8,128)(2,1)S(1)}, u32[]{:S(2)}, u32[]{:S(2)}) collective-permute-start(bf16[128,1024]{1,0:T(8,128)(2,1)S(1)} %pad_maximum_fusion.6), channel_id=1, source_target_pairs={{0,16},{2,18},{4,20},{6,22},{8,24},{10,26},{12,28},{14,30},{16,0},... | collective-permute-start | bytes 786440 | tf_op jit(solution)/shard_map/ppermute | solution.py:48
  33.0 24.2 %collective-permute-start.10 = (bf16[8,48,1024]{2,1,0:T(8,128)(2,1)}, bf16[8,48,1024]{2,1,0:T(8,128)(2,1)}, u32[]{:S(2)}, u32[]{:S(2)}) collective-permute-start(bf16[8,48,1024]{2,1,0:T(8,128)(2,1)} %constant_dynamic-update-slice_fusion.refs_0_), channel_id=1, source_target_pairs={{0,2},{2,0},{4,6},{6,4},{8,10},{10,8},{12,14},{14,12},{16,18},{18,... | collective-permute-start | bytes 2359304 | tf_op jit(solution)/shard_map/ppermute | solution.py:48
  41.5 16.1 %collective-permute-start.11 = (bf16[8,48,1024]{2,1,0:T(8,128)(2,1)}, bf16[8,48,1024]{2,1,0:T(8,128)(2,1)}, u32[]{:S(2)}, u32[]{:S(2)}) collective-permute-start(bf16[8,48,1024]{2,1,0:T(8,128)(2,1)} %constant_dynamic-update-slice_fusion.2.refs_1_), channel_id=1, source_target_pairs={{0,2},{2,0},{4,6},{6,4},{8,10},{10,8},{12,14},{14,12},{16,18},{18,... | collective-permute-start | bytes 2359304 | tf_op jit(solution)/shard_map/ppermute | solution.py:48
  42.6 15.0 %collective-permute-start.12 = (bf16[256,1024]{1,0:T(8,128)(2,1)}, bf16[256,1024]{1,0:T(8,128)(2,1)}, u32[]{:S(2)}, u32[]{:S(2)}) collective-permute-start(bf16[256,1024]{1,0:T(8,128)(2,1)} %get-tuple-element.277), channel_id=1, source_target_pairs={{0,1},{1,0},{2,3},{3,2},{4,5},{5,4},{6,7},{7,6},{8,9},{9,8},{10,11... | collective-permute-start | bytes 1572872 | tf_op jit(solution)/shard_map/ppermute | solution.py:48
  44.4 24.1 %collective-permute-start.16 = (bf16[256,1024]{1,0:T(8,128)(2,1)}, bf16[256,1024]{1,0:T(8,128)(2,1)}, u32[]{:S(2)}, u32[]{:S(2)}) collective-permute-start(bf16[256,1024]{1,0:T(8,128)(2,1)} %get-tuple-element.276), channel_id=1, source_target_pairs={{0,1},{1,0},{2,3},{3,2},{4,5},{5,4},{6,7},{7,6},{8,9},{9,8},{10,11... | collective-permute-start | bytes 1572872 | tf_op jit(solution)/shard_map/ppermute | solution.py:48
  44.8 10.3 %collective-permute-start.15 = (bf16[128,1024]{1,0:T(8,128)(2,1)S(1)}, bf16[128,1024]{1,0:T(8,128)(2,1)S(1)}, u32[]{:S(2)}, u32[]{:S(2)}) collective-permute-start(bf16[128,1024]{1,0:T(8,128)(2,1)S(1)} %pad_maximum_fusion.6), channel_id=1, source_target_pairs={{0,24},{2,26},{4,28},{6,30},{8,16},{10,18},{12,20},{14,22},{16,8},... | collective-permute-start | bytes 786440 | tf_op jit(solution)/shard_map/ppermute | solution.py:48
  68.6 33.1 %collective-permute-start.17 = (bf16[4,128,1024]{2,1,0:T(8,128)(2,1)}, bf16[4,128,1024]{2,1,0:T(8,128)(2,1)}, u32[]{:S(2)}, u32[]{:S(2)}) collective-permute-start(bf16[4,128,1024]{2,1,0:T(8,128)(2,1)} %pad_maximum_fusion), channel_id=1, source_target_pairs={{0,4},{2,6},{4,0},{6,2},{8,12},{10,14},{12,8},{14,10},{16,20},{18,... | collective-permute-start | bytes 3145736 | tf_op jit(solution)/shard_map/ppermute | solution.py:48
  138.3 17.8 %collective-permute-start.22 = (bf16[4,64,1024]{2,1,0:T(8,128)(2,1)S(1)}, bf16[4,64,1024]{2,1,0:T(8,128)(2,1)S(1)}, u32[]{:S(2)}, u32[]{:S(2)}) collective-permute-start(bf16[4,64,1024]{2,1,0:T(8,128)(2,1)S(1)} %get-tuple-element.181), channel_id=1, source_target_pairs={{0,4},{2,6},{4,0},{6,2},{8,12},{10,14},{12,8},{14,10},{16,20},{18,... | collective-permute-start | bytes 1572872 | tf_op jit(solution)/shard_map/ppermute | solution.py:48
  138.9 36.3 %collective-permute-start.23 = (bf16[512,1024]{1,0:T(8,128)(2,1)S(1)}, bf16[512,1024]{1,0:T(8,128)(2,1)S(1)}, u32[]{:S(2)}, u32[]{:S(2)}) collective-permute-start(bf16[512,1024]{1,0:T(8,128)(2,1)S(1)} %slice.253), channel_id=1, source_target_pairs={{0,1},{1,0},{2,3},{3,2},{4,5},{5,4},{6,7},{7,6},{8,9},{9,8},{10,11... | collective-permute-start | bytes 3145736 | tf_op jit(solution)/shard_map/ppermute | solution.py:48
  140.9 34.3 %collective-permute-start.24 = (bf16[4,64,1024]{2,1,0:T(8,128)(2,1)S(1)}, bf16[4,64,1024]{2,1,0:T(8,128)(2,1)S(1)}, u32[]{:S(2)}, u32[]{:S(2)}) collective-permute-start(bf16[4,64,1024]{2,1,0:T(8,128)(2,1)S(1)} %get-tuple-element.188), channel_id=1, source_target_pairs={{0,4},{2,6},{4,0},{6,2},{8,12},{10,14},{12,8},{14,10},{16,20},{18,... | collective-permute-start | bytes 1572872 | tf_op jit(solution)/shard_map/ppermute | solution.py:48
  157.3 18.0 %collective-permute-start.25 = (bf16[64,1024]{1,0:T(8,128)(2,1)S(1)}, bf16[64,1024]{1,0:T(8,128)(2,1)S(1)}, u32[]{:S(2)}, u32[]{:S(2)}) collective-permute-start(bf16[64,1024]{1,0:T(8,128)(2,1)S(1)} %get-tuple-element.283), channel_id=1, source_target_pairs={{0,8},{2,10},{4,12},{6,14},{8,0},{10,2},{12,4},{14,6},{16,24},{18,... | collective-permute-start | bytes 393224 | tf_op jit(solution)/shard_map/ppermute | solution.py:48
  159.1 16.2 %collective-permute-start.26 = (bf16[64,1024]{1,0:T(8,128)(2,1)S(1)}, bf16[64,1024]{1,0:T(8,128)(2,1)S(1)}, u32[]{:S(2)}, u32[]{:S(2)}) collective-permute-start(bf16[64,1024]{1,0:T(8,128)(2,1)S(1)} %get-tuple-element.282), channel_id=1, source_target_pairs={{0,16},{2,18},{4,20},{6,22},{8,24},{10,26},{12,28},{14,30},{16,0},... | collective-permute-start | bytes 393224 | tf_op jit(solution)/shard_map/ppermute | solution.py:48
  161.2 14.2 %collective-permute-start.27 = (bf16[64,1024]{1,0:T(8,128)(2,1)S(1)}, bf16[64,1024]{1,0:T(8,128)(2,1)S(1)}, u32[]{:S(2)}, u32[]{:S(2)}) collective-permute-start(bf16[64,1024]{1,0:T(8,128)(2,1)S(1)} %get-tuple-element.281), channel_id=1, source_target_pairs={{0,24},{2,26},{4,28},{6,30},{8,16},{10,18},{12,20},{14,22},{16,8},... | collective-permute-start | bytes 393224 | tf_op jit(solution)/shard_map/ppermute | solution.py:48
  177.3 15.6 %collective-permute-start.28 = (bf16[64,1024]{1,0:T(8,128)(2,1)S(1)}, bf16[64,1024]{1,0:T(8,128)(2,1)S(1)}, u32[]{:S(2)}, u32[]{:S(2)}) collective-permute-start(bf16[64,1024]{1,0:T(8,128)(2,1)S(1)} %get-tuple-element.280), channel_id=1, source_target_pairs={{0,8},{2,10},{4,12},{6,14},{8,0},{10,2},{12,4},{14,6},{16,24},{18,... | collective-permute-start | bytes 393224 | tf_op jit(solution)/shard_map/ppermute | solution.py:48
  178.2 14.7 %collective-permute-start.29 = (bf16[64,1024]{1,0:T(8,128)(2,1)S(1)}, bf16[64,1024]{1,0:T(8,128)(2,1)S(1)}, u32[]{:S(2)}, u32[]{:S(2)}) collective-permute-start(bf16[64,1024]{1,0:T(8,128)(2,1)S(1)} %get-tuple-element.279), channel_id=1, source_target_pairs={{0,16},{2,18},{4,20},{6,22},{8,24},{10,26},{12,28},{14,30},{16,0},... | collective-permute-start | bytes 393224 | tf_op jit(solution)/shard_map/ppermute | solution.py:48
  181.2 11.8 %collective-permute-start.30 = (bf16[64,1024]{1,0:T(8,128)(2,1)S(1)}, bf16[64,1024]{1,0:T(8,128)(2,1)S(1)}, u32[]{:S(2)}, u32[]{:S(2)}) collective-permute-start(bf16[64,1024]{1,0:T(8,128)(2,1)S(1)} %get-tuple-element.278), channel_id=1, source_target_pairs={{0,24},{2,26},{4,28},{6,30},{8,16},{10,18},{12,20},{14,22},{16,8},... | collective-permute-start | bytes 393224 | tf_op jit(solution)/shard_map/ppermute | solution.py:48
  203.0 16.9 %collective-permute-start.32 = (bf16[4,64,640]{2,1,0:T(8,128)(2,1)}, bf16[4,64,640]{2,1,0:T(8,128)(2,1)}, u32[]{:S(2)}, u32[]{:S(2)}) collective-permute-start(bf16[4,64,640]{2,1,0:T(8,128)(2,1)} %add_convert_fusion.3), channel_id=1, source_target_pairs={{0,4},{2,6},{4,0},{6,2},{8,12},{10,14},{12,8},{14,10},{16,20},{18,... | collective-permute-start | bytes 983048 | tf_op jit(solution)/shard_map/ppermute | solution.py:48
  225.7 14.8 %collective-permute-start.33 = (bf16[256,1024]{1,0:T(8,128)(2,1)S(1)}, bf16[256,1024]{1,0:T(8,128)(2,1)S(1)}, u32[]{:S(2)}, u32[]{:S(2)}) collective-permute-start(bf16[256,1024]{1,0:T(8,128)(2,1)S(1)} %get-tuple-element.275), channel_id=1, source_target_pairs={{0,1},{1,0},{2,3},{3,2},{4,5},{5,4},{6,7},{7,6},{8,9},{9,8},{10,11... | collective-permute-start | bytes 1572872 | tf_op jit(solution)/shard_map/ppermute | solution.py:48
  226.2 33.1 %collective-permute-start.40 = (bf16[256,1024]{1,0:T(8,128)(2,1)S(1)}, bf16[256,1024]{1,0:T(8,128)(2,1)S(1)}, u32[]{:S(2)}, u32[]{:S(2)}) collective-permute-start(bf16[256,1024]{1,0:T(8,128)(2,1)S(1)} %get-tuple-element.274), channel_id=1, source_target_pairs={{0,1},{1,0},{2,3},{3,2},{4,5},{5,4},{6,7},{7,6},{8,9},{9,8},{10,11... | collective-permute-start | bytes 1572872 | tf_op jit(solution)/shard_map/ppermute | solution.py:48
  240.6 12.0 %collective-permute-start.35 = (f32[1,14688]{1,0:T(1,128)S(1)}, f32[1,14688]{1,0:T(1,128)S(1)}, u32[]{:S(2)}, u32[]{:S(2)}) collective-permute-start(f32[1,14688]{1,0:T(1,128)S(1)} %pad_maximum_fusion.8), channel_id=1, source_target_pairs={{0,1},{1,0},{2,3},{3,2},{4,5},{5,4},{6,7},{7,6},{8,9},{9,8},{10,11... | collective-permute-start | bytes 176264 | tf_op jit(solution)/shard_map/ppermute | solution.py:48
  241.1 13.1 %collective-permute-start.36 = (bf16[64,640]{1,0:T(8,128)(2,1)S(1)}, bf16[64,640]{1,0:T(8,128)(2,1)S(1)}, u32[]{:S(2)}, u32[]{:S(2)}) collective-permute-start(bf16[64,640]{1,0:T(8,128)(2,1)S(1)} %get-tuple-element.289), channel_id=1, source_target_pairs={{0,8},{2,10},{4,12},{6,14},{8,0},{10,2},{12,4},{14,6},{16,24},{18,... | collective-permute-start | bytes 245768 | tf_op jit(solution)/shard_map/ppermute | solution.py:48
  241.3 12.9 %collective-permute-start.37 = (bf16[64,640]{1,0:T(8,128)(2,1)S(1)}, bf16[64,640]{1,0:T(8,128)(2,1)S(1)}, u32[]{:S(2)}, u32[]{:S(2)}) collective-permute-start(bf16[64,640]{1,0:T(8,128)(2,1)S(1)} %get-tuple-element.288), channel_id=1, source_target_pairs={{0,16},{2,18},{4,20},{6,22},{8,24},{10,26},{12,28},{14,30},{16,0},... | collective-permute-start | bytes 245768 | tf_op jit(solution)/shard_map/ppermute | solution.py:48
  252.6 10.7 %collective-permute-start.41 = (bf16[4,64,768]{2,1,0:T(8,128)(2,1)S(1)}, bf16[4,64,768]{2,1,0:T(8,128)(2,1)S(1)}, u32[]{:S(2)}, u32[]{:S(2)}) collective-permute-start(bf16[4,64,768]{2,1,0:T(8,128)(2,1)S(1)} %add_convert_fusion.2), channel_id=1, source_target_pairs={{0,4},{2,6},{4,0},{6,2},{8,12},{10,14},{12,8},{14,10},{16,20},{18,... | collective-permute-start | bytes 1179656 | tf_op jit(solution)/shard_map/ppermute | solution.py:48
  263.3 11.0 %collective-permute-start.46 = (f32[1,14688]{1,0:T(1,128)S(1)}, f32[1,14688]{1,0:T(1,128)S(1)}, u32[]{:S(2)}, u32[]{:S(2)}) collective-permute-start(f32[1,14688]{1,0:T(1,128)S(1)} %add.325), channel_id=1, source_target_pairs={{0,4},{2,6},{4,0},{6,2},{8,12},{10,14},{12,8},{14,10},{16,20},{18,... | collective-permute-start | bytes 176264 | tf_op jit(solution)/shard_map/ppermute | solution.py:48
  265.0 9.4 %collective-permute-start.42 = (bf16[64,768]{1,0:T(8,128)(2,1)S(1)}, bf16[64,768]{1,0:T(8,128)(2,1)S(1)}, u32[]{:S(2)}, u32[]{:S(2)}) collective-permute-start(bf16[64,768]{1,0:T(8,128)(2,1)S(1)} %get-tuple-element.284), channel_id=1, source_target_pairs={{0,8},{2,10},{4,12},{6,14},{8,0},{10,2},{12,4},{14,6},{16,24},{18,... | collective-permute-start | bytes 294920 | tf_op jit(solution)/shard_map/ppermute | solution.py:48
  265.1 9.4 %collective-permute-start.43 = (bf16[64,768]{1,0:T(8,128)(2,1)S(1)}, bf16[64,768]{1,0:T(8,128)(2,1)S(1)}, u32[]{:S(2)}, u32[]{:S(2)}) collective-permute-start(bf16[64,768]{1,0:T(8,128)(2,1)S(1)} %get-tuple-element.286), channel_id=1, source_target_pairs={{0,16},{2,18},{4,20},{6,22},{8,24},{10,26},{12,28},{14,30},{16,0},... | collective-permute-start | bytes 294920 | tf_op jit(solution)/shard_map/ppermute | solution.py:48
  (79 other events, 698.1 us)

commit v6 on v5

--- a/solution.py
+++ b/solution.py
@@ -492,7 +492,7 @@
         [shape(half, block, width, dtype=bf16)] * 2,
         [pltpu.VMEM((depth, length), bf16), pltpu.VMEM((depth, 256), f32)],
         2 * length * width * depth,
-        16,
+        10,
         scalars=1,
     )(dp_rank, lhs, rhs)
 
@@ -538,7 +538,7 @@
             pltpu.VMEM((depth, extra), f32),
         ],
         2 * length * (width + 2 * extra) * depth,
-        24,
+        15,
         scalars=1,
     )(dp_rank, lhs, dval, dcommon)
 
@@ -619,8 +619,7 @@
             small_rows += 1
         small = jnp.pad(small, (0, small_rows * width - small.size)).reshape(small_rows, width)
     small_pair = over_tensor(small)
-    residual_now, small_pair = tie(residual, small_pair)
-    token_pieces = pieces_of(residual_now)
+    token_pieces = pieces_of(residual)
 
     block_rows = D // dp
     value_shard = jnp.concatenate([inner_proj[1].astype(bf16), small_pair], axis=0)
@@ -639,11 +638,8 @@
     parts, token_pieces = parts[:-nt], parts[-nt:]
     second_near = jnp.concatenate([second_line] + parts, axis=0)
     cotangent_now, *token_pieces = tie(cotangent, *token_pieces)
-    cot_cut = rows_here // 2
-    cot_early = [swap(cotangent_now[:cot_cut], "tensor", nt, d) for d in range(1, nt)]
-    cot_late = [swap(cotangent_now[cot_cut:], "tensor", nt, d) for d in range(1, nt)]
-    fars = [swap(first_near, "dp", dp, 1), swap(second_near, "dp", dp, 1)]
-    first_far, second_far, *cot_early = tie(*fars, *cot_early)
+    cot_pieces = pieces_of(cotangent_now)
+    first_far, second_far = swap(first_near, "dp", dp, 1), swap(second_near, "dp", dp, 1)
     full = slice(None)
     moves = [(0, block_rows, full, 0, 1, 0, 0)]
     dims = [(dp, block_rows, width)]
@@ -721,10 +717,7 @@
 
     steps = length // wide
     in_half = lambda i: i % (steps // 2)
-    value_w, other_line, *cot_late = tie(value_w, other_line, *cot_late)
-    cot_pieces = [cotangent] + [
-        jnp.concatenate([early, late], axis=0) for early, late in zip(cot_early, cot_late)
-    ]
+    value_w, other_line, *cot_pieces = tie(value_w, other_line, *cot_pieces)
     plane = plane_parts(other_line, dp)
     tok_rank, tok0, tok1 = halves(token_pieces)
     normed, chans, pre, mixed, ssd, entering, step_in = call(
@@ -750,7 +743,7 @@
             pltpu.VMEM((CHUNK, width), f32), pltpu.VMEM((2, CHUNK, width), bf16),
         ],
         length * (2 * D * (width + common_width) + 12 * width * CHUNK),
-        48,
+        22,
         scalars=1,
     )(jnp.concatenate([tok_rank, t_me]), tok0, tok1, pre_gain, value_w, shared_here, conv_here, skip, head_rows, aux, segr)
 
@@ -778,7 +771,7 @@
         ],
         [],
         4 * length * D * width,
-        24,
+        15,
         scalars=1,
     )(cot_rank, normed, cot0, cot1, aux, ssd, gate_w, outer_t, post_gain)
     distance = 1
@@ -808,7 +801,7 @@
         ],
         [],
         2 * length * D * width,
-        24,
+        15,
         scalars=1,
     )(t_me, gate, scaled_grad, ssd, sums, outer_t, post_gain)
     outer_keep, outer_send = weight_grad(returned, scaled, dp, dp_me)
@@ -863,7 +856,7 @@
                 pltpu.VMEM((8, width), f32),
             ],
             count * CHUNK * 30 * width * CHUNK,
-            48,
+            14,
             scalars=1,
             aliases={17: 0, 18: 1} if filled else None,
         )(
@@ -908,34 +901,40 @@
             [shape(count * rows_here, D, dtype=dtype), shape(1, D)],
             [],
             4 * count * rows_here * D * (width + common_width),
-            24,
+            13,
             scalars=1,
         )(t_me, dgate, dval, dcommon, positions, gate_w, value_w, shared_here)
 
     keep, send = value_grad(normed, dval, dcommon, dp, dp_me)
     line, part = start_sum(keep, send, dp)
-    dgate, *part = tie(dgate, *part)
-    crossing = middle_swaps(part, dp)
+    two = width > 256
+    lines, parts = [line], [part]
+    if two:
+        dval, *parts[0] = tie(dval, *parts[0])
+        keep, send = weight_grad(normed, dval, dp, dp_me, skipped=1)
+        line, part = start_sum(keep, send, dp)
+        lines.append(line)
+        parts.append(part)
+    each = len(part)
+    dgate, *flat = tie(dgate, *[item for part in parts for item in part])
+    crossing = [middle_swaps(flat[at : at + each], dp) for at in range(0, len(flat), each)]
     others = token_pieces[1] if nt == 2 else jnp.concatenate(token_pieces[1:], axis=0)
     sent, pre_grad_sent = input_grad(nt - 1, per_piece, bf16, others, dgate)
-    sent = sent.reshape(nt - 1, 2, rows_here // 2, D)
-    received = [
-        [swap(sent[d - 1, at], "tensor", nt, d) for d in range(1, nt)] for at in range(2)
-    ]
-    dgate, pre_grad_sent = tie(dgate, pre_grad_sent)
+    sent = sent.reshape(nt - 1, rows_here, D)
+    received = [swap(sent[d - 1], "tensor", nt, d) for d in range(1, nt)]
+    small_grads = [item for each_part in back_parts for item in each_part]
+    dgate, pre_grad_sent, *rests = tie(dgate, pre_grad_sent, *crossing[0], *small_grads)
+    crossing[0], small_grads = rests[:each], rests[each:]
+    block, far = middle_sum(lines[0], crossing[0])
+    blocks, fars = [block], [high_swaps(far, dp)]
     own, pre_grad_own = input_grad(1, 0, f32, residual, dgate)
-    dval, pre_grad_own, *crossing = tie(dval, pre_grad_own, *crossing)
-    block, far = middle_sum(line, crossing)
-    fars = [high_swaps(far, dp)]
-    blocks = [block]
-    small_grads = [item for each in back_parts for item in each]
-    two = width > 256
     if two:
-        keep, send = weight_grad(normed, dval, dp, dp_me, skipped=1)
-        line, part = start_sum(keep, send, dp)
-        pre_grad_own, *rests = tie(pre_grad_own, *received[0], *part)
-        received[0], part = rests[: nt - 1], rests[nt - 1 :]
-        crossing = middle_swaps(part, dp)
+        pre_grad_own, *rests = tie(pre_grad_own, *crossing[1], *fars[0])
+        crossing[1], fars[0] = rests[:each], rests[each:]
+        block, far = middle_sum(lines[1], crossing[1])
+        pre_grad_own, *far = tie(pre_grad_own, *far)
+        blocks.append(block)
+        fars.append(high_swaps(far, dp))
     dconv, dheads = [sum(small_grads[at::2]) for at in range(2)]
     conv_grad = lax.dynamic_update_slice(
         jnp.pad(dconv[:kernel_rows, width:], ((0, 0), (DI, 0))),
@@ -958,13 +957,12 @@
     for stage, (axis, size, distance) in enumerate(sum_stages(dp, nt)):
         vector = vector + swap(vector, axis, size, distance)
         if stage == 0:
-            vector, *fars[0] = tie(vector, *fars[0])
             value_sums = [high_sum(blocks[0], fars[0])]
+        if stage == 1:
+            vector, *received = tie(vector, *received)
         if stage == 1 and two:
-            vector, *rests = tie(vector, *received[1], *crossing)
-            received[1], crossing = rests[: nt - 1], rests[nt - 1 :]
-            block, far = middle_sum(line, crossing)
-            value_sums.append(high_sum(block, high_swaps(far, dp)))
+            vector, *fars[1] = tie(vector, *fars[1])
+            value_sums.append(high_sum(blocks[1], fars[1]))
     shared_sum = value_sums[0][:, 256:].reshape(nt, shared_rows, common_width)
     shared_mine = lax.dynamic_index_in_dim(shared_sum, t_rank, 0, False)
     for d in range(1, nt):
@@ -983,8 +981,8 @@
     )
 
     normed_grad = own
-    for low, high in zip(*received):
-        normed_grad = normed_grad + jnp.concatenate([low, high], axis=0).astype(f32)
+    for piece in received:
+        normed_grad = normed_grad + piece.astype(f32)
     inverse = lax.rsqrt(jnp.mean(tokens * tokens, axis=1, keepdims=True) + norm_epsilon)
     normal_tokens = tokens * inverse
     normal_grad = normed_grad * pre_gain

time: 291 us -> 270 us (0.928)
  waiting for transfers between devices: 64.7 us -> 51 us
  starting transfers between devices: 60 us -> 53.5 us
  other arithmetic: 27.1 us -> 32.8 us
  Pallas kernels: 104 us -> 98.4 us
    ppermute x49 -> x47, waiting for transfers between devices: 64.7 us -> 51 us  [swap(): return lax.ppermute(value, axis, [(i, i ^ distance) for i in range(size)])]
    ppermute x49 -> x47, starting transfers between devices: 60 us -> 53.5 us  [swap(): return lax.ppermute(value, axis, [(i, i ^ distance) for i in range(size)])]
    pallas_call x3, Pallas kernels: 37.8 us -> 33.2 us  [shards(): call(functools.partial(scan_back_kernel, heads_here), (count,), [rows(CHU...]
    pallas_call x1, Pallas kernels: 26.4 us -> 23.1 us  [shards(): call(functools.partial(scan_kernel, heads_here), (steps,), [rows(wide, D,...]
    unnamed x128 -> x140, local copies, waits for them, and re-layouts: 21.3 us -> 22.8 us
  transfers between devices with their start and end apart: 49 -> 47, of which waited for: 20 -> 16; matrix products, arithmetic and copies ran while one was open for 10% -> 12% of each run, Pallas kernels for 26% -> 25%
where the time goes in v6:
time: 270 us; the launch traced here: 266 us
  Pallas kernels  98.4 us (36%)
  starting transfers between devices  53.5 us (20%)
  waiting for transfers between devices  51 us (19%)
  other arithmetic  32.8 us (12%)
  local copies, waits for them, and re-layouts  28.2 us (10%)
    ppermute x47, starting transfers between devices, swap(): return lax.ppermute(value, axis, [(i, i ^ distance) for i in range(size)])  53.5 us
    ppermute x47, waiting for transfers between devices, swap(): return lax.ppermute(value, axis, [(i, i ^ distance) for i in range(size)])  51 us
    pallas_call x3, Pallas kernels, shards(): call(functools.partial(scan_back_kernel, heads_here), (count,), [rows(CHU...  33.2 us
    pallas_call x1, Pallas kernels, shards(): call(functools.partial(scan_kernel, heads_here), (steps,), [rows(wide, D,...  23.1 us
    unnamed x140, local copies, waits for them, and re-layouts  22.8 us
    pallas_call x3, Pallas kernels, weight_grad(): call(functools.partial(weight_grad_kernel, dp), (width // 256,), [whole((...  12.8 us
    pallas_call x1, Pallas kernels, shards(): call(gate_kernel, (steps,), [rows(wide, D), rows(wide, D, in_half), rows(...  8.42 us
    pallas_call x2, Pallas kernels, input_grad(): call(input_grad_kernel, (count * per_piece,), [rel_rows(width, offset), r...  8.35 us
  transfers between devices with their start and end apart: 47, of which 16 were waited for; matrix products, arithmetic and copies ran while one was open for 12% of the time, Pallas kernels for 25%

profile of v6, /device:TPU:0, one launch (start us, length us, event | category | flops | bytes accessed | tf_op | source)
XLA Modules:
  0.0 266.0 jit_solution(5101798645161661719)
XLA Ops:
  1.8 3.1 %collective-permute-start.1 = (bf16[48,1024]{1,0:T(8,128)(2,1)S(1)}, bf16[48,1024]{1,0:T(8,128)(2,1)S(1)}, u32[]{:S(2)}, u32[]{:S(2)}) collective-permute-start(bf16[48,1024]{1,0:T(8,128)(2,1)S(1)} %get-tuple-element.303), channel_id=1, source_target_pairs={{0,8},{2,10},{4,12},{6,14},{8,0},{10,2},{12,4},{14,6},{16,24},{18,... | collective-permute-start | bytes 294920 | tf_op jit(solution)/shard_map/ppermute | solution.py:48
  4.9 2.6 collective-permute-start.2
  15.8 2.2 collective-permute-start.5
  21.8 3.3 %collective-permute-done.5 = bf16[48,1024]{1,0:T(8,128)(2,1)S(1)} collective-permute-done((bf16[48,1024]{1,0:T(8,128)(2,1)S(1)}, bf16[48,1024]{1,0:T(8,128)(2,1)S(1)}, u32[]{:S(2)}, u32[]{:S(2)}) %collective-permute-start.5) | collective-permute-done | bytes 98336 | tf_op jit(solution)/shard_map/ppermute | solution.py:48
  26.8 2.2 collective-permute-start.13
  31.2 7.9 %collective-permute-done.7 = bf16[4,48,1024]{2,1,0:T(8,128)(2,1)S(1)} collective-permute-done((bf16[4,48,1024]{2,1,0:T(8,128)(2,1)S(1)}, bf16[4,48,1024]{2,1,0:T(8,128)(2,1)S(1)}, u32[]{:S(2)}, u32[]{:S(2)}) %collective-permute-start.7) | collective-permute-done | bytes 393248 | tf_op jit(solution)/shard_map/ppermute | solution.py:48
  43.0 8.8 %collective-permute-done.14 = bf16[128,1024]{1,0:T(8,128)(2,1)} collective-permute-done((bf16[128,1024]{1,0:T(8,128)(2,1)S(1)}, bf16[128,1024]{1,0:T(8,128)(2,1)}, u32[]{:S(2)}, u32[]{:S(2)}) %collective-permute-start.14) | collective-permute-done | bytes 262176 | tf_op jit(solution)/shard_map/ppermute | solution.py:48
  58.1 4.2 %collective-permute-done.15.cot1 = bf16[512,1024]{1,0:T(8,128)(2,1)} collective-permute-done((bf16[512,1024]{1,0:T(8,128)(2,1)}, bf16[512,1024]{1,0:T(8,128)(2,1)}, u32[]{:S(2)}, u32[]{:S(2)}) %collective-permute-start.15) | collective-permute-done | bytes 1048608 | tf_op jit(solution)/shard_map/ppermute | solution.py:48
  67.5 23.1 %shard_map.357 = (bf16[1024,1024]{1,0:T(8,128)(2,1)S(1)}, f32[1024,1280]{1,0:T(8,128)S(1)}, f32[1024,1280]{1,0:T(8,128)S(1)}, bf16[1024,1280]{1,0:T(8,128)(2,1)S...) custom-call(s32[2]{0:T(128)S(1)} %pad_add_fusion.rank, ...), custom_call_target="tpu_custom_call" | custom-call | flops 285212672 | bytes 3014656 | tf_op jit(solution)/shard_map/pallas_call | solution.py:723
  90.6 2.3 copy-done
  96.4 4.1 %collective-permute-done.17.refs_1_ = bf16[8,128,1024]{2,1,0:T(8,128)(2,1)S(1)} collective-permute-done((bf16[8,128,1024]{2,1,0:T(8,128)(2,1)S(1)}, bf16[8,128,1024]{2,1,0:T(8,128)(2,1)S(1)}, u32[]{:S(2)}, u32[]{:S(2)}) %collective-permute-start.17) | collective-permute-done | bytes 2097184 | tf_op jit(solution)/shard_map/ppermute | solution.py:48
  100.8 8.4 %shard_map.359 = (f32[1024,1024]{1,0:T(8,128)S(1)}, f32[1024,1024]{1,0:T(8,128)S(1)}, bf16[1024,1024]{1,0:T(8,128)(2,1)S(1)}, f32[8,1024]{1,0:T(8,128)S(1)}) custom-call(s32[1]{0:T(128)} %bitcast.rank, bf16[1024,1024]{1,0:T(8,128)(2,1)S(1)} %get-tuple-element.157.normed.lhs, bf16[512,1024]{1,0:T(8,128)(2,1)} %cot0, ...), custom_call_target="tpu_custom_call" | custom-call | flops 268435456 | bytes 1314816 | tf_op jit(solution)/shard_map/pallas_call | solution.py:760
  110.7 2.6 collective-permute-done.18
  113.2 6.6 %shard_map.360 = (bf16[1024,1024]{1,0:T(8,128)(2,1)S(1)}, bf16[1024,1024]{1,0:T(8,128)(2,1)S(1)}, bf16[1024,1024]{1,0:T(8,128)(2,1)S(1)}, bf16[1024,1024]{1,0:T(8,128)(2,1)S(1)}, f32[1,1024]{1,0:T(1,128)S(1)}) custom-call(s32[1]{0:T(128)} %bitcast.rank, f32[1024,1024]{1,0:T(8,128)S(1)} %get-tuple-element.164.gate_r, ...), custom_call_target="tpu_custom_call" | custom-call | flops 134217728 | bytes 1049088 | tf_op jit(solution)/shard_map/pallas_call | solution.py:789
  119.9 4.3 %shard_map.361 = (bf16[8,64,1024]{2,1,0:T(8,128)(2,1)S(1)}, bf16[8,64,1024]{2,1,0:T(8,128)(2,1)S(1)}) custom-call(s32[1]{0:T(128)} %bitcast.12.me, bf16[1024,1024]{1,0:T(8,128)(2,1)S(1)} %get-tuple-element.169.lhs, bf16[1024,1024]{1,0:T(8,128)(2,1)S(1)} %get-tuple-element.170.rhs), custom_call_target="tpu_custom_call" | custom-call | flops 134217728 | bytes 262144 | tf_op jit(solution)/shard_map/pallas_call | solution.py:487
  124.2 4.5 %shard_map.362 = (bf16[8,64,1024]{2,1,0:T(8,128)(2,1)S(1)}, bf16[8,64,1024]{2,1,0:T(8,128)(2,1)S(1)}) custom-call(s32[1]{0:T(128)} %bitcast.12.me, bf16[1024,1024]{1,0:T(8,128)(2,1)S(1)} %get-tuple-element.157.normed.lhs, bf16[1024,1024]{1,0:T(8,128)(2,1)S(1)} %get-tuple-element.221.rhs.dgate), custom_call_target="tpu_custom_call" | custom-call | flops 134217728 | bytes 262144 | tf_op jit(solution)/shard_map/pallas_call | solution.py:487
  137.4 12.0 %shard_map.363 = (bf16[1024,1024]{1,0:T(8,128)(2,1)S(1)}, f32[1024,384]{1,0:T(8,128)S(1)}, f32[8,1280]{1,0:T(8,128)S(1)}, f32[8,128]{1,0:T(8,128)S(1)}, f32[128,...) custom-call(s32[1]{0:T(128)} %bitcast.rank, bf16[1024,1024]{1,0:T(8,128)(2,1)S(1)} %get-tuple-element.178.dssd, ...), custom_call_target="tpu_custom_call" | custom-call | flops 94371840 | bytes 535552 | tf_op jit(solution)/shard_map/pallas_call | solution.py:828
  152.8 2.2 collective-permute-start.26
  155.1 12.0 %shard_map.364 = (bf16[1024,1024]{1,0:T(8,128)(2,1)S(1)}, f32[1024,384]{1,0:T(8,128)S(1)}, f32[8,1280]{1,0:T(8,128)S(1)}, f32[8,128]{1,0:T(8,128)S(1)}, f32[128,...) custom-call(s32[1]{0:T(128)} %bitcast.rank, ...), custom_call_target="tpu_custom_call", output_to_operand_aliasing={{0}: (17, {}), {1}: (18, {})} | custom-call | flops 94371840 | bytes 535552 | tf_op jit(solution)/shard_map/pallas_call | solution.py:828
  170.7 2.2 collective-permute-start.29
  173.0 9.2 %shard_map.365 = (bf16[1024,1024]{1,0:T(8,128)(2,1)S(1)}, f32[1024,384]{1,0:T(8,128)S(1)}, f32[8,1280]{1,0:T(8,128)S(1)}, f32[8,128]{1,0:T(8,128)S(1)}, f32[128,...) custom-call(s32[1]{0:T(128)} %bitcast.rank, ...), custom_call_target="tpu_custom_call", output_to_operand_aliasing={{0}: (17, {}), {1}: (18, {})} | custom-call | flops 62914560 | bytes 535552 | tf_op jit(solution)/shard_map/pallas_call | solution.py:828
  182.3 4.0 %shard_map.366 = (bf16[8,64,640]{2,1,0:T(8,128)(2,1)S(1)}, bf16[8,64,640]{2,1,0:T(8,128)(2,1)S(1)}) custom-call(s32[1]{0:T(128)} %bitcast.12.me, bf16[1024,1024]{1,0:T(8,128)(2,1)S(1)} %get-tuple-element.157.normed.lhs, bf16[1024,1024]{1,0:T(8,128)(2,1)S(1)} %get-tuple-element.209.dval.rhs, f32[1024,384]{1,0:T(8,128)S(1)} %get-tuple-element.205.dcommon), custom_call_target="tpu_custom_call" | custom-call | flops 134217728 | bytes 163840 | tf_op jit(solution)/shard_map/pallas_call | solution.py:526
  189.4 4.0 %shard_map.367 = (bf16[8,64,768]{2,1,0:T(8,128)(2,1)S(1)}, bf16[8,64,768]{2,1,0:T(8,128)(2,1)}) custom-call(s32[1]{0:T(128)} %bitcast.12.me, bf16[1024,1024]{1,0:T(8,128)(2,1)S(1)} %get-tuple-element.157.normed.lhs, bf16[1024,1024]{1,0:T(8,128)(2,1)S(1)} %get-tuple-element.209.dval.rhs), custom_call_target="tpu_custom_call" | custom-call | flops 100663296 | bytes 196608 | tf_op jit(solution)/shard_map/pallas_call | solution.py:487
  199.6 2.3 multiply_subtract_fusion.1
  209.6 4.5 %shard_map.368 = (bf16[512,1024]{1,0:T(8,128)(2,1)}, f32[1,1024]{1,0:T(1,128)S(1)}) custom-call(s32[1]{0:T(128)} %bitcast.rank, bf16[1024,1024]{1,0:T(8,128)(2,1)S(1)} %copy-done.14, bf16[1024,1024]{1,0:T(8,128)(2,1)S(1)} %get-tuple-element.209.dval.rhs, f32[1024,384]{1,0:T(8,128)S(1)} %copy-done.2, bf16[512,1024]{1,0:T(8,128)(2,1)S(1)} %copy-done.24, ...), custom_call_target="tpu_custom_call" | custom-call | flops 184549376 | bytes 131584 | tf_op jit(solution)/shard_map/pallas_call | solution.py:893
  217.2 2.2 collective-permute-start.35
  228.5 3.9 %shard_map.369 = (f32[512,1024]{1,0:T(8,128)S(1)}, f32[1,1024]{1,0:T(1,128)S(1)}) custom-call(s32[1]{0:T(128)} %bitcast.rank, bf16[1024,1024]{1,0:T(8,128)(2,1)S(1)} %copy-done.15, bf16[1024,1024]{1,0:T(8,128)(2,1)S(1)} %get-tuple-element.209.dval.rhs, f32[1024,384]{1,0:T(8,128)S(1)} %copy-done.3, bf16[512,1024]{1,0:T(8,128)(2,1)S(1)} %copy-done.6, ...), custom_call_target="tpu_custom_call" | custom-call | flops 184549376 | bytes 262656 | tf_op jit(solution)/shard_map/pallas_call | solution.py:893
  238.6 2.2 collective-permute-start.42
  241.5 3.4 %collective-permute-done.43 = f32[32,384]{1,0:T(8,128)S(1)} collective-permute-done((f32[32,384]{1,0:T(8,128)S(1)}, f32[32,384]{1,0:T(8,128)S(1)}, u32[]{:S(2)}, u32[]{:S(2)}) %collective-permute-start.43) | collective-permute-done | bytes 49184 | tf_op jit(solution)/shard_map/ppermute | solution.py:48
  249.1 4.1 %fusion.6 = (bf16[512,1024]{1,0:T(8,128)(2,1)}, bf16[512,1024]{1,0:T(8,128)(2,1)}) fusion(bf16[512,1024]{1,0:T(8,128)(2,1)S(1)} %copy-done.6, bf16[512,1024]{1,0:T(8,128)(2,1)} %cot0, f32[512,1024]{1,0:T(8,128)S(1)} %get-tuple-element.222, bf16[512,1024]{1,0:T(8,128)(2,1)} %collective-permute-done.39, f32[512]{0:T(512)S(1)} %broadcast_multiply_fusion, ...), kind=kLoop, calls=%fused_computation.9 | loop fusion | flops 8912896 | bytes 9447424 | tf_op jit(solution)/shard_map/convert_element_type | solution.py:992
  254.3 3.4 %collective-permute-done.45 = f32[1,14688]{1,0:T(1,128)S(1)} collective-permute-done((f32[1,14688]{1,0:T(1,128)S(1)}, f32[1,14688]{1,0:T(1,128)S(1)}, u32[]{:S(2)}, u32[]{:S(2)}) %collective-permute-start.45) | collective-permute-done | bytes 58784 | tf_op jit(solution)/shard_map/ppermute | solution.py:48
  260.0 3.4 %collective-permute-done.46 = f32[1,14688]{1,0:T(1,128)S(1)} collective-permute-done((f32[1,14688]{1,0:T(1,128)S(1)}, f32[1,14688]{1,0:T(1,128)S(1)}, u32[]{:S(2)}, u32[]{:S(2)}) %collective-permute-start.46) | collective-permute-done | bytes 58784 | tf_op jit(solution)/shard_map/ppermute | solution.py:48
  (332 shorter events, 98.5 us)
Async XLA Ops:
  1.8 13.9 %collective-permute-start.1 = (bf16[48,1024]{1,0:T(8,128)(2,1)S(1)}, bf16[48,1024]{1,0:T(8,128)(2,1)S(1)}, u32[]{:S(2)}, u32[]{:S(2)}) collective-permute-start(bf16[48,1024]{1,0:T(8,128)(2,1)S(1)} %get-tuple-element.303), channel_id=1, source_target_pairs={{0,8},{2,10},{4,12},{6,14},{8,0},{10,2},{12,4},{14,6},{16,24},{18,... | collective-permute-start | bytes 294920 | tf_op jit(solution)/shard_map/ppermute | solution.py:48
  4.9 10.9 %collective-permute-start.2 = (bf16[48,1024]{1,0:T(8,128)(2,1)S(1)}, bf16[48,1024]{1,0:T(8,128)(2,1)S(1)}, u32[]{:S(2)}, u32[]{:S(2)}) collective-permute-start(bf16[48,1024]{1,0:T(8,128)(2,1)S(1)} %get-tuple-element.303), channel_id=1, source_target_pairs={{0,16},{2,18},{4,20},{6,22},{8,24},{10,26},{12,28},{14,30},{16,0},... | collective-permute-start | bytes 294920 | tf_op jit(solution)/shard_map/ppermute | solution.py:48
  7.5 8.3 %collective-permute-start.3 = (bf16[48,1024]{1,0:T(8,128)(2,1)S(1)}, bf16[48,1024]{1,0:T(8,128)(2,1)S(1)}, u32[]{:S(2)}, u32[]{:S(2)}) collective-permute-start(bf16[48,1024]{1,0:T(8,128)(2,1)S(1)} %get-tuple-element.303), channel_id=1, source_target_pairs={{0,24},{2,26},{4,28},{6,30},{8,16},{10,18},{12,20},{14,22},{16,8},... | collective-permute-start | bytes 294920 | tf_op jit(solution)/shard_map/ppermute | solution.py:48
  13.1 26.0 %collective-permute-start.8 = (bf16[512,1024]{1,0:T(8,128)(2,1)}, bf16[512,1024]{1,0:T(8,128)(2,1)S(1)}, u32[]{:S(2)}, u32[]{:S(2)}) collective-permute-start(bf16[512,1024]{1,0:T(8,128)(2,1)} %tok.1), channel_id=1, source_target_pairs={{0,1},{1,0},{2,3},{3,2},{4,5},{5,4},{6,7},{7,6},{8,9},{9,8},{10,11... | collective-permute-start | bytes 3145736 | tf_op jit(solution)/shard_map/ppermute | solution.py:48
  15.8 9.3 %collective-permute-start.5 = (bf16[48,1024]{1,0:T(8,128)(2,1)S(1)}, bf16[48,1024]{1,0:T(8,128)(2,1)S(1)}, u32[]{:S(2)}, u32[]{:S(2)}) collective-permute-start(bf16[48,1024]{1,0:T(8,128)(2,1)S(1)} %pad_maximum_fusion.5), channel_id=1, source_target_pairs={{0,16},{2,18},{4,20},{6,22},{8,24},{10,26},{12,28},{14,30},{16,0},... | collective-permute-start | bytes 294920 | tf_op jit(solution)/shard_map/ppermute | solution.py:48
  20.2 10.9 %collective-permute-start.9 = (bf16[4,48,1024]{2,1,0:T(8,128)(2,1)S(1)}, bf16[4,48,1024]{2,1,0:T(8,128)(2,1)S(1)}, u32[]{:S(2)}, u32[]{:S(2)}) collective-permute-start(bf16[4,48,1024]{2,1,0:T(8,128)(2,1)S(1)} %pad_maximum_fusion.2), channel_id=1, source_target_pairs={{0,4},{2,6},{4,0},{6,2},{8,12},{10,14},{12,8},{14,10},{16,20},{18,... | collective-permute-start | bytes 1179656 | tf_op jit(solution)/shard_map/ppermute | solution.py:48
  26.0 14.9 %collective-permute-start.12 = (bf16[128,1024]{1,0:T(8,128)(2,1)S(1)}, bf16[128,1024]{1,0:T(8,128)(2,1)S(1)}, u32[]{:S(2)}, u32[]{:S(2)}) collective-permute-start(bf16[128,1024]{1,0:T(8,128)(2,1)S(1)} %pad_maximum_fusion.4), channel_id=1, source_target_pairs={{0,8},{2,10},{4,12},{6,14},{8,0},{10,2},{12,4},{14,6},{16,24},{18,... | collective-permute-start | bytes 786440 | tf_op jit(solution)/shard_map/ppermute | solution.py:48
  26.8 16.1 %collective-permute-start.13 = (bf16[128,1024]{1,0:T(8,128)(2,1)S(1)}, bf16[128,1024]{1,0:T(8,128)(2,1)}, u32[]{:S(2)}, u32[]{:S(2)}) collective-permute-start(bf16[128,1024]{1,0:T(8,128)(2,1)S(1)} %pad_maximum_fusion.4), channel_id=1, source_target_pairs={{0,16},{2,18},{4,20},{6,22},{8,24},{10,26},{12,28},{14,30},{16,0},... | collective-permute-start | bytes 786440 | tf_op jit(solution)/shard_map/ppermute | solution.py:48
  29.3 9.8 %collective-permute-start.7 = (bf16[4,48,1024]{2,1,0:T(8,128)(2,1)S(1)}, bf16[4,48,1024]{2,1,0:T(8,128)(2,1)S(1)}, u32[]{:S(2)}, u32[]{:S(2)}) collective-permute-start(bf16[4,48,1024]{2,1,0:T(8,128)(2,1)S(1)} %pad_maximum_fusion.3), channel_id=1, source_target_pairs={{0,4},{2,6},{4,0},{6,2},{8,12},{10,14},{12,8},{14,10},{16,20},{18,... | collective-permute-start | bytes 1179656 | tf_op jit(solution)/shard_map/ppermute | solution.py:48
  31.2 22.8 %collective-permute-start.10 = (bf16[8,48,1024]{2,1,0:T(8,128)(2,1)S(1)}, bf16[8,48,1024]{2,1,0:T(8,128)(2,1)}, u32[]{:S(2)}, u32[]{:S(2)}) collective-permute-start(bf16[8,48,1024]{2,1,0:T(8,128)(2,1)S(1)} %constant_dynamic-update-slice_fusion.refs_0_), channel_id=1, source_target_pairs={{0,2},{2,0},{4,6},{6,4},{8,10},{10,8},{12,14},{14,12},{16,18},{18,... | collective-permute-start | bytes 2359304 | tf_op jit(solution)/shard_map/ppermute | solution.py:48
  39.1 23.2 %collective-permute-start.15 = (bf16[512,1024]{1,0:T(8,128)(2,1)}, bf16[512,1024]{1,0:T(8,128)(2,1)}, u32[]{:S(2)}, u32[]{:S(2)}) collective-permute-start(bf16[512,1024]{1,0:T(8,128)(2,1)} %cot0), channel_id=1, source_target_pairs={{0,1},{1,0},{2,3},{3,2},{4,5},{5,4},{6,7},{7,6},{8,9},{9,8},{10,11... | collective-permute-start | bytes 3145736 | tf_op jit(solution)/shard_map/ppermute | solution.py:48
  40.6 13.3 %collective-permute-start.11 = (bf16[8,48,1024]{2,1,0:T(8,128)(2,1)S(1)}, bf16[8,48,1024]{2,1,0:T(8,128)(2,1)}, u32[]{:S(2)}, u32[]{:S(2)}) collective-permute-start(bf16[8,48,1024]{2,1,0:T(8,128)(2,1)S(1)} %constant_dynamic-update-slice_fusion.2.refs_1_), channel_id=1, source_target_pairs={{0,2},{2,0},{4,6},{6,4},{8,10},{10,8},{12,14},{14,12},{16,18},{18,... | collective-permute-start | bytes 2359304 | tf_op jit(solution)/shard_map/ppermute | solution.py:48
  41.0 10.7 %collective-permute-start.14 = (bf16[128,1024]{1,0:T(8,128)(2,1)S(1)}, bf16[128,1024]{1,0:T(8,128)(2,1)}, u32[]{:S(2)}, u32[]{:S(2)}) collective-permute-start(bf16[128,1024]{1,0:T(8,128)(2,1)S(1)} %pad_maximum_fusion.4), channel_id=1, source_target_pairs={{0,24},{2,26},{4,28},{6,30},{8,16},{10,18},{12,20},{14,22},{16,8},... | collective-permute-start | bytes 786440 | tf_op jit(solution)/shard_map/ppermute | solution.py:48
  62.4 32.6 %collective-permute-start.16 = (bf16[4,128,1024]{2,1,0:T(8,128)(2,1)}, bf16[4,128,1024]{2,1,0:T(8,128)(2,1)}, u32[]{:S(2)}, u32[]{:S(2)}) collective-permute-start(bf16[4,128,1024]{2,1,0:T(8,128)(2,1)} %pad_maximum_fusion), channel_id=1, source_target_pairs={{0,4},{2,6},{4,0},{6,2},{8,12},{10,14},{12,8},{14,10},{16,20},{18,... | collective-permute-start | bytes 3145736 | tf_op jit(solution)/shard_map/ppermute | solution.py:48
  133.4 16.0 %collective-permute-start.21 = (bf16[4,64,1024]{2,1,0:T(8,128)(2,1)S(1)}, bf16[4,64,1024]{2,1,0:T(8,128)(2,1)S(1)}, u32[]{:S(2)}, u32[]{:S(2)}) collective-permute-start(bf16[4,64,1024]{2,1,0:T(8,128)(2,1)S(1)} %get-tuple-element.185), channel_id=1, source_target_pairs={{0,4},{2,6},{4,0},{6,2},{8,12},{10,14},{12,8},{14,10},{16,20},{18,... | collective-permute-start | bytes 1572872 | tf_op jit(solution)/shard_map/ppermute | solution.py:48
  134.0 33.0 %collective-permute-start.22 = (bf16[512,1024]{1,0:T(8,128)(2,1)S(1)}, bf16[512,1024]{1,0:T(8,128)(2,1)S(1)}, u32[]{:S(2)}, u32[]{:S(2)}) collective-permute-start(bf16[512,1024]{1,0:T(8,128)(2,1)S(1)} %slice.239), channel_id=1, source_target_pairs={{0,1},{1,0},{2,3},{3,2},{4,5},{5,4},{6,7},{7,6},{8,9},{9,8},{10,11... | collective-permute-start | bytes 3145736 | tf_op jit(solution)/shard_map/ppermute | solution.py:48
  135.7 31.4 %collective-permute-start.23 = (bf16[4,64,1024]{2,1,0:T(8,128)(2,1)S(1)}, bf16[4,64,1024]{2,1,0:T(8,128)(2,1)S(1)}, u32[]{:S(2)}, u32[]{:S(2)}) collective-permute-start(bf16[4,64,1024]{2,1,0:T(8,128)(2,1)S(1)} %get-tuple-element.192), channel_id=1, source_target_pairs={{0,4},{2,6},{4,0},{6,2},{8,12},{10,14},{12,8},{14,10},{16,20},{18,... | collective-permute-start | bytes 1572872 | tf_op jit(solution)/shard_map/ppermute | solution.py:48
  150.6 16.4 %collective-permute-start.24 = (bf16[64,1024]{1,0:T(8,128)(2,1)S(1)}, bf16[64,1024]{1,0:T(8,128)(2,1)S(1)}, u32[]{:S(2)}, u32[]{:S(2)}) collective-permute-start(bf16[64,1024]{1,0:T(8,128)(2,1)S(1)} %get-tuple-element.295), channel_id=1, source_target_pairs={{0,8},{2,10},{4,12},{6,14},{8,0},{10,2},{12,4},{14,6},{16,24},{18,... | collective-permute-start | bytes 393224 | tf_op jit(solution)/shard_map/ppermute | solution.py:48
  152.5 14.6 %collective-permute-start.25 = (bf16[64,1024]{1,0:T(8,128)(2,1)S(1)}, bf16[64,1024]{1,0:T(8,128)(2,1)S(1)}, u32[]{:S(2)}, u32[]{:S(2)}) collective-permute-start(bf16[64,1024]{1,0:T(8,128)(2,1)S(1)} %get-tuple-element.294), channel_id=1, source_target_pairs={{0,16},{2,18},{4,20},{6,22},{8,24},{10,26},{12,28},{14,30},{16,0},... | collective-permute-start | bytes 393224 | tf_op jit(solution)/shard_map/ppermute | solution.py:48
  152.8 14.3 %collective-permute-start.26 = (bf16[64,1024]{1,0:T(8,128)(2,1)S(1)}, bf16[64,1024]{1,0:T(8,128)(2,1)S(1)}, u32[]{:S(2)}, u32[]{:S(2)}) collective-permute-start(bf16[64,1024]{1,0:T(8,128)(2,1)S(1)} %get-tuple-element.293), channel_id=1, source_target_pairs={{0,24},{2,26},{4,28},{6,30},{8,16},{10,18},{12,20},{14,22},{16,8},... | collective-permute-start | bytes 393224 | tf_op jit(solution)/shard_map/ppermute | solution.py:48
  168.5 13.7 %collective-permute-start.27 = (bf16[64,1024]{1,0:T(8,128)(2,1)S(1)}, bf16[64,1024]{1,0:T(8,128)(2,1)S(1)}, u32[]{:S(2)}, u32[]{:S(2)}) collective-permute-start(bf16[64,1024]{1,0:T(8,128)(2,1)S(1)} %get-tuple-element.292), channel_id=1, source_target_pairs={{0,8},{2,10},{4,12},{6,14},{8,0},{10,2},{12,4},{14,6},{16,24},{18,... | collective-permute-start | bytes 393224 | tf_op jit(solution)/shard_map/ppermute | solution.py:48
  169.5 12.7 %collective-permute-start.28 = (bf16[64,1024]{1,0:T(8,128)(2,1)S(1)}, bf16[64,1024]{1,0:T(8,128)(2,1)S(1)}, u32[]{:S(2)}, u32[]{:S(2)}) collective-permute-start(bf16[64,1024]{1,0:T(8,128)(2,1)S(1)} %get-tuple-element.291), channel_id=1, source_target_pairs={{0,16},{2,18},{4,20},{6,22},{8,24},{10,26},{12,28},{14,30},{16,0},... | collective-permute-start | bytes 393224 | tf_op jit(solution)/shard_map/ppermute | solution.py:48
  170.7 11.5 %collective-permute-start.29 = (bf16[64,1024]{1,0:T(8,128)(2,1)S(1)}, bf16[64,1024]{1,0:T(8,128)(2,1)S(1)}, u32[]{:S(2)}, u32[]{:S(2)}) collective-permute-start(bf16[64,1024]{1,0:T(8,128)(2,1)S(1)} %get-tuple-element.290), channel_id=1, source_target_pairs={{0,24},{2,26},{4,28},{6,30},{8,16},{10,18},{12,20},{14,22},{16,8},... | collective-permute-start | bytes 393224 | tf_op jit(solution)/shard_map/ppermute | solution.py:48
  199.1 15.7 %collective-permute-start.32 = (bf16[4,64,640]{2,1,0:T(8,128)(2,1)S(1)}, bf16[4,64,640]{2,1,0:T(8,128)(2,1)S(1)}, u32[]{:S(2)}, u32[]{:S(2)}) collective-permute-start(bf16[4,64,640]{2,1,0:T(8,128)(2,1)S(1)} %copy-done.43), channel_id=1, source_target_pairs={{0,4},{2,6},{4,0},{6,2},{8,12},{10,14},{12,8},{14,10},{16,20},{18,... | collective-permute-start | bytes 983048 | tf_op jit(solution)/shard_map/ppermute | solution.py:48
  203.6 28.7 %collective-permute-start.33 = (bf16[4,64,768]{2,1,0:T(8,128)(2,1)}, bf16[4,64,768]{2,1,0:T(8,128)(2,1)}, u32[]{:S(2)}, u32[]{:S(2)}) collective-permute-start(bf16[4,64,768]{2,1,0:T(8,128)(2,1)} %add_convert_fusion.2), channel_id=1, source_target_pairs={{0,4},{2,6},{4,0},{6,2},{8,12},{10,14},{12,8},{14,10},{16,20},{18,... | collective-permute-start | bytes 1179656 | tf_op jit(solution)/shard_map/ppermute | solution.py:48
  214.1 32.2 %collective-permute-start.39 = (bf16[512,1024]{1,0:T(8,128)(2,1)}, bf16[512,1024]{1,0:T(8,128)(2,1)}, u32[]{:S(2)}, u32[]{:S(2)}) collective-permute-start(bf16[512,1024]{1,0:T(8,128)(2,1)} %get-tuple-element.237), channel_id=1, source_target_pairs={{0,1},{1,0},{2,3},{3,2},{4,5},{5,4},{6,7},{7,6},{8,9},{9,8},{10,11... | collective-permute-start | bytes 3145736 | tf_op jit(solution)/shard_map/ppermute | solution.py:48
  216.5 15.9 %collective-permute-start.34 = (bf16[64,640]{1,0:T(8,128)(2,1)}, bf16[64,640]{1,0:T(8,128)(2,1)S(1)}, u32[]{:S(2)}, u32[]{:S(2)}) collective-permute-start(bf16[64,640]{1,0:T(8,128)(2,1)} %get-tuple-element.301), channel_id=1, source_target_pairs={{0,8},{2,10},{4,12},{6,14},{8,0},{10,2},{12,4},{14,6},{16,24},{18,... | collective-permute-start | bytes 245768 | tf_op jit(solution)/shard_map/ppermute | solution.py:48
  217.2 15.2 %collective-permute-start.35 = (bf16[64,640]{1,0:T(8,128)(2,1)}, bf16[64,640]{1,0:T(8,128)(2,1)S(1)}, u32[]{:S(2)}, u32[]{:S(2)}) collective-permute-start(bf16[64,640]{1,0:T(8,128)(2,1)} %get-tuple-element.300), channel_id=1, source_target_pairs={{0,16},{2,18},{4,20},{6,22},{8,24},{10,26},{12,28},{14,30},{16,0},... | collective-permute-start | bytes 245768 | tf_op jit(solution)/shard_map/ppermute | solution.py:48
  219.4 13.0 %collective-permute-start.36 = (bf16[64,640]{1,0:T(8,128)(2,1)}, bf16[64,640]{1,0:T(8,128)(2,1)S(1)}, u32[]{:S(2)}, u32[]{:S(2)}) collective-permute-start(bf16[64,640]{1,0:T(8,128)(2,1)} %get-tuple-element.299), channel_id=1, source_target_pairs={{0,24},{2,26},{4,28},{6,30},{8,16},{10,18},{12,20},{14,22},{16,8},... | collective-permute-start | bytes 245768 | tf_op jit(solution)/shard_map/ppermute | solution.py:48
  236.4 9.9 %collective-permute-start.40 = (bf16[64,768]{1,0:T(8,128)(2,1)S(1)}, bf16[64,768]{1,0:T(8,128)(2,1)S(1)}, u32[]{:S(2)}, u32[]{:S(2)}) collective-permute-start(bf16[64,768]{1,0:T(8,128)(2,1)S(1)} %get-tuple-element.246), channel_id=1, source_target_pairs={{0,8},{2,10},{4,12},{6,14},{8,0},{10,2},{12,4},{14,6},{16,24},{18,... | collective-permute-start | bytes 294920 | tf_op jit(solution)/shard_map/ppermute | solution.py:48
  236.4 9.9 %collective-permute-start.41 = (bf16[64,768]{1,0:T(8,128)(2,1)S(1)}, bf16[64,768]{1,0:T(8,128)(2,1)S(1)}, u32[]{:S(2)}, u32[]{:S(2)}) collective-permute-start(bf16[64,768]{1,0:T(8,128)(2,1)S(1)} %get-tuple-element.247), channel_id=1, source_target_pairs={{0,16},{2,18},{4,20},{6,22},{8,24},{10,26},{12,28},{14,30},{16,0},... | collective-permute-start | bytes 294920 | tf_op jit(solution)/shard_map/ppermute | solution.py:48
  238.6 7.7 %collective-permute-start.42 = (bf16[64,768]{1,0:T(8,128)(2,1)S(1)}, bf16[64,768]{1,0:T(8,128)(2,1)S(1)}, u32[]{:S(2)}, u32[]{:S(2)}) collective-permute-start(bf16[64,768]{1,0:T(8,128)(2,1)S(1)} %get-tuple-element.248), channel_id=1, source_target_pairs={{0,24},{2,26},{4,28},{6,30},{8,16},{10,18},{12,20},{14,22},{16,8},... | collective-permute-start | bytes 294920 | tf_op jit(solution)/shard_map/ppermute | solution.py:48
  (83 other events, 614.0 us)

commit v7 on v6

--- a/solution.py
+++ b/solution.py
@@ -196,34 +196,36 @@
 
 
 def assemble_kernel(dp, parts, moves, me, *refs):
-    half = dp // CORES
-    sources, outs = refs[: 2 * parts], refs[2 * parts :]
+    high, middle = axis_parts(dp)
+    each = CORES * middle
+    sources, outs = refs[: parts * each], refs[parts * each :]
     for place, distance in enumerate(relative_places(dp)):
         block = me[0] ^ distance
         base = 0
         for part in range(parts):
-            source, at = (sources[part], place) if place < half else (sources[parts + part], place - half)
+            source, at = sources[part * each + place // high], place % high
             end = base + source.shape[1]
-            for first, last, lanes, out, each, extra, row in moves:
-                low, high = max(base, first), min(end, last)
-                if low < high:
+            for first, last, lanes, out, count, extra, row in moves:
+                low, top = max(base, first), min(end, last)
+                if low < top:
                     outs[out][
-                        block * each + extra, row + low - first : row + high - first, :
-                    ] = source[at, low - base : high - base, lanes]
+                        block * count + extra, row + low - first : row + top - first, :
+                    ] = source[at, low - base : top - base, lanes]
             base = end
 
 
-def assemble(nears, fars, dp, dp_rank, moves, shapes):
+def assemble(parts, dp, dp_rank, moves, shapes):
     vmem = pl.BlockSpec(memory_space=pltpu.VMEM)
-    moved = sum(4 * near.size * near.dtype.itemsize for near in nears)
+    lines = [line for part in parts for line in part]
+    moved = sum(2 * line.size * line.dtype.itemsize for line in lines)
     return pl.pallas_call(
-        functools.partial(assemble_kernel, dp, len(nears), moves),
-        in_specs=[pl.BlockSpec(memory_space=pltpu.SMEM)] + [vmem] * (2 * len(nears)),
+        functools.partial(assemble_kernel, dp, len(parts), moves),
+        in_specs=[pl.BlockSpec(memory_space=pltpu.SMEM)] + [vmem] * len(lines),
         out_specs=[vmem] * len(shapes),
         out_shape=[shape(*dims, dtype=bf16) for dims in shapes],
         compiler_params=pltpu.CompilerParams(vmem_limit_bytes=16 * 1024 * 1024),
         cost_estimate=pl.CostEstimate(flops=0, bytes_accessed=moved, transcendentals=0),
-    )(dp_rank, *nears, *fars)
+    )(dp_rank, *lines)
 
 
 def pick_half(rank, first, second):
@@ -543,17 +545,29 @@
     )(dp_rank, lhs, dval, dcommon)
 
 
-def input_grad_kernel(rank, dgate, dval, dcommon, tok, wg, wv, shw, ng_o, gain_o):
-    @pl.when(pl.program_id(0) == 0)
+def input_grad_kernel(
+    away, rank, dgate, dval, dcommon, tok0, tok1, wg, wv, shw, sent_o, own_o, gain_o
+):
+    step = pl.program_id(0)
+
+    @pl.when(step == 0)
     def _():
         gain_o[...] = jnp.zeros(gain_o.shape, f32)
 
     grad = mm(dgate[...], wg[...], 1, 1) + mm(dval[...], wv[...], 1, 1)
     grad = grad + mm_left(dcommon[...], shw[...], 1, 1)
-    x = tok[...].astype(f32)
+    first = jnp.broadcast_to((step < away).astype(jnp.int32), tok0.shape) == 1
+    x = jnp.where(first, tok0[...], tok1[...]).astype(f32)
     inverse = lax.rsqrt(jnp.mean(x * x, axis=1, keepdims=True) + norm_epsilon)
     gain_o[...] += jnp.sum(grad * (x * inverse), axis=0, keepdims=True)
-    ng_o[...] = grad.astype(ng_o.dtype)
+
+    @pl.when(step < away)
+    def _():
+        sent_o[...] = grad.astype(bf16)
+
+    @pl.when(step >= away)
+    def _():
+        own_o[...] = grad
 
 
 def shards(
@@ -628,18 +642,24 @@
     second_shard, first_line = tie(value_shard[cut:], first_line)
     second_line = gather_line(second_shard, dp)
     second_line, ids = tie(second_line, sequence_ids)
-    first_near = jnp.concatenate([first_line] + plane_parts(first_line, dp), axis=0)
+    first_near = [first_line] + plane_parts(first_line, dp)
     other_shard = jnp.concatenate(
         [inner_proj[0].astype(bf16), outer_proj.T.astype(bf16)], axis=0
     )
     other_shard, second_line = tie(other_shard, second_line)
     other_line = gather_line(other_shard, dp)
-    second_line, *parts = tie(second_line, *plane_parts(second_line, dp), *token_pieces)
-    parts, token_pieces = parts[:-nt], parts[-nt:]
-    second_near = jnp.concatenate([second_line] + parts, axis=0)
-    cotangent_now, *token_pieces = tie(cotangent, *token_pieces)
-    cot_pieces = pieces_of(cotangent_now)
-    first_far, second_far = swap(first_near, "dp", dp, 1), swap(second_near, "dp", dp, 1)
+    cot_cut = rows_here // 2
+    cot_early = [swap(cotangent[:cot_cut], "tensor", nt, d) for d in range(1, nt)]
+    second_line, *rests = tie(
+        second_line, *plane_parts(second_line, dp), *token_pieces, *cot_early
+    )
+    count = len(rests) - 2 * nt + 1
+    second_near = [second_line] + rests[:count]
+    token_pieces, cot_early = rests[count : count + nt], rests[count + nt :]
+    cotangent_now, *token_pieces = tie(cotangent[cot_cut:], *token_pieces)
+    cot_late = [swap(cotangent_now, "tensor", nt, d) for d in range(1, nt)]
+    first_all = first_near + [swap(line, "dp", dp, 1) for line in first_near]
+    second_all = second_near + [swap(line, "dp", dp, 1) for line in second_near]
     full = slice(None)
     moves = [(0, block_rows, full, 0, 1, 0, 0)]
     dims = [(dp, block_rows, width)]
@@ -653,9 +673,7 @@
     else:
         moves.append((block_rows, block_rows + small_rows * nt, full, 1, 1, 0, 0))
         dims += [(dp, small_rows * nt, width)]
-    value_w, *small_all = assemble(
-        [first_near, second_near], [first_far, second_far], dp, dp_me, moves, dims
-    )
+    value_w, *small_all = assemble([first_all, second_all], dp, dp_me, moves, dims)
     value_w = value_w.reshape(D, width)
 
     def halves(pieces):
@@ -717,7 +735,11 @@
 
     steps = length // wide
     in_half = lambda i: i % (steps // 2)
-    value_w, other_line, *cot_pieces = tie(value_w, other_line, *cot_pieces)
+    value_w, other_line, *cot_late = tie(value_w, other_line, *cot_late)
+    cot_pieces = [cotangent] + [
+        jnp.concatenate([early, late], axis=0) for early, late in zip(cot_early, cot_late)
+    ]
+    other_far = swap(other_line, "dp", dp, 1)
     plane = plane_parts(other_line, dp)
     tok_rank, tok0, tok1 = halves(token_pieces)
     normed, chans, pre, mixed, ssd, entering, step_in = call(
@@ -747,14 +769,12 @@
         scalars=1,
     )(jnp.concatenate([tok_rank, t_me]), tok0, tok1, pre_gain, value_w, shared_here, conv_here, skip, head_rows, aux, segr)
 
-    normed, *plane = tie(normed, *plane)
-    plane = jnp.concatenate([other_line] + plane, axis=0)
+    normed, other_far, *plane = tie(normed, other_far, *plane)
     moves = [
         (0, block_rows, full, 0, 1, 0, 0), (block_rows, 2 * block_rows, full, 1, 1, 0, 0)
     ]
-    gate_w, outer_t = assemble(
-        [plane], [swap(plane, "dp", dp, 1)], dp, dp_me, moves, [(dp, block_rows, width)] * 2
-    )
+    other_all = [other_line] + plane + [other_far] + [swap(line, "dp", dp, 1) for line in plane]
+    gate_w, outer_t = assemble([other_all], dp, dp_me, moves, [(dp, block_rows, width)] * 2)
     gate_w, outer_t = gate_w.reshape(D, width), outer_t.reshape(D, width)
     cot_rank, cot0, cot1 = halves(cot_pieces)
     gate, scaled_grad, returned, sums = call(
@@ -879,8 +899,6 @@
             gate_far = high_swaps(gate_far, dp)
     dval, dcommon = filled
     dval, *gate_far = tie(dval, *gate_far)
-    outer_part = high_sum(outer_block, outer_far)
-    gate_part = high_sum(gate_block, gate_far)
 
     branch_sum = branch[0].astype(f32)
     for piece in branch_received:
@@ -889,21 +907,33 @@
     tokens = residual.astype(f32)
     block_out = (tokens + branch_sum * live_here[:, None]).astype(bf16)
 
-    def input_grad(count, offset, dtype, positions, dgate):
+    away = (nt - 1) * per_piece
+
+    def input_grad(others, dgate):
+        away_rows = lambda width_here: pl.BlockSpec(
+            (band, width_here), lambda i, r: (jnp.minimum(i, away - 1), 0)
+        )
+        own_rows = lambda width_here: pl.BlockSpec(
+            (band, width_here), lambda i, r: (jnp.maximum(i - away, 0), 0)
+        )
+        turned = lambda i: lax.rem(i + per_piece, nt * per_piece)
+        here = lambda width_here: pl.BlockSpec(
+            (band, width_here), lambda i, r: (relative(turned(i), r[0]), 0)
+        )
         return call(
-            input_grad_kernel,
-            (count * per_piece,),
+            functools.partial(input_grad_kernel, away),
+            (nt * per_piece,),
             [
-                rel_rows(width, offset), rel_rows(width, offset), rel_rows(common_width, offset),
-                plain(D), whole((D, width)), whole((D, width)), whole((D, common_width)),
+                here(width), here(width), here(common_width), away_rows(D), own_rows(D),
+                whole((D, width)), whole((D, width)), whole((D, common_width)),
             ],
-            [plain(D), result((1, D))],
-            [shape(count * rows_here, D, dtype=dtype), shape(1, D)],
+            [away_rows(D), own_rows(D), result((1, D))],
+            [shape((nt - 1) * rows_here, D, dtype=bf16), shape(rows_here, D), shape(1, D)],
             [],
-            4 * count * rows_here * D * (width + common_width),
-            13,
+            4 * length * D * (width + common_width),
+            24,
             scalars=1,
-        )(t_me, dgate, dval, dcommon, positions, gate_w, value_w, shared_here)
+        )(t_me, dgate, dval, dcommon, others, residual, gate_w, value_w, shared_here)
 
     keep, send = value_grad(normed, dval, dcommon, dp, dp_me)
     line, part = start_sum(keep, send, dp)
@@ -915,24 +945,24 @@
         line, part = start_sum(keep, send, dp)
         lines.append(line)
         parts.append(part)
-    each = len(part)
-    dgate, *flat = tie(dgate, *[item for part in parts for item in part])
-    crossing = [middle_swaps(flat[at : at + each], dp) for at in range(0, len(flat), each)]
+    crossing = [middle_swaps(parts[0], dp)]
+    dgate, *part = tie(dgate, *part)
+    if two:
+        crossing.append(middle_swaps(part, dp))
     others = token_pieces[1] if nt == 2 else jnp.concatenate(token_pieces[1:], axis=0)
-    sent, pre_grad_sent = input_grad(nt - 1, per_piece, bf16, others, dgate)
+    sent, own, pre_grad = input_grad(others, dgate)
     sent = sent.reshape(nt - 1, rows_here, D)
     received = [swap(sent[d - 1], "tensor", nt, d) for d in range(1, nt)]
     small_grads = [item for each_part in back_parts for item in each_part]
-    dgate, pre_grad_sent, *rests = tie(dgate, pre_grad_sent, *crossing[0], *small_grads)
-    crossing[0], small_grads = rests[:each], rests[each:]
+    pre_grad, *rests = tie(pre_grad, *crossing[0], *small_grads)
+    crossing[0], small_grads = rests[: len(crossing[0])], rests[len(crossing[0]) :]
     block, far = middle_sum(lines[0], crossing[0])
+    pre_grad, *far = tie(pre_grad, *far)
     blocks, fars = [block], [high_swaps(far, dp)]
-    own, pre_grad_own = input_grad(1, 0, f32, residual, dgate)
     if two:
-        pre_grad_own, *rests = tie(pre_grad_own, *crossing[1], *fars[0])
-        crossing[1], fars[0] = rests[:each], rests[each:]
+        pre_grad, *crossing[1] = tie(pre_grad, *crossing[1])
         block, far = middle_sum(lines[1], crossing[1])
-        pre_grad_own, *far = tie(pre_grad_own, *far)
+        pre_grad, *far = tie(pre_grad, *far)
         blocks.append(block)
         fars.append(high_swaps(far, dp))
     dconv, dheads = [sum(small_grads[at::2]) for at in range(2)]
@@ -950,14 +980,18 @@
     )
     vector = jnp.concatenate(
         [
-            conv_grad.reshape(1, -1), pre_grad_sent + pre_grad_own, post_all, head_all.reshape(1, -1),
+            conv_grad.reshape(1, -1), pre_grad, post_all, head_all.reshape(1, -1),
         ],
         axis=1,
     )
     for stage, (axis, size, distance) in enumerate(sum_stages(dp, nt)):
         vector = vector + swap(vector, axis, size, distance)
         if stage == 0:
+            vector, *fars[0] = tie(vector, *fars[0])
             value_sums = [high_sum(blocks[0], fars[0])]
+            vector, outer_block, gate_block = tie(vector, outer_block, gate_block)
+            outer_part = high_sum(outer_block, outer_far)
+            gate_part = high_sum(gate_block, gate_far)
         if stage == 1:
             vector, *received = tie(vector, *received)
         if stage == 1 and two:

time: 270 us -> 279 us (1.033)
  waiting for transfers between devices: 51 us -> 59.4 us
  starting transfers between devices: 53.5 us -> 59 us
  other arithmetic: 32.8 us -> 27.4 us
    ppermute x47 -> x51, waiting for transfers between devices: 51 us -> 59.4 us  [swap(): return lax.ppermute(value, axis, [(i, i ^ distance) for i in range(size)])]
    ppermute x47 -> x51, starting transfers between devices: 53.5 us -> 59 us  [swap(): return lax.ppermute(value, axis, [(i, i ^ distance) for i in range(size)])]
    unnamed x140 -> x157, local copies, waits for them, and re-layouts: 22.8 us -> 19.2 us
    pallas_call x4 -> x3, Pallas kernels: 10.3 us -> 11.4 us  [the longest x1 7.76 us: input_grad(): call(functools.partial(input_grad_kernel, away), (nt * per_piece,), [here...]
  transfers between devices with their start and end apart: 47 -> 51, of which waited for: 16 -> 16; matrix products, arithmetic and copies ran while one was open for 12% -> 11% of each run, Pallas kernels for 25% -> 24%
where the time goes in v7:
time: 279 us; the launch traced here: 275 us
  Pallas kernels  97.9 us (35%)
  waiting for transfers between devices  59.4 us (21%)
  starting transfers between devices  59 us (21%)
  local copies, waits for them, and re-layouts  28.9 us (10%)
  other arithmetic  27.4 us (10%)
    ppermute x51, waiting for transfers between devices, swap(): return lax.ppermute(value, axis, [(i, i ^ distance) for i in range(size)])  59.4 us
    ppermute x51, starting transfers between devices, swap(): return lax.ppermute(value, axis, [(i, i ^ distance) for i in range(size)])  59 us
    pallas_call x3, Pallas kernels, shards(): call(functools.partial(scan_back_kernel, heads_here), (count,), [rows(CHU...  33.1 us
    pallas_call x1, Pallas kernels, shards(): call(functools.partial(scan_kernel, heads_here), (steps,), [rows(wide, D,...  23.5 us
    unnamed x157, local copies, waits for them, and re-layouts  19.2 us
    pallas_call x3, Pallas kernels, weight_grad(): call(functools.partial(weight_grad_kernel, dp), (width // 256,), [whole((...  12.8 us
    pallas_call x1, Pallas kernels, input_grad(): call(functools.partial(input_grad_kernel, away), (nt * per_piece,), [here...  7.76 us
    pallas_call x1, Pallas kernels, shards(): call(norm_kernel, (length // band,), [rel_rows(width), rel_rows(width), r...  6.56 us
  transfers between devices with their start and end apart: 51, of which 16 were waited for; matrix products, arithmetic and copies ran while one was open for 11% of the time, Pallas kernels for 24%

profile of v7, /device:TPU:0, one launch (start us, length us, event | category | flops | bytes accessed | tf_op | source)
XLA Modules:
  0.0 274.8 jit_solution(2566300684363364383)
XLA Ops:
  2.5 3.0 %collective-permute-start.1 = (bf16[48,1024]{1,0:T(8,128)(2,1)}, bf16[48,1024]{1,0:T(8,128)(2,1)S(1)}, u32[]{:S(2)}, u32[]{:S(2)}) collective-permute-start(bf16[48,1024]{1,0:T(8,128)(2,1)} %get-tuple-element.317), channel_id=1, source_target_pairs={{0,8},{2,10},{4,12},{6,14},{8,0},{10,2},{12,4},{14,6},{16,24},{18,... | collective-permute-start | bytes 294920 | tf_op jit(solution)/shard_map/ppermute | solution.py:48
  5.5 2.6 collective-permute-start.2
  23.5 5.0 %collective-permute-done.5 = bf16[48,1024]{1,0:T(8,128)(2,1)S(1)} collective-permute-done((bf16[48,1024]{1,0:T(8,128)(2,1)S(1)}, bf16[48,1024]{1,0:T(8,128)(2,1)S(1)}, u32[]{:S(2)}, u32[]{:S(2)}) %collective-permute-start.5) | collective-permute-done | bytes 98336 | tf_op jit(solution)/shard_map/ppermute | solution.py:48
  33.8 8.7 %collective-permute-done.7.refs_5_ = bf16[4,48,1024]{2,1,0:T(8,128)(2,1)} collective-permute-done((bf16[4,48,1024]{2,1,0:T(8,128)(2,1)S(1)}, bf16[4,48,1024]{2,1,0:T(8,128)(2,1)}, u32[]{:S(2)}, u32[]{:S(2)}) %collective-permute-start.7) | collective-permute-done | bytes 393248 | tf_op jit(solution)/shard_map/ppermute | solution.py:48
  42.5 3.9 %collective-permute-start.17 = (bf16[128,1024]{1,0:T(8,128)(2,1)S(1)}, bf16[128,1024]{1,0:T(8,128)(2,1)S(1)}, u32[]{:S(2)}, u32[]{:S(2)}) collective-permute-start(bf16[128,1024]{1,0:T(8,128)(2,1)S(1)} %pad_maximum_fusion.5), channel_id=1, source_target_pairs={{0,24},{2,26},{4,28},{6,30},{8,16},{10,18},{12,20},{14,22},{16,8},... | collective-permute-start | bytes 786440 | tf_op jit(solution)/shard_map/ppermute | solution.py:48
  46.7 4.1 %collective-permute-done.8.tok1.tok0 = bf16[512,1024]{1,0:T(8,128)(2,1)S(1)} collective-permute-done((bf16[512,1024]{1,0:T(8,128)(2,1)S(1)}, bf16[512,1024]{1,0:T(8,128)(2,1)S(1)}, u32[]{:S(2)}, u32[]{:S(2)}) %collective-permute-start.8) | collective-permute-done | bytes 1048608 | tf_op jit(solution)/shard_map/ppermute | solution.py:48
  60.5 3.3 %collective-permute-done.18 = bf16[256,1024]{1,0:T(8,128)(2,1)} collective-permute-done((bf16[256,1024]{1,0:T(8,128)(2,1)}, bf16[256,1024]{1,0:T(8,128)(2,1)}, u32[]{:S(2)}, u32[]{:S(2)}) %collective-permute-start.18) | collective-permute-done | bytes 524320 | tf_op jit(solution)/shard_map/ppermute | solution.py:48
  70.1 23.5 %shard_map.357 = (bf16[1024,1024]{1,0:T(8,128)(2,1)S(1)}, f32[1024,1280]{1,0:T(8,128)S(1)}, f32[1024,1280]{1,0:T(8,128)S(1)}, bf16[1024,1280]{1,0:T(8,128)(2,1)S...) custom-call(s32[2]{0:T(128)S(1)} %pad_add_fusion.rank, ...), custom_call_target="tpu_custom_call" | custom-call | flops 285212672 | bytes 3014656 | tf_op jit(solution)/shard_map/pallas_call | solution.py:745
  100.5 6.5 %shard_map.359 = (f32[1024,1024]{1,0:T(8,128)S(1)}, f32[1024,1024]{1,0:T(8,128)S(1)}, bf16[1024,1024]{1,0:T(8,128)(2,1)S(1)}, f32[8,1024]{1,0:T(8,128)S(1)}) custom-call(s32[1]{0:T(128)} %bitcast.rank, bf16[1024,1024]{1,0:T(8,128)(2,1)S(1)} %get-tuple-element.163.normed.lhs, bf16[512,1024]{1,0:T(8,128)(2,1)S(1)} %copy-done.8, ...), custom_call_target="tpu_custom_call" | custom-call | flops 268435456 | bytes 1314816 | tf_op jit(solution)/shard_map/pallas_call | solution.py:780
  107.7 3.4 %collective-permute-done.22 = f32[8,1024]{1,0:T(8,128)S(1)} collective-permute-done((f32[8,1024]{1,0:T(8,128)S(1)}, f32[8,1024]{1,0:T(8,128)S(1)}, u32[]{:S(2)}, u32[]{:S(2)}) %collective-permute-start.22) | collective-permute-done | bytes 32800 | tf_op jit(solution)/shard_map/ppermute | solution.py:48
  111.0 6.6 %shard_map.360 = (bf16[1024,1024]{1,0:T(8,128)(2,1)S(1)}, bf16[1024,1024]{1,0:T(8,128)(2,1)S(1)}, bf16[1024,1024]{1,0:T(8,128)(2,1)S(1)}, bf16[1024,1024]{1,0:T(8,128)(2,1)S(1)}, f32[1,1024]{1,0:T(1,128)S(1)}) custom-call(s32[1]{0:T(128)} %bitcast.rank, f32[1024,1024]{1,0:T(8,128)S(1)} %get-tuple-element.171.gate_r, ...), custom_call_target="tpu_custom_call" | custom-call | flops 134217728 | bytes 1049088 | tf_op jit(solution)/shard_map/pallas_call | solution.py:809
  117.6 4.3 %shard_map.361 = (bf16[8,64,1024]{2,1,0:T(8,128)(2,1)S(1)}, bf16[8,64,1024]{2,1,0:T(8,128)(2,1)S(1)}) custom-call(s32[1]{0:T(128)} %bitcast.12.me, bf16[1024,1024]{1,0:T(8,128)(2,1)S(1)} %get-tuple-element.176.lhs, bf16[1024,1024]{1,0:T(8,128)(2,1)S(1)} %get-tuple-element.177.rhs), custom_call_target="tpu_custom_call" | custom-call | flops 134217728 | bytes 262144 | tf_op jit(solution)/shard_map/pallas_call | solution.py:489
  122.0 4.5 %shard_map.362 = (bf16[8,64,1024]{2,1,0:T(8,128)(2,1)S(1)}, bf16[8,64,1024]{2,1,0:T(8,128)(2,1)S(1)}) custom-call(s32[1]{0:T(128)} %bitcast.12.me, bf16[1024,1024]{1,0:T(8,128)(2,1)S(1)} %get-tuple-element.163.normed.lhs, bf16[1024,1024]{1,0:T(8,128)(2,1)S(1)} %get-tuple-element.218.rhs.dgate), custom_call_target="tpu_custom_call" | custom-call | flops 134217728 | bytes 262144 | tf_op jit(solution)/shard_map/pallas_call | solution.py:489
  127.0 2.1 collective-permute-done.24
  134.3 12.0 %shard_map.363 = (bf16[1024,1024]{1,0:T(8,128)(2,1)S(1)}, f32[1024,384]{1,0:T(8,128)S(1)}, f32[8,1280]{1,0:T(8,128)S(1)}, f32[8,128]{1,0:T(8,128)S(1)}, f32[128,...) custom-call(s32[1]{0:T(128)} %bitcast.rank, bf16[1024,1024]{1,0:T(8,128)(2,1)S(1)} %get-tuple-element.185.dssd, ...), custom_call_target="tpu_custom_call" | custom-call | flops 94371840 | bytes 535552 | tf_op jit(solution)/shard_map/pallas_call | solution.py:848
  148.2 3.5 %collective-permute-start.29 = (bf16[64,1024]{1,0:T(8,128)(2,1)S(1)}, bf16[64,1024]{1,0:T(8,128)(2,1)S(1)}, u32[]{:S(2)}, u32[]{:S(2)}) collective-permute-start(bf16[64,1024]{1,0:T(8,128)(2,1)S(1)} %get-tuple-element.308), channel_id=1, source_target_pairs={{0,16},{2,18},{4,20},{6,22},{8,24},{10,26},{12,28},{14,30},{16,0},... | collective-permute-start | bytes 393224 | tf_op jit(solution)/shard_map/ppermute | solution.py:48
  152.0 12.0 %shard_map.364 = (bf16[1024,1024]{1,0:T(8,128)(2,1)S(1)}, f32[1024,384]{1,0:T(8,128)S(1)}, f32[8,1280]{1,0:T(8,128)S(1)}, f32[8,128]{1,0:T(8,128)S(1)}, f32[128,...) custom-call(s32[1]{0:T(128)} %bitcast.rank, ...), custom_call_target="tpu_custom_call", output_to_operand_aliasing={{0}: (17, {}), {1}: (18, {})} | custom-call | flops 94371840 | bytes 535552 | tf_op jit(solution)/shard_map/pallas_call | solution.py:848
  165.8 3.8 %collective-permute-start.32 = (bf16[64,1024]{1,0:T(8,128)(2,1)S(1)}, bf16[64,1024]{1,0:T(8,128)(2,1)S(1)}, u32[]{:S(2)}, u32[]{:S(2)}) collective-permute-start(bf16[64,1024]{1,0:T(8,128)(2,1)S(1)} %get-tuple-element.305), channel_id=1, source_target_pairs={{0,16},{2,18},{4,20},{6,22},{8,24},{10,26},{12,28},{14,30},{16,0},... | collective-permute-start | bytes 393224 | tf_op jit(solution)/shard_map/ppermute | solution.py:48
  169.9 9.1 %shard_map.365 = (bf16[1024,1024]{1,0:T(8,128)(2,1)S(1)}, f32[1024,384]{1,0:T(8,128)S(1)}, f32[8,1280]{1,0:T(8,128)S(1)}, f32[8,128]{1,0:T(8,128)S(1)}, f32[128,...) custom-call(s32[1]{0:T(128)} %bitcast.rank, ...), custom_call_target="tpu_custom_call", output_to_operand_aliasing={{0}: (17, {}), {1}: (18, {})} | custom-call | flops 62914560 | bytes 535552 | tf_op jit(solution)/shard_map/pallas_call | solution.py:848
  179.1 4.0 %shard_map.366 = (bf16[8,64,640]{2,1,0:T(8,128)(2,1)S(1)}, bf16[8,64,640]{2,1,0:T(8,128)(2,1)S(1)}) custom-call(s32[1]{0:T(128)} %bitcast.12.me, bf16[1024,1024]{1,0:T(8,128)(2,1)S(1)} %get-tuple-element.163.normed.lhs, bf16[1024,1024]{1,0:T(8,128)(2,1)S(1)} %get-tuple-element.215.dval.rhs, f32[1024,384]{1,0:T(8,128)S(1)} %get-tuple-element.212.dcommon), custom_call_target="tpu_custom_call" | custom-call | flops 134217728 | bytes 163840 | tf_op jit(solution)/shard_map/pallas_call | solution.py:528
  183.2 2.1 collective-permute-done.34
  186.2 4.0 %shard_map.367 = (bf16[8,64,768]{2,1,0:T(8,128)(2,1)S(1)}, bf16[8,64,768]{2,1,0:T(8,128)(2,1)}) custom-call(s32[1]{0:T(128)} %bitcast.12.me, bf16[1024,1024]{1,0:T(8,128)(2,1)S(1)} %get-tuple-element.163.normed.lhs, bf16[1024,1024]{1,0:T(8,128)(2,1)S(1)} %get-tuple-element.215.dval.rhs), custom_call_target="tpu_custom_call" | custom-call | flops 100663296 | bytes 196608 | tf_op jit(solution)/shard_map/pallas_call | solution.py:489
  202.0 7.8 %shard_map.368 = (bf16[512,1024]{1,0:T(8,128)(2,1)S(1)}, f32[512,1024]{1,0:T(8,128)S(1)}, f32[1,1024]{1,0:T(1,128)S(1)}) custom-call(s32[1]{0:T(128)} %bitcast.rank, bf16[1024,1024]{1,0:T(8,128)(2,1)S(1)} %copy-done.14, bf16[1024,1024]{1,0:T(8,128)(2,1)S(1)} %get-tuple-element.215.dval.rhs, f32[1024,384]{1,0:T(8,128)S(1)} %copy-done.5, ...), custom_call_target="tpu_custom_call" | custom-call | flops 369098752 | bytes 393728 | tf_op jit(solution)/shard_map/pallas_call | solution.py:923
  214.7 7.9 %collective-permute-done.37 = bf16[4,64,768]{2,1,0:T(8,128)(2,1)} collective-permute-done((bf16[4,64,768]{2,1,0:T(8,128)(2,1)}, bf16[4,64,768]{2,1,0:T(8,128)(2,1)}, u32[]{:S(2)}, u32[]{:S(2)}) %collective-permute-start.37) | collective-permute-done | bytes 393248 | tf_op jit(solution)/shard_map/ppermute | solution.py:48
  227.8 2.7 collective-permute-start.40
  231.9 3.7 %collective-permute-start.45 = (bf16[64,768]{1,0:T(8,128)(2,1)S(1)}, bf16[64,768]{1,0:T(8,128)(2,1)S(1)}, u32[]{:S(2)}, u32[]{:S(2)}) collective-permute-start(bf16[64,768]{1,0:T(8,128)(2,1)S(1)} %get-tuple-element.258), channel_id=1, source_target_pairs={{0,16},{2,18},{4,20},{6,22},{8,24},{10,26},{12,28},{14,30},{16,0},... | collective-permute-start | bytes 294920 | tf_op jit(solution)/shard_map/ppermute | solution.py:48
  235.6 2.6 collective-permute-done.40
  238.2 3.1 %collective-permute-start.46 = (bf16[64,768]{1,0:T(8,128)(2,1)S(1)}, bf16[64,768]{1,0:T(8,128)(2,1)S(1)}, u32[]{:S(2)}, u32[]{:S(2)}) collective-permute-start(bf16[64,768]{1,0:T(8,128)(2,1)S(1)} %get-tuple-element.259), channel_id=1, source_target_pairs={{0,24},{2,26},{4,28},{6,30},{8,16},{10,18},{12,20},{14,22},{16,8},... | collective-permute-start | bytes 294920 | tf_op jit(solution)/shard_map/ppermute | solution.py:48
  243.7 11.6 %collective-permute-done.47 = f32[32,384]{1,0:T(8,128)S(1)} collective-permute-done((f32[32,384]{1,0:T(8,128)S(1)}, f32[32,384]{1,0:T(8,128)S(1)}, u32[]{:S(2)}, u32[]{:S(2)}) %collective-permute-start.47) | collective-permute-done | bytes 49184 | tf_op jit(solution)/shard_map/ppermute | solution.py:48
  260.1 2.4 fusion.6
  263.4 3.6 %collective-permute-done.49 = f32[1,14688]{1,0:T(1,128)S(1)} collective-permute-done((f32[1,14688]{1,0:T(1,128)S(1)}, f32[1,14688]{1,0:T(1,128)S(1)}, u32[]{:S(2)}, u32[]{:S(2)}) %collective-permute-start.49) | collective-permute-done | bytes 58784 | tf_op jit(solution)/shard_map/ppermute | solution.py:48
  267.0 2.1 collective-permute-start.50
  (356 shorter events, 93.1 us)
Async XLA Ops:
  2.5 15.8 %collective-permute-start.1 = (bf16[48,1024]{1,0:T(8,128)(2,1)}, bf16[48,1024]{1,0:T(8,128)(2,1)S(1)}, u32[]{:S(2)}, u32[]{:S(2)}) collective-permute-start(bf16[48,1024]{1,0:T(8,128)(2,1)} %get-tuple-element.317), channel_id=1, source_target_pairs={{0,8},{2,10},{4,12},{6,14},{8,0},{10,2},{12,4},{14,6},{16,24},{18,... | collective-permute-start | bytes 294920 | tf_op jit(solution)/shard_map/ppermute | solution.py:48
  5.5 12.8 %collective-permute-start.2 = (bf16[48,1024]{1,0:T(8,128)(2,1)}, bf16[48,1024]{1,0:T(8,128)(2,1)S(1)}, u32[]{:S(2)}, u32[]{:S(2)}) collective-permute-start(bf16[48,1024]{1,0:T(8,128)(2,1)} %get-tuple-element.317), channel_id=1, source_target_pairs={{0,16},{2,18},{4,20},{6,22},{8,24},{10,26},{12,28},{14,30},{16,0},... | collective-permute-start | bytes 294920 | tf_op jit(solution)/shard_map/ppermute | solution.py:48
  8.1 10.2 %collective-permute-start.3 = (bf16[48,1024]{1,0:T(8,128)(2,1)}, bf16[48,1024]{1,0:T(8,128)(2,1)}, u32[]{:S(2)}, u32[]{:S(2)}) collective-permute-start(bf16[48,1024]{1,0:T(8,128)(2,1)} %get-tuple-element.317), channel_id=1, source_target_pairs={{0,24},{2,26},{4,28},{6,30},{8,16},{10,18},{12,20},{14,22},{16,8},... | collective-permute-start | bytes 294920 | tf_op jit(solution)/shard_map/ppermute | solution.py:48
  15.8 16.1 %collective-permute-start.9 = (bf16[256,1024]{1,0:T(8,128)(2,1)S(1)}, bf16[256,1024]{1,0:T(8,128)(2,1)S(1)}, u32[]{:S(2)}, u32[]{:S(2)}) collective-permute-start(bf16[256,1024]{1,0:T(8,128)(2,1)S(1)} %get-tuple-element.302), channel_id=1, source_target_pairs={{0,1},{1,0},{2,3},{3,2},{4,5},{5,4},{6,7},{7,6},{8,9},{9,8},{10,11... | collective-permute-start | bytes 1572872 | tf_op jit(solution)/shard_map/ppermute | solution.py:48
  16.4 34.5 %collective-permute-start.8 = (bf16[512,1024]{1,0:T(8,128)(2,1)S(1)}, bf16[512,1024]{1,0:T(8,128)(2,1)S(1)}, u32[]{:S(2)}, u32[]{:S(2)}) collective-permute-start(bf16[512,1024]{1,0:T(8,128)(2,1)S(1)} %copy-done.3), channel_id=1, source_target_pairs={{0,1},{1,0},{2,3},{3,2},{4,5},{5,4},{6,7},{7,6},{8,9},{9,8},{10,11... | collective-permute-start | bytes 3145736 | tf_op jit(solution)/shard_map/ppermute | solution.py:48
  19.2 9.3 %collective-permute-start.5 = (bf16[48,1024]{1,0:T(8,128)(2,1)S(1)}, bf16[48,1024]{1,0:T(8,128)(2,1)S(1)}, u32[]{:S(2)}, u32[]{:S(2)}) collective-permute-start(bf16[48,1024]{1,0:T(8,128)(2,1)S(1)} %pad_maximum_fusion.6), channel_id=1, source_target_pairs={{0,16},{2,18},{4,20},{6,22},{8,24},{10,26},{12,28},{14,30},{16,0},... | collective-permute-start | bytes 294920 | tf_op jit(solution)/shard_map/ppermute | solution.py:48
  28.5 24.2 %collective-permute-start.10 = (bf16[4,48,1024]{2,1,0:T(8,128)(2,1)S(1)}, bf16[4,48,1024]{2,1,0:T(8,128)(2,1)}, u32[]{:S(2)}, u32[]{:S(2)}) collective-permute-start(bf16[4,48,1024]{2,1,0:T(8,128)(2,1)S(1)} %pad_maximum_fusion.3.refs_0_), channel_id=1, source_target_pairs={{0,4},{2,6},{4,0},{6,2},{8,12},{10,14},{12,8},{14,10},{16,20},{18,... | collective-permute-start | bytes 1179656 | tf_op jit(solution)/shard_map/ppermute | solution.py:48
  30.2 12.3 %collective-permute-start.7 = (bf16[4,48,1024]{2,1,0:T(8,128)(2,1)S(1)}, bf16[4,48,1024]{2,1,0:T(8,128)(2,1)}, u32[]{:S(2)}, u32[]{:S(2)}) collective-permute-start(bf16[4,48,1024]{2,1,0:T(8,128)(2,1)S(1)} %pad_maximum_fusion.4.refs_4_), channel_id=1, source_target_pairs={{0,4},{2,6},{4,0},{6,2},{8,12},{10,14},{12,8},{14,10},{16,20},{18,... | collective-permute-start | bytes 1179656 | tf_op jit(solution)/shard_map/ppermute | solution.py:48
  30.8 21.8 %collective-permute-start.15 = (bf16[128,1024]{1,0:T(8,128)(2,1)S(1)}, bf16[128,1024]{1,0:T(8,128)(2,1)S(1)}, u32[]{:S(2)}, u32[]{:S(2)}) collective-permute-start(bf16[128,1024]{1,0:T(8,128)(2,1)S(1)} %pad_maximum_fusion.5), channel_id=1, source_target_pairs={{0,8},{2,10},{4,12},{6,14},{8,0},{10,2},{12,4},{14,6},{16,24},{18,... | collective-permute-start | bytes 786440 | tf_op jit(solution)/shard_map/ppermute | solution.py:48
  32.0 21.2 %collective-permute-start.16 = (bf16[128,1024]{1,0:T(8,128)(2,1)S(1)}, bf16[128,1024]{1,0:T(8,128)(2,1)S(1)}, u32[]{:S(2)}, u32[]{:S(2)}) collective-permute-start(bf16[128,1024]{1,0:T(8,128)(2,1)S(1)} %pad_maximum_fusion.5), channel_id=1, source_target_pairs={{0,16},{2,18},{4,20},{6,22},{8,24},{10,26},{12,28},{14,30},{16,0},... | collective-permute-start | bytes 786440 | tf_op jit(solution)/shard_map/ppermute | solution.py:48
  42.5 10.8 %collective-permute-start.17 = (bf16[128,1024]{1,0:T(8,128)(2,1)S(1)}, bf16[128,1024]{1,0:T(8,128)(2,1)S(1)}, u32[]{:S(2)}, u32[]{:S(2)}) collective-permute-start(bf16[128,1024]{1,0:T(8,128)(2,1)S(1)} %pad_maximum_fusion.5), channel_id=1, source_target_pairs={{0,24},{2,26},{4,28},{6,30},{8,16},{10,18},{12,20},{14,22},{16,8},... | collective-permute-start | bytes 786440 | tf_op jit(solution)/shard_map/ppermute | solution.py:48
  51.9 12.0 %collective-permute-start.18 = (bf16[256,1024]{1,0:T(8,128)(2,1)}, bf16[256,1024]{1,0:T(8,128)(2,1)}, u32[]{:S(2)}, u32[]{:S(2)}) collective-permute-start(bf16[256,1024]{1,0:T(8,128)(2,1)} %get-tuple-element.157), channel_id=1, source_target_pairs={{0,1},{1,0},{2,3},{3,2},{4,5},{5,4},{6,7},{7,6},{8,9},{9,8},{10,11... | collective-permute-start | bytes 1572872 | tf_op jit(solution)/shard_map/ppermute | solution.py:48
  63.9 31.9 %collective-permute-start.19 = (bf16[4,128,1024]{2,1,0:T(8,128)(2,1)S(1)}, bf16[4,128,1024]{2,1,0:T(8,128)(2,1)}, u32[]{:S(2)}, u32[]{:S(2)}) collective-permute-start(bf16[4,128,1024]{2,1,0:T(8,128)(2,1)S(1)} %pad_maximum_fusion.refs_0_), channel_id=1, source_target_pairs={{0,2},{2,0},{4,6},{6,4},{8,10},{10,8},{12,14},{14,12},{16,18},{18,... | collective-permute-start | bytes 3145736 | tf_op jit(solution)/shard_map/ppermute | solution.py:48
  63.9 31.9 %collective-permute-start.20 = (bf16[4,128,1024]{2,1,0:T(8,128)(2,1)S(1)}, bf16[4,128,1024]{2,1,0:T(8,128)(2,1)}, u32[]{:S(2)}, u32[]{:S(2)}) collective-permute-start(bf16[4,128,1024]{2,1,0:T(8,128)(2,1)S(1)} %pad_maximum_fusion.refs_0_), channel_id=1, source_target_pairs={{0,4},{2,6},{4,0},{6,2},{8,12},{10,14},{12,8},{14,10},{16,20},{18,... | collective-permute-start | bytes 3145736 | tf_op jit(solution)/shard_map/ppermute | solution.py:48
  131.1 15.2 %collective-permute-start.25 = (bf16[4,64,1024]{2,1,0:T(8,128)(2,1)S(1)}, bf16[4,64,1024]{2,1,0:T(8,128)(2,1)S(1)}, u32[]{:S(2)}, u32[]{:S(2)}) collective-permute-start(bf16[4,64,1024]{2,1,0:T(8,128)(2,1)S(1)} %get-tuple-element.192), channel_id=1, source_target_pairs={{0,4},{2,6},{4,0},{6,2},{8,12},{10,14},{12,8},{14,10},{16,20},{18,... | collective-permute-start | bytes 1572872 | tf_op jit(solution)/shard_map/ppermute | solution.py:48
  131.7 32.3 %collective-permute-start.26 = (bf16[512,1024]{1,0:T(8,128)(2,1)S(1)}, bf16[512,1024]{1,0:T(8,128)(2,1)S(1)}, u32[]{:S(2)}, u32[]{:S(2)}) collective-permute-start(bf16[512,1024]{1,0:T(8,128)(2,1)S(1)} %slice.247), channel_id=1, source_target_pairs={{0,1},{1,0},{2,3},{3,2},{4,5},{5,4},{6,7},{7,6},{8,9},{9,8},{10,11... | collective-permute-start | bytes 3145736 | tf_op jit(solution)/shard_map/ppermute | solution.py:48
  132.8 31.3 %collective-permute-start.27 = (bf16[4,64,1024]{2,1,0:T(8,128)(2,1)S(1)}, bf16[4,64,1024]{2,1,0:T(8,128)(2,1)S(1)}, u32[]{:S(2)}, u32[]{:S(2)}) collective-permute-start(bf16[4,64,1024]{2,1,0:T(8,128)(2,1)S(1)} %get-tuple-element.199), channel_id=1, source_target_pairs={{0,4},{2,6},{4,0},{6,2},{8,12},{10,14},{12,8},{14,10},{16,20},{18,... | collective-permute-start | bytes 1572872 | tf_op jit(solution)/shard_map/ppermute | solution.py:48
  147.5 16.5 %collective-permute-start.28 = (bf16[64,1024]{1,0:T(8,128)(2,1)S(1)}, bf16[64,1024]{1,0:T(8,128)(2,1)S(1)}, u32[]{:S(2)}, u32[]{:S(2)}) collective-permute-start(bf16[64,1024]{1,0:T(8,128)(2,1)S(1)} %get-tuple-element.309), channel_id=1, source_target_pairs={{0,8},{2,10},{4,12},{6,14},{8,0},{10,2},{12,4},{14,6},{16,24},{18,... | collective-permute-start | bytes 393224 | tf_op jit(solution)/shard_map/ppermute | solution.py:48
  148.2 15.9 %collective-permute-start.29 = (bf16[64,1024]{1,0:T(8,128)(2,1)S(1)}, bf16[64,1024]{1,0:T(8,128)(2,1)S(1)}, u32[]{:S(2)}, u32[]{:S(2)}) collective-permute-start(bf16[64,1024]{1,0:T(8,128)(2,1)S(1)} %get-tuple-element.308), channel_id=1, source_target_pairs={{0,16},{2,18},{4,20},{6,22},{8,24},{10,26},{12,28},{14,30},{16,0},... | collective-permute-start | bytes 393224 | tf_op jit(solution)/shard_map/ppermute | solution.py:48
  151.7 12.4 %collective-permute-start.30 = (bf16[64,1024]{1,0:T(8,128)(2,1)S(1)}, bf16[64,1024]{1,0:T(8,128)(2,1)S(1)}, u32[]{:S(2)}, u32[]{:S(2)}) collective-permute-start(bf16[64,1024]{1,0:T(8,128)(2,1)S(1)} %get-tuple-element.307), channel_id=1, source_target_pairs={{0,24},{2,26},{4,28},{6,30},{8,16},{10,18},{12,20},{14,22},{16,8},... | collective-permute-start | bytes 393224 | tf_op jit(solution)/shard_map/ppermute | solution.py:48
  165.5 13.5 %collective-permute-start.31 = (bf16[64,1024]{1,0:T(8,128)(2,1)S(1)}, bf16[64,1024]{1,0:T(8,128)(2,1)S(1)}, u32[]{:S(2)}, u32[]{:S(2)}) collective-permute-start(bf16[64,1024]{1,0:T(8,128)(2,1)S(1)} %get-tuple-element.306), channel_id=1, source_target_pairs={{0,8},{2,10},{4,12},{6,14},{8,0},{10,2},{12,4},{14,6},{16,24},{18,... | collective-permute-start | bytes 393224 | tf_op jit(solution)/shard_map/ppermute | solution.py:48
  165.8 13.3 %collective-permute-start.32 = (bf16[64,1024]{1,0:T(8,128)(2,1)S(1)}, bf16[64,1024]{1,0:T(8,128)(2,1)S(1)}, u32[]{:S(2)}, u32[]{:S(2)}) collective-permute-start(bf16[64,1024]{1,0:T(8,128)(2,1)S(1)} %get-tuple-element.305), channel_id=1, source_target_pairs={{0,16},{2,18},{4,20},{6,22},{8,24},{10,26},{12,28},{14,30},{16,0},... | collective-permute-start | bytes 393224 | tf_op jit(solution)/shard_map/ppermute | solution.py:48
  169.6 9.5 %collective-permute-start.33 = (bf16[64,1024]{1,0:T(8,128)(2,1)S(1)}, bf16[64,1024]{1,0:T(8,128)(2,1)S(1)}, u32[]{:S(2)}, u32[]{:S(2)}) collective-permute-start(bf16[64,1024]{1,0:T(8,128)(2,1)S(1)} %get-tuple-element.304), channel_id=1, source_target_pairs={{0,24},{2,26},{4,28},{6,30},{8,16},{10,18},{12,20},{14,22},{16,8},... | collective-permute-start | bytes 393224 | tf_op jit(solution)/shard_map/ppermute | solution.py:48
  191.6 19.4 %collective-permute-start.36 = (bf16[4,64,640]{2,1,0:T(8,128)(2,1)}, bf16[4,64,640]{2,1,0:T(8,128)(2,1)S(1)}, u32[]{:S(2)}, u32[]{:S(2)}) collective-permute-start(bf16[4,64,640]{2,1,0:T(8,128)(2,1)} %add_convert_fusion.3), channel_id=1, source_target_pairs={{0,4},{2,6},{4,0},{6,2},{8,12},{10,14},{12,8},{14,10},{16,20},{18,... | collective-permute-start | bytes 983048 | tf_op jit(solution)/shard_map/ppermute | solution.py:48
  211.1 11.5 %collective-permute-start.37 = (bf16[4,64,768]{2,1,0:T(8,128)(2,1)}, bf16[4,64,768]{2,1,0:T(8,128)(2,1)}, u32[]{:S(2)}, u32[]{:S(2)}) collective-permute-start(bf16[4,64,768]{2,1,0:T(8,128)(2,1)} %add_convert_fusion.2), channel_id=1, source_target_pairs={{0,4},{2,6},{4,0},{6,2},{8,12},{10,14},{12,8},{14,10},{16,20},{18,... | collective-permute-start | bytes 1179656 | tf_op jit(solution)/shard_map/ppermute | solution.py:48
  227.8 10.4 %collective-permute-start.40 = (bf16[64,640]{1,0:T(8,128)(2,1)}, bf16[64,640]{1,0:T(8,128)(2,1)S(1)}, u32[]{:S(2)}, u32[]{:S(2)}) collective-permute-start(bf16[64,640]{1,0:T(8,128)(2,1)} %get-tuple-element.243), channel_id=1, source_target_pairs={{0,16},{2,18},{4,20},{6,22},{8,24},{10,26},{12,28},{14,30},{16,0},... | collective-permute-start | bytes 245768 | tf_op jit(solution)/shard_map/ppermute | solution.py:48
  230.5 10.8 %collective-permute-start.41 = (bf16[64,640]{1,0:T(8,128)(2,1)S(1)}, bf16[64,640]{1,0:T(8,128)(2,1)S(1)}, u32[]{:S(2)}, u32[]{:S(2)}) collective-permute-start(bf16[64,640]{1,0:T(8,128)(2,1)S(1)} %get-tuple-element.244), channel_id=1, source_target_pairs={{0,24},{2,26},{4,28},{6,30},{8,16},{10,18},{12,20},{14,22},{16,8},... | collective-permute-start | bytes 245768 | tf_op jit(solution)/shard_map/ppermute | solution.py:48
  230.9 25.7 %collective-permute-start.43 = (bf16[512,1024]{1,0:T(8,128)(2,1)S(1)}, bf16[512,1024]{1,0:T(8,128)(2,1)S(1)}, u32[]{:S(2)}, u32[]{:S(2)}) collective-permute-start(bf16[512,1024]{1,0:T(8,128)(2,1)S(1)} %copy-done.32), channel_id=1, source_target_pairs={{0,1},{1,0},{2,3},{3,2},{4,5},{5,4},{6,7},{7,6},{8,9},{9,8},{10,11... | collective-permute-start | bytes 3145736 | tf_op jit(solution)/shard_map/ppermute | solution.py:48
  231.5 25.0 %collective-permute-start.44 = (bf16[64,768]{1,0:T(8,128)(2,1)S(1)}, bf16[64,768]{1,0:T(8,128)(2,1)S(1)}, u32[]{:S(2)}, u32[]{:S(2)}) collective-permute-start(bf16[64,768]{1,0:T(8,128)(2,1)S(1)} %get-tuple-element.257), channel_id=1, source_target_pairs={{0,8},{2,10},{4,12},{6,14},{8,0},{10,2},{12,4},{14,6},{16,24},{18,... | collective-permute-start | bytes 294920 | tf_op jit(solution)/shard_map/ppermute | solution.py:48
  231.9 24.6 %collective-permute-start.45 = (bf16[64,768]{1,0:T(8,128)(2,1)S(1)}, bf16[64,768]{1,0:T(8,128)(2,1)S(1)}, u32[]{:S(2)}, u32[]{:S(2)}) collective-permute-start(bf16[64,768]{1,0:T(8,128)(2,1)S(1)} %get-tuple-element.258), channel_id=1, source_target_pairs={{0,16},{2,18},{4,20},{6,22},{8,24},{10,26},{12,28},{14,30},{16,0},... | collective-permute-start | bytes 294920 | tf_op jit(solution)/shard_map/ppermute | solution.py:48
  238.2 18.3 %collective-permute-start.46 = (bf16[64,768]{1,0:T(8,128)(2,1)S(1)}, bf16[64,768]{1,0:T(8,128)(2,1)S(1)}, u32[]{:S(2)}, u32[]{:S(2)}) collective-permute-start(bf16[64,768]{1,0:T(8,128)(2,1)S(1)} %get-tuple-element.259), channel_id=1, source_target_pairs={{0,24},{2,26},{4,28},{6,30},{8,16},{10,18},{12,20},{14,22},{16,8},... | collective-permute-start | bytes 294920 | tf_op jit(solution)/shard_map/ppermute | solution.py:48
  242.4 12.8 %collective-permute-start.47 = (f32[32,384]{1,0:T(8,128)S(1)}, f32[32,384]{1,0:T(8,128)S(1)}, u32[]{:S(2)}, u32[]{:S(2)}) collective-permute-start(f32[32,384]{1,0:T(8,128)S(1)} %get-tuple-element.321), channel_id=1, source_target_pairs={{0,1},{1,0},{2,3},{3,2},{4,5},{5,4},{6,7},{7,6},{8,9},{9,8},{10,11... | collective-permute-start | bytes 147464 | tf_op jit(solution)/shard_map/ppermute | solution.py:48
  (97 other events, 897.7 us)

commit v8 on v7

--- a/solution.py
+++ b/solution.py
@@ -521,7 +521,7 @@
 
 
 def value_grad(lhs, dval, dcommon, dp, dp_rank):
-    length, width = dval.shape[0], 256
+    length, width = dval.shape
     depth, extra = lhs.shape[1], dcommon.shape[1]
     block, half, per = depth // dp, dp // CORES, width // 256
     dims = (half, block, width + extra)
@@ -633,33 +633,35 @@
             small_rows += 1
         small = jnp.pad(small, (0, small_rows * width - small.size)).reshape(small_rows, width)
     small_pair = over_tensor(small)
-    token_pieces = pieces_of(residual)
+    cut_rows = rows_here // 2
+
+    def exchange(value):
+        return [swap(value, "tensor", nt, d) for d in range(1, nt)]
+
+    tok_early, tok_late = exchange(residual[:cut_rows]), exchange(residual[cut_rows:])
 
     block_rows = D // dp
     value_shard = jnp.concatenate([inner_proj[1].astype(bf16), small_pair], axis=0)
     cut = -(-value_shard.shape[0] // 32) * 16
-    first_line = gather_line(value_shard[:cut], dp)
+    first_line, *tok_early = tie(gather_line(value_shard[:cut], dp), *tok_early)
     second_shard, first_line = tie(value_shard[cut:], first_line)
     second_line = gather_line(second_shard, dp)
-    second_line, ids = tie(second_line, sequence_ids)
+    second_line, ids, *tok_late = tie(second_line, sequence_ids, *tok_late)
+    token_pieces = [residual] + [
+        jnp.concatenate([early, late], axis=0) for early, late in zip(tok_early, tok_late)
+    ]
     first_near = [first_line] + plane_parts(first_line, dp)
     other_shard = jnp.concatenate(
         [inner_proj[0].astype(bf16), outer_proj.T.astype(bf16)], axis=0
     )
     other_shard, second_line = tie(other_shard, second_line)
     other_line = gather_line(other_shard, dp)
-    cot_cut = rows_here // 2
-    cot_early = [swap(cotangent[:cot_cut], "tensor", nt, d) for d in range(1, nt)]
-    second_line, *rests = tie(
-        second_line, *plane_parts(second_line, dp), *token_pieces, *cot_early
-    )
-    count = len(rests) - 2 * nt + 1
-    second_near = [second_line] + rests[:count]
-    token_pieces, cot_early = rests[count : count + nt], rests[count + nt :]
-    cotangent_now, *token_pieces = tie(cotangent[cot_cut:], *token_pieces)
-    cot_late = [swap(cotangent_now, "tensor", nt, d) for d in range(1, nt)]
+    cot_early, cot_late = exchange(cotangent[:cut_rows]), exchange(cotangent[cut_rows:])
+    second_line, *rests = tie(second_line, *plane_parts(second_line, dp), *cot_early)
+    second_near, cot_early = [second_line] + rests[: 1 - nt], rests[1 - nt :]
     first_all = first_near + [swap(line, "dp", dp, 1) for line in first_near]
     second_all = second_near + [swap(line, "dp", dp, 1) for line in second_near]
+    second_all[-1], *cot_late = tie(second_all[-1], *cot_late)
     full = slice(None)
     moves = [(0, block_rows, full, 0, 1, 0, 0)]
     dims = [(dp, block_rows, width)]
@@ -735,7 +737,7 @@
 
     steps = length // wide
     in_half = lambda i: i % (steps // 2)
-    value_w, other_line, *cot_late = tie(value_w, other_line, *cot_late)
+    value_w, other_line = tie(value_w, other_line)
     cot_pieces = [cotangent] + [
         jnp.concatenate([early, late], axis=0) for early, late in zip(cot_early, cot_late)
     ]
@@ -935,36 +937,17 @@
             scalars=1,
         )(t_me, dgate, dval, dcommon, others, residual, gate_w, value_w, shared_here)
 
+    others = token_pieces[1] if nt == 2 else jnp.concatenate(token_pieces[1:], axis=0)
+    sent, own, pre_grad = input_grad(others, dgate)
+    sent, dval = tie(sent, dval)
+    sent = sent.reshape(nt - 1, rows_here, D)
+    received = [swap(sent[d - 1], "tensor", nt, d) for d in range(1, nt)]
     keep, send = value_grad(normed, dval, dcommon, dp, dp_me)
     line, part = start_sum(keep, send, dp)
-    two = width > 256
-    lines, parts = [line], [part]
-    if two:
-        dval, *parts[0] = tie(dval, *parts[0])
-        keep, send = weight_grad(normed, dval, dp, dp_me, skipped=1)
-        line, part = start_sum(keep, send, dp)
-        lines.append(line)
-        parts.append(part)
-    crossing = [middle_swaps(parts[0], dp)]
-    dgate, *part = tie(dgate, *part)
-    if two:
-        crossing.append(middle_swaps(part, dp))
-    others = token_pieces[1] if nt == 2 else jnp.concatenate(token_pieces[1:], axis=0)
-    sent, own, pre_grad = input_grad(others, dgate)
-    sent = sent.reshape(nt - 1, rows_here, D)
-    received = [swap(sent[d - 1], "tensor", nt, d) for d in range(1, nt)]
+    line, *part = tie(line, *part)
+    crossing = middle_swaps(part, dp)
     small_grads = [item for each_part in back_parts for item in each_part]
-    pre_grad, *rests = tie(pre_grad, *crossing[0], *small_grads)
-    crossing[0], small_grads = rests[: len(crossing[0])], rests[len(crossing[0]) :]
-    block, far = middle_sum(lines[0], crossing[0])
-    pre_grad, *far = tie(pre_grad, *far)
-    blocks, fars = [block], [high_swaps(far, dp)]
-    if two:
-        pre_grad, *crossing[1] = tie(pre_grad, *crossing[1])
-        block, far = middle_sum(lines[1], crossing[1])
-        pre_grad, *far = tie(pre_grad, *far)
-        blocks.append(block)
-        fars.append(high_swaps(far, dp))
+
     dconv, dheads = [sum(small_grads[at::2]) for at in range(2)]
     conv_grad = lax.dynamic_update_slice(
         jnp.pad(dconv[:kernel_rows, width:], ((0, 0), (DI, 0))),
@@ -987,23 +970,25 @@
     for stage, (axis, size, distance) in enumerate(sum_stages(dp, nt)):
         vector = vector + swap(vector, axis, size, distance)
         if stage == 0:
-            vector, *fars[0] = tie(vector, *fars[0])
-            value_sums = [high_sum(blocks[0], fars[0])]
-            vector, outer_block, gate_block = tie(vector, outer_block, gate_block)
+            vector, line, *crossing = tie(vector, line, *crossing)
+            block, far = middle_sum(line, crossing)
+            far = high_swaps(far, dp)
+        if stage == 2:
+            vector, outer_block, gate_block, *received = tie(
+                vector, outer_block, gate_block, *received
+            )
             outer_part = high_sum(outer_block, outer_far)
             gate_part = high_sum(gate_block, gate_far)
-        if stage == 1:
-            vector, *received = tie(vector, *received)
-        if stage == 1 and two:
-            vector, *fars[1] = tie(vector, *fars[1])
-            value_sums.append(high_sum(blocks[1], fars[1]))
-    shared_sum = value_sums[0][:, 256:].reshape(nt, shared_rows, common_width)
+        if stage == 3:
+            vector, *far = tie(vector, *far)
+            value_sum = high_sum(block, far)
+    shared_sum = value_sum[:, width:].reshape(nt, shared_rows, common_width)
     shared_mine = lax.dynamic_index_in_dim(shared_sum, t_rank, 0, False)
     for d in range(1, nt):
         piece = lax.dynamic_index_in_dim(shared_sum, t_rank ^ d, 0, False)
         shared_mine = shared_mine + swap(piece, "tensor", nt, d)
     shared_part = shared_mine[:, : 2 * N + H]
-    value_part = jnp.concatenate([value_sums[0][:, :256]] + value_sums[1:], axis=1)
+    value_part = value_sum[:, :width]
     conv_size = kernel_rows * (DI + 2 * N)
     place = d_rank * nt + t_rank
     conv_part = lax.dynamic_slice_in_dim(

time: 279 us -> 294 us (1.054)
  local copies, waits for them, and re-layouts: 28.9 us -> 53.7 us
  waiting for transfers between devices: 59.4 us -> 54.3 us
    unnamed x157 -> x160, local copies, waits for them, and re-layouts: 19.2 us -> 42.1 us
    ppermute x51 -> x47, waiting for transfers between devices: 59.4 us -> 54.3 us  [swap(): return lax.ppermute(value, axis, [(i, i ^ distance) for i in range(size)])]
    pallas_call x3 -> x2, Pallas kernels: 12.8 us -> 8.78 us  [weight_grad(): call(functools.partial(weight_grad_kernel, dp), (width // 256,), [whole((...]
    ppermute x51 -> x47, starting transfers between devices: 59 us -> 56.9 us  [swap(): return lax.ppermute(value, axis, [(i, i ^ distance) for i in range(size)])]
  transfers between devices with their start and end apart: 51 -> 47, of which waited for: 16 -> 18; matrix products, arithmetic and copies ran while one was open for 11% -> 11% of each run, Pallas kernels for 24% -> 19%
where the time goes in v8:
time: 294 us; the launch traced here: 290 us
  Pallas kernels  96.4 us (33%)
  starting transfers between devices  56.9 us (19%)
  waiting for transfers between devices  54.3 us (18%)
  local copies, waits for them, and re-layouts  53.7 us (18%)
  other arithmetic  26.4 us (9%)
    ppermute x47, starting transfers between devices, swap(): return lax.ppermute(value, axis, [(i, i ^ distance) for i in range(size)])  56.9 us
    ppermute x47, waiting for transfers between devices, swap(): return lax.ppermute(value, axis, [(i, i ^ distance) for i in range(size)])  54.3 us
    unnamed x160, local copies, waits for them, and re-layouts  42.1 us
    pallas_call x3, Pallas kernels, shards(): call(functools.partial(scan_back_kernel, heads_here), (count,), [rows(CHU...  32.4 us
    pallas_call x1, Pallas kernels, shards(): call(functools.partial(scan_kernel, heads_here), (steps,), [rows(wide, D,...  23.3 us
    pallas_call x2, Pallas kernels, weight_grad(): call(functools.partial(weight_grad_kernel, dp), (width // 256,), [whole((...  8.78 us
    pallas_call x1, Pallas kernels, input_grad(): call(functools.partial(input_grad_kernel, away), (nt * per_piece,), [here...  7.68 us
    pallas_call x1, Pallas kernels, value_grad(): call(functools.partial(value_grad_kernel, dp), (per + 1,), [whole((length...  6.81 us
  transfers between devices with their start and end apart: 47, of which 18 were waited for; matrix products, arithmetic and copies ran while one was open for 11% of the time, Pallas kernels for 19%

profile of v8, /device:TPU:0, one launch (start us, length us, event | category | flops | bytes accessed | tf_op | source)
XLA Modules:
  0.0 289.8 jit_solution(2164073473426807549)
XLA Ops:
  1.9 3.1 %collective-permute-start = (bf16[48,1024]{1,0:T(8,128)(2,1)S(1)}, bf16[48,1024]{1,0:T(8,128)(2,1)S(1)}, u32[]{:S(2)}, u32[]{:S(2)}) collective-permute-start(bf16[48,1024]{1,0:T(8,128)(2,1)S(1)} %get-tuple-element.272), channel_id=1, source_target_pairs={{0,8},{2,10},{4,12},{6,14},{8,0},{10,2},{12,4},{14,6},{16,24},{18,... | collective-permute-start | bytes 294920 | tf_op jit(solution)/shard_map/ppermute | solution.py:48
  5.0 2.6 collective-permute-start.1
  13.3 2.2 fusion.46
  20.9 9.6 %collective-permute-done.3 = bf16[256,1024]{1,0:T(8,128)(2,1)S(1)} collective-permute-done((bf16[256,1024]{1,0:T(8,128)(2,1)}, bf16[256,1024]{1,0:T(8,128)(2,1)S(1)}, u32[]{:S(2)}, u32[]{:S(2)}) %collective-permute-start.3) | collective-permute-done | bytes 524320 | tf_op jit(solution)/shard_map/ppermute | solution.py:48
  31.3 3.5 %collective-permute-start.6 = (bf16[48,1024]{1,0:T(8,128)(2,1)S(1)}, bf16[48,1024]{1,0:T(8,128)(2,1)S(1)}, u32[]{:S(2)}, u32[]{:S(2)}) collective-permute-start(bf16[48,1024]{1,0:T(8,128)(2,1)S(1)} %pad_maximum_fusion.6), channel_id=1, source_target_pairs={{0,16},{2,18},{4,20},{6,22},{8,24},{10,26},{12,28},{14,30},{16,0},... | collective-permute-start | bytes 294920 | tf_op jit(solution)/shard_map/ppermute | solution.py:48
  38.4 2.9 collective-permute-done.7
  42.6 3.5 %collective-permute-start.18 = (bf16[128,1024]{1,0:T(8,128)(2,1)S(1)}, bf16[128,1024]{1,0:T(8,128)(2,1)S(1)}, u32[]{:S(2)}, u32[]{:S(2)}) collective-permute-start(bf16[128,1024]{1,0:T(8,128)(2,1)S(1)} %pad_maximum_fusion.5), channel_id=1, source_target_pairs={{0,16},{2,18},{4,20},{6,22},{8,24},{10,26},{12,28},{14,30},{16,0},... | collective-permute-start | bytes 786440 | tf_op jit(solution)/shard_map/ppermute | solution.py:48
  48.1 2.7 collective-permute-done.13
  50.8 3.5 %collective-permute-start.19 = (bf16[128,1024]{1,0:T(8,128)(2,1)S(1)}, bf16[128,1024]{1,0:T(8,128)(2,1)S(1)}, u32[]{:S(2)}, u32[]{:S(2)}) collective-permute-start(bf16[128,1024]{1,0:T(8,128)(2,1)S(1)} %pad_maximum_fusion.5), channel_id=1, source_target_pairs={{0,24},{2,26},{4,28},{6,30},{8,16},{10,18},{12,20},{14,22},{16,8},... | collective-permute-start | bytes 786440 | tf_op jit(solution)/shard_map/ppermute | solution.py:48
  55.5 3.7 %collective-permute-done.18 = bf16[128,1024]{1,0:T(8,128)(2,1)S(1)} collective-permute-done((bf16[128,1024]{1,0:T(8,128)(2,1)S(1)}, bf16[128,1024]{1,0:T(8,128)(2,1)S(1)}, u32[]{:S(2)}, u32[]{:S(2)}) %collective-permute-start.18) | collective-permute-done | bytes 262176 | tf_op jit(solution)/shard_map/ppermute | solution.py:48
  61.5 2.7 pad_maximum_fusion.refs_0_
  76.8 23.3 %shard_map.357 = (bf16[1024,1024]{1,0:T(8,128)(2,1)S(1)}, f32[1024,1280]{1,0:T(8,128)S(1)}, f32[1024,1280]{1,0:T(8,128)S(1)}, bf16[1024,1280]{1,0:T(8,128)(2,1)S...) custom-call(s32[2]{0:T(128)S(1)} %pad_add_fusion.rank, ...), custom_call_target="tpu_custom_call" | custom-call | flops 285212672 | bytes 3014656 | tf_op jit(solution)/shard_map/pallas_call | solution.py:747
  100.2 2.3 copy-done.2
  102.5 2.3 copy-done.4
  113.3 6.6 %shard_map.359 = (f32[1024,1024]{1,0:T(8,128)S(1)}, f32[1024,1024]{1,0:T(8,128)S(1)}, bf16[1024,1024]{1,0:T(8,128)(2,1)S(1)}, f32[8,1024]{1,0:T(8,128)S(1)}) custom-call(s32[1]{0:T(128)} %bitcast.rank, bf16[1024,1024]{1,0:T(8,128)(2,1)S(1)} %get-tuple-element.139.normed.lhs, bf16[512,1024]{1,0:T(8,128)(2,1)S(1)} %copy-done.19, ...), custom_call_target="tpu_custom_call" | custom-call | flops 268435456 | bytes 1314816 | tf_op jit(solution)/shard_map/pallas_call | solution.py:782
  120.5 3.4 %collective-permute-done.23 = f32[8,1024]{1,0:T(8,128)S(1)} collective-permute-done((f32[8,1024]{1,0:T(8,128)S(1)}, f32[8,1024]{1,0:T(8,128)S(1)}, u32[]{:S(2)}, u32[]{:S(2)}) %collective-permute-start.23) | collective-permute-done | bytes 32800 | tf_op jit(solution)/shard_map/ppermute | solution.py:48
  123.9 6.8 %shard_map.360 = (bf16[1024,1024]{1,0:T(8,128)(2,1)S(1)}, bf16[1024,1024]{1,0:T(8,128)(2,1)S(1)}, bf16[1024,1024]{1,0:T(8,128)(2,1)S(1)}, bf16[1024,1024]{1,0:T(8,128)(2,1)S(1)}, f32[1,1024]{1,0:T(1,128)S(1)}) custom-call(s32[1]{0:T(128)} %bitcast.rank, f32[1024,1024]{1,0:T(8,128)S(1)} %get-tuple-element.147.gate_r, ...), custom_call_target="tpu_custom_call" | custom-call | flops 134217728 | bytes 1049088 | tf_op jit(solution)/shard_map/pallas_call | solution.py:811
  130.7 4.3 %shard_map.361 = (bf16[8,64,1024]{2,1,0:T(8,128)(2,1)S(1)}, bf16[8,64,1024]{2,1,0:T(8,128)(2,1)S(1)}) custom-call(s32[1]{0:T(128)} %bitcast.10.me, bf16[1024,1024]{1,0:T(8,128)(2,1)S(1)} %get-tuple-element.152.lhs, bf16[1024,1024]{1,0:T(8,128)(2,1)S(1)} %get-tuple-element.153.rhs), custom_call_target="tpu_custom_call" | custom-call | flops 134217728 | bytes 262144 | tf_op jit(solution)/shard_map/pallas_call | solution.py:489
  135.1 4.5 %shard_map.362 = (bf16[8,64,1024]{2,1,0:T(8,128)(2,1)S(1)}, bf16[8,64,1024]{2,1,0:T(8,128)(2,1)S(1)}) custom-call(s32[1]{0:T(128)} %bitcast.10.me, bf16[1024,1024]{1,0:T(8,128)(2,1)S(1)} %get-tuple-element.139.normed.lhs, bf16[1024,1024]{1,0:T(8,128)(2,1)S(1)} %get-tuple-element.158.rhs.dgate), custom_call_target="tpu_custom_call" | custom-call | flops 134217728 | bytes 262144 | tf_op jit(solution)/shard_map/pallas_call | solution.py:489
  152.3 2.5 copy-done.3
  154.8 2.5 copy-done.5
  161.1 11.8 %shard_map.363 = (bf16[1024,1024]{1,0:T(8,128)(2,1)S(1)}, f32[1024,384]{1,0:T(8,128)S(1)}, f32[8,1280]{1,0:T(8,128)S(1)}, f32[8,128]{1,0:T(8,128)S(1)}, f32[128,...) custom-call(s32[1]{0:T(128)} %bitcast.rank, bf16[1024,1024]{1,0:T(8,128)(2,1)S(1)} %copy-done.18, ...), custom_call_target="tpu_custom_call" | custom-call | flops 94371840 | bytes 535552 | tf_op jit(solution)/shard_map/pallas_call | solution.py:850
  174.2 4.1 %collective-permute-start.29 = (bf16[64,1024]{1,0:T(8,128)(2,1)S(1)}, bf16[64,1024]{1,0:T(8,128)(2,1)S(1)}, u32[]{:S(2)}, u32[]{:S(2)}) collective-permute-start(bf16[64,1024]{1,0:T(8,128)(2,1)S(1)} %get-tuple-element.268), channel_id=1, source_target_pairs={{0,8},{2,10},{4,12},{6,14},{8,0},{10,2},{12,4},{14,6},{16,24},{18,... | collective-permute-start | bytes 393224 | tf_op jit(solution)/shard_map/ppermute | solution.py:48
  180.7 11.8 %shard_map.364 = (bf16[1024,1024]{1,0:T(8,128)(2,1)S(1)}, f32[1024,384]{1,0:T(8,128)S(1)}, f32[8,1280]{1,0:T(8,128)S(1)}, f32[8,128]{1,0:T(8,128)S(1)}, f32[128,...) custom-call(s32[1]{0:T(128)} %bitcast.rank, ...), custom_call_target="tpu_custom_call", output_to_operand_aliasing={{0}: (17, {}), {1}: (18, {})} | custom-call | flops 94371840 | bytes 535552 | tf_op jit(solution)/shard_map/pallas_call | solution.py:850
  200.3 8.9 %shard_map.365 = (bf16[1024,1024]{1,0:T(8,128)(2,1)S(1)}, f32[1024,384]{1,0:T(8,128)S(1)}, f32[8,1280]{1,0:T(8,128)S(1)}, f32[8,128]{1,0:T(8,128)S(1)}, f32[128,...) custom-call(s32[1]{0:T(128)} %bitcast.rank, ...), custom_call_target="tpu_custom_call", output_to_operand_aliasing={{0}: (17, {}), {1}: (18, {})} | custom-call | flops 62914560 | bytes 535552 | tf_op jit(solution)/shard_map/pallas_call | solution.py:850
  223.2 7.7 %shard_map.366 = (bf16[512,1024]{1,0:T(8,128)(2,1)S(1)}, f32[512,1024]{1,0:T(8,128)S(1)}, f32[1,1024]{1,0:T(1,128)S(1)}) custom-call(s32[1]{0:T(128)} %bitcast.rank, bf16[1024,1024]{1,0:T(8,128)(2,1)S(1)} %copy-done.25, bf16[1024,1024]{1,0:T(8,128)(2,1)S(1)} %copy-done.10, f32[1024,384]{1,0:T(8,128)S(1)} %copy-done.12, bf16[512,1024]{1,0:T(8,128)(2,1)S(1)} %copy-done.30, ...), custom_call_target="tpu_custom_call" | custom-call | flops 369098752 | bytes 393728 | tf_op jit(solution)/shard_map/pallas_call | solution.py:925
  230.9 6.8 %shard_map.367 = (bf16[8,64,1408]{2,1,0:T(8,128)(2,1)S(1)}, bf16[8,64,1408]{2,1,0:T(8,128)(2,1)S(1)}) custom-call(s32[1]{0:T(128)} %bitcast.10.me, bf16[1024,1024]{1,0:T(8,128)(2,1)S(1)} %copy-done.16, bf16[1024,1024]{1,0:T(8,128)(2,1)S(1)} %copy-done.10, f32[1024,384]{1,0:T(8,128)S(1)} %copy-done.12), custom_call_target="tpu_custom_call" | custom-call | flops 234881024 | bytes 360448 | tf_op jit(solution)/shard_map/pallas_call | solution.py:528
  242.4 17.2 %collective-permute-done.37 = bf16[4,64,1408]{2,1,0:T(8,128)(2,1)S(1)} collective-permute-done((bf16[4,64,1408]{2,1,0:T(8,128)(2,1)S(1)}, bf16[4,64,1408]{2,1,0:T(8,128)(2,1)S(1)}, u32[]{:S(2)}, u32[]{:S(2)}) %collective-permute-start.37) | collective-permute-done | bytes 720928 | tf_op jit(solution)/shard_map/ppermute | solution.py:48
  261.7 2.8 collective-permute-start.43
  268.4 2.5 fusion.6
  274.9 2.9 %collective-permute-done.43 = bf16[64,1408]{1,0:T(8,128)(2,1)S(1)} collective-permute-done((bf16[64,1408]{1,0:T(8,128)(2,1)S(1)}, bf16[64,1408]{1,0:T(8,128)(2,1)S(1)}, u32[]{:S(2)}, u32[]{:S(2)}) %collective-permute-start.43) | collective-permute-done | bytes 180256 | tf_op jit(solution)/shard_map/ppermute | solution.py:48
  278.0 4.3 %collective-permute-start.46 = (f32[1,14688]{1,0:T(1,128)S(1)}, f32[1,14688]{1,0:T(1,128)S(1)}, u32[]{:S(2)}, u32[]{:S(2)}) collective-permute-start(f32[1,14688]{1,0:T(1,128)S(1)} %add.309), channel_id=1, source_target_pairs={{0,16},{2,18},{4,20},{6,22},{8,24},{10,26},{12,28},{14,30},{16,0},... | collective-permute-start | bytes 176264 | tf_op jit(solution)/shard_map/ppermute | solution.py:48
  (346 shorter events, 108.7 us)
Async XLA Ops:
  1.9 17.1 %collective-permute-start = (bf16[48,1024]{1,0:T(8,128)(2,1)S(1)}, bf16[48,1024]{1,0:T(8,128)(2,1)S(1)}, u32[]{:S(2)}, u32[]{:S(2)}) collective-permute-start(bf16[48,1024]{1,0:T(8,128)(2,1)S(1)} %get-tuple-element.272), channel_id=1, source_target_pairs={{0,8},{2,10},{4,12},{6,14},{8,0},{10,2},{12,4},{14,6},{16,24},{18,... | collective-permute-start | bytes 294920 | tf_op jit(solution)/shard_map/ppermute | solution.py:48
  5.0 14.4 %collective-permute-start.1 = (bf16[48,1024]{1,0:T(8,128)(2,1)S(1)}, bf16[48,1024]{1,0:T(8,128)(2,1)S(1)}, u32[]{:S(2)}, u32[]{:S(2)}) collective-permute-start(bf16[48,1024]{1,0:T(8,128)(2,1)S(1)} %get-tuple-element.272), channel_id=1, source_target_pairs={{0,16},{2,18},{4,20},{6,22},{8,24},{10,26},{12,28},{14,30},{16,0},... | collective-permute-start | bytes 294920 | tf_op jit(solution)/shard_map/ppermute | solution.py:48
  7.6 11.8 %collective-permute-start.2 = (bf16[48,1024]{1,0:T(8,128)(2,1)S(1)}, bf16[48,1024]{1,0:T(8,128)(2,1)S(1)}, u32[]{:S(2)}, u32[]{:S(2)}) collective-permute-start(bf16[48,1024]{1,0:T(8,128)(2,1)S(1)} %get-tuple-element.272), channel_id=1, source_target_pairs={{0,24},{2,26},{4,28},{6,30},{8,16},{10,18},{12,20},{14,22},{16,8},... | collective-permute-start | bytes 294920 | tf_op jit(solution)/shard_map/ppermute | solution.py:48
  15.5 15.1 %collective-permute-start.3 = (bf16[256,1024]{1,0:T(8,128)(2,1)}, bf16[256,1024]{1,0:T(8,128)(2,1)S(1)}, u32[]{:S(2)}, u32[]{:S(2)}) collective-permute-start(bf16[256,1024]{1,0:T(8,128)(2,1)} %get-tuple-element.259), channel_id=1, source_target_pairs={{0,1},{1,0},{2,3},{3,2},{4,5},{5,4},{6,7},{7,6},{8,9},{9,8},{10,11... | collective-permute-start | bytes 1572872 | tf_op jit(solution)/shard_map/ppermute | solution.py:48
  17.2 24.7 %collective-permute-start.8 = (bf16[256,1024]{1,0:T(8,128)(2,1)}, bf16[256,1024]{1,0:T(8,128)(2,1)}, u32[]{:S(2)}, u32[]{:S(2)}) collective-permute-start(bf16[256,1024]{1,0:T(8,128)(2,1)} %get-tuple-element.258), channel_id=1, source_target_pairs={{0,1},{1,0},{2,3},{3,2},{4,5},{5,4},{6,7},{7,6},{8,9},{9,8},{10,11... | collective-permute-start | bytes 1572872 | tf_op jit(solution)/shard_map/ppermute | solution.py:48
  19.0 31.8 %collective-permute-start.13 = (bf16[256,1024]{1,0:T(8,128)(2,1)}, bf16[256,1024]{1,0:T(8,128)(2,1)S(1)}, u32[]{:S(2)}, u32[]{:S(2)}) collective-permute-start(bf16[256,1024]{1,0:T(8,128)(2,1)} %get-tuple-element.257), channel_id=1, source_target_pairs={{0,1},{1,0},{2,3},{3,2},{4,5},{5,4},{6,7},{7,6},{8,9},{9,8},{10,11... | collective-permute-start | bytes 1572872 | tf_op jit(solution)/shard_map/ppermute | solution.py:48
  36.1 18.9 %collective-permute-start.9 = (bf16[4,48,1024]{2,1,0:T(8,128)(2,1)S(1)}, bf16[4,48,1024]{2,1,0:T(8,128)(2,1)}, u32[]{:S(2)}, u32[]{:S(2)}) collective-permute-start(bf16[4,48,1024]{2,1,0:T(8,128)(2,1)S(1)} %pad_maximum_fusion.3.refs_0_), channel_id=1, source_target_pairs={{0,4},{2,6},{4,0},{6,2},{8,12},{10,14},{12,8},{14,10},{16,20},{18,... | collective-permute-start | bytes 1179656 | tf_op jit(solution)/shard_map/ppermute | solution.py:48
  41.9 13.1 %collective-permute-start.17 = (bf16[128,1024]{1,0:T(8,128)(2,1)S(1)}, bf16[128,1024]{1,0:T(8,128)(2,1)S(1)}, u32[]{:S(2)}, u32[]{:S(2)}) collective-permute-start(bf16[128,1024]{1,0:T(8,128)(2,1)S(1)} %pad_maximum_fusion.5), channel_id=1, source_target_pairs={{0,8},{2,10},{4,12},{6,14},{8,0},{10,2},{12,4},{14,6},{16,24},{18,... | collective-permute-start | bytes 786440 | tf_op jit(solution)/shard_map/ppermute | solution.py:48
  42.6 16.6 %collective-permute-start.18 = (bf16[128,1024]{1,0:T(8,128)(2,1)S(1)}, bf16[128,1024]{1,0:T(8,128)(2,1)S(1)}, u32[]{:S(2)}, u32[]{:S(2)}) collective-permute-start(bf16[128,1024]{1,0:T(8,128)(2,1)S(1)} %pad_maximum_fusion.5), channel_id=1, source_target_pairs={{0,16},{2,18},{4,20},{6,22},{8,24},{10,26},{12,28},{14,30},{16,0},... | collective-permute-start | bytes 786440 | tf_op jit(solution)/shard_map/ppermute | solution.py:48
  46.2 8.3 %collective-permute-start.12 = (bf16[4,48,1024]{2,1,0:T(8,128)(2,1)S(1)}, bf16[4,48,1024]{2,1,0:T(8,128)(2,1)}, u32[]{:S(2)}, u32[]{:S(2)}) collective-permute-start(bf16[4,48,1024]{2,1,0:T(8,128)(2,1)S(1)} %pad_maximum_fusion.4.refs_4_), channel_id=1, source_target_pairs={{0,4},{2,6},{4,0},{6,2},{8,12},{10,14},{12,8},{14,10},{16,20},{18,... | collective-permute-start | bytes 1179656 | tf_op jit(solution)/shard_map/ppermute | solution.py:48
  50.8 8.4 %collective-permute-start.19 = (bf16[128,1024]{1,0:T(8,128)(2,1)S(1)}, bf16[128,1024]{1,0:T(8,128)(2,1)S(1)}, u32[]{:S(2)}, u32[]{:S(2)}) collective-permute-start(bf16[128,1024]{1,0:T(8,128)(2,1)S(1)} %pad_maximum_fusion.5), channel_id=1, source_target_pairs={{0,24},{2,26},{4,28},{6,30},{8,16},{10,18},{12,20},{14,22},{16,8},... | collective-permute-start | bytes 786440 | tf_op jit(solution)/shard_map/ppermute | solution.py:48
  54.5 11.8 %collective-permute-start.16 = (bf16[256,1024]{1,0:T(8,128)(2,1)}, bf16[256,1024]{1,0:T(8,128)(2,1)}, u32[]{:S(2)}, u32[]{:S(2)}) collective-permute-start(bf16[256,1024]{1,0:T(8,128)(2,1)} %get-tuple-element.256), channel_id=1, source_target_pairs={{0,1},{1,0},{2,3},{3,2},{4,5},{5,4},{6,7},{7,6},{8,9},{9,8},{10,11... | collective-permute-start | bytes 1572872 | tf_op jit(solution)/shard_map/ppermute | solution.py:48
  55.0 11.2 %collective-permute-start.10 = (bf16[4,48,1024]{2,1,0:T(8,128)(2,1)S(1)}, bf16[4,48,1024]{2,1,0:T(8,128)(2,1)}, u32[]{:S(2)}, u32[]{:S(2)}) collective-permute-start(bf16[4,48,1024]{2,1,0:T(8,128)(2,1)S(1)} %pad_maximum_fusion.3.refs_0_), channel_id=1, source_target_pairs={{0,2},{2,0},{4,6},{6,4},{8,10},{10,8},{12,14},{14,12},{16,18},{18,... | collective-permute-start | bytes 1179656 | tf_op jit(solution)/shard_map/ppermute | solution.py:48
  55.0 11.2 %collective-permute-start.11 = (bf16[4,48,1024]{2,1,0:T(8,128)(2,1)}, bf16[4,48,1024]{2,1,0:T(8,128)(2,1)}, u32[]{:S(2)}, u32[]{:S(2)}) collective-permute-start(bf16[4,48,1024]{2,1,0:T(8,128)(2,1)} %collective-permute-done.9.refs_1_), channel_id=1, source_target_pairs={{0,2},{2,0},{4,6},{6,4},{8,10},{10,8},{12,14},{14,12},{16,18},{18,... | collective-permute-start | bytes 1179656 | tf_op jit(solution)/shard_map/ppermute | solution.py:48
  70.5 37.8 %collective-permute-start.20 = (bf16[4,128,1024]{2,1,0:T(8,128)(2,1)}, bf16[4,128,1024]{2,1,0:T(8,128)(2,1)}, u32[]{:S(2)}, u32[]{:S(2)}) collective-permute-start(bf16[4,128,1024]{2,1,0:T(8,128)(2,1)} %pad_maximum_fusion.refs_0_), channel_id=1, source_target_pairs={{0,2},{2,0},{4,6},{6,4},{8,10},{10,8},{12,14},{14,12},{16,18},{18,... | collective-permute-start | bytes 3145736 | tf_op jit(solution)/shard_map/ppermute | solution.py:48
  70.5 37.8 %collective-permute-start.21 = (bf16[4,128,1024]{2,1,0:T(8,128)(2,1)}, bf16[4,128,1024]{2,1,0:T(8,128)(2,1)}, u32[]{:S(2)}, u32[]{:S(2)}) collective-permute-start(bf16[4,128,1024]{2,1,0:T(8,128)(2,1)} %pad_maximum_fusion.refs_0_), channel_id=1, source_target_pairs={{0,4},{2,6},{4,0},{6,2},{8,12},{10,14},{12,8},{14,10},{16,20},{18,... | collective-permute-start | bytes 3145736 | tf_op jit(solution)/shard_map/ppermute | solution.py:48
  145.3 27.6 %collective-permute-start.26 = (bf16[4,64,1024]{2,1,0:T(8,128)(2,1)}, bf16[4,64,1024]{2,1,0:T(8,128)(2,1)}, u32[]{:S(2)}, u32[]{:S(2)}) collective-permute-start(bf16[4,64,1024]{2,1,0:T(8,128)(2,1)} %get-tuple-element.168), channel_id=1, source_target_pairs={{0,4},{2,6},{4,0},{6,2},{8,12},{10,14},{12,8},{14,10},{16,20},{18,... | collective-permute-start | bytes 1572872 | tf_op jit(solution)/shard_map/ppermute | solution.py:48
  147.8 45.4 %collective-permute-start.27 = (bf16[512,1024]{1,0:T(8,128)(2,1)S(1)}, bf16[512,1024]{1,0:T(8,128)(2,1)S(1)}, u32[]{:S(2)}, u32[]{:S(2)}) collective-permute-start(bf16[512,1024]{1,0:T(8,128)(2,1)S(1)} %slice.236), channel_id=1, source_target_pairs={{0,1},{1,0},{2,3},{3,2},{4,5},{5,4},{6,7},{7,6},{8,9},{9,8},{10,11... | collective-permute-start | bytes 3145736 | tf_op jit(solution)/shard_map/ppermute | solution.py:48
  148.5 44.7 %collective-permute-start.28 = (bf16[4,64,1024]{2,1,0:T(8,128)(2,1)S(1)}, bf16[4,64,1024]{2,1,0:T(8,128)(2,1)S(1)}, u32[]{:S(2)}, u32[]{:S(2)}) collective-permute-start(bf16[4,64,1024]{2,1,0:T(8,128)(2,1)S(1)} %copy-done.48), channel_id=1, source_target_pairs={{0,4},{2,6},{4,0},{6,2},{8,12},{10,14},{12,8},{14,10},{16,20},{18,... | collective-permute-start | bytes 1572872 | tf_op jit(solution)/shard_map/ppermute | solution.py:48
  174.2 19.0 %collective-permute-start.29 = (bf16[64,1024]{1,0:T(8,128)(2,1)S(1)}, bf16[64,1024]{1,0:T(8,128)(2,1)S(1)}, u32[]{:S(2)}, u32[]{:S(2)}) collective-permute-start(bf16[64,1024]{1,0:T(8,128)(2,1)S(1)} %get-tuple-element.268), channel_id=1, source_target_pairs={{0,8},{2,10},{4,12},{6,14},{8,0},{10,2},{12,4},{14,6},{16,24},{18,... | collective-permute-start | bytes 393224 | tf_op jit(solution)/shard_map/ppermute | solution.py:48
  178.2 15.0 %collective-permute-start.30 = (bf16[64,1024]{1,0:T(8,128)(2,1)S(1)}, bf16[64,1024]{1,0:T(8,128)(2,1)S(1)}, u32[]{:S(2)}, u32[]{:S(2)}) collective-permute-start(bf16[64,1024]{1,0:T(8,128)(2,1)S(1)} %get-tuple-element.267), channel_id=1, source_target_pairs={{0,16},{2,18},{4,20},{6,22},{8,24},{10,26},{12,28},{14,30},{16,0},... | collective-permute-start | bytes 393224 | tf_op jit(solution)/shard_map/ppermute | solution.py:48
  179.2 14.0 %collective-permute-start.31 = (bf16[64,1024]{1,0:T(8,128)(2,1)S(1)}, bf16[64,1024]{1,0:T(8,128)(2,1)S(1)}, u32[]{:S(2)}, u32[]{:S(2)}) collective-permute-start(bf16[64,1024]{1,0:T(8,128)(2,1)S(1)} %get-tuple-element.266), channel_id=1, source_target_pairs={{0,24},{2,26},{4,28},{6,30},{8,16},{10,18},{12,20},{14,22},{16,8},... | collective-permute-start | bytes 393224 | tf_op jit(solution)/shard_map/ppermute | solution.py:48
  195.9 17.2 %collective-permute-start.32 = (bf16[64,1024]{1,0:T(8,128)(2,1)}, bf16[64,1024]{1,0:T(8,128)(2,1)}, u32[]{:S(2)}, u32[]{:S(2)}) collective-permute-start(bf16[64,1024]{1,0:T(8,128)(2,1)} %get-tuple-element.265), channel_id=1, source_target_pairs={{0,8},{2,10},{4,12},{6,14},{8,0},{10,2},{12,4},{14,6},{16,24},{18,... | collective-permute-start | bytes 393224 | tf_op jit(solution)/shard_map/ppermute | solution.py:48
  197.0 16.1 %collective-permute-start.33 = (bf16[64,1024]{1,0:T(8,128)(2,1)}, bf16[64,1024]{1,0:T(8,128)(2,1)}, u32[]{:S(2)}, u32[]{:S(2)}) collective-permute-start(bf16[64,1024]{1,0:T(8,128)(2,1)} %get-tuple-element.264), channel_id=1, source_target_pairs={{0,16},{2,18},{4,20},{6,22},{8,24},{10,26},{12,28},{14,30},{16,0},... | collective-permute-start | bytes 393224 | tf_op jit(solution)/shard_map/ppermute | solution.py:48
  198.8 14.3 %collective-permute-start.34 = (bf16[64,1024]{1,0:T(8,128)(2,1)}, bf16[64,1024]{1,0:T(8,128)(2,1)}, u32[]{:S(2)}, u32[]{:S(2)}) collective-permute-start(bf16[64,1024]{1,0:T(8,128)(2,1)} %get-tuple-element.263), channel_id=1, source_target_pairs={{0,24},{2,26},{4,28},{6,30},{8,16},{10,18},{12,20},{14,22},{16,8},... | collective-permute-start | bytes 393224 | tf_op jit(solution)/shard_map/ppermute | solution.py:48
  239.5 26.5 %collective-permute-start.40 = (bf16[512,1024]{1,0:T(8,128)(2,1)S(1)}, bf16[512,1024]{1,0:T(8,128)(2,1)S(1)}, u32[]{:S(2)}, u32[]{:S(2)}) collective-permute-start(bf16[512,1024]{1,0:T(8,128)(2,1)S(1)} %get-tuple-element.205), channel_id=1, source_target_pairs={{0,1},{1,0},{2,3},{3,2},{4,5},{5,4},{6,7},{7,6},{8,9},{9,8},{10,11... | collective-permute-start | bytes 3145736 | tf_op jit(solution)/shard_map/ppermute | solution.py:48
  241.4 18.2 %collective-permute-start.37 = (bf16[4,64,1408]{2,1,0:T(8,128)(2,1)S(1)}, bf16[4,64,1408]{2,1,0:T(8,128)(2,1)S(1)}, u32[]{:S(2)}, u32[]{:S(2)}) collective-permute-start(bf16[4,64,1408]{2,1,0:T(8,128)(2,1)S(1)} %get-tuple-element.203), channel_id=1, source_target_pairs={{0,4},{2,6},{4,0},{6,2},{8,12},{10,14},{12,8},{14,10},{16,20},{18,... | collective-permute-start | bytes 2162696 | tf_op jit(solution)/shard_map/ppermute | solution.py:48
  261.5 13.3 %collective-permute-start.42 = (bf16[64,1408]{1,0:T(8,128)(2,1)S(1)}, bf16[64,1408]{1,0:T(8,128)(2,1)S(1)}, u32[]{:S(2)}, u32[]{:S(2)}) collective-permute-start(bf16[64,1408]{1,0:T(8,128)(2,1)S(1)} %get-tuple-element.262), channel_id=1, source_target_pairs={{0,8},{2,10},{4,12},{6,14},{8,0},{10,2},{12,4},{14,6},{16,24},{18,... | collective-permute-start | bytes 540680 | tf_op jit(solution)/shard_map/ppermute | solution.py:48
  261.7 16.1 %collective-permute-start.43 = (bf16[64,1408]{1,0:T(8,128)(2,1)S(1)}, bf16[64,1408]{1,0:T(8,128)(2,1)S(1)}, u32[]{:S(2)}, u32[]{:S(2)}) collective-permute-start(bf16[64,1408]{1,0:T(8,128)(2,1)S(1)} %get-tuple-element.261), channel_id=1, source_target_pairs={{0,16},{2,18},{4,20},{6,22},{8,24},{10,26},{12,28},{14,30},{16,0},... | collective-permute-start | bytes 540680 | tf_op jit(solution)/shard_map/ppermute | solution.py:48
  264.5 13.3 %collective-permute-start.44 = (bf16[64,1408]{1,0:T(8,128)(2,1)S(1)}, bf16[64,1408]{1,0:T(8,128)(2,1)S(1)}, u32[]{:S(2)}, u32[]{:S(2)}) collective-permute-start(bf16[64,1408]{1,0:T(8,128)(2,1)S(1)} %get-tuple-element.260), channel_id=1, source_target_pairs={{0,24},{2,26},{4,28},{6,30},{8,16},{10,18},{12,20},{14,22},{16,8},... | collective-permute-start | bytes 540680 | tf_op jit(solution)/shard_map/ppermute | solution.py:48
  266.1 8.7 %collective-permute-start.41 = (f32[1,14688]{1,0:T(1,128)S(1)}, f32[1,14688]{1,0:T(1,128)S(1)}, u32[]{:S(2)}, u32[]{:S(2)}) collective-permute-start(f32[1,14688]{1,0:T(1,128)S(1)} %add.302), channel_id=1, source_target_pairs={{0,8},{2,10},{4,12},{6,14},{8,0},{10,2},{12,4},{14,6},{16,24},{18,... | collective-permute-start | bytes 176264 | tf_op jit(solution)/shard_map/ppermute | solution.py:48
  278.0 9.2 %collective-permute-start.46 = (f32[1,14688]{1,0:T(1,128)S(1)}, f32[1,14688]{1,0:T(1,128)S(1)}, u32[]{:S(2)}, u32[]{:S(2)}) collective-permute-start(f32[1,14688]{1,0:T(1,128)S(1)} %add.309), channel_id=1, source_target_pairs={{0,16},{2,18},{4,20},{6,22},{8,24},{10,26},{12,28},{14,30},{16,0},... | collective-permute-start | bytes 176264 | tf_op jit(solution)/shard_map/ppermute | solution.py:48
  (93 other events, 614.7 us)

commit v9 on v8

--- a/solution.py
+++ b/solution.py
@@ -633,35 +633,33 @@
             small_rows += 1
         small = jnp.pad(small, (0, small_rows * width - small.size)).reshape(small_rows, width)
     small_pair = over_tensor(small)
-    cut_rows = rows_here // 2
-
-    def exchange(value):
-        return [swap(value, "tensor", nt, d) for d in range(1, nt)]
-
-    tok_early, tok_late = exchange(residual[:cut_rows]), exchange(residual[cut_rows:])
+    token_pieces = pieces_of(residual)
 
     block_rows = D // dp
     value_shard = jnp.concatenate([inner_proj[1].astype(bf16), small_pair], axis=0)
     cut = -(-value_shard.shape[0] // 32) * 16
-    first_line, *tok_early = tie(gather_line(value_shard[:cut], dp), *tok_early)
+    first_line = gather_line(value_shard[:cut], dp)
     second_shard, first_line = tie(value_shard[cut:], first_line)
     second_line = gather_line(second_shard, dp)
-    second_line, ids, *tok_late = tie(second_line, sequence_ids, *tok_late)
-    token_pieces = [residual] + [
-        jnp.concatenate([early, late], axis=0) for early, late in zip(tok_early, tok_late)
-    ]
+    second_line, ids = tie(second_line, sequence_ids)
     first_near = [first_line] + plane_parts(first_line, dp)
     other_shard = jnp.concatenate(
         [inner_proj[0].astype(bf16), outer_proj.T.astype(bf16)], axis=0
     )
     other_shard, second_line = tie(other_shard, second_line)
     other_line = gather_line(other_shard, dp)
-    cot_early, cot_late = exchange(cotangent[:cut_rows]), exchange(cotangent[cut_rows:])
-    second_line, *rests = tie(second_line, *plane_parts(second_line, dp), *cot_early)
-    second_near, cot_early = [second_line] + rests[: 1 - nt], rests[1 - nt :]
+    cot_cut = rows_here // 2
+    cot_early = [swap(cotangent[:cot_cut], "tensor", nt, d) for d in range(1, nt)]
+    second_line, *rests = tie(
+        second_line, *plane_parts(second_line, dp), *token_pieces, *cot_early
+    )
+    count = len(rests) - 2 * nt + 1
+    second_near = [second_line] + rests[:count]
+    token_pieces, cot_early = rests[count : count + nt], rests[count + nt :]
+    cotangent_now, *token_pieces = tie(cotangent[cot_cut:], *token_pieces)
+    cot_late = [swap(cotangent_now, "tensor", nt, d) for d in range(1, nt)]
     first_all = first_near + [swap(line, "dp", dp, 1) for line in first_near]
     second_all = second_near + [swap(line, "dp", dp, 1) for line in second_near]
-    second_all[-1], *cot_late = tie(second_all[-1], *cot_late)
     full = slice(None)
     moves = [(0, block_rows, full, 0, 1, 0, 0)]
     dims = [(dp, block_rows, width)]
@@ -737,7 +735,7 @@
 
     steps = length // wide
     in_half = lambda i: i % (steps // 2)
-    value_w, other_line = tie(value_w, other_line)
+    value_w, other_line, *cot_late = tie(value_w, other_line, *cot_late)
     cot_pieces = [cotangent] + [
         jnp.concatenate([early, late], axis=0) for early, late in zip(cot_early, cot_late)
     ]
@@ -933,7 +931,7 @@
             [shape((nt - 1) * rows_here, D, dtype=bf16), shape(rows_here, D), shape(1, D)],
             [],
             4 * length * D * (width + common_width),
-            24,
+            50,
             scalars=1,
         )(t_me, dgate, dval, dcommon, others, residual, gate_w, value_w, shared_here)
 

time: 294 us -> 286 us (0.973)
  local copies, waits for them, and re-layouts: 53.7 us -> 48.6 us
  starting transfers between devices: 56.9 us -> 53.2 us
  other arithmetic: 26.4 us -> 22.9 us
    pallas_call x1, Pallas kernels: 7.68 us -> 11.8 us  [input_grad(): call(functools.partial(input_grad_kernel, away), (nt * per_piece,), [here...]
    ppermute x47 -> x46, starting transfers between devices: 56.9 us -> 53.2 us  [swap(): return lax.ppermute(value, axis, [(i, i ^ distance) for i in range(size)])]
    unnamed x160 -> x151, local copies, waits for them, and re-layouts: 42.1 us -> 39.1 us
    ppermute x47 -> x46, waiting for transfers between devices: 54.3 us -> 56.5 us  [swap(): return lax.ppermute(value, axis, [(i, i ^ distance) for i in range(size)])]
  transfers between devices with their start and end apart: 47 -> 46, of which waited for: 18 -> 15; matrix products, arithmetic and copies ran while one was open for 11% -> 9% of each run, Pallas kernels for 19% -> 20%
where the time goes in v9:
time: 286 us; the launch traced here: 282 us
  Pallas kernels  98.5 us (34%)
  waiting for transfers between devices  56.5 us (20%)
  starting transfers between devices  53.2 us (19%)
  local copies, waits for them, and re-layouts  48.6 us (17%)
  other arithmetic  22.9 us (8%)
    ppermute x46, waiting for transfers between devices, swap(): return lax.ppermute(value, axis, [(i, i ^ distance) for i in range(size)])  56.5 us
    ppermute x46, starting transfers between devices, swap(): return lax.ppermute(value, axis, [(i, i ^ distance) for i in range(size)])  53.2 us
    unnamed x151, local copies, waits for them, and re-layouts  39.1 us
    pallas_call x3, Pallas kernels, shards(): call(functools.partial(scan_back_kernel, heads_here), (count,), [rows(CHU...  31.8 us
    pallas_call x1, Pallas kernels, shards(): call(functools.partial(scan_kernel, heads_here), (steps,), [rows(wide, D,...  23 us
    pallas_call x1, Pallas kernels, input_grad(): call(functools.partial(input_grad_kernel, away), (nt * per_piece,), [here...  11.8 us
    pallas_call x2, Pallas kernels, weight_grad(): call(functools.partial(weight_grad_kernel, dp), (width // 256,), [whole((...  8.77 us
    pallas_call x1, Pallas kernels, value_grad(): call(functools.partial(value_grad_kernel, dp), (per + 1,), [whole((length...  6.78 us
  transfers between devices with their start and end apart: 46, of which 15 were waited for; matrix products, arithmetic and copies ran while one was open for 9% of the time, Pallas kernels for 20%

profile of v9, /device:TPU:0, one launch (start us, length us, event | category | flops | bytes accessed | tf_op | source)
XLA Modules:
  0.0 281.8 jit_solution(3541380131400650464)
XLA Ops:
  1.8 3.1 %collective-permute-start.1 = (bf16[48,1024]{1,0:T(8,128)(2,1)S(1)}, bf16[48,1024]{1,0:T(8,128)(2,1)S(1)}, u32[]{:S(2)}, u32[]{:S(2)}) collective-permute-start(bf16[48,1024]{1,0:T(8,128)(2,1)S(1)} %get-tuple-element.270), channel_id=1, source_target_pairs={{0,8},{2,10},{4,12},{6,14},{8,0},{10,2},{12,4},{14,6},{16,24},{18,... | collective-permute-start | bytes 294920 | tf_op jit(solution)/shard_map/ppermute | solution.py:48
  4.9 2.6 collective-permute-start.2
  13.2 2.2 fusion.45
  22.3 5.0 %collective-permute-done.5 = bf16[48,1024]{1,0:T(8,128)(2,1)S(1)} collective-permute-done((bf16[48,1024]{1,0:T(8,128)(2,1)S(1)}, bf16[48,1024]{1,0:T(8,128)(2,1)S(1)}, u32[]{:S(2)}, u32[]{:S(2)}) %collective-permute-start.5) | collective-permute-done | bytes 98336 | tf_op jit(solution)/shard_map/ppermute | solution.py:48
  32.5 8.7 %collective-permute-done.7.refs_5_ = bf16[4,48,1024]{2,1,0:T(8,128)(2,1)} collective-permute-done((bf16[4,48,1024]{2,1,0:T(8,128)(2,1)S(1)}, bf16[4,48,1024]{2,1,0:T(8,128)(2,1)}, u32[]{:S(2)}, u32[]{:S(2)}) %collective-permute-start.7) | collective-permute-done | bytes 393248 | tf_op jit(solution)/shard_map/ppermute | solution.py:48
  41.2 3.9 %collective-permute-start.17 = (bf16[128,1024]{1,0:T(8,128)(2,1)S(1)}, bf16[128,1024]{1,0:T(8,128)(2,1)S(1)}, u32[]{:S(2)}, u32[]{:S(2)}) collective-permute-start(bf16[128,1024]{1,0:T(8,128)(2,1)S(1)} %pad_maximum_fusion.5), channel_id=1, source_target_pairs={{0,24},{2,26},{4,28},{6,30},{8,16},{10,18},{12,20},{14,22},{16,8},... | collective-permute-start | bytes 786440 | tf_op jit(solution)/shard_map/ppermute | solution.py:48
  45.5 5.2 %collective-permute-done.8.tok1.tok0 = bf16[512,1024]{1,0:T(8,128)(2,1)S(1)} collective-permute-done((bf16[512,1024]{1,0:T(8,128)(2,1)S(1)}, bf16[512,1024]{1,0:T(8,128)(2,1)S(1)}, u32[]{:S(2)}, u32[]{:S(2)}) %collective-permute-start.8) | collective-permute-done | bytes 1048608 | tf_op jit(solution)/shard_map/ppermute | solution.py:48
  60.4 3.3 %collective-permute-done.18 = bf16[256,1024]{1,0:T(8,128)(2,1)} collective-permute-done((bf16[256,1024]{1,0:T(8,128)(2,1)}, bf16[256,1024]{1,0:T(8,128)(2,1)}, u32[]{:S(2)}, u32[]{:S(2)}) %collective-permute-start.18) | collective-permute-done | bytes 524320 | tf_op jit(solution)/shard_map/ppermute | solution.py:48
  70.0 23.0 %shard_map.357 = (bf16[1024,1024]{1,0:T(8,128)(2,1)S(1)}, f32[1024,1280]{1,0:T(8,128)S(1)}, f32[1024,1280]{1,0:T(8,128)S(1)}, bf16[1024,1280]{1,0:T(8,128)(2,1)S...) custom-call(s32[2]{0:T(128)S(1)} %pad_add_fusion.rank, ...), custom_call_target="tpu_custom_call" | custom-call | flops 285212672 | bytes 3014656 | tf_op jit(solution)/shard_map/pallas_call | solution.py:745
  93.0 2.3 copy-done.2
  95.3 2.3 copy-done.4
  106.6 6.3 %shard_map.359 = (f32[1024,1024]{1,0:T(8,128)S(1)}, f32[1024,1024]{1,0:T(8,128)S(1)}, bf16[1024,1024]{1,0:T(8,128)(2,1)S(1)}, f32[8,1024]{1,0:T(8,128)S(1)}) custom-call(s32[1]{0:T(128)} %bitcast.rank, bf16[1024,1024]{1,0:T(8,128)(2,1)S(1)} %get-tuple-element.141.normed.lhs, bf16[512,1024]{1,0:T(8,128)(2,1)S(1)} %copy-done.23, ...), custom_call_target="tpu_custom_call" | custom-call | flops 268435456 | bytes 1314816 | tf_op jit(solution)/shard_map/pallas_call | solution.py:780
  113.6 3.4 %collective-permute-done.22 = f32[8,1024]{1,0:T(8,128)S(1)} collective-permute-done((f32[8,1024]{1,0:T(8,128)S(1)}, f32[8,1024]{1,0:T(8,128)S(1)}, u32[]{:S(2)}, u32[]{:S(2)}) %collective-permute-start.22) | collective-permute-done | bytes 32800 | tf_op jit(solution)/shard_map/ppermute | solution.py:48
  117.0 6.4 %shard_map.360 = (bf16[1024,1024]{1,0:T(8,128)(2,1)S(1)}, bf16[1024,1024]{1,0:T(8,128)(2,1)S(1)}, bf16[1024,1024]{1,0:T(8,128)(2,1)S(1)}, bf16[1024,1024]{1,0:T(8,128)(2,1)S(1)}, f32[1,1024]{1,0:T(1,128)S(1)}) custom-call(s32[1]{0:T(128)} %bitcast.rank, f32[1024,1024]{1,0:T(8,128)S(1)} %get-tuple-element.149.gate_r, ...), custom_call_target="tpu_custom_call" | custom-call | flops 134217728 | bytes 1049088 | tf_op jit(solution)/shard_map/pallas_call | solution.py:809
  124.8 4.3 %shard_map.361 = (bf16[8,64,1024]{2,1,0:T(8,128)(2,1)S(1)}, bf16[8,64,1024]{2,1,0:T(8,128)(2,1)S(1)}) custom-call(s32[1]{0:T(128)} %bitcast.12.me, bf16[1024,1024]{1,0:T(8,128)(2,1)S(1)} %get-tuple-element.154.lhs, bf16[1024,1024]{1,0:T(8,128)(2,1)S(1)} %get-tuple-element.155.rhs), custom_call_target="tpu_custom_call" | custom-call | flops 134217728 | bytes 262144 | tf_op jit(solution)/shard_map/pallas_call | solution.py:489
  129.1 4.5 %shard_map.362 = (bf16[8,64,1024]{2,1,0:T(8,128)(2,1)S(1)}, bf16[8,64,1024]{2,1,0:T(8,128)(2,1)S(1)}) custom-call(s32[1]{0:T(128)} %bitcast.12.me, bf16[1024,1024]{1,0:T(8,128)(2,1)S(1)} %get-tuple-element.141.normed.lhs, bf16[1024,1024]{1,0:T(8,128)(2,1)S(1)} %get-tuple-element.160.rhs.dgate), custom_call_target="tpu_custom_call" | custom-call | flops 134217728 | bytes 262144 | tf_op jit(solution)/shard_map/pallas_call | solution.py:489
  146.2 2.5 copy-done.3
  148.7 2.5 copy-done.5
  151.2 2.2 copy-done.7
  157.0 11.5 %shard_map.363 = (bf16[1024,1024]{1,0:T(8,128)(2,1)S(1)}, f32[1024,384]{1,0:T(8,128)S(1)}, f32[8,1280]{1,0:T(8,128)S(1)}, f32[8,128]{1,0:T(8,128)S(1)}, f32[128,...) custom-call(s32[1]{0:T(128)} %bitcast.rank, bf16[1024,1024]{1,0:T(8,128)(2,1)S(1)} %copy-done.22, ...), custom_call_target="tpu_custom_call" | custom-call | flops 94371840 | bytes 535552 | tf_op jit(solution)/shard_map/pallas_call | solution.py:848
  170.6 3.5 %collective-permute-start.29 = (bf16[64,1024]{1,0:T(8,128)(2,1)S(1)}, bf16[64,1024]{1,0:T(8,128)(2,1)S(1)}, u32[]{:S(2)}, u32[]{:S(2)}) collective-permute-start(bf16[64,1024]{1,0:T(8,128)(2,1)S(1)} %get-tuple-element.267), channel_id=1, source_target_pairs={{0,16},{2,18},{4,20},{6,22},{8,24},{10,26},{12,28},{14,30},{16,0},... | collective-permute-start | bytes 393224 | tf_op jit(solution)/shard_map/ppermute | solution.py:48
  174.4 11.6 %shard_map.364 = (bf16[1024,1024]{1,0:T(8,128)(2,1)S(1)}, f32[1024,384]{1,0:T(8,128)S(1)}, f32[8,1280]{1,0:T(8,128)S(1)}, f32[8,128]{1,0:T(8,128)S(1)}, f32[128,...) custom-call(s32[1]{0:T(128)} %bitcast.rank, ...), custom_call_target="tpu_custom_call", output_to_operand_aliasing={{0}: (17, {}), {1}: (18, {})} | custom-call | flops 94371840 | bytes 535552 | tf_op jit(solution)/shard_map/pallas_call | solution.py:848
  189.7 3.8 %collective-permute-start.32 = (bf16[64,1024]{1,0:T(8,128)(2,1)}, bf16[64,1024]{1,0:T(8,128)(2,1)S(1)}, u32[]{:S(2)}, u32[]{:S(2)}) collective-permute-start(bf16[64,1024]{1,0:T(8,128)(2,1)} %get-tuple-element.264), channel_id=1, source_target_pairs={{0,16},{2,18},{4,20},{6,22},{8,24},{10,26},{12,28},{14,30},{16,0},... | collective-permute-start | bytes 393224 | tf_op jit(solution)/shard_map/ppermute | solution.py:48
  193.8 8.7 %shard_map.365 = (bf16[1024,1024]{1,0:T(8,128)(2,1)S(1)}, f32[1024,384]{1,0:T(8,128)S(1)}, f32[8,1280]{1,0:T(8,128)S(1)}, f32[8,128]{1,0:T(8,128)S(1)}, f32[128,...) custom-call(s32[1]{0:T(128)} %bitcast.rank, ...), custom_call_target="tpu_custom_call", output_to_operand_aliasing={{0}: (17, {}), {1}: (18, {})} | custom-call | flops 62914560 | bytes 535552 | tf_op jit(solution)/shard_map/pallas_call | solution.py:848
  210.0 11.8 %shard_map.366 = (bf16[512,1024]{1,0:T(8,128)(2,1)S(1)}, f32[512,1024]{1,0:T(8,128)}, f32[1,1024]{1,0:T(1,128)S(1)}) custom-call(s32[1]{0:T(128)} %bitcast.rank, bf16[1024,1024]{1,0:T(8,128)(2,1)} %copy-done.27, bf16[1024,1024]{1,0:T(8,128)(2,1)} %copy-done.8, f32[1024,384]{1,0:T(8,128)} %copy-done.12, bf16[512,1024]{1,0:T(8,128)(2,1)S(1)} %copy-done.33, ...), custom_call_target="tpu_custom_call" | custom-call | flops 369098752 | bytes 393728 | tf_op jit(solution)/shard_map/pallas_call | solution.py:923
  221.8 6.8 %shard_map.367 = (bf16[8,64,1408]{2,1,0:T(8,128)(2,1)S(1)}, bf16[8,64,1408]{2,1,0:T(8,128)(2,1)S(1)}) custom-call(s32[1]{0:T(128)} %bitcast.12.me, bf16[1024,1024]{1,0:T(8,128)(2,1)S(1)} %copy-done.20, bf16[1024,1024]{1,0:T(8,128)(2,1)S(1)} %copy-done.9, f32[1024,384]{1,0:T(8,128)S(1)} %copy-done.13), custom_call_target="tpu_custom_call" | custom-call | flops 234881024 | bytes 360448 | tf_op jit(solution)/shard_map/pallas_call | solution.py:528
  233.2 17.2 %collective-permute-done.36 = bf16[4,64,1408]{2,1,0:T(8,128)(2,1)S(1)} collective-permute-done((bf16[4,64,1408]{2,1,0:T(8,128)(2,1)S(1)}, bf16[4,64,1408]{2,1,0:T(8,128)(2,1)S(1)}, u32[]{:S(2)}, u32[]{:S(2)}) %collective-permute-start.36) | collective-permute-done | bytes 720928 | tf_op jit(solution)/shard_map/ppermute | solution.py:48
  252.7 3.8 %collective-permute-start.42 = (bf16[64,1408]{1,0:T(8,128)(2,1)S(1)}, bf16[64,1408]{1,0:T(8,128)(2,1)S(1)}, u32[]{:S(2)}, u32[]{:S(2)}) collective-permute-start(bf16[64,1408]{1,0:T(8,128)(2,1)S(1)} %get-tuple-element.261), channel_id=1, source_target_pairs={{0,16},{2,18},{4,20},{6,22},{8,24},{10,26},{12,28},{14,30},{16,0},... | collective-permute-start | bytes 540680 | tf_op jit(solution)/shard_map/ppermute | solution.py:48
  259.4 2.4 fusion.6
  263.0 2.9 %collective-permute-done.40 = f32[1,14688]{1,0:T(1,128)S(1)} collective-permute-done((f32[1,14688]{1,0:T(1,128)S(1)}, f32[1,14688]{1,0:T(1,128)S(1)}, u32[]{:S(2)}, u32[]{:S(2)}) %collective-permute-start.40) | collective-permute-done | bytes 58784 | tf_op jit(solution)/shard_map/ppermute | solution.py:48
  265.9 3.7 %collective-permute-done.42 = bf16[64,1408]{1,0:T(8,128)(2,1)S(1)} collective-permute-done((bf16[64,1408]{1,0:T(8,128)(2,1)S(1)}, bf16[64,1408]{1,0:T(8,128)(2,1)S(1)}, u32[]{:S(2)}, u32[]{:S(2)}) %collective-permute-start.42) | collective-permute-done | bytes 180256 | tf_op jit(solution)/shard_map/ppermute | solution.py:48
  269.8 4.5 %collective-permute-start.45 = (f32[1,14688]{1,0:T(1,128)S(1)}, f32[1,14688]{1,0:T(1,128)S(1)}, u32[]{:S(2)}, u32[]{:S(2)}) collective-permute-start(f32[1,14688]{1,0:T(1,128)S(1)} %add.309), channel_id=1, source_target_pairs={{0,16},{2,18},{4,20},{6,22},{8,24},{10,26},{12,28},{14,30},{16,0},... | collective-permute-start | bytes 176264 | tf_op jit(solution)/shard_map/ppermute | solution.py:48
  (333 shorter events, 94.0 us)
Async XLA Ops:
  1.8 16.0 %collective-permute-start.1 = (bf16[48,1024]{1,0:T(8,128)(2,1)S(1)}, bf16[48,1024]{1,0:T(8,128)(2,1)S(1)}, u32[]{:S(2)}, u32[]{:S(2)}) collective-permute-start(bf16[48,1024]{1,0:T(8,128)(2,1)S(1)} %get-tuple-element.270), channel_id=1, source_target_pairs={{0,8},{2,10},{4,12},{6,14},{8,0},{10,2},{12,4},{14,6},{16,24},{18,... | collective-permute-start | bytes 294920 | tf_op jit(solution)/shard_map/ppermute | solution.py:48
  4.9 12.9 %collective-permute-start.2 = (bf16[48,1024]{1,0:T(8,128)(2,1)S(1)}, bf16[48,1024]{1,0:T(8,128)(2,1)S(1)}, u32[]{:S(2)}, u32[]{:S(2)}) collective-permute-start(bf16[48,1024]{1,0:T(8,128)(2,1)S(1)} %get-tuple-element.270), channel_id=1, source_target_pairs={{0,16},{2,18},{4,20},{6,22},{8,24},{10,26},{12,28},{14,30},{16,0},... | collective-permute-start | bytes 294920 | tf_op jit(solution)/shard_map/ppermute | solution.py:48
  7.5 10.4 %collective-permute-start.3 = (bf16[48,1024]{1,0:T(8,128)(2,1)S(1)}, bf16[48,1024]{1,0:T(8,128)(2,1)S(1)}, u32[]{:S(2)}, u32[]{:S(2)}) collective-permute-start(bf16[48,1024]{1,0:T(8,128)(2,1)S(1)} %get-tuple-element.270), channel_id=1, source_target_pairs={{0,24},{2,26},{4,28},{6,30},{8,16},{10,18},{12,20},{14,22},{16,8},... | collective-permute-start | bytes 294920 | tf_op jit(solution)/shard_map/ppermute | solution.py:48
  15.4 15.2 %collective-permute-start.9 = (bf16[256,1024]{1,0:T(8,128)(2,1)}, bf16[256,1024]{1,0:T(8,128)(2,1)S(1)}, u32[]{:S(2)}, u32[]{:S(2)}) collective-permute-start(bf16[256,1024]{1,0:T(8,128)(2,1)} %get-tuple-element.258), channel_id=1, source_target_pairs={{0,1},{1,0},{2,3},{3,2},{4,5},{5,4},{6,7},{7,6},{8,9},{9,8},{10,11... | collective-permute-start | bytes 1572872 | tf_op jit(solution)/shard_map/ppermute | solution.py:48
  16.0 34.7 %collective-permute-start.8 = (bf16[512,1024]{1,0:T(8,128)(2,1)S(1)}, bf16[512,1024]{1,0:T(8,128)(2,1)S(1)}, u32[]{:S(2)}, u32[]{:S(2)}) collective-permute-start(bf16[512,1024]{1,0:T(8,128)(2,1)S(1)} %copy-done.10), channel_id=1, source_target_pairs={{0,1},{1,0},{2,3},{3,2},{4,5},{5,4},{6,7},{7,6},{8,9},{9,8},{10,11... | collective-permute-start | bytes 3145736 | tf_op jit(solution)/shard_map/ppermute | solution.py:48
  17.9 9.3 %collective-permute-start.5 = (bf16[48,1024]{1,0:T(8,128)(2,1)S(1)}, bf16[48,1024]{1,0:T(8,128)(2,1)S(1)}, u32[]{:S(2)}, u32[]{:S(2)}) collective-permute-start(bf16[48,1024]{1,0:T(8,128)(2,1)S(1)} %pad_maximum_fusion.6), channel_id=1, source_target_pairs={{0,16},{2,18},{4,20},{6,22},{8,24},{10,26},{12,28},{14,30},{16,0},... | collective-permute-start | bytes 294920 | tf_op jit(solution)/shard_map/ppermute | solution.py:48
  19.7 9.1 %collective-permute-start.6 = (bf16[48,1024]{1,0:T(8,128)(2,1)S(1)}, bf16[48,1024]{1,0:T(8,128)(2,1)S(1)}, u32[]{:S(2)}, u32[]{:S(2)}) collective-permute-start(bf16[48,1024]{1,0:T(8,128)(2,1)S(1)} %pad_maximum_fusion.6), channel_id=1, source_target_pairs={{0,24},{2,26},{4,28},{6,30},{8,16},{10,18},{12,20},{14,22},{16,8},... | collective-permute-start | bytes 294920 | tf_op jit(solution)/shard_map/ppermute | solution.py:48
  21.7 7.1 %collective-permute-start.4 = (bf16[48,1024]{1,0:T(8,128)(2,1)S(1)}, bf16[48,1024]{1,0:T(8,128)(2,1)S(1)}, u32[]{:S(2)}, u32[]{:S(2)}) collective-permute-start(bf16[48,1024]{1,0:T(8,128)(2,1)S(1)} %pad_maximum_fusion.6), channel_id=1, source_target_pairs={{0,8},{2,10},{4,12},{6,14},{8,0},{10,2},{12,4},{14,6},{16,24},{18,... | collective-permute-start | bytes 294920 | tf_op jit(solution)/shard_map/ppermute | solution.py:48
  27.2 25.2 %collective-permute-start.10 = (bf16[4,48,1024]{2,1,0:T(8,128)(2,1)S(1)}, bf16[4,48,1024]{2,1,0:T(8,128)(2,1)}, u32[]{:S(2)}, u32[]{:S(2)}) collective-permute-start(bf16[4,48,1024]{2,1,0:T(8,128)(2,1)S(1)} %pad_maximum_fusion.3.refs_0_), channel_id=1, source_target_pairs={{0,4},{2,6},{4,0},{6,2},{8,12},{10,14},{12,8},{14,10},{16,20},{18,... | collective-permute-start | bytes 1179656 | tf_op jit(solution)/shard_map/ppermute | solution.py:48
  28.9 12.3 %collective-permute-start.7 = (bf16[4,48,1024]{2,1,0:T(8,128)(2,1)S(1)}, bf16[4,48,1024]{2,1,0:T(8,128)(2,1)}, u32[]{:S(2)}, u32[]{:S(2)}) collective-permute-start(bf16[4,48,1024]{2,1,0:T(8,128)(2,1)S(1)} %pad_maximum_fusion.4.refs_4_), channel_id=1, source_target_pairs={{0,4},{2,6},{4,0},{6,2},{8,12},{10,14},{12,8},{14,10},{16,20},{18,... | collective-permute-start | bytes 1179656 | tf_op jit(solution)/shard_map/ppermute | solution.py:48
  29.5 22.9 %collective-permute-start.15 = (bf16[128,1024]{1,0:T(8,128)(2,1)S(1)}, bf16[128,1024]{1,0:T(8,128)(2,1)}, u32[]{:S(2)}, u32[]{:S(2)}) collective-permute-start(bf16[128,1024]{1,0:T(8,128)(2,1)S(1)} %pad_maximum_fusion.5), channel_id=1, source_target_pairs={{0,8},{2,10},{4,12},{6,14},{8,0},{10,2},{12,4},{14,6},{16,24},{18,... | collective-permute-start | bytes 786440 | tf_op jit(solution)/shard_map/ppermute | solution.py:48
  30.7 22.3 %collective-permute-start.16 = (bf16[128,1024]{1,0:T(8,128)(2,1)S(1)}, bf16[128,1024]{1,0:T(8,128)(2,1)S(1)}, u32[]{:S(2)}, u32[]{:S(2)}) collective-permute-start(bf16[128,1024]{1,0:T(8,128)(2,1)S(1)} %pad_maximum_fusion.5), channel_id=1, source_target_pairs={{0,16},{2,18},{4,20},{6,22},{8,24},{10,26},{12,28},{14,30},{16,0},... | collective-permute-start | bytes 786440 | tf_op jit(solution)/shard_map/ppermute | solution.py:48
  41.2 11.9 %collective-permute-start.17 = (bf16[128,1024]{1,0:T(8,128)(2,1)S(1)}, bf16[128,1024]{1,0:T(8,128)(2,1)S(1)}, u32[]{:S(2)}, u32[]{:S(2)}) collective-permute-start(bf16[128,1024]{1,0:T(8,128)(2,1)S(1)} %pad_maximum_fusion.5), channel_id=1, source_target_pairs={{0,24},{2,26},{4,28},{6,30},{8,16},{10,18},{12,20},{14,22},{16,8},... | collective-permute-start | bytes 786440 | tf_op jit(solution)/shard_map/ppermute | solution.py:48
  51.7 12.0 %collective-permute-start.18 = (bf16[256,1024]{1,0:T(8,128)(2,1)}, bf16[256,1024]{1,0:T(8,128)(2,1)}, u32[]{:S(2)}, u32[]{:S(2)}) collective-permute-start(bf16[256,1024]{1,0:T(8,128)(2,1)} %get-tuple-element.135), channel_id=1, source_target_pairs={{0,1},{1,0},{2,3},{3,2},{4,5},{5,4},{6,7},{7,6},{8,9},{9,8},{10,11... | collective-permute-start | bytes 1572872 | tf_op jit(solution)/shard_map/ppermute | solution.py:48
  63.7 38.2 %collective-permute-start.19 = (bf16[4,128,1024]{2,1,0:T(8,128)(2,1)S(1)}, bf16[4,128,1024]{2,1,0:T(8,128)(2,1)}, u32[]{:S(2)}, u32[]{:S(2)}) collective-permute-start(bf16[4,128,1024]{2,1,0:T(8,128)(2,1)S(1)} %pad_maximum_fusion.refs_0_), channel_id=1, source_target_pairs={{0,2},{2,0},{4,6},{6,4},{8,10},{10,8},{12,14},{14,12},{16,18},{18,... | collective-permute-start | bytes 3145736 | tf_op jit(solution)/shard_map/ppermute | solution.py:48
  63.7 38.2 %collective-permute-start.20 = (bf16[4,128,1024]{2,1,0:T(8,128)(2,1)S(1)}, bf16[4,128,1024]{2,1,0:T(8,128)(2,1)}, u32[]{:S(2)}, u32[]{:S(2)}) collective-permute-start(bf16[4,128,1024]{2,1,0:T(8,128)(2,1)S(1)} %pad_maximum_fusion.refs_0_), channel_id=1, source_target_pairs={{0,4},{2,6},{4,0},{6,2},{8,12},{10,14},{12,8},{14,10},{16,20},{18,... | collective-permute-start | bytes 3145736 | tf_op jit(solution)/shard_map/ppermute | solution.py:48
  139.2 29.4 %collective-permute-start.25 = (bf16[4,64,1024]{2,1,0:T(8,128)(2,1)S(1)}, bf16[4,64,1024]{2,1,0:T(8,128)(2,1)}, u32[]{:S(2)}, u32[]{:S(2)}) collective-permute-start(bf16[4,64,1024]{2,1,0:T(8,128)(2,1)S(1)} %get-tuple-element.170), channel_id=1, source_target_pairs={{0,4},{2,6},{4,0},{6,2},{8,12},{10,14},{12,8},{14,10},{16,20},{18,... | collective-permute-start | bytes 1572872 | tf_op jit(solution)/shard_map/ppermute | solution.py:48
  141.6 45.1 %collective-permute-start.26 = (bf16[512,1024]{1,0:T(8,128)(2,1)S(1)}, bf16[512,1024]{1,0:T(8,128)(2,1)S(1)}, u32[]{:S(2)}, u32[]{:S(2)}) collective-permute-start(bf16[512,1024]{1,0:T(8,128)(2,1)S(1)} %slice.228), channel_id=1, source_target_pairs={{0,1},{1,0},{2,3},{3,2},{4,5},{5,4},{6,7},{7,6},{8,9},{9,8},{10,11... | collective-permute-start | bytes 3145736 | tf_op jit(solution)/shard_map/ppermute | solution.py:48
  142.5 44.2 %collective-permute-start.27 = (bf16[4,64,1024]{2,1,0:T(8,128)(2,1)}, bf16[4,64,1024]{2,1,0:T(8,128)(2,1)S(1)}, u32[]{:S(2)}, u32[]{:S(2)}) collective-permute-start(bf16[4,64,1024]{2,1,0:T(8,128)(2,1)} %get-tuple-element.177), channel_id=1, source_target_pairs={{0,4},{2,6},{4,0},{6,2},{8,12},{10,14},{12,8},{14,10},{16,20},{18,... | collective-permute-start | bytes 1572872 | tf_op jit(solution)/shard_map/ppermute | solution.py:48
  170.0 16.8 %collective-permute-start.28 = (bf16[64,1024]{1,0:T(8,128)(2,1)S(1)}, bf16[64,1024]{1,0:T(8,128)(2,1)S(1)}, u32[]{:S(2)}, u32[]{:S(2)}) collective-permute-start(bf16[64,1024]{1,0:T(8,128)(2,1)S(1)} %get-tuple-element.268), channel_id=1, source_target_pairs={{0,8},{2,10},{4,12},{6,14},{8,0},{10,2},{12,4},{14,6},{16,24},{18,... | collective-permute-start | bytes 393224 | tf_op jit(solution)/shard_map/ppermute | solution.py:48
  170.6 16.2 %collective-permute-start.29 = (bf16[64,1024]{1,0:T(8,128)(2,1)S(1)}, bf16[64,1024]{1,0:T(8,128)(2,1)S(1)}, u32[]{:S(2)}, u32[]{:S(2)}) collective-permute-start(bf16[64,1024]{1,0:T(8,128)(2,1)S(1)} %get-tuple-element.267), channel_id=1, source_target_pairs={{0,16},{2,18},{4,20},{6,22},{8,24},{10,26},{12,28},{14,30},{16,0},... | collective-permute-start | bytes 393224 | tf_op jit(solution)/shard_map/ppermute | solution.py:48
  174.1 12.7 %collective-permute-start.30 = (bf16[64,1024]{1,0:T(8,128)(2,1)S(1)}, bf16[64,1024]{1,0:T(8,128)(2,1)S(1)}, u32[]{:S(2)}, u32[]{:S(2)}) collective-permute-start(bf16[64,1024]{1,0:T(8,128)(2,1)S(1)} %get-tuple-element.266), channel_id=1, source_target_pairs={{0,24},{2,26},{4,28},{6,30},{8,16},{10,18},{12,20},{14,22},{16,8},... | collective-permute-start | bytes 393224 | tf_op jit(solution)/shard_map/ppermute | solution.py:48
  189.4 16.9 %collective-permute-start.31 = (bf16[64,1024]{1,0:T(8,128)(2,1)}, bf16[64,1024]{1,0:T(8,128)(2,1)S(1)}, u32[]{:S(2)}, u32[]{:S(2)}) collective-permute-start(bf16[64,1024]{1,0:T(8,128)(2,1)} %get-tuple-element.265), channel_id=1, source_target_pairs={{0,8},{2,10},{4,12},{6,14},{8,0},{10,2},{12,4},{14,6},{16,24},{18,... | collective-permute-start | bytes 393224 | tf_op jit(solution)/shard_map/ppermute | solution.py:48
  189.7 16.7 %collective-permute-start.32 = (bf16[64,1024]{1,0:T(8,128)(2,1)}, bf16[64,1024]{1,0:T(8,128)(2,1)S(1)}, u32[]{:S(2)}, u32[]{:S(2)}) collective-permute-start(bf16[64,1024]{1,0:T(8,128)(2,1)} %get-tuple-element.264), channel_id=1, source_target_pairs={{0,16},{2,18},{4,20},{6,22},{8,24},{10,26},{12,28},{14,30},{16,0},... | collective-permute-start | bytes 393224 | tf_op jit(solution)/shard_map/ppermute | solution.py:48
  193.5 12.9 %collective-permute-start.33 = (bf16[64,1024]{1,0:T(8,128)(2,1)}, bf16[64,1024]{1,0:T(8,128)(2,1)S(1)}, u32[]{:S(2)}, u32[]{:S(2)}) collective-permute-start(bf16[64,1024]{1,0:T(8,128)(2,1)} %get-tuple-element.263), channel_id=1, source_target_pairs={{0,24},{2,26},{4,28},{6,30},{8,16},{10,18},{12,20},{14,22},{16,8},... | collective-permute-start | bytes 393224 | tf_op jit(solution)/shard_map/ppermute | solution.py:48
  230.4 26.7 %collective-permute-start.39 = (bf16[512,1024]{1,0:T(8,128)(2,1)S(1)}, bf16[512,1024]{1,0:T(8,128)(2,1)S(1)}, u32[]{:S(2)}, u32[]{:S(2)}) collective-permute-start(bf16[512,1024]{1,0:T(8,128)(2,1)S(1)} %get-tuple-element.207), channel_id=1, source_target_pairs={{0,1},{1,0},{2,3},{3,2},{4,5},{5,4},{6,7},{7,6},{8,9},{9,8},{10,11... | collective-permute-start | bytes 3145736 | tf_op jit(solution)/shard_map/ppermute | solution.py:48
  232.2 18.2 %collective-permute-start.36 = (bf16[4,64,1408]{2,1,0:T(8,128)(2,1)S(1)}, bf16[4,64,1408]{2,1,0:T(8,128)(2,1)S(1)}, u32[]{:S(2)}, u32[]{:S(2)}) collective-permute-start(bf16[4,64,1408]{2,1,0:T(8,128)(2,1)S(1)} %get-tuple-element.205), channel_id=1, source_target_pairs={{0,4},{2,6},{4,0},{6,2},{8,12},{10,14},{12,8},{14,10},{16,20},{18,... | collective-permute-start | bytes 2162696 | tf_op jit(solution)/shard_map/ppermute | solution.py:48
  252.6 13.3 %collective-permute-start.41 = (bf16[64,1408]{1,0:T(8,128)(2,1)S(1)}, bf16[64,1408]{1,0:T(8,128)(2,1)S(1)}, u32[]{:S(2)}, u32[]{:S(2)}) collective-permute-start(bf16[64,1408]{1,0:T(8,128)(2,1)S(1)} %get-tuple-element.262), channel_id=1, source_target_pairs={{0,8},{2,10},{4,12},{6,14},{8,0},{10,2},{12,4},{14,6},{16,24},{18,... | collective-permute-start | bytes 540680 | tf_op jit(solution)/shard_map/ppermute | solution.py:48
  252.7 16.9 %collective-permute-start.42 = (bf16[64,1408]{1,0:T(8,128)(2,1)S(1)}, bf16[64,1408]{1,0:T(8,128)(2,1)S(1)}, u32[]{:S(2)}, u32[]{:S(2)}) collective-permute-start(bf16[64,1408]{1,0:T(8,128)(2,1)S(1)} %get-tuple-element.261), channel_id=1, source_target_pairs={{0,16},{2,18},{4,20},{6,22},{8,24},{10,26},{12,28},{14,30},{16,0},... | collective-permute-start | bytes 540680 | tf_op jit(solution)/shard_map/ppermute | solution.py:48
  256.5 13.1 %collective-permute-start.43 = (bf16[64,1408]{1,0:T(8,128)(2,1)S(1)}, bf16[64,1408]{1,0:T(8,128)(2,1)S(1)}, u32[]{:S(2)}, u32[]{:S(2)}) collective-permute-start(bf16[64,1408]{1,0:T(8,128)(2,1)S(1)} %get-tuple-element.260), channel_id=1, source_target_pairs={{0,24},{2,26},{4,28},{6,30},{8,16},{10,18},{12,20},{14,22},{16,8},... | collective-permute-start | bytes 540680 | tf_op jit(solution)/shard_map/ppermute | solution.py:48
  257.1 8.7 %collective-permute-start.40 = (f32[1,14688]{1,0:T(1,128)S(1)}, f32[1,14688]{1,0:T(1,128)S(1)}, u32[]{:S(2)}, u32[]{:S(2)}) collective-permute-start(f32[1,14688]{1,0:T(1,128)S(1)} %add.302), channel_id=1, source_target_pairs={{0,8},{2,10},{4,12},{6,14},{8,0},{10,2},{12,4},{14,6},{16,24},{18,... | collective-permute-start | bytes 176264 | tf_op jit(solution)/shard_map/ppermute | solution.py:48
  269.8 9.4 %collective-permute-start.45 = (f32[1,14688]{1,0:T(1,128)S(1)}, f32[1,14688]{1,0:T(1,128)S(1)}, u32[]{:S(2)}, u32[]{:S(2)}) collective-permute-start(f32[1,14688]{1,0:T(1,128)S(1)} %add.309), channel_id=1, source_target_pairs={{0,16},{2,18},{4,20},{6,22},{8,24},{10,26},{12,28},{14,30},{16,0},... | collective-permute-start | bytes 176264 | tf_op jit(solution)/shard_map/ppermute | solution.py:48
  (88 other events, 646.1 us)

commit v10 on v6

--- a/solution.py
+++ b/solution.py
@@ -879,8 +879,6 @@
             gate_far = high_swaps(gate_far, dp)
     dval, dcommon = filled
     dval, *gate_far = tie(dval, *gate_far)
-    outer_part = high_sum(outer_block, outer_far)
-    gate_part = high_sum(gate_block, gate_far)
 
     branch_sum = branch[0].astype(f32)
     for piece in branch_received:
@@ -958,6 +956,9 @@
         vector = vector + swap(vector, axis, size, distance)
         if stage == 0:
             value_sums = [high_sum(blocks[0], fars[0])]
+            vector, outer_block, gate_block = tie(vector, outer_block, gate_block)
+            outer_part = high_sum(outer_block, outer_far)
+            gate_part = high_sum(gate_block, gate_far)
         if stage == 1:
             vector, *received = tie(vector, *received)
         if stage == 1 and two:

time: 270 us -> 271 us (level)
  local copies, waits for them, and re-layouts: 28.2 us -> 33.2 us
  waiting for transfers between devices: 51 us -> 47.1 us
  other arithmetic: 32.8 us -> 29.9 us
    ppermute x47, waiting for transfers between devices: 51 us -> 47.1 us  [swap(): return lax.ppermute(value, axis, [(i, i ^ distance) for i in range(size)])]
    squeeze x0 -> x2, local copies, waits for them, and re-layouts: none -> 3.34 us  [middle_sum(): return (line[0], [part.astype(bf16) for part in line[1:]])]
    unnamed x140 -> x150, local copies, waits for them, and re-layouts: 22.8 us -> 24.4 us
  transfers between devices with their start and end apart: 47 -> 47, of which waited for: 16 -> 17; matrix products, arithmetic and copies ran while one was open for 12% -> 12% of each run, Pallas kernels for 25% -> 25%
where the time goes in v10:
time: 271 us; the launch traced here: 267 us
  Pallas kernels  98.4 us (36%)
  starting transfers between devices  55.8 us (21%)
  waiting for transfers between devices  47.1 us (17%)
  local copies, waits for them, and re-layouts  33.2 us (12%)
  other arithmetic  29.9 us (11%)
    ppermute x47, starting transfers between devices, swap(): return lax.ppermute(value, axis, [(i, i ^ distance) for i in range(size)])  55.8 us
    ppermute x47, waiting for transfers between devices, swap(): return lax.ppermute(value, axis, [(i, i ^ distance) for i in range(size)])  47.1 us
    pallas_call x3, Pallas kernels, shards(): call(functools.partial(scan_back_kernel, heads_here), (count,), [rows(CHU...  32.8 us
    unnamed x150, local copies, waits for them, and re-layouts  24.4 us
    pallas_call x1, Pallas kernels, shards(): call(functools.partial(scan_kernel, heads_here), (steps,), [rows(wide, D,...  23.4 us
    pallas_call x3, Pallas kernels, weight_grad(): call(functools.partial(weight_grad_kernel, dp), (width // 256,), [whole((...  12.8 us
    pallas_call x2, Pallas kernels, input_grad(): call(input_grad_kernel, (count * per_piece,), [rel_rows(width, offset), r...  8.42 us
    pallas_call x1, Pallas kernels, shards(): call(gate_kernel, (steps,), [rows(wide, D), rows(wide, D, in_half), rows(...  8.41 us
  transfers between devices with their start and end apart: 47, of which 17 were waited for; matrix products, arithmetic and copies ran while one was open for 12% of the time, Pallas kernels for 25%

profile of v10, /device:TPU:0, one launch (start us, length us, event | category | flops | bytes accessed | tf_op | source)
XLA Modules:
  0.0 266.7 jit_solution(10434294984610719777)
XLA Ops:
  1.8 3.1 %collective-permute-start.1 = (bf16[48,1024]{1,0:T(8,128)(2,1)S(1)}, bf16[48,1024]{1,0:T(8,128)(2,1)S(1)}, u32[]{:S(2)}, u32[]{:S(2)}) collective-permute-start(bf16[48,1024]{1,0:T(8,128)(2,1)S(1)} %get-tuple-element.309), channel_id=1, source_target_pairs={{0,8},{2,10},{4,12},{6,14},{8,0},{10,2},{12,4},{14,6},{16,24},{18,... | collective-permute-start | bytes 294920 | tf_op jit(solution)/shard_map/ppermute | solution.py:48
  4.9 2.6 collective-permute-start.2
  15.8 2.2 collective-permute-start.5
  21.8 3.3 %collective-permute-done.5 = bf16[48,1024]{1,0:T(8,128)(2,1)S(1)} collective-permute-done((bf16[48,1024]{1,0:T(8,128)(2,1)S(1)}, bf16[48,1024]{1,0:T(8,128)(2,1)S(1)}, u32[]{:S(2)}, u32[]{:S(2)}) %collective-permute-start.5) | collective-permute-done | bytes 98336 | tf_op jit(solution)/shard_map/ppermute | solution.py:48
  26.8 2.2 collective-permute-start.13
  31.2 7.9 %collective-permute-done.7 = bf16[4,48,1024]{2,1,0:T(8,128)(2,1)S(1)} collective-permute-done((bf16[4,48,1024]{2,1,0:T(8,128)(2,1)S(1)}, bf16[4,48,1024]{2,1,0:T(8,128)(2,1)S(1)}, u32[]{:S(2)}, u32[]{:S(2)}) %collective-permute-start.7) | collective-permute-done | bytes 393248 | tf_op jit(solution)/shard_map/ppermute | solution.py:48
  43.0 8.8 %collective-permute-done.14 = bf16[128,1024]{1,0:T(8,128)(2,1)} collective-permute-done((bf16[128,1024]{1,0:T(8,128)(2,1)S(1)}, bf16[128,1024]{1,0:T(8,128)(2,1)}, u32[]{:S(2)}, u32[]{:S(2)}) %collective-permute-start.14) | collective-permute-done | bytes 262176 | tf_op jit(solution)/shard_map/ppermute | solution.py:48
  51.7 2.2 pad_maximum_fusion
  58.1 4.2 %collective-permute-done.15.cot1 = bf16[512,1024]{1,0:T(8,128)(2,1)} collective-permute-done((bf16[512,1024]{1,0:T(8,128)(2,1)}, bf16[512,1024]{1,0:T(8,128)(2,1)}, u32[]{:S(2)}, u32[]{:S(2)}) %collective-permute-start.15) | collective-permute-done | bytes 1048608 | tf_op jit(solution)/shard_map/ppermute | solution.py:48
  67.5 23.4 %shard_map.357 = (bf16[1024,1024]{1,0:T(8,128)(2,1)S(1)}, f32[1024,1280]{1,0:T(8,128)S(1)}, f32[1024,1280]{1,0:T(8,128)S(1)}, bf16[1024,1280]{1,0:T(8,128)(2,1)S...) custom-call(s32[2]{0:T(128)S(1)} %pad_add_fusion.rank, ...), custom_call_target="tpu_custom_call" | custom-call | flops 285212672 | bytes 3014656 | tf_op jit(solution)/shard_map/pallas_call | solution.py:723
  91.0 2.3 copy-done
  96.7 4.1 %collective-permute-done.17.refs_1_ = bf16[8,128,1024]{2,1,0:T(8,128)(2,1)S(1)} collective-permute-done((bf16[8,128,1024]{2,1,0:T(8,128)(2,1)S(1)}, bf16[8,128,1024]{2,1,0:T(8,128)(2,1)S(1)}, u32[]{:S(2)}, u32[]{:S(2)}) %collective-permute-start.17) | collective-permute-done | bytes 2097184 | tf_op jit(solution)/shard_map/ppermute | solution.py:48
  101.2 8.4 %shard_map.359 = (f32[1024,1024]{1,0:T(8,128)S(1)}, f32[1024,1024]{1,0:T(8,128)S(1)}, bf16[1024,1024]{1,0:T(8,128)(2,1)S(1)}, f32[8,1024]{1,0:T(8,128)S(1)}) custom-call(s32[1]{0:T(128)} %bitcast.rank, bf16[1024,1024]{1,0:T(8,128)(2,1)S(1)} %get-tuple-element.160.normed.lhs, bf16[512,1024]{1,0:T(8,128)(2,1)} %cot0, ...), custom_call_target="tpu_custom_call" | custom-call | flops 268435456 | bytes 1314816 | tf_op jit(solution)/shard_map/pallas_call | solution.py:760
  111.0 2.6 collective-permute-done.18
  113.6 6.6 %shard_map.360 = (bf16[1024,1024]{1,0:T(8,128)(2,1)S(1)}, bf16[1024,1024]{1,0:T(8,128)(2,1)S(1)}, bf16[1024,1024]{1,0:T(8,128)(2,1)S(1)}, bf16[1024,1024]{1,0:T(8,128)(2,1)S(1)}, f32[1,1024]{1,0:T(1,128)S(1)}) custom-call(s32[1]{0:T(128)} %bitcast.rank, f32[1024,1024]{1,0:T(8,128)S(1)} %get-tuple-element.167.gate_r, ...), custom_call_target="tpu_custom_call" | custom-call | flops 134217728 | bytes 1049088 | tf_op jit(solution)/shard_map/pallas_call | solution.py:789
  120.3 4.3 %shard_map.361 = (bf16[8,64,1024]{2,1,0:T(8,128)(2,1)S(1)}, bf16[8,64,1024]{2,1,0:T(8,128)(2,1)S(1)}) custom-call(s32[1]{0:T(128)} %bitcast.12.me, bf16[1024,1024]{1,0:T(8,128)(2,1)S(1)} %get-tuple-element.172.lhs, bf16[1024,1024]{1,0:T(8,128)(2,1)S(1)} %get-tuple-element.173.rhs), custom_call_target="tpu_custom_call" | custom-call | flops 134217728 | bytes 262144 | tf_op jit(solution)/shard_map/pallas_call | solution.py:487
  124.6 4.5 %shard_map.362 = (bf16[8,64,1024]{2,1,0:T(8,128)(2,1)S(1)}, bf16[8,64,1024]{2,1,0:T(8,128)(2,1)S(1)}) custom-call(s32[1]{0:T(128)} %bitcast.12.me, bf16[1024,1024]{1,0:T(8,128)(2,1)S(1)} %get-tuple-element.160.normed.lhs, bf16[1024,1024]{1,0:T(8,128)(2,1)S(1)} %get-tuple-element.224.rhs.dgate), custom_call_target="tpu_custom_call" | custom-call | flops 134217728 | bytes 262144 | tf_op jit(solution)/shard_map/pallas_call | solution.py:487
  129.7 2.1 collective-permute-done.20
  137.7 11.9 %shard_map.363 = (bf16[1024,1024]{1,0:T(8,128)(2,1)S(1)}, f32[1024,384]{1,0:T(8,128)S(1)}, f32[8,1280]{1,0:T(8,128)S(1)}, f32[8,128]{1,0:T(8,128)S(1)}, f32[128,...) custom-call(s32[1]{0:T(128)} %bitcast.rank, bf16[1024,1024]{1,0:T(8,128)(2,1)S(1)} %get-tuple-element.181.dssd, ...), custom_call_target="tpu_custom_call" | custom-call | flops 94371840 | bytes 535552 | tf_op jit(solution)/shard_map/pallas_call | solution.py:828
  153.1 2.2 collective-permute-start.26
  155.3 11.8 %shard_map.364 = (bf16[1024,1024]{1,0:T(8,128)(2,1)S(1)}, f32[1024,384]{1,0:T(8,128)S(1)}, f32[8,1280]{1,0:T(8,128)S(1)}, f32[8,128]{1,0:T(8,128)S(1)}, f32[128,...) custom-call(s32[1]{0:T(128)} %bitcast.rank, ...), custom_call_target="tpu_custom_call", output_to_operand_aliasing={{0}: (17, {}), {1}: (18, {})} | custom-call | flops 94371840 | bytes 535552 | tf_op jit(solution)/shard_map/pallas_call | solution.py:828
  170.8 2.2 collective-permute-start.29
  173.1 9.0 %shard_map.365 = (bf16[1024,1024]{1,0:T(8,128)(2,1)S(1)}, f32[1024,384]{1,0:T(8,128)S(1)}, f32[8,1280]{1,0:T(8,128)S(1)}, f32[8,128]{1,0:T(8,128)S(1)}, f32[128,...) custom-call(s32[1]{0:T(128)} %bitcast.rank, ...), custom_call_target="tpu_custom_call", output_to_operand_aliasing={{0}: (17, {}), {1}: (18, {})} | custom-call | flops 62914560 | bytes 535552 | tf_op jit(solution)/shard_map/pallas_call | solution.py:828
  182.1 4.0 %shard_map.366 = (bf16[8,64,640]{2,1,0:T(8,128)(2,1)S(1)}, bf16[8,64,640]{2,1,0:T(8,128)(2,1)S(1)}) custom-call(s32[1]{0:T(128)} %bitcast.12.me, bf16[1024,1024]{1,0:T(8,128)(2,1)S(1)} %get-tuple-element.160.normed.lhs, bf16[1024,1024]{1,0:T(8,128)(2,1)S(1)} %get-tuple-element.212.dval.rhs, f32[1024,384]{1,0:T(8,128)S(1)} %get-tuple-element.208.dcommon), custom_call_target="tpu_custom_call" | custom-call | flops 134217728 | bytes 163840 | tf_op jit(solution)/shard_map/pallas_call | solution.py:526
  189.3 4.0 %shard_map.367 = (bf16[8,64,768]{2,1,0:T(8,128)(2,1)S(1)}, bf16[8,64,768]{2,1,0:T(8,128)(2,1)}) custom-call(s32[1]{0:T(128)} %bitcast.12.me, bf16[1024,1024]{1,0:T(8,128)(2,1)S(1)} %get-tuple-element.160.normed.lhs, bf16[1024,1024]{1,0:T(8,128)(2,1)S(1)} %get-tuple-element.212.dval.rhs), custom_call_target="tpu_custom_call" | custom-call | flops 100663296 | bytes 196608 | tf_op jit(solution)/shard_map/pallas_call | solution.py:487
  194.8 2.1 collective-permute-done.31
  210.2 4.5 %shard_map.368 = (bf16[512,1024]{1,0:T(8,128)(2,1)}, f32[1,1024]{1,0:T(1,128)S(1)}) custom-call(s32[1]{0:T(128)} %bitcast.rank, bf16[1024,1024]{1,0:T(8,128)(2,1)S(1)} %copy-done.14, bf16[1024,1024]{1,0:T(8,128)(2,1)S(1)} %get-tuple-element.212.dval.rhs, f32[1024,384]{1,0:T(8,128)S(1)} %copy-done.2, bf16[512,1024]{1,0:T(8,128)(2,1)S(1)} %copy-done.24, ...), custom_call_target="tpu_custom_call" | custom-call | flops 184549376 | bytes 131584 | tf_op jit(solution)/shard_map/pallas_call | solution.py:891
  229.1 3.9 %shard_map.369 = (f32[512,1024]{1,0:T(8,128)S(1)}, f32[1,1024]{1,0:T(1,128)S(1)}) custom-call(s32[1]{0:T(128)} %bitcast.rank, bf16[1024,1024]{1,0:T(8,128)(2,1)S(1)} %copy-done.15, bf16[1024,1024]{1,0:T(8,128)(2,1)S(1)} %get-tuple-element.212.dval.rhs, f32[1024,384]{1,0:T(8,128)S(1)} %copy-done.3, bf16[512,1024]{1,0:T(8,128)(2,1)S(1)} %copy-done.6, ...), custom_call_target="tpu_custom_call" | custom-call | flops 184549376 | bytes 262656 | tf_op jit(solution)/shard_map/pallas_call | solution.py:891
  238.1 2.9 %collective-permute-start.41 = (bf16[64,768]{1,0:T(8,128)(2,1)S(1)}, bf16[64,768]{1,0:T(8,128)(2,1)S(1)}, u32[]{:S(2)}, u32[]{:S(2)}) collective-permute-start(bf16[64,768]{1,0:T(8,128)(2,1)S(1)} %get-tuple-element.252), channel_id=1, source_target_pairs={{0,16},{2,18},{4,20},{6,22},{8,24},{10,26},{12,28},{14,30},{16,0},... | collective-permute-start | bytes 294920 | tf_op jit(solution)/shard_map/ppermute | solution.py:48
  250.4 4.1 %fusion.6 = (bf16[512,1024]{1,0:T(8,128)(2,1)}, bf16[512,1024]{1,0:T(8,128)(2,1)}) fusion(bf16[512,1024]{1,0:T(8,128)(2,1)S(1)} %copy-done.6, bf16[512,1024]{1,0:T(8,128)(2,1)} %cot0, f32[512,1024]{1,0:T(8,128)S(1)} %get-tuple-element.225, bf16[512,1024]{1,0:T(8,128)(2,1)} %collective-permute-done.39, f32[512]{0:T(512)S(1)} %broadcast_multiply_fusion, ...), kind=kLoop, calls=%fused_computation.9 | loop fusion | flops 8912896 | bytes 9447424 | tf_op jit(solution)/shard_map/convert_element_type | solution.py:993
  256.3 2.6 collective-permute-done.45
  259.0 2.4 collective-permute-start.46
  (344 shorter events, 101.7 us)
Async XLA Ops:
  1.8 13.9 %collective-permute-start.1 = (bf16[48,1024]{1,0:T(8,128)(2,1)S(1)}, bf16[48,1024]{1,0:T(8,128)(2,1)S(1)}, u32[]{:S(2)}, u32[]{:S(2)}) collective-permute-start(bf16[48,1024]{1,0:T(8,128)(2,1)S(1)} %get-tuple-element.309), channel_id=1, source_target_pairs={{0,8},{2,10},{4,12},{6,14},{8,0},{10,2},{12,4},{14,6},{16,24},{18,... | collective-permute-start | bytes 294920 | tf_op jit(solution)/shard_map/ppermute | solution.py:48
  4.9 10.9 %collective-permute-start.2 = (bf16[48,1024]{1,0:T(8,128)(2,1)S(1)}, bf16[48,1024]{1,0:T(8,128)(2,1)S(1)}, u32[]{:S(2)}, u32[]{:S(2)}) collective-permute-start(bf16[48,1024]{1,0:T(8,128)(2,1)S(1)} %get-tuple-element.309), channel_id=1, source_target_pairs={{0,16},{2,18},{4,20},{6,22},{8,24},{10,26},{12,28},{14,30},{16,0},... | collective-permute-start | bytes 294920 | tf_op jit(solution)/shard_map/ppermute | solution.py:48
  7.5 8.3 %collective-permute-start.3 = (bf16[48,1024]{1,0:T(8,128)(2,1)S(1)}, bf16[48,1024]{1,0:T(8,128)(2,1)S(1)}, u32[]{:S(2)}, u32[]{:S(2)}) collective-permute-start(bf16[48,1024]{1,0:T(8,128)(2,1)S(1)} %get-tuple-element.309), channel_id=1, source_target_pairs={{0,24},{2,26},{4,28},{6,30},{8,16},{10,18},{12,20},{14,22},{16,8},... | collective-permute-start | bytes 294920 | tf_op jit(solution)/shard_map/ppermute | solution.py:48
  13.1 26.0 %collective-permute-start.8 = (bf16[512,1024]{1,0:T(8,128)(2,1)}, bf16[512,1024]{1,0:T(8,128)(2,1)S(1)}, u32[]{:S(2)}, u32[]{:S(2)}) collective-permute-start(bf16[512,1024]{1,0:T(8,128)(2,1)} %tok.1), channel_id=1, source_target_pairs={{0,1},{1,0},{2,3},{3,2},{4,5},{5,4},{6,7},{7,6},{8,9},{9,8},{10,11... | collective-permute-start | bytes 3145736 | tf_op jit(solution)/shard_map/ppermute | solution.py:48
  15.8 9.3 %collective-permute-start.5 = (bf16[48,1024]{1,0:T(8,128)(2,1)S(1)}, bf16[48,1024]{1,0:T(8,128)(2,1)S(1)}, u32[]{:S(2)}, u32[]{:S(2)}) collective-permute-start(bf16[48,1024]{1,0:T(8,128)(2,1)S(1)} %pad_maximum_fusion.5), channel_id=1, source_target_pairs={{0,16},{2,18},{4,20},{6,22},{8,24},{10,26},{12,28},{14,30},{16,0},... | collective-permute-start | bytes 294920 | tf_op jit(solution)/shard_map/ppermute | solution.py:48
  18.0 7.1 %collective-permute-start.6 = (bf16[48,1024]{1,0:T(8,128)(2,1)S(1)}, bf16[48,1024]{1,0:T(8,128)(2,1)S(1)}, u32[]{:S(2)}, u32[]{:S(2)}) collective-permute-start(bf16[48,1024]{1,0:T(8,128)(2,1)S(1)} %pad_maximum_fusion.5), channel_id=1, source_target_pairs={{0,24},{2,26},{4,28},{6,30},{8,16},{10,18},{12,20},{14,22},{16,8},... | collective-permute-start | bytes 294920 | tf_op jit(solution)/shard_map/ppermute | solution.py:48
  20.2 10.9 %collective-permute-start.9 = (bf16[4,48,1024]{2,1,0:T(8,128)(2,1)S(1)}, bf16[4,48,1024]{2,1,0:T(8,128)(2,1)S(1)}, u32[]{:S(2)}, u32[]{:S(2)}) collective-permute-start(bf16[4,48,1024]{2,1,0:T(8,128)(2,1)S(1)} %pad_maximum_fusion.2), channel_id=1, source_target_pairs={{0,4},{2,6},{4,0},{6,2},{8,12},{10,14},{12,8},{14,10},{16,20},{18,... | collective-permute-start | bytes 1179656 | tf_op jit(solution)/shard_map/ppermute | solution.py:48
  26.0 14.9 %collective-permute-start.12 = (bf16[128,1024]{1,0:T(8,128)(2,1)S(1)}, bf16[128,1024]{1,0:T(8,128)(2,1)S(1)}, u32[]{:S(2)}, u32[]{:S(2)}) collective-permute-start(bf16[128,1024]{1,0:T(8,128)(2,1)S(1)} %pad_maximum_fusion.4), channel_id=1, source_target_pairs={{0,8},{2,10},{4,12},{6,14},{8,0},{10,2},{12,4},{14,6},{16,24},{18,... | collective-permute-start | bytes 786440 | tf_op jit(solution)/shard_map/ppermute | solution.py:48
  26.8 16.1 %collective-permute-start.13 = (bf16[128,1024]{1,0:T(8,128)(2,1)S(1)}, bf16[128,1024]{1,0:T(8,128)(2,1)}, u32[]{:S(2)}, u32[]{:S(2)}) collective-permute-start(bf16[128,1024]{1,0:T(8,128)(2,1)S(1)} %pad_maximum_fusion.4), channel_id=1, source_target_pairs={{0,16},{2,18},{4,20},{6,22},{8,24},{10,26},{12,28},{14,30},{16,0},... | collective-permute-start | bytes 786440 | tf_op jit(solution)/shard_map/ppermute | solution.py:48
  29.3 9.8 %collective-permute-start.7 = (bf16[4,48,1024]{2,1,0:T(8,128)(2,1)S(1)}, bf16[4,48,1024]{2,1,0:T(8,128)(2,1)S(1)}, u32[]{:S(2)}, u32[]{:S(2)}) collective-permute-start(bf16[4,48,1024]{2,1,0:T(8,128)(2,1)S(1)} %pad_maximum_fusion.3), channel_id=1, source_target_pairs={{0,4},{2,6},{4,0},{6,2},{8,12},{10,14},{12,8},{14,10},{16,20},{18,... | collective-permute-start | bytes 1179656 | tf_op jit(solution)/shard_map/ppermute | solution.py:48
  31.2 22.8 %collective-permute-start.10 = (bf16[8,48,1024]{2,1,0:T(8,128)(2,1)S(1)}, bf16[8,48,1024]{2,1,0:T(8,128)(2,1)}, u32[]{:S(2)}, u32[]{:S(2)}) collective-permute-start(bf16[8,48,1024]{2,1,0:T(8,128)(2,1)S(1)} %constant_dynamic-update-slice_fusion.refs_0_), channel_id=1, source_target_pairs={{0,2},{2,0},{4,6},{6,4},{8,10},{10,8},{12,14},{14,12},{16,18},{18,... | collective-permute-start | bytes 2359304 | tf_op jit(solution)/shard_map/ppermute | solution.py:48
  39.1 23.2 %collective-permute-start.15 = (bf16[512,1024]{1,0:T(8,128)(2,1)}, bf16[512,1024]{1,0:T(8,128)(2,1)}, u32[]{:S(2)}, u32[]{:S(2)}) collective-permute-start(bf16[512,1024]{1,0:T(8,128)(2,1)} %cot0), channel_id=1, source_target_pairs={{0,1},{1,0},{2,3},{3,2},{4,5},{5,4},{6,7},{7,6},{8,9},{9,8},{10,11... | collective-permute-start | bytes 3145736 | tf_op jit(solution)/shard_map/ppermute | solution.py:48
  40.6 13.3 %collective-permute-start.11 = (bf16[8,48,1024]{2,1,0:T(8,128)(2,1)S(1)}, bf16[8,48,1024]{2,1,0:T(8,128)(2,1)}, u32[]{:S(2)}, u32[]{:S(2)}) collective-permute-start(bf16[8,48,1024]{2,1,0:T(8,128)(2,1)S(1)} %constant_dynamic-update-slice_fusion.2.refs_1_), channel_id=1, source_target_pairs={{0,2},{2,0},{4,6},{6,4},{8,10},{10,8},{12,14},{14,12},{16,18},{18,... | collective-permute-start | bytes 2359304 | tf_op jit(solution)/shard_map/ppermute | solution.py:48
  41.0 10.7 %collective-permute-start.14 = (bf16[128,1024]{1,0:T(8,128)(2,1)S(1)}, bf16[128,1024]{1,0:T(8,128)(2,1)}, u32[]{:S(2)}, u32[]{:S(2)}) collective-permute-start(bf16[128,1024]{1,0:T(8,128)(2,1)S(1)} %pad_maximum_fusion.4), channel_id=1, source_target_pairs={{0,24},{2,26},{4,28},{6,30},{8,16},{10,18},{12,20},{14,22},{16,8},... | collective-permute-start | bytes 786440 | tf_op jit(solution)/shard_map/ppermute | solution.py:48
  62.4 33.0 %collective-permute-start.16 = (bf16[4,128,1024]{2,1,0:T(8,128)(2,1)}, bf16[4,128,1024]{2,1,0:T(8,128)(2,1)}, u32[]{:S(2)}, u32[]{:S(2)}) collective-permute-start(bf16[4,128,1024]{2,1,0:T(8,128)(2,1)} %pad_maximum_fusion), channel_id=1, source_target_pairs={{0,4},{2,6},{4,0},{6,2},{8,12},{10,14},{12,8},{14,10},{16,20},{18,... | collective-permute-start | bytes 3145736 | tf_op jit(solution)/shard_map/ppermute | solution.py:48
  133.7 15.9 %collective-permute-start.21 = (bf16[4,64,1024]{2,1,0:T(8,128)(2,1)S(1)}, bf16[4,64,1024]{2,1,0:T(8,128)(2,1)S(1)}, u32[]{:S(2)}, u32[]{:S(2)}) collective-permute-start(bf16[4,64,1024]{2,1,0:T(8,128)(2,1)S(1)} %get-tuple-element.188), channel_id=1, source_target_pairs={{0,4},{2,6},{4,0},{6,2},{8,12},{10,14},{12,8},{14,10},{16,20},{18,... | collective-permute-start | bytes 1572872 | tf_op jit(solution)/shard_map/ppermute | solution.py:48
  134.3 32.8 %collective-permute-start.22 = (bf16[512,1024]{1,0:T(8,128)(2,1)S(1)}, bf16[512,1024]{1,0:T(8,128)(2,1)S(1)}, u32[]{:S(2)}, u32[]{:S(2)}) collective-permute-start(bf16[512,1024]{1,0:T(8,128)(2,1)S(1)} %slice.239), channel_id=1, source_target_pairs={{0,1},{1,0},{2,3},{3,2},{4,5},{5,4},{6,7},{7,6},{8,9},{9,8},{10,11... | collective-permute-start | bytes 3145736 | tf_op jit(solution)/shard_map/ppermute | solution.py:48
  135.9 31.2 %collective-permute-start.23 = (bf16[4,64,1024]{2,1,0:T(8,128)(2,1)S(1)}, bf16[4,64,1024]{2,1,0:T(8,128)(2,1)S(1)}, u32[]{:S(2)}, u32[]{:S(2)}) collective-permute-start(bf16[4,64,1024]{2,1,0:T(8,128)(2,1)S(1)} %get-tuple-element.195), channel_id=1, source_target_pairs={{0,4},{2,6},{4,0},{6,2},{8,12},{10,14},{12,8},{14,10},{16,20},{18,... | collective-permute-start | bytes 1572872 | tf_op jit(solution)/shard_map/ppermute | solution.py:48
  150.9 16.3 %collective-permute-start.24 = (bf16[64,1024]{1,0:T(8,128)(2,1)S(1)}, bf16[64,1024]{1,0:T(8,128)(2,1)S(1)}, u32[]{:S(2)}, u32[]{:S(2)}) collective-permute-start(bf16[64,1024]{1,0:T(8,128)(2,1)S(1)} %get-tuple-element.301), channel_id=1, source_target_pairs={{0,8},{2,10},{4,12},{6,14},{8,0},{10,2},{12,4},{14,6},{16,24},{18,... | collective-permute-start | bytes 393224 | tf_op jit(solution)/shard_map/ppermute | solution.py:48
  152.7 14.4 %collective-permute-start.25 = (bf16[64,1024]{1,0:T(8,128)(2,1)S(1)}, bf16[64,1024]{1,0:T(8,128)(2,1)S(1)}, u32[]{:S(2)}, u32[]{:S(2)}) collective-permute-start(bf16[64,1024]{1,0:T(8,128)(2,1)S(1)} %get-tuple-element.300), channel_id=1, source_target_pairs={{0,16},{2,18},{4,20},{6,22},{8,24},{10,26},{12,28},{14,30},{16,0},... | collective-permute-start | bytes 393224 | tf_op jit(solution)/shard_map/ppermute | solution.py:48
  153.1 14.1 %collective-permute-start.26 = (bf16[64,1024]{1,0:T(8,128)(2,1)S(1)}, bf16[64,1024]{1,0:T(8,128)(2,1)S(1)}, u32[]{:S(2)}, u32[]{:S(2)}) collective-permute-start(bf16[64,1024]{1,0:T(8,128)(2,1)S(1)} %get-tuple-element.299), channel_id=1, source_target_pairs={{0,24},{2,26},{4,28},{6,30},{8,16},{10,18},{12,20},{14,22},{16,8},... | collective-permute-start | bytes 393224 | tf_op jit(solution)/shard_map/ppermute | solution.py:48
  168.6 13.5 %collective-permute-start.27 = (bf16[64,1024]{1,0:T(8,128)(2,1)S(1)}, bf16[64,1024]{1,0:T(8,128)(2,1)S(1)}, u32[]{:S(2)}, u32[]{:S(2)}) collective-permute-start(bf16[64,1024]{1,0:T(8,128)(2,1)S(1)} %get-tuple-element.298), channel_id=1, source_target_pairs={{0,8},{2,10},{4,12},{6,14},{8,0},{10,2},{12,4},{14,6},{16,24},{18,... | collective-permute-start | bytes 393224 | tf_op jit(solution)/shard_map/ppermute | solution.py:48
  169.6 12.5 %collective-permute-start.28 = (bf16[64,1024]{1,0:T(8,128)(2,1)S(1)}, bf16[64,1024]{1,0:T(8,128)(2,1)S(1)}, u32[]{:S(2)}, u32[]{:S(2)}) collective-permute-start(bf16[64,1024]{1,0:T(8,128)(2,1)S(1)} %get-tuple-element.297), channel_id=1, source_target_pairs={{0,16},{2,18},{4,20},{6,22},{8,24},{10,26},{12,28},{14,30},{16,0},... | collective-permute-start | bytes 393224 | tf_op jit(solution)/shard_map/ppermute | solution.py:48
  170.8 11.3 %collective-permute-start.29 = (bf16[64,1024]{1,0:T(8,128)(2,1)S(1)}, bf16[64,1024]{1,0:T(8,128)(2,1)S(1)}, u32[]{:S(2)}, u32[]{:S(2)}) collective-permute-start(bf16[64,1024]{1,0:T(8,128)(2,1)S(1)} %get-tuple-element.296), channel_id=1, source_target_pairs={{0,24},{2,26},{4,28},{6,30},{8,16},{10,18},{12,20},{14,22},{16,8},... | collective-permute-start | bytes 393224 | tf_op jit(solution)/shard_map/ppermute | solution.py:48
  198.8 16.5 %collective-permute-start.32 = (bf16[4,64,640]{2,1,0:T(8,128)(2,1)}, bf16[4,64,640]{2,1,0:T(8,128)(2,1)S(1)}, u32[]{:S(2)}, u32[]{:S(2)}) collective-permute-start(bf16[4,64,640]{2,1,0:T(8,128)(2,1)} %add_convert_fusion.3), channel_id=1, source_target_pairs={{0,4},{2,6},{4,0},{6,2},{8,12},{10,14},{12,8},{14,10},{16,20},{18,... | collective-permute-start | bytes 983048 | tf_op jit(solution)/shard_map/ppermute | solution.py:48
  202.7 30.4 %collective-permute-start.33 = (bf16[4,64,768]{2,1,0:T(8,128)(2,1)}, bf16[4,64,768]{2,1,0:T(8,128)(2,1)}, u32[]{:S(2)}, u32[]{:S(2)}) collective-permute-start(bf16[4,64,768]{2,1,0:T(8,128)(2,1)} %add_convert_fusion.2), channel_id=1, source_target_pairs={{0,4},{2,6},{4,0},{6,2},{8,12},{10,14},{12,8},{14,10},{16,20},{18,... | collective-permute-start | bytes 1179656 | tf_op jit(solution)/shard_map/ppermute | solution.py:48
  214.7 30.3 %collective-permute-start.39 = (bf16[512,1024]{1,0:T(8,128)(2,1)}, bf16[512,1024]{1,0:T(8,128)(2,1)}, u32[]{:S(2)}, u32[]{:S(2)}) collective-permute-start(bf16[512,1024]{1,0:T(8,128)(2,1)} %get-tuple-element.241), channel_id=1, source_target_pairs={{0,1},{1,0},{2,3},{3,2},{4,5},{5,4},{6,7},{7,6},{8,9},{9,8},{10,11... | collective-permute-start | bytes 3145736 | tf_op jit(solution)/shard_map/ppermute | solution.py:48
  217.1 16.0 %collective-permute-start.34 = (bf16[64,640]{1,0:T(8,128)(2,1)}, bf16[64,640]{1,0:T(8,128)(2,1)S(1)}, u32[]{:S(2)}, u32[]{:S(2)}) collective-permute-start(bf16[64,640]{1,0:T(8,128)(2,1)} %get-tuple-element.307), channel_id=1, source_target_pairs={{0,8},{2,10},{4,12},{6,14},{8,0},{10,2},{12,4},{14,6},{16,24},{18,... | collective-permute-start | bytes 245768 | tf_op jit(solution)/shard_map/ppermute | solution.py:48
  218.0 15.1 %collective-permute-start.35 = (bf16[64,640]{1,0:T(8,128)(2,1)}, bf16[64,640]{1,0:T(8,128)(2,1)}, u32[]{:S(2)}, u32[]{:S(2)}) collective-permute-start(bf16[64,640]{1,0:T(8,128)(2,1)} %get-tuple-element.306), channel_id=1, source_target_pairs={{0,16},{2,18},{4,20},{6,22},{8,24},{10,26},{12,28},{14,30},{16,0},... | collective-permute-start | bytes 245768 | tf_op jit(solution)/shard_map/ppermute | solution.py:48
  220.0 13.1 %collective-permute-start.36 = (bf16[64,640]{1,0:T(8,128)(2,1)}, bf16[64,640]{1,0:T(8,128)(2,1)}, u32[]{:S(2)}, u32[]{:S(2)}) collective-permute-start(bf16[64,640]{1,0:T(8,128)(2,1)} %get-tuple-element.305), channel_id=1, source_target_pairs={{0,24},{2,26},{4,28},{6,30},{8,16},{10,18},{12,20},{14,22},{16,8},... | collective-permute-start | bytes 245768 | tf_op jit(solution)/shard_map/ppermute | solution.py:48
  238.1 6.9 %collective-permute-start.40 = (bf16[64,768]{1,0:T(8,128)(2,1)S(1)}, bf16[64,768]{1,0:T(8,128)(2,1)S(1)}, u32[]{:S(2)}, u32[]{:S(2)}) collective-permute-start(bf16[64,768]{1,0:T(8,128)(2,1)S(1)} %get-tuple-element.251), channel_id=1, source_target_pairs={{0,8},{2,10},{4,12},{6,14},{8,0},{10,2},{12,4},{14,6},{16,24},{18,... | collective-permute-start | bytes 294920 | tf_op jit(solution)/shard_map/ppermute | solution.py:48
  238.1 8.4 %collective-permute-start.41 = (bf16[64,768]{1,0:T(8,128)(2,1)S(1)}, bf16[64,768]{1,0:T(8,128)(2,1)S(1)}, u32[]{:S(2)}, u32[]{:S(2)}) collective-permute-start(bf16[64,768]{1,0:T(8,128)(2,1)S(1)} %get-tuple-element.252), channel_id=1, source_target_pairs={{0,16},{2,18},{4,20},{6,22},{8,24},{10,26},{12,28},{14,30},{16,0},... | collective-permute-start | bytes 294920 | tf_op jit(solution)/shard_map/ppermute | solution.py:48
  (88 other events, 655.9 us)
